TPU v7x, 32 devices: a whole 2x2x4 slice. The times are simulated.
32 devices in a mesh: groups: 2 (over y), blk: 4 (over z), rep: 4 (over x, core).
Axes of the slice: x: 2, y: 2, z: 4, core: 2. Of those that a mesh axis runs over, the one named last changes fastest.
Arguments:
- embeddings: float32 [8192, 128], P(('groups', 'blk')), parts along dimension 0, may hold values from -6 to 6
- degrees: int32 [8192], P(('groups', 'blk')), parts along dimension 0, may hold values from 1 to 12800, as said below
- tile_values: bfloat16 [8, 4, 1, 24, 128, 128], P(('groups', 'blk'), 'rep'), parts along dimension 0
- tile_rows: int32 [8, 4, 1, 24], P(('groups', 'blk'), 'rep'), parts along dimension 0, may hold values from 0 to 7
- tile_columns: int32 [8, 4, 1, 24], P(('groups', 'blk'), 'rep'), parts along dimension 0, may hold values from 0 to 7
- slot_counts: int32 [8, 4, 1], P(('groups', 'blk'), 'rep'), parts along dimension 0, may hold values from 6 to 24, as said below
Outputs:
- combined: float32 [8192, 128], P(('groups', 'blk', 'rep')), parts along dimension 0
There are 2 independent parts, one for each index of `groups`. A program takes and returns all parts, laid end to end along the dimension named above; each array names one. Nothing has to cross between parts.
Inputs may be any that keep to these rules, and one draw needn't show every extreme that they name: `degrees`: each node's degree is at least the number of nonzero entries in its row of A. `slot_counts`: some arc position of some device has all 24 slots live in every draw.
All inputs are finite; a program needn't handle non-finite values.
Results may differ from a plain program's by a relative error of at most 0.0003.
Values sent between devices are 32-bit elements; how exact they have to be, the bound alone decides.
No kernel may reach another device: no remote copies, remote signals or barrier semaphores. Data moves between devices by JAX's collectives and lax.ppermute only.
A program may use at most 64 MiB of HBM per device.

v0:
```python
import functools

import jax
import jax.numpy as jnp
from jax import lax
from jax.experimental import pallas as pl
from jax.experimental.pallas import tpu as pltpu
from jax.sharding import PartitionSpec as P

LAYERS = 2
VMEM_LIMIT = 16 * 1024 * 1024
VMEM = pl.BlockSpec(memory_space=pltpu.VMEM)
ANY = pl.BlockSpec(memory_space=pl.ANY)


def pair_teams(team_index, column, team_count):
    columns = team_count // 2
    return 2 * lax.rem(team_index // 2 + column, columns) + lax.rem(team_index, 2)


def source_team(team, turn, team_count):
    if team_count == 4:
        return (2 * (team % 2) + team // 2) ^ turn
    return (team + turn) % team_count


def norm_columns(degrees):
    return jnp.transpose(lax.rsqrt(degrees.astype(jnp.float32)))


def prepare_kernel(degrees_ref, embeddings_ref, tiles_ref, held_tiles_ref, own_ref, norm_ref, panel_ref, sems):
    share_rows, width = own_ref.shape
    block_count, tile_size = degrees_ref.shape
    team_index = lax.axis_index("rep")
    at = pl.ds(pl.multiple_of(team_index * share_rows, share_rows), share_rows)
    tiles_copy = pltpu.make_async_copy(tiles_ref, held_tiles_ref, sems.at[0])
    own_copy = pltpu.make_async_copy(embeddings_ref.at[at, :], own_ref, sems.at[1])
    tiles_copy.start()
    own_copy.start()
    norms = norm_columns(degrees_ref[...])
    for block in range(block_count):
        panel_ref[block * tile_size : (block + 1) * tile_size, :] = jnp.broadcast_to(
            norms[:, block : block + 1], (tile_size, width)
        )
    norm_ref[...] = panel_ref[at, :]
    own_copy.wait()
    tiles_copy.wait()


def prepare(degrees, embeddings, tile_values):
    panel_rows, width = embeddings.shape
    share = jax.ShapeDtypeStruct((panel_rows // lax.axis_size("rep"), width), jnp.float32)
    return pl.pallas_call(
        prepare_kernel,
        out_shape=[jax.ShapeDtypeStruct(tile_values.shape, tile_values.dtype), share, share],
        in_specs=[VMEM, ANY, ANY],
        out_specs=[VMEM] * 3,
        scratch_shapes=[pltpu.VMEM((panel_rows, width), jnp.float32), pltpu.SemaphoreType.DMA((2,))],
        compiler_params=pltpu.CompilerParams(vmem_limit_bytes=VMEM_LIMIT),
        cost_estimate=pl.CostEstimate(
            flops=panel_rows * width, bytes_accessed=4 * panel_rows * width, transcendentals=0
        ),
    )(degrees, embeddings, tile_values)


def arc_kernel(info_ref, tiles_ref, *refs, team_count, piece_count, scaled, partial_count):
    columns = team_count // 2
    pieces, refs = refs[:piece_count], refs[piece_count:]
    partials, refs = refs[:partial_count], refs[partial_count:]
    outs, (table_ref, split_ref, sums_ref, sem) = refs[:team_count], refs[team_count:]
    team_index = lax.axis_index("rep")
    slot_total, tile_size, _ = tiles_ref.shape
    panel_rows, width = split_ref.shape[0], split_ref.shape[1] // 2
    share_rows = panel_rows // team_count
    block_count = panel_rows // tile_size
    table_copy = pltpu.make_async_copy(info_ref, table_ref, sem)
    table_copy.start()

    def split(value, at):
        high = value.astype(jnp.bfloat16)
        split_ref[at, :width] = high
        split_ref[at, width:] = (value - high.astype(jnp.float32)).astype(jnp.bfloat16)

    def split_scaled(degrees_ref, panel_ref):
        norms = norm_columns(degrees_ref[...])
        for block in range(block_count):
            at = pl.ds(block * tile_size, tile_size)
            split(panel_ref[at, :] * norms[:, block : block + 1], at)

    if scaled:

        @pl.when(team_index == 0)
        def _():
            split_scaled(*pieces[:2])

        @pl.when(team_index > 0)
        def _():
            split_scaled(*pieces[2:])
    else:
        for k in range(piece_count):
            owner = source_team(team_index, k, team_count)
            split(pieces[k][...], pl.ds(pl.multiple_of(owner * share_rows, share_rows), share_rows))
    sums_ref[...] = jnp.zeros_like(sums_ref)
    table_copy.wait()
    live_count = table_ref[0]
    for j in range(slot_total):
        source = pl.multiple_of(table_ref[1 + slot_total + j] * tile_size, tile_size)
        product = jnp.dot(
            tiles_ref[j],
            split_ref[pl.ds(source, tile_size), :],
            preferred_element_type=jnp.float32,
        )
        row = jnp.where(j < live_count, table_ref[1 + j], block_count)
        at = pl.ds(pl.multiple_of(row * tile_size, tile_size), tile_size)
        sums_ref[at, :] += product[:, :width] + product[:, width:]

    for parity in range(2):
        for column in range(columns):
            team = pair_teams(team_index, column, team_count)
            team = team if parity == 0 else team ^ 1
            value = sums_ref[pl.ds(pl.multiple_of(team * share_rows, share_rows), share_rows), :]
            at = parity * columns + column
            outs[at][...] = value + partials[at][...] if partials else value


def arc_step(info, tiles, pieces, partials, scaled):
    team_count = lax.axis_size("rep")
    panel_rows = pieces[1].shape[0] if scaled else sum(piece.shape[0] for piece in pieces)
    width = pieces[1].shape[1]
    slot_total, tile_size, _ = tiles.shape
    share = jax.ShapeDtypeStruct((panel_rows // team_count, width), jnp.float32)
    operands = [info, tiles, *pieces, *partials]
    return pl.pallas_call(
        functools.partial(
            arc_kernel,
            team_count=team_count,
            piece_count=len(pieces),
            scaled=scaled,
            partial_count=len(partials),
        ),
        out_shape=[share] * team_count,
        in_specs=[ANY] + [VMEM] * (len(operands) - 1),
        out_specs=[VMEM] * team_count,
        scratch_shapes=[
            pltpu.SMEM(info.shape, info.dtype),
            pltpu.VMEM((panel_rows, 2 * width), jnp.bfloat16),
            pltpu.VMEM((panel_rows + tile_size, width), jnp.float32),
            pltpu.SemaphoreType.DMA,
        ],
        compiler_params=pltpu.CompilerParams(vmem_limit_bytes=VMEM_LIMIT),
        cost_estimate=pl.CostEstimate(
            flops=4 * slot_total * tile_size * tile_size * width, bytes_accessed=8 * panel_rows * width, transcendentals=0
        ),
    )(*operands)


def fetch(value, source_team, teams, arc_length):
    cycle, team_count = lax.axis_size("blk"), lax.axis_size("rep")
    pairs = []
    for shard in range(cycle):
        for team in teams:
            to_shard = (shard + team * arc_length) % cycle
            pairs.append((shard * team_count + source_team(team), to_shard * team_count + team))
    return lax.ppermute(value, ("blk", "rep"), pairs)


def next_shard(value):
    cycle = lax.axis_size("blk")
    return lax.ppermute(value, "blk", [(i, (i + 1) % cycle) for i in range(cycle)])


def from_mate(value):
    team_count = lax.axis_size("rep")
    return lax.ppermute(value, "rep", [(team, team ^ 1) for team in range(team_count)])


def from_column(value, distance):
    team_count = lax.axis_size("rep")
    pairs = [((team + 2 * distance) % team_count, team) for team in range(team_count)]
    return lax.ppermute(value, "rep", pairs)


def team_sum(sums):
    columns = len(sums) // 2
    total = None
    for distance in [*range(1, columns), 0]:
        at = (columns - distance) % columns
        share = sums[at] + from_mate(sums[columns + at])
        share = from_column(share, distance) if distance else share
        total = share if total is None else total + share
    return total


def per_device(embeddings, degrees, tile_values, tile_rows, tile_columns, slot_counts):
    arc_length, _, tile_size, _ = tile_values.shape[2:]
    panel_rows = embeddings.shape[0]
    team_count = lax.axis_size("rep")
    spread = (0, 1, 2, 0) if team_count == 4 else tuple(range(team_count))
    degrees = degrees.reshape(panel_rows // tile_size, tile_size)

    pieces = [degrees, embeddings]
    panel = fetch(embeddings, lambda team: spread[team], range(1, team_count), arc_length)
    pieces += [fetch(degrees, lambda team: spread[team], range(1, team_count), arc_length), panel]
    tiles, own, norm_scale = prepare(degrees, embeddings, tile_values[0, 0])
    info = jnp.concatenate([slot_counts[0, 0][:, None], tile_rows[0, 0], tile_columns[0, 0]], axis=1)

    combined = own
    for layer in range(LAYERS):
        sums = ()
        for arc_slot in range(arc_length):
            sums = arc_step(info[arc_slot], tiles[arc_slot], pieces, sums, layer == 0)
            if arc_slot + 1 < arc_length:
                pieces = [next_shard(piece) for piece in pieces]
        current = team_sum(sums) * norm_scale
        combined = combined + current
        if layer + 1 < LAYERS:
            source = current * norm_scale
            pieces = [
                fetch(source, lambda team, k=k: source_team(team, k, team_count), range(team_count), arc_length)
                for k in range(team_count)
            ]
    return combined / (LAYERS + 1.0)


def solution(mesh):
    in_specs = (
        P(("groups", "blk"), None),
        P(("groups", "blk")),
        P(("groups", "blk"), "rep", None, None, None, None),
        P(("groups", "blk"), "rep", None, None),
        P(("groups", "blk"), "rep", None, None),
        P(("groups", "blk"), "rep", None),
    )
    out_specs = P(("groups", "blk", "rep"), None)
    return jax.shard_map(
        per_device, mesh=mesh, in_specs=in_specs, out_specs=out_specs, check_vma=False
    )
```

profile of v0, /device:TPU:0, one launch (start us, length us, event | category | flops | bytes accessed | tf_op | source)
XLA Modules:
  0.0 51.4 jit_solution(8361874352890833724)
XLA Ops:
  0.0 7.3 %collective-permute-start.1 = (f32[1024,128]{1,0:T(8,128)}, f32[1024,128]{1,0:T(8,128)S(1)}, u32[]{:S(2)}, u32[]{:S(2)}) collective-permute-start(f32[1024,128]{1,0:T(8,128)} %refs_1_.1), channel_id=1, source_target_pairs={{1,5},{2,10},{0,15},{5,9},{6,14},{4,3},{9,13},{10,2},{8,7},{13,1},... | collective-permute-start | bytes 1572872 | tf_op jit(solution)/shard_map/ppermute | solution.py:164
  7.4 1.3 %collective-permute-start = (s32[8,128]{1,0:T(8,128)}, s32[8,128]{1,0:T(8,128)S(1)}, u32[]{:S(2)}, u32[]{:S(2)}) collective-permute-start(s32[8,128]{1,0:T(8,128)} %bitcast.12), channel_id=1, source_target_pairs={{1,5},{2,10},{0,15},{5,9},{6,14},{4,3},{9,13},{10,2},{8,7},{13,1},... | collective-permute-start | bytes 12296 | tf_op jit(solution)/shard_map/ppermute | solution.py:164
  9.3 0.6 %copy-done.3 = s32[1,1,1,24]{3,2,1,0:T(1,128)S(1)} copy-done((s32[1,1,1,24]{3,2,1,0:T(1,128)S(1)}, s32[1,1,1,24]{3,2,1,0:T(1,128)}, u32[]{:S(2)}) %copy-start.3) | copy-done | bytes 120
  9.9 0.0 copy-done.4
  10.0 0.1 add_bitcast_fusion.info_ref
  10.0 1.0 %copy-done = f32[1024,128]{1,0:T(8,128)S(1)} copy-done((f32[1024,128]{1,0:T(8,128)S(1)}, f32[1024,128]{1,0:T(8,128)}, u32[]{:S(2)}) %copy-start) | copy-done | bytes 524312
  11.1 1.1 %copy-done.1 = bf16[1,1,1,24,128,128]{5,4,3,2,1,0:T(8,128)(2,1)S(1)} copy-done((bf16[1,1,1,24,128,128]{5,4,3,2,1,0:T(8,128)(2,1)S(1)}, bf16[1,1,1,24,128,128]{5,4,3,2,1,0:T(8,128)(2,1)}, u32[]{:S(2)}) %copy-start.1) | copy-done | bytes 786456
  12.2 0.6 %shard_map.64 = (bf16[1,24,128,128]{3,2,1,0:T(8,128)(2,1)S(1)}, f32[256,128]{1,0:T(8,128)S(1)}, f32[256,128]{1,0:T(8,128)S(1)}) custom-call(s32[8,128]{1,0:T(8,128)S(1)} %bitcast.13, f32[1024,128]{1,0:T(8,128)S(1)} %copy-done, bf16[1,24,128,128]{3,2,1,0:T(8,128)(2,1)S(1)} %bitcast.11), custom_call_target="tpu_custom_call" | custom-call | flops 131072 | bytes 524288 | tf_op jit(solution)/shard_map/pallas_call | solution.py:53
  12.8 3.7 %collective-permute-done.refs_2_ = s32[8,128]{1,0:T(8,128)S(1)} collective-permute-done((s32[8,128]{1,0:T(8,128)}, s32[8,128]{1,0:T(8,128)S(1)}, u32[]{:S(2)}, u32[]{:S(2)}) %collective-permute-start) | collective-permute-done | bytes 4128 | tf_op jit(solution)/shard_map/ppermute | solution.py:164
  16.5 0.0 collective-permute-done.1.refs_3_
  16.5 1.2 %shard_map.65 = (f32[256,128]{1,0:T(8,128)S(1)}, f32[256,128]{1,0:T(8,128)S(1)}, f32[256,128]{1,0:T(8,128)S(1)}, f32[256,128]{1,0:T(8,128)S(1)}) custom-call(s32[49]{0:T(128)S(1)} %add_bitcast_fusion.info_ref, bf16[24,128,128]{2,1,0:T(8,128)(2,1)S(1)} %bitcast.9, s32[8,128]{1,0:T(8,128)S(1)} %bitcast.14, f32[1024,128]{1,0:T(8,128)S(1)} %copy-done, ...), custom_call_target="tpu_custom_call" | custom-call | flops 201326592 | bytes 1048576 | tf_op jit(solution)/shard_map/pallas_call | solution.py:133
  17.7 0.8 %collective-permute-start.2 = (f32[256,128]{1,0:T(8,128)S(1)}, f32[256,128]{1,0:T(8,128)S(1)}, u32[]{:S(2)}, u32[]{:S(2)}) collective-permute-start(f32[256,128]{1,0:T(8,128)S(1)} %get-tuple-element.19), channel_id=1, source_target_pairs={{0,1},{1,0},{2,3},{3,2},{4,5},{5,4},{6,7},{7,6},{8,9},{9,8},{10,11... | collective-permute-start | bytes 393224 | tf_op jit(solution)/shard_map/ppermute | solution.py:174
  18.5 0.1 collective-permute-start.4
  18.6 0.9 %collective-permute-done.2 = f32[256,128]{1,0:T(8,128)S(1)} collective-permute-done((f32[256,128]{1,0:T(8,128)S(1)}, f32[256,128]{1,0:T(8,128)S(1)}, u32[]{:S(2)}, u32[]{:S(2)}) %collective-permute-start.2) | collective-permute-done | bytes 131104 | tf_op jit(solution)/shard_map/ppermute | solution.py:174
  19.5 4.0 %collective-permute-start.3 = (f32[256,128]{1,0:T(8,128)S(1)}, f32[256,128]{1,0:T(8,128)S(1)}, u32[]{:S(2)}, u32[]{:S(2)}) collective-permute-start(f32[256,128]{1,0:T(8,128)S(1)} %add.24), channel_id=1, source_target_pairs={{2,0},{3,1},{0,2},{1,3},{6,4},{7,5},{4,6},{5,7},{10,8},{11,9},{8,1... | collective-permute-start | bytes 393224 | tf_op jit(solution)/shard_map/ppermute | solution.py:180
  23.5 0.0 collective-permute-done.4
  23.5 3.8 %collective-permute-done.3 = f32[256,128]{1,0:T(8,128)S(1)} collective-permute-done((f32[256,128]{1,0:T(8,128)S(1)}, f32[256,128]{1,0:T(8,128)S(1)}, u32[]{:S(2)}, u32[]{:S(2)}) %collective-permute-start.3) | collective-permute-done | bytes 131104 | tf_op jit(solution)/shard_map/ppermute | solution.py:180
  27.3 3.6 %collective-permute-start.8 = (f32[256,128]{1,0:T(8,128)S(1)}, f32[256,128]{1,0:T(8,128)S(1)}, u32[]{:S(2)}, u32[]{:S(2)}) collective-permute-start(f32[256,128]{1,0:T(8,128)S(1)} %fusion), channel_id=1, source_target_pairs={{3,0},{1,5},{2,10},{0,15},{7,4},{5,9},{6,14},{4,3},{11,8},{9,13},{... | collective-permute-start | bytes 393224 | tf_op jit(solution)/shard_map/ppermute | solution.py:164
  31.0 0.0 collective-permute-start.7
  31.0 0.5 collective-permute-start.6
  31.5 0.7 %collective-permute-start.5 = (f32[256,128]{1,0:T(8,128)S(1)}, f32[256,128]{1,0:T(8,128)S(1)}, u32[]{:S(2)}, u32[]{:S(2)}) collective-permute-start(f32[256,128]{1,0:T(8,128)S(1)} %fusion), channel_id=1, source_target_pairs={{0,0},{2,5},{1,10},{3,15},{4,4},{6,9},{5,14},{7,3},{8,8},{10,13},{... | collective-permute-start | bytes 393224 | tf_op jit(solution)/shard_map/ppermute | solution.py:164
  32.2 2.3 %collective-permute-done.8.refs_3_ = f32[256,128]{1,0:T(8,128)S(1)} collective-permute-done((f32[256,128]{1,0:T(8,128)S(1)}, f32[256,128]{1,0:T(8,128)S(1)}, u32[]{:S(2)}, u32[]{:S(2)}) %collective-permute-start.8) | collective-permute-done | bytes 131104 | tf_op jit(solution)/shard_map/ppermute | solution.py:164
  34.5 1.8 %collective-permute-done.7.refs_2_ = f32[256,128]{1,0:T(8,128)S(1)} collective-permute-done((f32[256,128]{1,0:T(8,128)S(1)}, f32[256,128]{1,0:T(8,128)S(1)}, u32[]{:S(2)}, u32[]{:S(2)}) %collective-permute-start.7) | collective-permute-done | bytes 131104 | tf_op jit(solution)/shard_map/ppermute | solution.py:164
  36.3 2.8 %collective-permute-done.6.refs_1_ = f32[256,128]{1,0:T(8,128)S(1)} collective-permute-done((f32[256,128]{1,0:T(8,128)S(1)}, f32[256,128]{1,0:T(8,128)S(1)}, u32[]{:S(2)}, u32[]{:S(2)}) %collective-permute-start.6) | collective-permute-done | bytes 131104 | tf_op jit(solution)/shard_map/ppermute | solution.py:164
  39.1 0.0 collective-permute-done.5.refs_0_
  39.1 1.2 %shard_map.66 = (f32[256,128]{1,0:T(8,128)S(1)}, f32[256,128]{1,0:T(8,128)S(1)}, f32[256,128]{1,0:T(8,128)S(1)}, f32[256,128]{1,0:T(8,128)S(1)}) custom-call(s32[49]{0:T(128)S(1)} %add_bitcast_fusion.info_ref, bf16[24,128,128]{2,1,0:T(8,128)(2,1)S(1)} %bitcast.10, f32[256,128]{1,0:T(8,128)S(1)} %collective-permute-done.5.refs_0_, ...), custom_call_target="tpu_custom_call" | custom-call | flops 201326592 | bytes 1048576 | tf_op jit(solution)/shard_map/pallas_call | solution.py:133
  40.3 3.0 %collective-permute-start.9 = (f32[256,128]{1,0:T(8,128)S(1)}, f32[256,128]{1,0:T(8,128)S(1)}, u32[]{:S(2)}, u32[]{:S(2)}) collective-permute-start(f32[256,128]{1,0:T(8,128)S(1)} %get-tuple-element.24), channel_id=1, source_target_pairs={{0,1},{1,0},{2,3},{3,2},{4,5},{5,4},{6,7},{7,6},{8,9},{9,8},{10,11... | collective-permute-start | bytes 393224 | tf_op jit(solution)/shard_map/ppermute | solution.py:174
  43.3 0.1 collective-permute-start.11
  43.4 0.9 %collective-permute-done.9 = f32[256,128]{1,0:T(8,128)S(1)} collective-permute-done((f32[256,128]{1,0:T(8,128)S(1)}, f32[256,128]{1,0:T(8,128)S(1)}, u32[]{:S(2)}, u32[]{:S(2)}) %collective-permute-start.9) | collective-permute-done | bytes 131104 | tf_op jit(solution)/shard_map/ppermute | solution.py:174
  44.3 2.5 %collective-permute-start.10 = (f32[256,128]{1,0:T(8,128)S(1)}, f32[256,128]{1,0:T(8,128)S(1)}, u32[]{:S(2)}, u32[]{:S(2)}) collective-permute-start(f32[256,128]{1,0:T(8,128)S(1)} %add.28), channel_id=1, source_target_pairs={{2,0},{3,1},{0,2},{1,3},{6,4},{7,5},{4,6},{5,7},{10,8},{11,9},{8,1... | collective-permute-start | bytes 393224 | tf_op jit(solution)/shard_map/ppermute | solution.py:180
  46.8 3.8 %collective-permute-done.10 = f32[256,128]{1,0:T(8,128)S(1)} collective-permute-done((f32[256,128]{1,0:T(8,128)S(1)}, f32[256,128]{1,0:T(8,128)S(1)}, u32[]{:S(2)}, u32[]{:S(2)}) %collective-permute-start.10) | collective-permute-done | bytes 131104 | tf_op jit(solution)/shard_map/ppermute | solution.py:180
  50.6 0.7 %add_multiply_fusion = f32[256,128]{1,0:T(8,128)} fusion(f32[256,128]{1,0:T(8,128)S(1)} %get-tuple-element.22, f32[256,128]{1,0:T(8,128)S(1)} %collective-permute-done.10, f32[256,128]{1,0:T(8,128)S(1)} %get-tuple-element.25, f32[256,128]{1,0:T(8,128)S(1)} %collective-permute-done.11, f32[256,128]{1,0:T(8,128)S(1)} %get-tuple-element.16, ...), kind=kLoop, calls=%fused_computation | loop fusion | flops 294912 | bytes 1179648 | tf_op jit(solution)/shard_map/div | solution.py:222
  (10 shorter events, 0.1 us)
Async XLA Ops:
  0.0 16.5 %collective-permute-start.1 = (f32[1024,128]{1,0:T(8,128)}, f32[1024,128]{1,0:T(8,128)S(1)}, u32[]{:S(2)}, u32[]{:S(2)}) collective-permute-start(f32[1024,128]{1,0:T(8,128)} %refs_1_.1), channel_id=1, source_target_pairs={{1,5},{2,10},{0,15},{5,9},{6,14},{4,3},{9,13},{10,2},{8,7},{13,1},... | collective-permute-start | bytes 1572872 | tf_op jit(solution)/shard_map/ppermute | solution.py:164
  7.4 9.1 %collective-permute-start = (s32[8,128]{1,0:T(8,128)}, s32[8,128]{1,0:T(8,128)S(1)}, u32[]{:S(2)}, u32[]{:S(2)}) collective-permute-start(s32[8,128]{1,0:T(8,128)} %bitcast.12), channel_id=1, source_target_pairs={{1,5},{2,10},{0,15},{5,9},{6,14},{4,3},{9,13},{10,2},{8,7},{13,1},... | collective-permute-start | bytes 12296 | tf_op jit(solution)/shard_map/ppermute | solution.py:164
  9.3 0.7 %copy-start.3 = (s32[1,1,1,24]{3,2,1,0:T(1,128)S(1)}, s32[1,1,1,24]{3,2,1,0:T(1,128)}, u32[]{:S(2)}) copy-start(s32[1,1,1,24]{3,2,1,0:T(1,128)} %param.10) | copy-start | bytes 292
  9.3 0.7 %copy-start.4 = (s32[1,1,1,24]{3,2,1,0:T(1,128)S(1)}, s32[1,1,1,24]{3,2,1,0:T(1,128)}, u32[]{:S(2)}) copy-start(s32[1,1,1,24]{3,2,1,0:T(1,128)} %param.9) | copy-start | bytes 292
  9.3 0.7 %copy-start.2 = (s32[1024]{0:T(1024)S(1)}, s32[1024]{0:T(1024)}, u32[]{:S(2)}) copy-start(s32[1024]{0:T(1024)} %param.7) | copy-start | bytes 12292
  10.0 1.0 %copy-start = (f32[1024,128]{1,0:T(8,128)S(1)}, f32[1024,128]{1,0:T(8,128)}, u32[]{:S(2)}) copy-start(f32[1024,128]{1,0:T(8,128)} %refs_1_.1) | copy-start | bytes 1572868
  11.1 1.1 %copy-start.1 = (bf16[1,1,1,24,128,128]{5,4,3,2,1,0:T(8,128)(2,1)S(1)}, bf16[1,1,1,24,128,128]{5,4,3,2,1,0:T(8,128)(2,1)}, u32[]{:S(2)}) copy-start(bf16[1,1,1,24,128,128]{5,4,3,2,1,0:T(8,128)(2,1)} %param.8) | copy-start | bytes 2359300
  17.7 1.8 %collective-permute-start.2 = (f32[256,128]{1,0:T(8,128)S(1)}, f32[256,128]{1,0:T(8,128)S(1)}, u32[]{:S(2)}, u32[]{:S(2)}) collective-permute-start(f32[256,128]{1,0:T(8,128)S(1)} %get-tuple-element.19), channel_id=1, source_target_pairs={{0,1},{1,0},{2,3},{3,2},{4,5},{5,4},{6,7},{7,6},{8,9},{9,8},{10,11... | collective-permute-start | bytes 393224 | tf_op jit(solution)/shard_map/ppermute | solution.py:174
  18.5 5.0 %collective-permute-start.4 = (f32[256,128]{1,0:T(8,128)S(1)}, f32[256,128]{1,0:T(8,128)S(1)}, u32[]{:S(2)}, u32[]{:S(2)}) collective-permute-start(f32[256,128]{1,0:T(8,128)S(1)} %get-tuple-element.21), channel_id=1, source_target_pairs={{0,1},{1,0},{2,3},{3,2},{4,5},{5,4},{6,7},{7,6},{8,9},{9,8},{10,11... | collective-permute-start | bytes 393224 | tf_op jit(solution)/shard_map/ppermute | solution.py:174
  19.5 7.8 %collective-permute-start.3 = (f32[256,128]{1,0:T(8,128)S(1)}, f32[256,128]{1,0:T(8,128)S(1)}, u32[]{:S(2)}, u32[]{:S(2)}) collective-permute-start(f32[256,128]{1,0:T(8,128)S(1)} %add.24), channel_id=1, source_target_pairs={{2,0},{3,1},{0,2},{1,3},{6,4},{7,5},{4,6},{5,7},{10,8},{11,9},{8,1... | collective-permute-start | bytes 393224 | tf_op jit(solution)/shard_map/ppermute | solution.py:180
  27.3 7.1 %collective-permute-start.8 = (f32[256,128]{1,0:T(8,128)S(1)}, f32[256,128]{1,0:T(8,128)S(1)}, u32[]{:S(2)}, u32[]{:S(2)}) collective-permute-start(f32[256,128]{1,0:T(8,128)S(1)} %fusion), channel_id=1, source_target_pairs={{3,0},{1,5},{2,10},{0,15},{7,4},{5,9},{6,14},{4,3},{11,8},{9,13},{... | collective-permute-start | bytes 393224 | tf_op jit(solution)/shard_map/ppermute | solution.py:164
  31.0 5.3 %collective-permute-start.7 = (f32[256,128]{1,0:T(8,128)S(1)}, f32[256,128]{1,0:T(8,128)S(1)}, u32[]{:S(2)}, u32[]{:S(2)}) collective-permute-start(f32[256,128]{1,0:T(8,128)S(1)} %fusion), channel_id=1, source_target_pairs={{2,0},{0,5},{3,10},{1,15},{6,4},{4,9},{7,14},{5,3},{10,8},{8,13},{... | collective-permute-start | bytes 393224 | tf_op jit(solution)/shard_map/ppermute | solution.py:164
  31.0 8.2 %collective-permute-start.6 = (f32[256,128]{1,0:T(8,128)S(1)}, f32[256,128]{1,0:T(8,128)S(1)}, u32[]{:S(2)}, u32[]{:S(2)}) collective-permute-start(f32[256,128]{1,0:T(8,128)S(1)} %fusion), channel_id=1, source_target_pairs={{1,0},{3,5},{0,10},{2,15},{5,4},{7,9},{4,14},{6,3},{9,8},{11,13},{... | collective-permute-start | bytes 393224 | tf_op jit(solution)/shard_map/ppermute | solution.py:164
  31.5 7.7 %collective-permute-start.5 = (f32[256,128]{1,0:T(8,128)S(1)}, f32[256,128]{1,0:T(8,128)S(1)}, u32[]{:S(2)}, u32[]{:S(2)}) collective-permute-start(f32[256,128]{1,0:T(8,128)S(1)} %fusion), channel_id=1, source_target_pairs={{0,0},{2,5},{1,10},{3,15},{4,4},{6,9},{5,14},{7,3},{8,8},{10,13},{... | collective-permute-start | bytes 393224 | tf_op jit(solution)/shard_map/ppermute | solution.py:164
  40.3 4.0 %collective-permute-start.9 = (f32[256,128]{1,0:T(8,128)S(1)}, f32[256,128]{1,0:T(8,128)S(1)}, u32[]{:S(2)}, u32[]{:S(2)}) collective-permute-start(f32[256,128]{1,0:T(8,128)S(1)} %get-tuple-element.24), channel_id=1, source_target_pairs={{0,1},{1,0},{2,3},{3,2},{4,5},{5,4},{6,7},{7,6},{8,9},{9,8},{10,11... | collective-permute-start | bytes 393224 | tf_op jit(solution)/shard_map/ppermute | solution.py:174
  43.3 3.5 %collective-permute-start.11 = (f32[256,128]{1,0:T(8,128)S(1)}, f32[256,128]{1,0:T(8,128)S(1)}, u32[]{:S(2)}, u32[]{:S(2)}) collective-permute-start(f32[256,128]{1,0:T(8,128)S(1)} %get-tuple-element.26), channel_id=1, source_target_pairs={{0,1},{1,0},{2,3},{3,2},{4,5},{5,4},{6,7},{7,6},{8,9},{9,8},{10,11... | collective-permute-start | bytes 393224 | tf_op jit(solution)/shard_map/ppermute | solution.py:174
  44.3 6.4 %collective-permute-start.10 = (f32[256,128]{1,0:T(8,128)S(1)}, f32[256,128]{1,0:T(8,128)S(1)}, u32[]{:S(2)}, u32[]{:S(2)}) collective-permute-start(f32[256,128]{1,0:T(8,128)S(1)} %add.28), channel_id=1, source_target_pairs={{2,0},{3,1},{0,2},{1,3},{6,4},{7,5},{4,6},{5,7},{10,8},{11,9},{8,1... | collective-permute-start | bytes 393224 | tf_op jit(solution)/shard_map/ppermute | solution.py:180
where the time goes:
time: 51.6 us; the launch traced here: 51.4 us
  starting transfers between devices  23.9 us (46%)
  waiting for transfers between devices  20.1 us (39%)
  Pallas kernels  2.9 us (6%)
  local copies, waits for them, and re-layouts  2.83 us (5%)
  other arithmetic  0.86 us (2%)
  between operations  0.74 us (1%)
    ppermute x6, starting transfers between devices, fetch(): return lax.ppermute(value, ('blk', 'rep'), pairs)  13.4 us
    ppermute x6, waiting for transfers between devices, fetch(): return lax.ppermute(value, ('blk', 'rep'), pairs)  10.7 us
    ppermute x2, waiting for transfers between devices, from_column(): return lax.ppermute(value, 'rep', pairs)  7.61 us
    ppermute x2, starting transfers between devices, from_column(): return lax.ppermute(value, 'rep', pairs)  6.53 us
    ppermute x4, starting transfers between devices, from_mate(): lax.ppermute(value, 'rep', [(team, team ^ 1) for team in range(team_count)])  3.95 us
    unnamed x10, local copies, waits for them, and re-layouts  2.83 us
    pallas_call x2, Pallas kernels, arc_step(): pl.pallas_call(functools.partial(arc_kernel, team_count=team_count, piece...  2.33 us
    ppermute x4, waiting for transfers between devices, from_mate(): lax.ppermute(value, 'rep', [(team, team ^ 1) for team in range(team_count)])  1.82 us
  transfers between devices with their start and end apart: 12, of which 8 were waited for; matrix products, arithmetic and copies ran while one was open for 0% of the time, Pallas kernels for 1%

commit v1 on v0

--- a/solution.py
+++ b/solution.py
@@ -81,21 +81,12 @@
         split_ref[at, :width] = high
         split_ref[at, width:] = (value - high.astype(jnp.float32)).astype(jnp.bfloat16)
 
-    def split_scaled(degrees_ref, panel_ref):
+    if scaled:
+        degrees_ref, panel_ref = pieces
         norms = norm_columns(degrees_ref[...])
         for block in range(block_count):
             at = pl.ds(block * tile_size, tile_size)
             split(panel_ref[at, :] * norms[:, block : block + 1], at)
-
-    if scaled:
-
-        @pl.when(team_index == 0)
-        def _():
-            split_scaled(*pieces[:2])
-
-        @pl.when(team_index > 0)
-        def _():
-            split_scaled(*pieces[2:])
     else:
         for k in range(piece_count):
             owner = source_team(team_index, k, team_count)
@@ -154,11 +145,11 @@
     )(*operands)
 
 
-def fetch(value, source_team, teams, arc_length):
+def fetch(value, source_team, arc_length):
     cycle, team_count = lax.axis_size("blk"), lax.axis_size("rep")
     pairs = []
     for shard in range(cycle):
-        for team in teams:
+        for team in range(team_count):
             to_shard = (shard + team * arc_length) % cycle
             pairs.append((shard * team_count + source_team(team), to_shard * team_count + team))
     return lax.ppermute(value, ("blk", "rep"), pairs)
@@ -195,12 +186,11 @@
     arc_length, _, tile_size, _ = tile_values.shape[2:]
     panel_rows = embeddings.shape[0]
     team_count = lax.axis_size("rep")
-    spread = (0, 1, 2, 0) if team_count == 4 else tuple(range(team_count))
+    spread = (3, 1, 2, 0) if team_count == 4 else tuple(range(team_count))
     degrees = degrees.reshape(panel_rows // tile_size, tile_size)
 
-    pieces = [degrees, embeddings]
-    panel = fetch(embeddings, lambda team: spread[team], range(1, team_count), arc_length)
-    pieces += [fetch(degrees, lambda team: spread[team], range(1, team_count), arc_length), panel]
+    panel = fetch(embeddings, lambda team: spread[team], arc_length)
+    pieces = [fetch(degrees, lambda team: spread[team], arc_length), panel]
     tiles, own, norm_scale = prepare(degrees, embeddings, tile_values[0, 0])
     info = jnp.concatenate([slot_counts[0, 0][:, None], tile_rows[0, 0], tile_columns[0, 0]], axis=1)
 
@@ -216,7 +206,7 @@
         if layer + 1 < LAYERS:
             source = current * norm_scale
             pieces = [
-                fetch(source, lambda team, k=k: source_team(team, k, team_count), range(team_count), arc_length)
+                fetch(source, lambda team, k=k: source_team(team, k, team_count), arc_length)
                 for k in range(team_count)
             ]
     return combined / (LAYERS + 1.0)

time: 51.6 us -> 49.7 us (0.963)
  starting transfers between devices: 23.9 us -> 21.5 us
    ppermute x6, starting transfers between devices: 13.4 us -> 11 us  [fetch(): return lax.ppermute(value, ('blk', 'rep'), pairs)]
    ppermute x6, waiting for transfers between devices: 10.7 us -> 11.2 us  [fetch(): return lax.ppermute(value, ('blk', 'rep'), pairs)]
where the time goes in v1:
time: 49.7 us; the launch traced here: 49.5 us
  starting transfers between devices  21.5 us (43%)
  waiting for transfers between devices  20.6 us (41%)
  Pallas kernels  2.9 us (6%)
  local copies, waits for them, and re-layouts  2.83 us (6%)
  other arithmetic  0.88 us (2%)
  between operations  0.73 us (1%)
    ppermute x6, waiting for transfers between devices, fetch(): return lax.ppermute(value, ('blk', 'rep'), pairs)  11.2 us
    ppermute x6, starting transfers between devices, fetch(): return lax.ppermute(value, ('blk', 'rep'), pairs)  11 us
    ppermute x2, waiting for transfers between devices, from_column(): return lax.ppermute(value, 'rep', pairs)  7.61 us
    ppermute x2, starting transfers between devices, from_column(): return lax.ppermute(value, 'rep', pairs)  6.56 us
    ppermute x4, starting transfers between devices, from_mate(): lax.ppermute(value, 'rep', [(team, team ^ 1) for team in range(team_count)])  3.92 us
    unnamed x10, local copies, waits for them, and re-layouts  2.83 us
    pallas_call x2, Pallas kernels, arc_step(): pl.pallas_call(functools.partial(arc_kernel, team_count=team_count, piece...  2.33 us
    ppermute x4, waiting for transfers between devices, from_mate(): lax.ppermute(value, 'rep', [(team, team ^ 1) for team in range(team_count)])  1.82 us
  transfers between devices with their start and end apart: 12, of which 8 were waited for; matrix products, arithmetic and copies ran while one was open for 0% of the time, Pallas kernels for 1%

profile of v1, /device:TPU:0, one launch (start us, length us, event | category | flops | bytes accessed | tf_op | source)
XLA Modules:
  0.0 49.5 jit_solution(5863898148279720705)
XLA Ops:
  0.0 5.4 %collective-permute-start.1 = (f32[1024,128]{1,0:T(8,128)}, f32[1024,128]{1,0:T(8,128)S(1)}, u32[]{:S(2)}, u32[]{:S(2)}) collective-permute-start(f32[1024,128]{1,0:T(8,128)} %embeddings_ref.1), channel_id=1, source_target_pairs={{3,0},{1,5},{2,10},{0,15},{7,4},{5,9},{6,14},{4,3},{11,8},{9,13},{... | collective-permute-start | bytes 1572872 | tf_op jit(solution)/shard_map/ppermute | solution.py:155
  5.4 0.8 %collective-permute-start = (s32[8,128]{1,0:T(8,128)}, s32[8,128]{1,0:T(8,128)S(1)}, u32[]{:S(2)}, u32[]{:S(2)}) collective-permute-start(s32[8,128]{1,0:T(8,128)} %bitcast.12), channel_id=1, source_target_pairs={{3,0},{1,5},{2,10},{0,15},{7,4},{5,9},{6,14},{4,3},{11,8},{9,13},{... | collective-permute-start | bytes 12296 | tf_op jit(solution)/shard_map/ppermute | solution.py:155
  6.9 0.6 %copy-done.3 = s32[1,1,1,24]{3,2,1,0:T(1,128)S(1)} copy-done((s32[1,1,1,24]{3,2,1,0:T(1,128)S(1)}, s32[1,1,1,24]{3,2,1,0:T(1,128)}, u32[]{:S(2)}) %copy-start.3) | copy-done | bytes 120
  7.5 0.0 copy-done.4
  7.6 0.1 add_bitcast_fusion.info_ref
  7.6 1.1 %copy-done = bf16[1,1,1,24,128,128]{5,4,3,2,1,0:T(8,128)(2,1)S(1)} copy-done((bf16[1,1,1,24,128,128]{5,4,3,2,1,0:T(8,128)(2,1)S(1)}, bf16[1,1,1,24,128,128]{5,4,3,2,1,0:T(8,128)(2,1)}, u32[]{:S(2)}) %copy-start) | copy-done | bytes 786456
  8.8 1.0 %copy-done.1 = f32[1024,128]{1,0:T(8,128)S(1)} copy-done((f32[1024,128]{1,0:T(8,128)S(1)}, f32[1024,128]{1,0:T(8,128)}, u32[]{:S(2)}) %copy-start.1) | copy-done | bytes 524312
  9.8 0.6 %shard_map.64 = (bf16[1,24,128,128]{3,2,1,0:T(8,128)(2,1)S(1)}, f32[256,128]{1,0:T(8,128)S(1)}, f32[256,128]{1,0:T(8,128)S(1)}) custom-call(s32[8,128]{1,0:T(8,128)S(1)} %bitcast.13, f32[1024,128]{1,0:T(8,128)S(1)} %copy-done.1, bf16[1,24,128,128]{3,2,1,0:T(8,128)(2,1)S(1)} %bitcast.11), custom_call_target="tpu_custom_call" | custom-call | flops 131072 | bytes 524288 | tf_op jit(solution)/shard_map/pallas_call | solution.py:53
  10.4 4.2 %collective-permute-done.refs_0_ = s32[8,128]{1,0:T(8,128)S(1)} collective-permute-done((s32[8,128]{1,0:T(8,128)}, s32[8,128]{1,0:T(8,128)S(1)}, u32[]{:S(2)}, u32[]{:S(2)}) %collective-permute-start) | collective-permute-done | bytes 4128 | tf_op jit(solution)/shard_map/ppermute | solution.py:155
  14.6 0.0 collective-permute-done.1.refs_1_
  14.6 1.2 %shard_map.65 = (f32[256,128]{1,0:T(8,128)S(1)}, f32[256,128]{1,0:T(8,128)S(1)}, f32[256,128]{1,0:T(8,128)S(1)}, f32[256,128]{1,0:T(8,128)S(1)}) custom-call(s32[49]{0:T(128)S(1)} %add_bitcast_fusion.info_ref, bf16[24,128,128]{2,1,0:T(8,128)(2,1)S(1)} %bitcast.9, s32[8,128]{1,0:T(8,128)S(1)} %collective-permute-done.refs_0_, ...), custom_call_target="tpu_custom_call" | custom-call | flops 201326592 | bytes 1048576 | tf_op jit(solution)/shard_map/pallas_call | solution.py:124
  15.8 0.8 %collective-permute-start.2 = (f32[256,128]{1,0:T(8,128)S(1)}, f32[256,128]{1,0:T(8,128)S(1)}, u32[]{:S(2)}, u32[]{:S(2)}) collective-permute-start(f32[256,128]{1,0:T(8,128)S(1)} %get-tuple-element.19), channel_id=1, source_target_pairs={{0,1},{1,0},{2,3},{3,2},{4,5},{5,4},{6,7},{7,6},{8,9},{9,8},{10,11... | collective-permute-start | bytes 393224 | tf_op jit(solution)/shard_map/ppermute | solution.py:165
  16.6 0.1 collective-permute-start.4
  16.7 0.9 %collective-permute-done.2 = f32[256,128]{1,0:T(8,128)S(1)} collective-permute-done((f32[256,128]{1,0:T(8,128)S(1)}, f32[256,128]{1,0:T(8,128)S(1)}, u32[]{:S(2)}, u32[]{:S(2)}) %collective-permute-start.2) | collective-permute-done | bytes 131104 | tf_op jit(solution)/shard_map/ppermute | solution.py:165
  17.6 4.0 %collective-permute-start.3 = (f32[256,128]{1,0:T(8,128)S(1)}, f32[256,128]{1,0:T(8,128)S(1)}, u32[]{:S(2)}, u32[]{:S(2)}) collective-permute-start(f32[256,128]{1,0:T(8,128)S(1)} %add.24), channel_id=1, source_target_pairs={{2,0},{3,1},{0,2},{1,3},{6,4},{7,5},{4,6},{5,7},{10,8},{11,9},{8,1... | collective-permute-start | bytes 393224 | tf_op jit(solution)/shard_map/ppermute | solution.py:171
  21.6 0.0 collective-permute-done.4
  21.6 3.8 %collective-permute-done.3 = f32[256,128]{1,0:T(8,128)S(1)} collective-permute-done((f32[256,128]{1,0:T(8,128)S(1)}, f32[256,128]{1,0:T(8,128)S(1)}, u32[]{:S(2)}, u32[]{:S(2)}) %collective-permute-start.3) | collective-permute-done | bytes 131104 | tf_op jit(solution)/shard_map/ppermute | solution.py:171
  25.5 3.6 %collective-permute-start.8 = (f32[256,128]{1,0:T(8,128)S(1)}, f32[256,128]{1,0:T(8,128)S(1)}, u32[]{:S(2)}, u32[]{:S(2)}) collective-permute-start(f32[256,128]{1,0:T(8,128)S(1)} %fusion), channel_id=1, source_target_pairs={{3,0},{1,5},{2,10},{0,15},{7,4},{5,9},{6,14},{4,3},{11,8},{9,13},{... | collective-permute-start | bytes 393224 | tf_op jit(solution)/shard_map/ppermute | solution.py:155
  29.1 0.5 %collective-permute-start.6 = (f32[256,128]{1,0:T(8,128)S(1)}, f32[256,128]{1,0:T(8,128)S(1)}, u32[]{:S(2)}, u32[]{:S(2)}) collective-permute-start(f32[256,128]{1,0:T(8,128)S(1)} %fusion), channel_id=1, source_target_pairs={{1,0},{3,5},{0,10},{2,15},{5,4},{7,9},{4,14},{6,3},{9,8},{11,13},{... | collective-permute-start | bytes 393224 | tf_op jit(solution)/shard_map/ppermute | solution.py:155
  29.6 0.7 %collective-permute-start.5 = (f32[256,128]{1,0:T(8,128)S(1)}, f32[256,128]{1,0:T(8,128)S(1)}, u32[]{:S(2)}, u32[]{:S(2)}) collective-permute-start(f32[256,128]{1,0:T(8,128)S(1)} %fusion), channel_id=1, source_target_pairs={{0,0},{2,5},{1,10},{3,15},{4,4},{6,9},{5,14},{7,3},{8,8},{10,13},{... | collective-permute-start | bytes 393224 | tf_op jit(solution)/shard_map/ppermute | solution.py:155
  30.3 2.3 %collective-permute-done.8.refs_3_ = f32[256,128]{1,0:T(8,128)S(1)} collective-permute-done((f32[256,128]{1,0:T(8,128)S(1)}, f32[256,128]{1,0:T(8,128)S(1)}, u32[]{:S(2)}, u32[]{:S(2)}) %collective-permute-start.8) | collective-permute-done | bytes 131104 | tf_op jit(solution)/shard_map/ppermute | solution.py:155
  32.6 1.8 %collective-permute-done.7.refs_2_ = f32[256,128]{1,0:T(8,128)S(1)} collective-permute-done((f32[256,128]{1,0:T(8,128)S(1)}, f32[256,128]{1,0:T(8,128)S(1)}, u32[]{:S(2)}, u32[]{:S(2)}) %collective-permute-start.7) | collective-permute-done | bytes 131104 | tf_op jit(solution)/shard_map/ppermute | solution.py:155
  34.4 2.8 %collective-permute-done.6.refs_1_ = f32[256,128]{1,0:T(8,128)S(1)} collective-permute-done((f32[256,128]{1,0:T(8,128)S(1)}, f32[256,128]{1,0:T(8,128)S(1)}, u32[]{:S(2)}, u32[]{:S(2)}) %collective-permute-start.6) | collective-permute-done | bytes 131104 | tf_op jit(solution)/shard_map/ppermute | solution.py:155
  37.3 0.0 collective-permute-done.5.refs_0_
  37.3 1.2 %shard_map.66 = (f32[256,128]{1,0:T(8,128)S(1)}, f32[256,128]{1,0:T(8,128)S(1)}, f32[256,128]{1,0:T(8,128)S(1)}, f32[256,128]{1,0:T(8,128)S(1)}) custom-call(s32[49]{0:T(128)S(1)} %add_bitcast_fusion.info_ref, bf16[24,128,128]{2,1,0:T(8,128)(2,1)S(1)} %bitcast.10, f32[256,128]{1,0:T(8,128)S(1)} %collective-permute-done.5.refs_0_, ...), custom_call_target="tpu_custom_call" | custom-call | flops 201326592 | bytes 1048576 | tf_op jit(solution)/shard_map/pallas_call | solution.py:124
  38.4 3.0 %collective-permute-start.9 = (f32[256,128]{1,0:T(8,128)S(1)}, f32[256,128]{1,0:T(8,128)S(1)}, u32[]{:S(2)}, u32[]{:S(2)}) collective-permute-start(f32[256,128]{1,0:T(8,128)S(1)} %get-tuple-element.24), channel_id=1, source_target_pairs={{0,1},{1,0},{2,3},{3,2},{4,5},{5,4},{6,7},{7,6},{8,9},{9,8},{10,11... | collective-permute-start | bytes 393224 | tf_op jit(solution)/shard_map/ppermute | solution.py:165
  41.4 0.1 collective-permute-start.11
  41.5 0.9 %collective-permute-done.9 = f32[256,128]{1,0:T(8,128)S(1)} collective-permute-done((f32[256,128]{1,0:T(8,128)S(1)}, f32[256,128]{1,0:T(8,128)S(1)}, u32[]{:S(2)}, u32[]{:S(2)}) %collective-permute-start.9) | collective-permute-done | bytes 131104 | tf_op jit(solution)/shard_map/ppermute | solution.py:165
  42.4 2.5 %collective-permute-start.10 = (f32[256,128]{1,0:T(8,128)S(1)}, f32[256,128]{1,0:T(8,128)S(1)}, u32[]{:S(2)}, u32[]{:S(2)}) collective-permute-start(f32[256,128]{1,0:T(8,128)S(1)} %add.28), channel_id=1, source_target_pairs={{2,0},{3,1},{0,2},{1,3},{6,4},{7,5},{4,6},{5,7},{10,8},{11,9},{8,1... | collective-permute-start | bytes 393224 | tf_op jit(solution)/shard_map/ppermute | solution.py:171
  45.0 0.0 collective-permute-done.11
  45.0 3.8 %collective-permute-done.10 = f32[256,128]{1,0:T(8,128)S(1)} collective-permute-done((f32[256,128]{1,0:T(8,128)S(1)}, f32[256,128]{1,0:T(8,128)S(1)}, u32[]{:S(2)}, u32[]{:S(2)}) %collective-permute-start.10) | collective-permute-done | bytes 131104 | tf_op jit(solution)/shard_map/ppermute | solution.py:171
  48.8 0.7 %add_multiply_fusion = f32[256,128]{1,0:T(8,128)} fusion(f32[256,128]{1,0:T(8,128)S(1)} %get-tuple-element.22, f32[256,128]{1,0:T(8,128)S(1)} %collective-permute-done.10, f32[256,128]{1,0:T(8,128)S(1)} %get-tuple-element.25, f32[256,128]{1,0:T(8,128)S(1)} %collective-permute-done.11, f32[256,128]{1,0:T(8,128)S(1)} %get-tuple-element.16, ...), kind=kLoop, calls=%fused_computation | loop fusion | flops 294912 | bytes 1179648 | tf_op jit(solution)/shard_map/div | solution.py:212
  (10 shorter events, 0.1 us)
Async XLA Ops:
  0.0 14.6 %collective-permute-start.1 = (f32[1024,128]{1,0:T(8,128)}, f32[1024,128]{1,0:T(8,128)S(1)}, u32[]{:S(2)}, u32[]{:S(2)}) collective-permute-start(f32[1024,128]{1,0:T(8,128)} %embeddings_ref.1), channel_id=1, source_target_pairs={{3,0},{1,5},{2,10},{0,15},{7,4},{5,9},{6,14},{4,3},{11,8},{9,13},{... | collective-permute-start | bytes 1572872 | tf_op jit(solution)/shard_map/ppermute | solution.py:155
  5.4 9.2 %collective-permute-start = (s32[8,128]{1,0:T(8,128)}, s32[8,128]{1,0:T(8,128)S(1)}, u32[]{:S(2)}, u32[]{:S(2)}) collective-permute-start(s32[8,128]{1,0:T(8,128)} %bitcast.12), channel_id=1, source_target_pairs={{3,0},{1,5},{2,10},{0,15},{7,4},{5,9},{6,14},{4,3},{11,8},{9,13},{... | collective-permute-start | bytes 12296 | tf_op jit(solution)/shard_map/ppermute | solution.py:155
  6.9 0.7 %copy-start.3 = (s32[1,1,1,24]{3,2,1,0:T(1,128)S(1)}, s32[1,1,1,24]{3,2,1,0:T(1,128)}, u32[]{:S(2)}) copy-start(s32[1,1,1,24]{3,2,1,0:T(1,128)} %param.10) | copy-start | bytes 292
  6.9 0.7 %copy-start.4 = (s32[1,1,1,24]{3,2,1,0:T(1,128)S(1)}, s32[1,1,1,24]{3,2,1,0:T(1,128)}, u32[]{:S(2)}) copy-start(s32[1,1,1,24]{3,2,1,0:T(1,128)} %param.9) | copy-start | bytes 292
  6.9 0.7 %copy-start.2 = (s32[1024]{0:T(1024)S(1)}, s32[1024]{0:T(1024)}, u32[]{:S(2)}) copy-start(s32[1024]{0:T(1024)} %param.7) | copy-start | bytes 12292
  7.6 1.1 %copy-start = (bf16[1,1,1,24,128,128]{5,4,3,2,1,0:T(8,128)(2,1)S(1)}, bf16[1,1,1,24,128,128]{5,4,3,2,1,0:T(8,128)(2,1)}, u32[]{:S(2)}) copy-start(bf16[1,1,1,24,128,128]{5,4,3,2,1,0:T(8,128)(2,1)} %param.8) | copy-start | bytes 2359300
  8.8 1.0 %copy-start.1 = (f32[1024,128]{1,0:T(8,128)S(1)}, f32[1024,128]{1,0:T(8,128)}, u32[]{:S(2)}) copy-start(f32[1024,128]{1,0:T(8,128)} %embeddings_ref.1) | copy-start | bytes 1572868
  15.8 1.8 %collective-permute-start.2 = (f32[256,128]{1,0:T(8,128)S(1)}, f32[256,128]{1,0:T(8,128)S(1)}, u32[]{:S(2)}, u32[]{:S(2)}) collective-permute-start(f32[256,128]{1,0:T(8,128)S(1)} %get-tuple-element.19), channel_id=1, source_target_pairs={{0,1},{1,0},{2,3},{3,2},{4,5},{5,4},{6,7},{7,6},{8,9},{9,8},{10,11... | collective-permute-start | bytes 393224 | tf_op jit(solution)/shard_map/ppermute | solution.py:165
  16.6 5.0 %collective-permute-start.4 = (f32[256,128]{1,0:T(8,128)S(1)}, f32[256,128]{1,0:T(8,128)S(1)}, u32[]{:S(2)}, u32[]{:S(2)}) collective-permute-start(f32[256,128]{1,0:T(8,128)S(1)} %get-tuple-element.21), channel_id=1, source_target_pairs={{0,1},{1,0},{2,3},{3,2},{4,5},{5,4},{6,7},{7,6},{8,9},{9,8},{10,11... | collective-permute-start | bytes 393224 | tf_op jit(solution)/shard_map/ppermute | solution.py:165
  17.6 7.8 %collective-permute-start.3 = (f32[256,128]{1,0:T(8,128)S(1)}, f32[256,128]{1,0:T(8,128)S(1)}, u32[]{:S(2)}, u32[]{:S(2)}) collective-permute-start(f32[256,128]{1,0:T(8,128)S(1)} %add.24), channel_id=1, source_target_pairs={{2,0},{3,1},{0,2},{1,3},{6,4},{7,5},{4,6},{5,7},{10,8},{11,9},{8,1... | collective-permute-start | bytes 393224 | tf_op jit(solution)/shard_map/ppermute | solution.py:171
  25.5 7.1 %collective-permute-start.8 = (f32[256,128]{1,0:T(8,128)S(1)}, f32[256,128]{1,0:T(8,128)S(1)}, u32[]{:S(2)}, u32[]{:S(2)}) collective-permute-start(f32[256,128]{1,0:T(8,128)S(1)} %fusion), channel_id=1, source_target_pairs={{3,0},{1,5},{2,10},{0,15},{7,4},{5,9},{6,14},{4,3},{11,8},{9,13},{... | collective-permute-start | bytes 393224 | tf_op jit(solution)/shard_map/ppermute | solution.py:155
  29.1 5.3 %collective-permute-start.7 = (f32[256,128]{1,0:T(8,128)S(1)}, f32[256,128]{1,0:T(8,128)S(1)}, u32[]{:S(2)}, u32[]{:S(2)}) collective-permute-start(f32[256,128]{1,0:T(8,128)S(1)} %fusion), channel_id=1, source_target_pairs={{2,0},{0,5},{3,10},{1,15},{6,4},{4,9},{7,14},{5,3},{10,8},{8,13},{... | collective-permute-start | bytes 393224 | tf_op jit(solution)/shard_map/ppermute | solution.py:155
  29.1 8.2 %collective-permute-start.6 = (f32[256,128]{1,0:T(8,128)S(1)}, f32[256,128]{1,0:T(8,128)S(1)}, u32[]{:S(2)}, u32[]{:S(2)}) collective-permute-start(f32[256,128]{1,0:T(8,128)S(1)} %fusion), channel_id=1, source_target_pairs={{1,0},{3,5},{0,10},{2,15},{5,4},{7,9},{4,14},{6,3},{9,8},{11,13},{... | collective-permute-start | bytes 393224 | tf_op jit(solution)/shard_map/ppermute | solution.py:155
  29.6 7.7 %collective-permute-start.5 = (f32[256,128]{1,0:T(8,128)S(1)}, f32[256,128]{1,0:T(8,128)S(1)}, u32[]{:S(2)}, u32[]{:S(2)}) collective-permute-start(f32[256,128]{1,0:T(8,128)S(1)} %fusion), channel_id=1, source_target_pairs={{0,0},{2,5},{1,10},{3,15},{4,4},{6,9},{5,14},{7,3},{8,8},{10,13},{... | collective-permute-start | bytes 393224 | tf_op jit(solution)/shard_map/ppermute | solution.py:155
  38.4 3.9 %collective-permute-start.9 = (f32[256,128]{1,0:T(8,128)S(1)}, f32[256,128]{1,0:T(8,128)S(1)}, u32[]{:S(2)}, u32[]{:S(2)}) collective-permute-start(f32[256,128]{1,0:T(8,128)S(1)} %get-tuple-element.24), channel_id=1, source_target_pairs={{0,1},{1,0},{2,3},{3,2},{4,5},{5,4},{6,7},{7,6},{8,9},{9,8},{10,11... | collective-permute-start | bytes 393224 | tf_op jit(solution)/shard_map/ppermute | solution.py:165
  41.4 3.6 %collective-permute-start.11 = (f32[256,128]{1,0:T(8,128)S(1)}, f32[256,128]{1,0:T(8,128)S(1)}, u32[]{:S(2)}, u32[]{:S(2)}) collective-permute-start(f32[256,128]{1,0:T(8,128)S(1)} %get-tuple-element.26), channel_id=1, source_target_pairs={{0,1},{1,0},{2,3},{3,2},{4,5},{5,4},{6,7},{7,6},{8,9},{9,8},{10,11... | collective-permute-start | bytes 393224 | tf_op jit(solution)/shard_map/ppermute | solution.py:165
  42.4 6.4 %collective-permute-start.10 = (f32[256,128]{1,0:T(8,128)S(1)}, f32[256,128]{1,0:T(8,128)S(1)}, u32[]{:S(2)}, u32[]{:S(2)}) collective-permute-start(f32[256,128]{1,0:T(8,128)S(1)} %add.28), channel_id=1, source_target_pairs={{2,0},{3,1},{0,2},{1,3},{6,4},{7,5},{4,6},{5,7},{10,8},{11,9},{8,1... | collective-permute-start | bytes 393224 | tf_op jit(solution)/shard_map/ppermute | solution.py:171

commit v2 on v1

--- a/solution.py
+++ b/solution.py
@@ -20,8 +20,8 @@
 
 def source_team(team, turn, team_count):
     if team_count == 4:
-        return (2 * (team % 2) + team // 2) ^ turn
-    return (team + turn) % team_count
+        return (2 * ((team + 1) % 2) + team // 2) ^ (3 * turn)
+    return (team + 2 * turn) % team_count
 
 
 def norm_columns(degrees):
@@ -89,8 +89,10 @@
             split(panel_ref[at, :] * norms[:, block : block + 1], at)
     else:
         for k in range(piece_count):
-            owner = source_team(team_index, k, team_count)
-            split(pieces[k][...], pl.ds(pl.multiple_of(owner * share_rows, share_rows), share_rows))
+            source = source_team(team_index, k, team_count)
+            for at, owner in enumerate((source, source ^ 1)):
+                value = pieces[k][at * share_rows : (at + 1) * share_rows, :]
+                split(value, pl.ds(pl.multiple_of(owner * share_rows, share_rows), share_rows))
     sums_ref[...] = jnp.zeros_like(sums_ref)
     table_copy.wait()
     live_count = table_ref[0]
@@ -205,9 +207,10 @@
         combined = combined + current
         if layer + 1 < LAYERS:
             source = current * norm_scale
+            source = jnp.concatenate([source, from_mate(source)])
             pieces = [
                 fetch(source, lambda team, k=k: source_team(team, k, team_count), arc_length)
-                for k in range(team_count)
+                for k in range(team_count // 2)
             ]
     return combined / (LAYERS + 1.0)
 

time: 49.7 us -> 51.3 us (1.032)
  waiting for transfers between devices: 20.6 us -> 25.3 us
  starting transfers between devices: 21.5 us -> 18.4 us
    ppermute x6 -> x4, starting transfers between devices: 11 us -> 7.51 us  [fetch(): return lax.ppermute(value, ('blk', 'rep'), pairs)]
    ppermute x6 -> x4, waiting for transfers between devices: 11.2 us -> 14.5 us  [fetch(): return lax.ppermute(value, ('blk', 'rep'), pairs)]
    ppermute x4 -> x5, waiting for transfers between devices: 1.82 us -> 3.15 us  [from_mate(): lax.ppermute(value, 'rep', [(team, team ^ 1) for team in range(team_count)])]
    ppermute x2, starting transfers between devices: 6.56 us -> 7.2 us  [from_column(): return lax.ppermute(value, 'rep', pairs)]
    ppermute x4 -> x5, starting transfers between devices: 3.92 us -> 3.71 us  [from_mate(): lax.ppermute(value, 'rep', [(team, team ^ 1) for team in range(team_count)])]
  transfers between devices with their start and end apart: 12 -> 11, of which waited for: 8 -> 8; matrix products, arithmetic and copies ran while one was open for 0% -> 0% of each run, Pallas kernels for 1% -> 1%
where the time goes in v2:
time: 51.3 us; the launch traced here: 51 us
  waiting for transfers between devices  25.3 us (49%)
  starting transfers between devices  18.4 us (36%)
  Pallas kernels  2.9 us (6%)
  local copies, waits for them, and re-layouts  2.83 us (6%)
  other arithmetic  0.91 us (2%)
  between operations  0.73 us (1%)
    ppermute x4, waiting for transfers between devices, fetch(): return lax.ppermute(value, ('blk', 'rep'), pairs)  14.5 us
    ppermute x2, waiting for transfers between devices, from_column(): return lax.ppermute(value, 'rep', pairs)  7.61 us
    ppermute x4, starting transfers between devices, fetch(): return lax.ppermute(value, ('blk', 'rep'), pairs)  7.51 us
    ppermute x2, starting transfers between devices, from_column(): return lax.ppermute(value, 'rep', pairs)  7.2 us
    ppermute x5, starting transfers between devices, from_mate(): lax.ppermute(value, 'rep', [(team, team ^ 1) for team in range(team_count)])  3.71 us
    ppermute x5, waiting for transfers between devices, from_mate(): lax.ppermute(value, 'rep', [(team, team ^ 1) for team in range(team_count)])  3.15 us
    unnamed x10, local copies, waits for them, and re-layouts  2.83 us
    pallas_call x2, Pallas kernels, arc_step(): pl.pallas_call(functools.partial(arc_kernel, team_count=team_count, piece...  2.33 us
  transfers between devices with their start and end apart: 11, of which 8 were waited for; matrix products, arithmetic and copies ran while one was open for 0% of the time, Pallas kernels for 1%

profile of v2, /device:TPU:0, one launch (start us, length us, event | category | flops | bytes accessed | tf_op | source)
XLA Modules:
  0.0 51.0 jit_solution(13922578730130814823)
XLA Ops:
  0.0 5.4 %collective-permute-start.1 = (f32[1024,128]{1,0:T(8,128)}, f32[1024,128]{1,0:T(8,128)S(1)}, u32[]{:S(2)}, u32[]{:S(2)}) collective-permute-start(f32[1024,128]{1,0:T(8,128)} %embeddings_ref.1), channel_id=1, source_target_pairs={{3,0},{1,5},{2,10},{0,15},{7,4},{5,9},{6,14},{4,3},{11,8},{9,13},{... | collective-permute-start | bytes 1572872 | tf_op jit(solution)/shard_map/ppermute | solution.py:157
  5.4 0.8 %collective-permute-start = (s32[8,128]{1,0:T(8,128)}, s32[8,128]{1,0:T(8,128)S(1)}, u32[]{:S(2)}, u32[]{:S(2)}) collective-permute-start(s32[8,128]{1,0:T(8,128)} %bitcast.12), channel_id=1, source_target_pairs={{3,0},{1,5},{2,10},{0,15},{7,4},{5,9},{6,14},{4,3},{11,8},{9,13},{... | collective-permute-start | bytes 12296 | tf_op jit(solution)/shard_map/ppermute | solution.py:157
  6.9 0.6 %copy-done.3 = s32[1,1,1,24]{3,2,1,0:T(1,128)S(1)} copy-done((s32[1,1,1,24]{3,2,1,0:T(1,128)S(1)}, s32[1,1,1,24]{3,2,1,0:T(1,128)}, u32[]{:S(2)}) %copy-start.3) | copy-done | bytes 120
  7.5 0.0 copy-done.4
  7.6 0.1 add_bitcast_fusion.info_ref
  7.6 0.0 copy-done.2
  7.6 1.1 %copy-done = bf16[1,1,1,24,128,128]{5,4,3,2,1,0:T(8,128)(2,1)S(1)} copy-done((bf16[1,1,1,24,128,128]{5,4,3,2,1,0:T(8,128)(2,1)S(1)}, bf16[1,1,1,24,128,128]{5,4,3,2,1,0:T(8,128)(2,1)}, u32[]{:S(2)}) %copy-start) | copy-done | bytes 786456
  8.8 1.0 %copy-done.1 = f32[1024,128]{1,0:T(8,128)S(1)} copy-done((f32[1024,128]{1,0:T(8,128)S(1)}, f32[1024,128]{1,0:T(8,128)}, u32[]{:S(2)}) %copy-start.1) | copy-done | bytes 524312
  9.8 0.6 %shard_map.64 = (bf16[1,24,128,128]{3,2,1,0:T(8,128)(2,1)S(1)}, f32[256,128]{1,0:T(8,128)S(1)}, f32[256,128]{1,0:T(8,128)S(1)}) custom-call(s32[8,128]{1,0:T(8,128)S(1)} %bitcast.13, f32[1024,128]{1,0:T(8,128)S(1)} %copy-done.1, bf16[1,24,128,128]{3,2,1,0:T(8,128)(2,1)S(1)} %bitcast.11), custom_call_target="tpu_custom_call" | custom-call | flops 131072 | bytes 524288 | tf_op jit(solution)/shard_map/pallas_call | solution.py:53
  10.4 4.2 %collective-permute-done.refs_0_ = s32[8,128]{1,0:T(8,128)S(1)} collective-permute-done((s32[8,128]{1,0:T(8,128)}, s32[8,128]{1,0:T(8,128)S(1)}, u32[]{:S(2)}, u32[]{:S(2)}) %collective-permute-start) | collective-permute-done | bytes 4128 | tf_op jit(solution)/shard_map/ppermute | solution.py:157
  14.6 0.0 collective-permute-done.1.refs_1_
  14.6 1.2 %shard_map.65 = (f32[256,128]{1,0:T(8,128)S(1)}, f32[256,128]{1,0:T(8,128)S(1)}, f32[256,128]{1,0:T(8,128)S(1)}, f32[256,128]{1,0:T(8,128)S(1)}) custom-call(s32[49]{0:T(128)S(1)} %add_bitcast_fusion.info_ref, bf16[24,128,128]{2,1,0:T(8,128)(2,1)S(1)} %bitcast.9, s32[8,128]{1,0:T(8,128)S(1)} %collective-permute-done.refs_0_, ...), custom_call_target="tpu_custom_call" | custom-call | flops 201326592 | bytes 1048576 | tf_op jit(solution)/shard_map/pallas_call | solution.py:126
  15.8 0.8 %collective-permute-start.2 = (f32[256,128]{1,0:T(8,128)S(1)}, f32[256,128]{1,0:T(8,128)S(1)}, u32[]{:S(2)}, u32[]{:S(2)}) collective-permute-start(f32[256,128]{1,0:T(8,128)S(1)} %get-tuple-element.19), channel_id=1, source_target_pairs={{0,1},{1,0},{2,3},{3,2},{4,5},{5,4},{6,7},{7,6},{8,9},{9,8},{10,11... | collective-permute-start | bytes 393224 | tf_op jit(solution)/shard_map/ppermute | solution.py:167
  16.6 0.1 collective-permute-start.4
  16.7 0.9 %collective-permute-done.2 = f32[256,128]{1,0:T(8,128)S(1)} collective-permute-done((f32[256,128]{1,0:T(8,128)S(1)}, f32[256,128]{1,0:T(8,128)S(1)}, u32[]{:S(2)}, u32[]{:S(2)}) %collective-permute-start.2) | collective-permute-done | bytes 131104 | tf_op jit(solution)/shard_map/ppermute | solution.py:167
  17.6 4.0 %collective-permute-start.3 = (f32[256,128]{1,0:T(8,128)S(1)}, f32[256,128]{1,0:T(8,128)S(1)}, u32[]{:S(2)}, u32[]{:S(2)}) collective-permute-start(f32[256,128]{1,0:T(8,128)S(1)} %add.24), channel_id=1, source_target_pairs={{2,0},{3,1},{0,2},{1,3},{6,4},{7,5},{4,6},{5,7},{10,8},{11,9},{8,1... | collective-permute-start | bytes 393224 | tf_op jit(solution)/shard_map/ppermute | solution.py:173
  21.6 0.0 collective-permute-done.4
  21.6 3.8 %collective-permute-done.3 = f32[256,128]{1,0:T(8,128)S(1)} collective-permute-done((f32[256,128]{1,0:T(8,128)S(1)}, f32[256,128]{1,0:T(8,128)S(1)}, u32[]{:S(2)}, u32[]{:S(2)}) %collective-permute-start.3) | collective-permute-done | bytes 131104 | tf_op jit(solution)/shard_map/ppermute | solution.py:173
  25.5 0.1 collective-permute-start.5
  25.5 1.3 %collective-permute-done.5 = f32[256,128]{1,0:T(8,128)S(1)} collective-permute-done((f32[256,128]{1,0:T(8,128)S(1)}, f32[256,128]{1,0:T(8,128)S(1)}, u32[]{:S(2)}, u32[]{:S(2)}) %collective-permute-start.5) | collective-permute-done | bytes 131104 | tf_op jit(solution)/shard_map/ppermute | solution.py:167
  26.9 1.3 %collective-permute-start.7 = (f32[512,128]{1,0:T(8,128)S(1)}, f32[512,128]{1,0:T(8,128)S(1)}, u32[]{:S(2)}, u32[]{:S(2)}) collective-permute-start(f32[512,128]{1,0:T(8,128)S(1)} %pad_maximum_fusion), channel_id=1, source_target_pairs={{1,0},{3,5},{0,10},{2,15},{5,4},{7,9},{4,14},{6,3},{9,8},{11,13},{... | collective-permute-start | bytes 786440 | tf_op jit(solution)/shard_map/ppermute | solution.py:157
  28.2 0.0 collective-permute-start.6
  28.2 3.9 %collective-permute-done.7.refs_1_ = f32[512,128]{1,0:T(8,128)S(1)} collective-permute-done((f32[512,128]{1,0:T(8,128)S(1)}, f32[512,128]{1,0:T(8,128)S(1)}, u32[]{:S(2)}, u32[]{:S(2)}) %collective-permute-start.7) | collective-permute-done | bytes 262176 | tf_op jit(solution)/shard_map/ppermute | solution.py:157
  32.1 6.4 %collective-permute-done.6.refs_0_ = f32[512,128]{1,0:T(8,128)S(1)} collective-permute-done((f32[512,128]{1,0:T(8,128)S(1)}, f32[512,128]{1,0:T(8,128)S(1)}, u32[]{:S(2)}, u32[]{:S(2)}) %collective-permute-start.6) | collective-permute-done | bytes 262176 | tf_op jit(solution)/shard_map/ppermute | solution.py:157
  38.4 1.2 %shard_map.66 = (f32[256,128]{1,0:T(8,128)S(1)}, f32[256,128]{1,0:T(8,128)S(1)}, f32[256,128]{1,0:T(8,128)S(1)}, f32[256,128]{1,0:T(8,128)S(1)}) custom-call(s32[49]{0:T(128)S(1)} %add_bitcast_fusion.info_ref, bf16[24,128,128]{2,1,0:T(8,128)(2,1)S(1)} %bitcast.10, f32[512,128]{1,0:T(8,128)S(1)} %collective-permute-done.6.refs_0_, ...), custom_call_target="tpu_custom_call" | custom-call | flops 201326592 | bytes 1048576 | tf_op jit(solution)/shard_map/pallas_call | solution.py:126
  39.6 2.7 %collective-permute-start.8 = (f32[256,128]{1,0:T(8,128)S(1)}, f32[256,128]{1,0:T(8,128)S(1)}, u32[]{:S(2)}, u32[]{:S(2)}) collective-permute-start(f32[256,128]{1,0:T(8,128)S(1)} %get-tuple-element.24), channel_id=1, source_target_pairs={{0,1},{1,0},{2,3},{3,2},{4,5},{5,4},{6,7},{7,6},{8,9},{9,8},{10,11... | collective-permute-start | bytes 393224 | tf_op jit(solution)/shard_map/ppermute | solution.py:167
  42.3 0.1 collective-permute-start.10
  42.4 0.9 %collective-permute-done.8 = f32[256,128]{1,0:T(8,128)S(1)} collective-permute-done((f32[256,128]{1,0:T(8,128)S(1)}, f32[256,128]{1,0:T(8,128)S(1)}, u32[]{:S(2)}, u32[]{:S(2)}) %collective-permute-start.8) | collective-permute-done | bytes 131104 | tf_op jit(solution)/shard_map/ppermute | solution.py:167
  43.3 3.2 %collective-permute-start.9 = (f32[256,128]{1,0:T(8,128)S(1)}, f32[256,128]{1,0:T(8,128)S(1)}, u32[]{:S(2)}, u32[]{:S(2)}) collective-permute-start(f32[256,128]{1,0:T(8,128)S(1)} %add.28), channel_id=1, source_target_pairs={{2,0},{3,1},{0,2},{1,3},{6,4},{7,5},{4,6},{5,7},{10,8},{11,9},{8,1... | collective-permute-start | bytes 393224 | tf_op jit(solution)/shard_map/ppermute | solution.py:173
  46.5 0.0 collective-permute-done.10
  46.5 3.8 %collective-permute-done.9 = f32[256,128]{1,0:T(8,128)S(1)} collective-permute-done((f32[256,128]{1,0:T(8,128)S(1)}, f32[256,128]{1,0:T(8,128)S(1)}, u32[]{:S(2)}, u32[]{:S(2)}) %collective-permute-start.9) | collective-permute-done | bytes 131104 | tf_op jit(solution)/shard_map/ppermute | solution.py:173
  50.3 0.7 %add_multiply_fusion = f32[256,128]{1,0:T(8,128)} fusion(f32[256,128]{1,0:T(8,128)S(1)} %get-tuple-element.22, f32[256,128]{1,0:T(8,128)S(1)} %collective-permute-done.9, f32[256,128]{1,0:T(8,128)S(1)} %get-tuple-element.25, f32[256,128]{1,0:T(8,128)S(1)} %collective-permute-done.10, f32[256,128]{1,0:T(8,128)S(1)} %get-tuple-element.16, ...), kind=kLoop, calls=%fused_computation.1 | loop fusion | flops 294912 | bytes 1179648 | tf_op jit(solution)/shard_map/div | solution.py:215
  (9 shorter events, 0.1 us)
Async XLA Ops:
  0.0 14.6 %collective-permute-start.1 = (f32[1024,128]{1,0:T(8,128)}, f32[1024,128]{1,0:T(8,128)S(1)}, u32[]{:S(2)}, u32[]{:S(2)}) collective-permute-start(f32[1024,128]{1,0:T(8,128)} %embeddings_ref.1), channel_id=1, source_target_pairs={{3,0},{1,5},{2,10},{0,15},{7,4},{5,9},{6,14},{4,3},{11,8},{9,13},{... | collective-permute-start | bytes 1572872 | tf_op jit(solution)/shard_map/ppermute | solution.py:157
  5.4 9.2 %collective-permute-start = (s32[8,128]{1,0:T(8,128)}, s32[8,128]{1,0:T(8,128)S(1)}, u32[]{:S(2)}, u32[]{:S(2)}) collective-permute-start(s32[8,128]{1,0:T(8,128)} %bitcast.12), channel_id=1, source_target_pairs={{3,0},{1,5},{2,10},{0,15},{7,4},{5,9},{6,14},{4,3},{11,8},{9,13},{... | collective-permute-start | bytes 12296 | tf_op jit(solution)/shard_map/ppermute | solution.py:157
  6.9 0.7 %copy-start.3 = (s32[1,1,1,24]{3,2,1,0:T(1,128)S(1)}, s32[1,1,1,24]{3,2,1,0:T(1,128)}, u32[]{:S(2)}) copy-start(s32[1,1,1,24]{3,2,1,0:T(1,128)} %param.10) | copy-start | bytes 292
  6.9 0.7 %copy-start.4 = (s32[1,1,1,24]{3,2,1,0:T(1,128)S(1)}, s32[1,1,1,24]{3,2,1,0:T(1,128)}, u32[]{:S(2)}) copy-start(s32[1,1,1,24]{3,2,1,0:T(1,128)} %param.9) | copy-start | bytes 292
  6.9 0.7 %copy-start.2 = (s32[1024]{0:T(1024)S(1)}, s32[1024]{0:T(1024)}, u32[]{:S(2)}) copy-start(s32[1024]{0:T(1024)} %param.7) | copy-start | bytes 12292
  7.6 1.1 %copy-start = (bf16[1,1,1,24,128,128]{5,4,3,2,1,0:T(8,128)(2,1)S(1)}, bf16[1,1,1,24,128,128]{5,4,3,2,1,0:T(8,128)(2,1)}, u32[]{:S(2)}) copy-start(bf16[1,1,1,24,128,128]{5,4,3,2,1,0:T(8,128)(2,1)} %param.8) | copy-start | bytes 2359300
  8.8 1.0 %copy-start.1 = (f32[1024,128]{1,0:T(8,128)S(1)}, f32[1024,128]{1,0:T(8,128)}, u32[]{:S(2)}) copy-start(f32[1024,128]{1,0:T(8,128)} %embeddings_ref.1) | copy-start | bytes 1572868
  15.8 1.8 %collective-permute-start.2 = (f32[256,128]{1,0:T(8,128)S(1)}, f32[256,128]{1,0:T(8,128)S(1)}, u32[]{:S(2)}, u32[]{:S(2)}) collective-permute-start(f32[256,128]{1,0:T(8,128)S(1)} %get-tuple-element.19), channel_id=1, source_target_pairs={{0,1},{1,0},{2,3},{3,2},{4,5},{5,4},{6,7},{7,6},{8,9},{9,8},{10,11... | collective-permute-start | bytes 393224 | tf_op jit(solution)/shard_map/ppermute | solution.py:167
  16.6 5.0 %collective-permute-start.4 = (f32[256,128]{1,0:T(8,128)S(1)}, f32[256,128]{1,0:T(8,128)S(1)}, u32[]{:S(2)}, u32[]{:S(2)}) collective-permute-start(f32[256,128]{1,0:T(8,128)S(1)} %get-tuple-element.21), channel_id=1, source_target_pairs={{0,1},{1,0},{2,3},{3,2},{4,5},{5,4},{6,7},{7,6},{8,9},{9,8},{10,11... | collective-permute-start | bytes 393224 | tf_op jit(solution)/shard_map/ppermute | solution.py:167
  17.6 7.8 %collective-permute-start.3 = (f32[256,128]{1,0:T(8,128)S(1)}, f32[256,128]{1,0:T(8,128)S(1)}, u32[]{:S(2)}, u32[]{:S(2)}) collective-permute-start(f32[256,128]{1,0:T(8,128)S(1)} %add.24), channel_id=1, source_target_pairs={{2,0},{3,1},{0,2},{1,3},{6,4},{7,5},{4,6},{5,7},{10,8},{11,9},{8,1... | collective-permute-start | bytes 393224 | tf_op jit(solution)/shard_map/ppermute | solution.py:173
  25.5 1.4 %collective-permute-start.5 = (f32[256,128]{1,0:T(8,128)S(1)}, f32[256,128]{1,0:T(8,128)S(1)}, u32[]{:S(2)}, u32[]{:S(2)}) collective-permute-start(f32[256,128]{1,0:T(8,128)S(1)} %fusion), channel_id=1, source_target_pairs={{0,1},{1,0},{2,3},{3,2},{4,5},{5,4},{6,7},{7,6},{8,9},{9,8},{10,11... | collective-permute-start | bytes 393224 | tf_op jit(solution)/shard_map/ppermute | solution.py:167
  26.9 5.2 %collective-permute-start.7 = (f32[512,128]{1,0:T(8,128)S(1)}, f32[512,128]{1,0:T(8,128)S(1)}, u32[]{:S(2)}, u32[]{:S(2)}) collective-permute-start(f32[512,128]{1,0:T(8,128)S(1)} %pad_maximum_fusion), channel_id=1, source_target_pairs={{1,0},{3,5},{0,10},{2,15},{5,4},{7,9},{4,14},{6,3},{9,8},{11,13},{... | collective-permute-start | bytes 786440 | tf_op jit(solution)/shard_map/ppermute | solution.py:157
  28.2 10.3 %collective-permute-start.6 = (f32[512,128]{1,0:T(8,128)S(1)}, f32[512,128]{1,0:T(8,128)S(1)}, u32[]{:S(2)}, u32[]{:S(2)}) collective-permute-start(f32[512,128]{1,0:T(8,128)S(1)} %pad_maximum_fusion), channel_id=1, source_target_pairs={{2,0},{0,5},{3,10},{1,15},{6,4},{4,9},{7,14},{5,3},{10,8},{8,13},{... | collective-permute-start | bytes 786440 | tf_op jit(solution)/shard_map/ppermute | solution.py:157
  39.6 3.7 %collective-permute-start.8 = (f32[256,128]{1,0:T(8,128)S(1)}, f32[256,128]{1,0:T(8,128)S(1)}, u32[]{:S(2)}, u32[]{:S(2)}) collective-permute-start(f32[256,128]{1,0:T(8,128)S(1)} %get-tuple-element.24), channel_id=1, source_target_pairs={{0,1},{1,0},{2,3},{3,2},{4,5},{5,4},{6,7},{7,6},{8,9},{9,8},{10,11... | collective-permute-start | bytes 393224 | tf_op jit(solution)/shard_map/ppermute | solution.py:167
  42.3 4.2 %collective-permute-start.10 = (f32[256,128]{1,0:T(8,128)S(1)}, f32[256,128]{1,0:T(8,128)S(1)}, u32[]{:S(2)}, u32[]{:S(2)}) collective-permute-start(f32[256,128]{1,0:T(8,128)S(1)} %get-tuple-element.26), channel_id=1, source_target_pairs={{0,1},{1,0},{2,3},{3,2},{4,5},{5,4},{6,7},{7,6},{8,9},{9,8},{10,11... | collective-permute-start | bytes 393224 | tf_op jit(solution)/shard_map/ppermute | solution.py:167
  43.3 7.0 %collective-permute-start.9 = (f32[256,128]{1,0:T(8,128)S(1)}, f32[256,128]{1,0:T(8,128)S(1)}, u32[]{:S(2)}, u32[]{:S(2)}) collective-permute-start(f32[256,128]{1,0:T(8,128)S(1)} %add.28), channel_id=1, source_target_pairs={{2,0},{3,1},{0,2},{1,3},{6,4},{7,5},{4,6},{5,7},{10,8},{11,9},{8,1... | collective-permute-start | bytes 393224 | tf_op jit(solution)/shard_map/ppermute | solution.py:173

commit v3 on v1

--- a/solution.py
+++ b/solution.py
@@ -20,7 +20,7 @@
 
 def source_team(team, turn, team_count):
     if team_count == 4:
-        return (2 * (team % 2) + team // 2) ^ turn
+        return (2 * (team % 2) + team // 2) ^ (3 - turn)
     return (team + turn) % team_count
 
 

time: 49.7 us -> 52.2 us (1.050)
  starting transfers between devices: 21.5 us -> 25.9 us
  waiting for transfers between devices: 20.6 us -> 18.8 us
    ppermute x6, starting transfers between devices: 11 us -> 15.6 us  [fetch(): return lax.ppermute(value, ('blk', 'rep'), pairs)]
    ppermute x4, starting transfers between devices: 3.92 us -> 1.79 us  [from_mate(): lax.ppermute(value, 'rep', [(team, team ^ 1) for team in range(team_count)])]
    ppermute x6, waiting for transfers between devices: 11.2 us -> 9.14 us  [fetch(): return lax.ppermute(value, ('blk', 'rep'), pairs)]
    ppermute x2, starting transfers between devices: 6.56 us -> 8.48 us  [from_column(): return lax.ppermute(value, 'rep', pairs)]
where the time goes in v3:
time: 52.2 us; the launch traced here: 52 us
  starting transfers between devices  25.9 us (50%)
  waiting for transfers between devices  18.8 us (36%)
  Pallas kernels  2.9 us (6%)
  local copies, waits for them, and re-layouts  2.83 us (5%)
  other arithmetic  0.88 us (2%)
  between operations  0.73 us (1%)
    ppermute x6, starting transfers between devices, fetch(): return lax.ppermute(value, ('blk', 'rep'), pairs)  15.6 us
    ppermute x6, waiting for transfers between devices, fetch(): return lax.ppermute(value, ('blk', 'rep'), pairs)  9.14 us
    ppermute x2, starting transfers between devices, from_column(): return lax.ppermute(value, 'rep', pairs)  8.48 us
    ppermute x2, waiting for transfers between devices, from_column(): return lax.ppermute(value, 'rep', pairs)  7.81 us
    unnamed x10, local copies, waits for them, and re-layouts  2.83 us
    pallas_call x2, Pallas kernels, arc_step(): pl.pallas_call(functools.partial(arc_kernel, team_count=team_count, piece...  2.33 us
    ppermute x4, waiting for transfers between devices, from_mate(): lax.ppermute(value, 'rep', [(team, team ^ 1) for team in range(team_count)])  1.82 us
    ppermute x4, starting transfers between devices, from_mate(): lax.ppermute(value, 'rep', [(team, team ^ 1) for team in range(team_count)])  1.79 us
  transfers between devices with their start and end apart: 12, of which 8 were waited for; matrix products, arithmetic and copies ran while one was open for 0% of the time, Pallas kernels for 1%

profile of v3, /device:TPU:0, one launch (start us, length us, event | category | flops | bytes accessed | tf_op | source)
XLA Modules:
  0.0 52.0 jit_solution(16785860629607638885)
XLA Ops:
  0.0 5.4 %collective-permute-start.1 = (f32[1024,128]{1,0:T(8,128)}, f32[1024,128]{1,0:T(8,128)S(1)}, u32[]{:S(2)}, u32[]{:S(2)}) collective-permute-start(f32[1024,128]{1,0:T(8,128)} %embeddings_ref.1), channel_id=1, source_target_pairs={{3,0},{1,5},{2,10},{0,15},{7,4},{5,9},{6,14},{4,3},{11,8},{9,13},{... | collective-permute-start | bytes 1572872 | tf_op jit(solution)/shard_map/ppermute | solution.py:155
  5.4 0.8 %collective-permute-start = (s32[8,128]{1,0:T(8,128)}, s32[8,128]{1,0:T(8,128)S(1)}, u32[]{:S(2)}, u32[]{:S(2)}) collective-permute-start(s32[8,128]{1,0:T(8,128)} %bitcast.12), channel_id=1, source_target_pairs={{3,0},{1,5},{2,10},{0,15},{7,4},{5,9},{6,14},{4,3},{11,8},{9,13},{... | collective-permute-start | bytes 12296 | tf_op jit(solution)/shard_map/ppermute | solution.py:155
  6.9 0.6 %copy-done.3 = s32[1,1,1,24]{3,2,1,0:T(1,128)S(1)} copy-done((s32[1,1,1,24]{3,2,1,0:T(1,128)S(1)}, s32[1,1,1,24]{3,2,1,0:T(1,128)}, u32[]{:S(2)}) %copy-start.3) | copy-done | bytes 120
  7.5 0.0 copy-done.4
  7.6 0.1 add_bitcast_fusion.info_ref
  7.6 1.1 %copy-done = bf16[1,1,1,24,128,128]{5,4,3,2,1,0:T(8,128)(2,1)S(1)} copy-done((bf16[1,1,1,24,128,128]{5,4,3,2,1,0:T(8,128)(2,1)S(1)}, bf16[1,1,1,24,128,128]{5,4,3,2,1,0:T(8,128)(2,1)}, u32[]{:S(2)}) %copy-start) | copy-done | bytes 786456
  8.8 1.0 %copy-done.1 = f32[1024,128]{1,0:T(8,128)S(1)} copy-done((f32[1024,128]{1,0:T(8,128)S(1)}, f32[1024,128]{1,0:T(8,128)}, u32[]{:S(2)}) %copy-start.1) | copy-done | bytes 524312
  9.8 0.6 %shard_map.64 = (bf16[1,24,128,128]{3,2,1,0:T(8,128)(2,1)S(1)}, f32[256,128]{1,0:T(8,128)S(1)}, f32[256,128]{1,0:T(8,128)S(1)}) custom-call(s32[8,128]{1,0:T(8,128)S(1)} %bitcast.13, f32[1024,128]{1,0:T(8,128)S(1)} %copy-done.1, bf16[1,24,128,128]{3,2,1,0:T(8,128)(2,1)S(1)} %bitcast.11), custom_call_target="tpu_custom_call" | custom-call | flops 131072 | bytes 524288 | tf_op jit(solution)/shard_map/pallas_call | solution.py:53
  10.4 4.2 %collective-permute-done.refs_0_ = s32[8,128]{1,0:T(8,128)S(1)} collective-permute-done((s32[8,128]{1,0:T(8,128)}, s32[8,128]{1,0:T(8,128)S(1)}, u32[]{:S(2)}, u32[]{:S(2)}) %collective-permute-start) | collective-permute-done | bytes 4128 | tf_op jit(solution)/shard_map/ppermute | solution.py:155
  14.6 0.0 collective-permute-done.1.refs_1_
  14.6 1.2 %shard_map.65 = (f32[256,128]{1,0:T(8,128)S(1)}, f32[256,128]{1,0:T(8,128)S(1)}, f32[256,128]{1,0:T(8,128)S(1)}, f32[256,128]{1,0:T(8,128)S(1)}) custom-call(s32[49]{0:T(128)S(1)} %add_bitcast_fusion.info_ref, bf16[24,128,128]{2,1,0:T(8,128)(2,1)S(1)} %bitcast.9, s32[8,128]{1,0:T(8,128)S(1)} %collective-permute-done.refs_0_, ...), custom_call_target="tpu_custom_call" | custom-call | flops 201326592 | bytes 1048576 | tf_op jit(solution)/shard_map/pallas_call | solution.py:124
  15.8 0.8 %collective-permute-start.2 = (f32[256,128]{1,0:T(8,128)S(1)}, f32[256,128]{1,0:T(8,128)S(1)}, u32[]{:S(2)}, u32[]{:S(2)}) collective-permute-start(f32[256,128]{1,0:T(8,128)S(1)} %get-tuple-element.19), channel_id=1, source_target_pairs={{0,1},{1,0},{2,3},{3,2},{4,5},{5,4},{6,7},{7,6},{8,9},{9,8},{10,11... | collective-permute-start | bytes 393224 | tf_op jit(solution)/shard_map/ppermute | solution.py:165
  16.6 0.1 collective-permute-start.4
  16.7 0.9 %collective-permute-done.2 = f32[256,128]{1,0:T(8,128)S(1)} collective-permute-done((f32[256,128]{1,0:T(8,128)S(1)}, f32[256,128]{1,0:T(8,128)S(1)}, u32[]{:S(2)}, u32[]{:S(2)}) %collective-permute-start.2) | collective-permute-done | bytes 131104 | tf_op jit(solution)/shard_map/ppermute | solution.py:165
  17.6 4.0 %collective-permute-start.3 = (f32[256,128]{1,0:T(8,128)S(1)}, f32[256,128]{1,0:T(8,128)S(1)}, u32[]{:S(2)}, u32[]{:S(2)}) collective-permute-start(f32[256,128]{1,0:T(8,128)S(1)} %add.24), channel_id=1, source_target_pairs={{2,0},{3,1},{0,2},{1,3},{6,4},{7,5},{4,6},{5,7},{10,8},{11,9},{8,1... | collective-permute-start | bytes 393224 | tf_op jit(solution)/shard_map/ppermute | solution.py:171
  21.6 0.0 collective-permute-done.4
  21.6 3.8 %collective-permute-done.3 = f32[256,128]{1,0:T(8,128)S(1)} collective-permute-done((f32[256,128]{1,0:T(8,128)S(1)}, f32[256,128]{1,0:T(8,128)S(1)}, u32[]{:S(2)}, u32[]{:S(2)}) %collective-permute-start.3) | collective-permute-done | bytes 131104 | tf_op jit(solution)/shard_map/ppermute | solution.py:171
  25.5 0.7 %collective-permute-start.8 = (f32[256,128]{1,0:T(8,128)S(1)}, f32[256,128]{1,0:T(8,128)S(1)}, u32[]{:S(2)}, u32[]{:S(2)}) collective-permute-start(f32[256,128]{1,0:T(8,128)S(1)} %fusion), channel_id=1, source_target_pairs={{0,0},{2,5},{1,10},{3,15},{4,4},{6,9},{5,14},{7,3},{8,8},{10,13},{... | collective-permute-start | bytes 393224 | tf_op jit(solution)/shard_map/ppermute | solution.py:155
  26.1 5.5 %collective-permute-start.7 = (f32[256,128]{1,0:T(8,128)S(1)}, f32[256,128]{1,0:T(8,128)S(1)}, u32[]{:S(2)}, u32[]{:S(2)}) collective-permute-start(f32[256,128]{1,0:T(8,128)S(1)} %fusion), channel_id=1, source_target_pairs={{1,0},{3,5},{0,10},{2,15},{5,4},{7,9},{4,14},{6,3},{9,8},{11,13},{... | collective-permute-start | bytes 393224 | tf_op jit(solution)/shard_map/ppermute | solution.py:155
  31.6 0.8 %collective-permute-start.6 = (f32[256,128]{1,0:T(8,128)S(1)}, f32[256,128]{1,0:T(8,128)S(1)}, u32[]{:S(2)}, u32[]{:S(2)}) collective-permute-start(f32[256,128]{1,0:T(8,128)S(1)} %fusion), channel_id=1, source_target_pairs={{2,0},{0,5},{3,10},{1,15},{6,4},{4,9},{7,14},{5,3},{10,8},{8,13},{... | collective-permute-start | bytes 393224 | tf_op jit(solution)/shard_map/ppermute | solution.py:155
  32.5 2.4 %collective-permute-start.5 = (f32[256,128]{1,0:T(8,128)S(1)}, f32[256,128]{1,0:T(8,128)S(1)}, u32[]{:S(2)}, u32[]{:S(2)}) collective-permute-start(f32[256,128]{1,0:T(8,128)S(1)} %fusion), channel_id=1, source_target_pairs={{3,0},{1,5},{2,10},{0,15},{7,4},{5,9},{6,14},{4,3},{11,8},{9,13},{... | collective-permute-start | bytes 393224 | tf_op jit(solution)/shard_map/ppermute | solution.py:155
  34.9 0.0 collective-permute-done.8.refs_3_
  34.9 0.2 collective-permute-done.7.refs_2_
  35.0 4.3 %collective-permute-done.6.refs_1_ = f32[256,128]{1,0:T(8,128)S(1)} collective-permute-done((f32[256,128]{1,0:T(8,128)S(1)}, f32[256,128]{1,0:T(8,128)S(1)}, u32[]{:S(2)}, u32[]{:S(2)}) %collective-permute-start.6) | collective-permute-done | bytes 131104 | tf_op jit(solution)/shard_map/ppermute | solution.py:155
  39.3 0.5 collective-permute-done.5.refs_0_
  39.8 1.2 %shard_map.66 = (f32[256,128]{1,0:T(8,128)S(1)}, f32[256,128]{1,0:T(8,128)S(1)}, f32[256,128]{1,0:T(8,128)S(1)}, f32[256,128]{1,0:T(8,128)S(1)}) custom-call(s32[49]{0:T(128)S(1)} %add_bitcast_fusion.info_ref, bf16[24,128,128]{2,1,0:T(8,128)(2,1)S(1)} %bitcast.10, f32[256,128]{1,0:T(8,128)S(1)} %collective-permute-done.5.refs_0_, ...), custom_call_target="tpu_custom_call" | custom-call | flops 201326592 | bytes 1048576 | tf_op jit(solution)/shard_map/pallas_call | solution.py:124
  41.0 0.8 %collective-permute-start.9 = (f32[256,128]{1,0:T(8,128)S(1)}, f32[256,128]{1,0:T(8,128)S(1)}, u32[]{:S(2)}, u32[]{:S(2)}) collective-permute-start(f32[256,128]{1,0:T(8,128)S(1)} %get-tuple-element.24), channel_id=1, source_target_pairs={{0,1},{1,0},{2,3},{3,2},{4,5},{5,4},{6,7},{7,6},{8,9},{9,8},{10,11... | collective-permute-start | bytes 393224 | tf_op jit(solution)/shard_map/ppermute | solution.py:165
  41.8 0.1 collective-permute-start.11
  41.9 0.9 %collective-permute-done.9 = f32[256,128]{1,0:T(8,128)S(1)} collective-permute-done((f32[256,128]{1,0:T(8,128)S(1)}, f32[256,128]{1,0:T(8,128)S(1)}, u32[]{:S(2)}, u32[]{:S(2)}) %collective-permute-start.9) | collective-permute-done | bytes 131104 | tf_op jit(solution)/shard_map/ppermute | solution.py:165
  42.8 4.5 %collective-permute-start.10 = (f32[256,128]{1,0:T(8,128)S(1)}, f32[256,128]{1,0:T(8,128)S(1)}, u32[]{:S(2)}, u32[]{:S(2)}) collective-permute-start(f32[256,128]{1,0:T(8,128)S(1)} %add.28), channel_id=1, source_target_pairs={{2,0},{3,1},{0,2},{1,3},{6,4},{7,5},{4,6},{5,7},{10,8},{11,9},{8,1... | collective-permute-start | bytes 393224 | tf_op jit(solution)/shard_map/ppermute | solution.py:171
  47.3 4.0 %collective-permute-done.10 = f32[256,128]{1,0:T(8,128)S(1)} collective-permute-done((f32[256,128]{1,0:T(8,128)S(1)}, f32[256,128]{1,0:T(8,128)S(1)}, u32[]{:S(2)}, u32[]{:S(2)}) %collective-permute-start.10) | collective-permute-done | bytes 131104 | tf_op jit(solution)/shard_map/ppermute | solution.py:171
  51.3 0.7 %add_multiply_fusion = f32[256,128]{1,0:T(8,128)} fusion(f32[256,128]{1,0:T(8,128)S(1)} %get-tuple-element.22, f32[256,128]{1,0:T(8,128)S(1)} %collective-permute-done.10, f32[256,128]{1,0:T(8,128)S(1)} %get-tuple-element.25, f32[256,128]{1,0:T(8,128)S(1)} %collective-permute-done.11, f32[256,128]{1,0:T(8,128)S(1)} %get-tuple-element.16, ...), kind=kLoop, calls=%fused_computation | loop fusion | flops 294912 | bytes 1179648 | tf_op jit(solution)/shard_map/div | solution.py:212
  (10 shorter events, 0.1 us)
Async XLA Ops:
  0.0 14.6 %collective-permute-start.1 = (f32[1024,128]{1,0:T(8,128)}, f32[1024,128]{1,0:T(8,128)S(1)}, u32[]{:S(2)}, u32[]{:S(2)}) collective-permute-start(f32[1024,128]{1,0:T(8,128)} %embeddings_ref.1), channel_id=1, source_target_pairs={{3,0},{1,5},{2,10},{0,15},{7,4},{5,9},{6,14},{4,3},{11,8},{9,13},{... | collective-permute-start | bytes 1572872 | tf_op jit(solution)/shard_map/ppermute | solution.py:155
  5.4 9.2 %collective-permute-start = (s32[8,128]{1,0:T(8,128)}, s32[8,128]{1,0:T(8,128)S(1)}, u32[]{:S(2)}, u32[]{:S(2)}) collective-permute-start(s32[8,128]{1,0:T(8,128)} %bitcast.12), channel_id=1, source_target_pairs={{3,0},{1,5},{2,10},{0,15},{7,4},{5,9},{6,14},{4,3},{11,8},{9,13},{... | collective-permute-start | bytes 12296 | tf_op jit(solution)/shard_map/ppermute | solution.py:155
  6.9 0.7 %copy-start.3 = (s32[1,1,1,24]{3,2,1,0:T(1,128)S(1)}, s32[1,1,1,24]{3,2,1,0:T(1,128)}, u32[]{:S(2)}) copy-start(s32[1,1,1,24]{3,2,1,0:T(1,128)} %param.10) | copy-start | bytes 292
  6.9 0.7 %copy-start.4 = (s32[1,1,1,24]{3,2,1,0:T(1,128)S(1)}, s32[1,1,1,24]{3,2,1,0:T(1,128)}, u32[]{:S(2)}) copy-start(s32[1,1,1,24]{3,2,1,0:T(1,128)} %param.9) | copy-start | bytes 292
  6.9 0.7 %copy-start.2 = (s32[1024]{0:T(1024)S(1)}, s32[1024]{0:T(1024)}, u32[]{:S(2)}) copy-start(s32[1024]{0:T(1024)} %param.7) | copy-start | bytes 12292
  7.6 1.1 %copy-start = (bf16[1,1,1,24,128,128]{5,4,3,2,1,0:T(8,128)(2,1)S(1)}, bf16[1,1,1,24,128,128]{5,4,3,2,1,0:T(8,128)(2,1)}, u32[]{:S(2)}) copy-start(bf16[1,1,1,24,128,128]{5,4,3,2,1,0:T(8,128)(2,1)} %param.8) | copy-start | bytes 2359300
  8.8 1.0 %copy-start.1 = (f32[1024,128]{1,0:T(8,128)S(1)}, f32[1024,128]{1,0:T(8,128)}, u32[]{:S(2)}) copy-start(f32[1024,128]{1,0:T(8,128)} %embeddings_ref.1) | copy-start | bytes 1572868
  15.8 1.8 %collective-permute-start.2 = (f32[256,128]{1,0:T(8,128)S(1)}, f32[256,128]{1,0:T(8,128)S(1)}, u32[]{:S(2)}, u32[]{:S(2)}) collective-permute-start(f32[256,128]{1,0:T(8,128)S(1)} %get-tuple-element.19), channel_id=1, source_target_pairs={{0,1},{1,0},{2,3},{3,2},{4,5},{5,4},{6,7},{7,6},{8,9},{9,8},{10,11... | collective-permute-start | bytes 393224 | tf_op jit(solution)/shard_map/ppermute | solution.py:165
  16.6 5.0 %collective-permute-start.4 = (f32[256,128]{1,0:T(8,128)S(1)}, f32[256,128]{1,0:T(8,128)S(1)}, u32[]{:S(2)}, u32[]{:S(2)}) collective-permute-start(f32[256,128]{1,0:T(8,128)S(1)} %get-tuple-element.21), channel_id=1, source_target_pairs={{0,1},{1,0},{2,3},{3,2},{4,5},{5,4},{6,7},{7,6},{8,9},{9,8},{10,11... | collective-permute-start | bytes 393224 | tf_op jit(solution)/shard_map/ppermute | solution.py:165
  17.6 7.8 %collective-permute-start.3 = (f32[256,128]{1,0:T(8,128)S(1)}, f32[256,128]{1,0:T(8,128)S(1)}, u32[]{:S(2)}, u32[]{:S(2)}) collective-permute-start(f32[256,128]{1,0:T(8,128)S(1)} %add.24), channel_id=1, source_target_pairs={{2,0},{3,1},{0,2},{1,3},{6,4},{7,5},{4,6},{5,7},{10,8},{11,9},{8,1... | collective-permute-start | bytes 393224 | tf_op jit(solution)/shard_map/ppermute | solution.py:171
  25.5 9.4 %collective-permute-start.8 = (f32[256,128]{1,0:T(8,128)S(1)}, f32[256,128]{1,0:T(8,128)S(1)}, u32[]{:S(2)}, u32[]{:S(2)}) collective-permute-start(f32[256,128]{1,0:T(8,128)S(1)} %fusion), channel_id=1, source_target_pairs={{0,0},{2,5},{1,10},{3,15},{4,4},{6,9},{5,14},{7,3},{8,8},{10,13},{... | collective-permute-start | bytes 393224 | tf_op jit(solution)/shard_map/ppermute | solution.py:155
  26.1 8.9 %collective-permute-start.7 = (f32[256,128]{1,0:T(8,128)S(1)}, f32[256,128]{1,0:T(8,128)S(1)}, u32[]{:S(2)}, u32[]{:S(2)}) collective-permute-start(f32[256,128]{1,0:T(8,128)S(1)} %fusion), channel_id=1, source_target_pairs={{1,0},{3,5},{0,10},{2,15},{5,4},{7,9},{4,14},{6,3},{9,8},{11,13},{... | collective-permute-start | bytes 393224 | tf_op jit(solution)/shard_map/ppermute | solution.py:155
  31.6 7.7 %collective-permute-start.6 = (f32[256,128]{1,0:T(8,128)S(1)}, f32[256,128]{1,0:T(8,128)S(1)}, u32[]{:S(2)}, u32[]{:S(2)}) collective-permute-start(f32[256,128]{1,0:T(8,128)S(1)} %fusion), channel_id=1, source_target_pairs={{2,0},{0,5},{3,10},{1,15},{6,4},{4,9},{7,14},{5,3},{10,8},{8,13},{... | collective-permute-start | bytes 393224 | tf_op jit(solution)/shard_map/ppermute | solution.py:155
  32.5 7.3 %collective-permute-start.5 = (f32[256,128]{1,0:T(8,128)S(1)}, f32[256,128]{1,0:T(8,128)S(1)}, u32[]{:S(2)}, u32[]{:S(2)}) collective-permute-start(f32[256,128]{1,0:T(8,128)S(1)} %fusion), channel_id=1, source_target_pairs={{3,0},{1,5},{2,10},{0,15},{7,4},{5,9},{6,14},{4,3},{11,8},{9,13},{... | collective-permute-start | bytes 393224 | tf_op jit(solution)/shard_map/ppermute | solution.py:155
  41.0 1.8 %collective-permute-start.9 = (f32[256,128]{1,0:T(8,128)S(1)}, f32[256,128]{1,0:T(8,128)S(1)}, u32[]{:S(2)}, u32[]{:S(2)}) collective-permute-start(f32[256,128]{1,0:T(8,128)S(1)} %get-tuple-element.24), channel_id=1, source_target_pairs={{0,1},{1,0},{2,3},{3,2},{4,5},{5,4},{6,7},{7,6},{8,9},{9,8},{10,11... | collective-permute-start | bytes 393224 | tf_op jit(solution)/shard_map/ppermute | solution.py:165
  41.8 5.5 %collective-permute-start.11 = (f32[256,128]{1,0:T(8,128)S(1)}, f32[256,128]{1,0:T(8,128)S(1)}, u32[]{:S(2)}, u32[]{:S(2)}) collective-permute-start(f32[256,128]{1,0:T(8,128)S(1)} %get-tuple-element.26), channel_id=1, source_target_pairs={{0,1},{1,0},{2,3},{3,2},{4,5},{5,4},{6,7},{7,6},{8,9},{9,8},{10,11... | collective-permute-start | bytes 393224 | tf_op jit(solution)/shard_map/ppermute | solution.py:165
  42.8 8.5 %collective-permute-start.10 = (f32[256,128]{1,0:T(8,128)S(1)}, f32[256,128]{1,0:T(8,128)S(1)}, u32[]{:S(2)}, u32[]{:S(2)}) collective-permute-start(f32[256,128]{1,0:T(8,128)S(1)} %add.28), channel_id=1, source_target_pairs={{2,0},{3,1},{0,2},{1,3},{6,4},{7,5},{4,6},{5,7},{10,8},{11,9},{8,1... | collective-permute-start | bytes 393224 | tf_op jit(solution)/shard_map/ppermute | solution.py:171

commit v4 on v1

--- a/solution.py
+++ b/solution.py
@@ -186,7 +186,7 @@
     arc_length, _, tile_size, _ = tile_values.shape[2:]
     panel_rows = embeddings.shape[0]
     team_count = lax.axis_size("rep")
-    spread = (3, 1, 2, 0) if team_count == 4 else tuple(range(team_count))
+    spread = (1, 3, 0, 2) if team_count == 4 else tuple(range(team_count))
     degrees = degrees.reshape(panel_rows // tile_size, tile_size)
 
     panel = fetch(embeddings, lambda team: spread[team], arc_length)

time: 49.7 us -> 50.6 us (1.018)
  starting transfers between devices: 21.5 us -> 23.8 us
  waiting for transfers between devices: 20.6 us -> 19.3 us
    ppermute x4, starting transfers between devices: 3.92 us -> 8.35 us  [from_mate(): lax.ppermute(value, 'rep', [(team, team ^ 1) for team in range(team_count)])]
    ppermute x6, waiting for transfers between devices: 11.2 us -> 9.85 us  [fetch(): return lax.ppermute(value, ('blk', 'rep'), pairs)]
    ppermute x6, starting transfers between devices: 11 us -> 9.81 us  [fetch(): return lax.ppermute(value, ('blk', 'rep'), pairs)]
    ppermute x2, starting transfers between devices: 6.56 us -> 5.61 us  [from_column(): return lax.ppermute(value, 'rep', pairs)]
where the time goes in v4:
time: 50.6 us; the launch traced here: 50.4 us
  starting transfers between devices  23.8 us (47%)
  waiting for transfers between devices  19.3 us (38%)
  Pallas kernels  2.9 us (6%)
  local copies, waits for them, and re-layouts  2.83 us (6%)
  other arithmetic  0.88 us (2%)
  between operations  0.73 us (1%)
    ppermute x6, waiting for transfers between devices, fetch(): return lax.ppermute(value, ('blk', 'rep'), pairs)  9.85 us
    ppermute x6, starting transfers between devices, fetch(): return lax.ppermute(value, ('blk', 'rep'), pairs)  9.81 us
    ppermute x4, starting transfers between devices, from_mate(): lax.ppermute(value, 'rep', [(team, team ^ 1) for team in range(team_count)])  8.35 us
    ppermute x2, waiting for transfers between devices, from_column(): return lax.ppermute(value, 'rep', pairs)  7.61 us
    ppermute x2, starting transfers between devices, from_column(): return lax.ppermute(value, 'rep', pairs)  5.61 us
    unnamed x10, local copies, waits for them, and re-layouts  2.83 us
    pallas_call x2, Pallas kernels, arc_step(): pl.pallas_call(functools.partial(arc_kernel, team_count=team_count, piece...  2.33 us
    ppermute x4, waiting for transfers between devices, from_mate(): lax.ppermute(value, 'rep', [(team, team ^ 1) for team in range(team_count)])  1.82 us
  transfers between devices with their start and end apart: 12, of which 8 were waited for; matrix products, arithmetic and copies ran while one was open for 0% of the time, Pallas kernels for 1%

profile of v4, /device:TPU:0, one launch (start us, length us, event | category | flops | bytes accessed | tf_op | source)
XLA Modules:
  0.0 50.4 jit_solution(1925642926500999338)
XLA Ops:
  0.0 5.0 %collective-permute-start.1 = (f32[1024,128]{1,0:T(8,128)}, f32[1024,128]{1,0:T(8,128)S(1)}, u32[]{:S(2)}, u32[]{:S(2)}) collective-permute-start(f32[1024,128]{1,0:T(8,128)} %embeddings_ref.1), channel_id=1, source_target_pairs={{1,0},{3,5},{0,10},{2,15},{5,4},{7,9},{4,14},{6,3},{9,8},{11,13},{... | collective-permute-start | bytes 1572872 | tf_op jit(solution)/shard_map/ppermute | solution.py:155
  5.0 0.0 collective-permute-start
  5.7 0.6 %copy-done.3 = s32[1,1,1,24]{3,2,1,0:T(1,128)S(1)} copy-done((s32[1,1,1,24]{3,2,1,0:T(1,128)S(1)}, s32[1,1,1,24]{3,2,1,0:T(1,128)}, u32[]{:S(2)}) %copy-start.3) | copy-done | bytes 120
  6.3 0.0 copy-done.4
  6.3 0.1 add_bitcast_fusion.info_ref
  6.4 1.1 %copy-done = bf16[1,1,1,24,128,128]{5,4,3,2,1,0:T(8,128)(2,1)S(1)} copy-done((bf16[1,1,1,24,128,128]{5,4,3,2,1,0:T(8,128)(2,1)S(1)}, bf16[1,1,1,24,128,128]{5,4,3,2,1,0:T(8,128)(2,1)}, u32[]{:S(2)}) %copy-start) | copy-done | bytes 786456
  7.5 1.0 %copy-done.1 = f32[1024,128]{1,0:T(8,128)S(1)} copy-done((f32[1024,128]{1,0:T(8,128)S(1)}, f32[1024,128]{1,0:T(8,128)}, u32[]{:S(2)}) %copy-start.1) | copy-done | bytes 524312
  8.6 0.6 %shard_map.64 = (bf16[1,24,128,128]{3,2,1,0:T(8,128)(2,1)S(1)}, f32[256,128]{1,0:T(8,128)S(1)}, f32[256,128]{1,0:T(8,128)S(1)}) custom-call(s32[8,128]{1,0:T(8,128)S(1)} %bitcast.13, f32[1024,128]{1,0:T(8,128)S(1)} %copy-done.1, bf16[1,24,128,128]{3,2,1,0:T(8,128)(2,1)S(1)} %bitcast.11), custom_call_target="tpu_custom_call" | custom-call | flops 131072 | bytes 524288 | tf_op jit(solution)/shard_map/pallas_call | solution.py:53
  9.2 2.9 %collective-permute-done.refs_0_ = s32[8,128]{1,0:T(8,128)S(1)} collective-permute-done((s32[8,128]{1,0:T(8,128)}, s32[8,128]{1,0:T(8,128)S(1)}, u32[]{:S(2)}, u32[]{:S(2)}) %collective-permute-start) | collective-permute-done | bytes 4128 | tf_op jit(solution)/shard_map/ppermute | solution.py:155
  12.0 0.0 collective-permute-done.1.refs_1_
  12.0 1.2 %shard_map.65 = (f32[256,128]{1,0:T(8,128)S(1)}, f32[256,128]{1,0:T(8,128)S(1)}, f32[256,128]{1,0:T(8,128)S(1)}, f32[256,128]{1,0:T(8,128)S(1)}) custom-call(s32[49]{0:T(128)S(1)} %add_bitcast_fusion.info_ref, bf16[24,128,128]{2,1,0:T(8,128)(2,1)S(1)} %bitcast.9, s32[8,128]{1,0:T(8,128)S(1)} %collective-permute-done.refs_0_, ...), custom_call_target="tpu_custom_call" | custom-call | flops 201326592 | bytes 1048576 | tf_op jit(solution)/shard_map/pallas_call | solution.py:124
  13.2 5.2 %collective-permute-start.2 = (f32[256,128]{1,0:T(8,128)S(1)}, f32[256,128]{1,0:T(8,128)S(1)}, u32[]{:S(2)}, u32[]{:S(2)}) collective-permute-start(f32[256,128]{1,0:T(8,128)S(1)} %get-tuple-element.19), channel_id=1, source_target_pairs={{0,1},{1,0},{2,3},{3,2},{4,5},{5,4},{6,7},{7,6},{8,9},{9,8},{10,11... | collective-permute-start | bytes 393224 | tf_op jit(solution)/shard_map/ppermute | solution.py:165
  18.4 0.1 collective-permute-start.4
  18.5 0.9 %collective-permute-done.2 = f32[256,128]{1,0:T(8,128)S(1)} collective-permute-done((f32[256,128]{1,0:T(8,128)S(1)}, f32[256,128]{1,0:T(8,128)S(1)}, u32[]{:S(2)}, u32[]{:S(2)}) %collective-permute-start.2) | collective-permute-done | bytes 131104 | tf_op jit(solution)/shard_map/ppermute | solution.py:165
  19.4 3.1 %collective-permute-start.3 = (f32[256,128]{1,0:T(8,128)S(1)}, f32[256,128]{1,0:T(8,128)S(1)}, u32[]{:S(2)}, u32[]{:S(2)}) collective-permute-start(f32[256,128]{1,0:T(8,128)S(1)} %add.24), channel_id=1, source_target_pairs={{2,0},{3,1},{0,2},{1,3},{6,4},{7,5},{4,6},{5,7},{10,8},{11,9},{8,1... | collective-permute-start | bytes 393224 | tf_op jit(solution)/shard_map/ppermute | solution.py:171
  22.5 3.8 %collective-permute-done.3 = f32[256,128]{1,0:T(8,128)S(1)} collective-permute-done((f32[256,128]{1,0:T(8,128)S(1)}, f32[256,128]{1,0:T(8,128)S(1)}, u32[]{:S(2)}, u32[]{:S(2)}) %collective-permute-start.3) | collective-permute-done | bytes 131104 | tf_op jit(solution)/shard_map/ppermute | solution.py:171
  26.4 3.6 %collective-permute-start.8 = (f32[256,128]{1,0:T(8,128)S(1)}, f32[256,128]{1,0:T(8,128)S(1)}, u32[]{:S(2)}, u32[]{:S(2)}) collective-permute-start(f32[256,128]{1,0:T(8,128)S(1)} %fusion), channel_id=1, source_target_pairs={{3,0},{1,5},{2,10},{0,15},{7,4},{5,9},{6,14},{4,3},{11,8},{9,13},{... | collective-permute-start | bytes 393224 | tf_op jit(solution)/shard_map/ppermute | solution.py:155
  30.0 0.0 collective-permute-start.7
  30.0 0.5 %collective-permute-start.6 = (f32[256,128]{1,0:T(8,128)S(1)}, f32[256,128]{1,0:T(8,128)S(1)}, u32[]{:S(2)}, u32[]{:S(2)}) collective-permute-start(f32[256,128]{1,0:T(8,128)S(1)} %fusion), channel_id=1, source_target_pairs={{1,0},{3,5},{0,10},{2,15},{5,4},{7,9},{4,14},{6,3},{9,8},{11,13},{... | collective-permute-start | bytes 393224 | tf_op jit(solution)/shard_map/ppermute | solution.py:155
  30.5 0.7 %collective-permute-start.5 = (f32[256,128]{1,0:T(8,128)S(1)}, f32[256,128]{1,0:T(8,128)S(1)}, u32[]{:S(2)}, u32[]{:S(2)}) collective-permute-start(f32[256,128]{1,0:T(8,128)S(1)} %fusion), channel_id=1, source_target_pairs={{0,0},{2,5},{1,10},{3,15},{4,4},{6,9},{5,14},{7,3},{8,8},{10,13},{... | collective-permute-start | bytes 393224 | tf_op jit(solution)/shard_map/ppermute | solution.py:155
  31.2 2.3 %collective-permute-done.8.refs_3_ = f32[256,128]{1,0:T(8,128)S(1)} collective-permute-done((f32[256,128]{1,0:T(8,128)S(1)}, f32[256,128]{1,0:T(8,128)S(1)}, u32[]{:S(2)}, u32[]{:S(2)}) %collective-permute-start.8) | collective-permute-done | bytes 131104 | tf_op jit(solution)/shard_map/ppermute | solution.py:155
  33.5 1.8 %collective-permute-done.7.refs_2_ = f32[256,128]{1,0:T(8,128)S(1)} collective-permute-done((f32[256,128]{1,0:T(8,128)S(1)}, f32[256,128]{1,0:T(8,128)S(1)}, u32[]{:S(2)}, u32[]{:S(2)}) %collective-permute-start.7) | collective-permute-done | bytes 131104 | tf_op jit(solution)/shard_map/ppermute | solution.py:155
  35.3 2.8 %collective-permute-done.6.refs_1_ = f32[256,128]{1,0:T(8,128)S(1)} collective-permute-done((f32[256,128]{1,0:T(8,128)S(1)}, f32[256,128]{1,0:T(8,128)S(1)}, u32[]{:S(2)}, u32[]{:S(2)}) %collective-permute-start.6) | collective-permute-done | bytes 131104 | tf_op jit(solution)/shard_map/ppermute | solution.py:155
  38.2 0.0 collective-permute-done.5.refs_0_
  38.2 1.2 %shard_map.66 = (f32[256,128]{1,0:T(8,128)S(1)}, f32[256,128]{1,0:T(8,128)S(1)}, f32[256,128]{1,0:T(8,128)S(1)}, f32[256,128]{1,0:T(8,128)S(1)}) custom-call(s32[49]{0:T(128)S(1)} %add_bitcast_fusion.info_ref, bf16[24,128,128]{2,1,0:T(8,128)(2,1)S(1)} %bitcast.10, f32[256,128]{1,0:T(8,128)S(1)} %collective-permute-done.5.refs_0_, ...), custom_call_target="tpu_custom_call" | custom-call | flops 201326592 | bytes 1048576 | tf_op jit(solution)/shard_map/pallas_call | solution.py:124
  39.3 3.0 %collective-permute-start.9 = (f32[256,128]{1,0:T(8,128)S(1)}, f32[256,128]{1,0:T(8,128)S(1)}, u32[]{:S(2)}, u32[]{:S(2)}) collective-permute-start(f32[256,128]{1,0:T(8,128)S(1)} %get-tuple-element.24), channel_id=1, source_target_pairs={{0,1},{1,0},{2,3},{3,2},{4,5},{5,4},{6,7},{7,6},{8,9},{9,8},{10,11... | collective-permute-start | bytes 393224 | tf_op jit(solution)/shard_map/ppermute | solution.py:165
  42.3 0.1 collective-permute-start.11
  42.4 0.9 %collective-permute-done.9 = f32[256,128]{1,0:T(8,128)S(1)} collective-permute-done((f32[256,128]{1,0:T(8,128)S(1)}, f32[256,128]{1,0:T(8,128)S(1)}, u32[]{:S(2)}, u32[]{:S(2)}) %collective-permute-start.9) | collective-permute-done | bytes 131104 | tf_op jit(solution)/shard_map/ppermute | solution.py:165
  43.3 2.5 %collective-permute-start.10 = (f32[256,128]{1,0:T(8,128)S(1)}, f32[256,128]{1,0:T(8,128)S(1)}, u32[]{:S(2)}, u32[]{:S(2)}) collective-permute-start(f32[256,128]{1,0:T(8,128)S(1)} %add.28), channel_id=1, source_target_pairs={{2,0},{3,1},{0,2},{1,3},{6,4},{7,5},{4,6},{5,7},{10,8},{11,9},{8,1... | collective-permute-start | bytes 393224 | tf_op jit(solution)/shard_map/ppermute | solution.py:171
  45.8 0.0 collective-permute-done.11
  45.9 3.8 %collective-permute-done.10 = f32[256,128]{1,0:T(8,128)S(1)} collective-permute-done((f32[256,128]{1,0:T(8,128)S(1)}, f32[256,128]{1,0:T(8,128)S(1)}, u32[]{:S(2)}, u32[]{:S(2)}) %collective-permute-start.10) | collective-permute-done | bytes 131104 | tf_op jit(solution)/shard_map/ppermute | solution.py:171
  49.7 0.7 %add_multiply_fusion = f32[256,128]{1,0:T(8,128)} fusion(f32[256,128]{1,0:T(8,128)S(1)} %get-tuple-element.22, f32[256,128]{1,0:T(8,128)S(1)} %collective-permute-done.10, f32[256,128]{1,0:T(8,128)S(1)} %get-tuple-element.25, f32[256,128]{1,0:T(8,128)S(1)} %collective-permute-done.11, f32[256,128]{1,0:T(8,128)S(1)} %get-tuple-element.16, ...), kind=kLoop, calls=%fused_computation | loop fusion | flops 294912 | bytes 1179648 | tf_op jit(solution)/shard_map/div | solution.py:212
  (10 shorter events, 0.1 us)
Async XLA Ops:
  0.0 12.0 %collective-permute-start.1 = (f32[1024,128]{1,0:T(8,128)}, f32[1024,128]{1,0:T(8,128)S(1)}, u32[]{:S(2)}, u32[]{:S(2)}) collective-permute-start(f32[1024,128]{1,0:T(8,128)} %embeddings_ref.1), channel_id=1, source_target_pairs={{1,0},{3,5},{0,10},{2,15},{5,4},{7,9},{4,14},{6,3},{9,8},{11,13},{... | collective-permute-start | bytes 1572872 | tf_op jit(solution)/shard_map/ppermute | solution.py:155
  5.0 7.1 %collective-permute-start = (s32[8,128]{1,0:T(8,128)}, s32[8,128]{1,0:T(8,128)S(1)}, u32[]{:S(2)}, u32[]{:S(2)}) collective-permute-start(s32[8,128]{1,0:T(8,128)} %bitcast.12), channel_id=1, source_target_pairs={{1,0},{3,5},{0,10},{2,15},{5,4},{7,9},{4,14},{6,3},{9,8},{11,13},{... | collective-permute-start | bytes 12296 | tf_op jit(solution)/shard_map/ppermute | solution.py:155
  5.6 0.7 %copy-start.3 = (s32[1,1,1,24]{3,2,1,0:T(1,128)S(1)}, s32[1,1,1,24]{3,2,1,0:T(1,128)}, u32[]{:S(2)}) copy-start(s32[1,1,1,24]{3,2,1,0:T(1,128)} %param.10) | copy-start | bytes 292
  5.7 0.7 %copy-start.4 = (s32[1,1,1,24]{3,2,1,0:T(1,128)S(1)}, s32[1,1,1,24]{3,2,1,0:T(1,128)}, u32[]{:S(2)}) copy-start(s32[1,1,1,24]{3,2,1,0:T(1,128)} %param.9) | copy-start | bytes 292
  5.7 0.7 %copy-start.2 = (s32[1024]{0:T(1024)S(1)}, s32[1024]{0:T(1024)}, u32[]{:S(2)}) copy-start(s32[1024]{0:T(1024)} %param.7) | copy-start | bytes 12292
  6.4 1.1 %copy-start = (bf16[1,1,1,24,128,128]{5,4,3,2,1,0:T(8,128)(2,1)S(1)}, bf16[1,1,1,24,128,128]{5,4,3,2,1,0:T(8,128)(2,1)}, u32[]{:S(2)}) copy-start(bf16[1,1,1,24,128,128]{5,4,3,2,1,0:T(8,128)(2,1)} %param.8) | copy-start | bytes 2359300
  7.5 1.0 %copy-start.1 = (f32[1024,128]{1,0:T(8,128)S(1)}, f32[1024,128]{1,0:T(8,128)}, u32[]{:S(2)}) copy-start(f32[1024,128]{1,0:T(8,128)} %embeddings_ref.1) | copy-start | bytes 1572868
  13.2 6.2 %collective-permute-start.2 = (f32[256,128]{1,0:T(8,128)S(1)}, f32[256,128]{1,0:T(8,128)S(1)}, u32[]{:S(2)}, u32[]{:S(2)}) collective-permute-start(f32[256,128]{1,0:T(8,128)S(1)} %get-tuple-element.19), channel_id=1, source_target_pairs={{0,1},{1,0},{2,3},{3,2},{4,5},{5,4},{6,7},{7,6},{8,9},{9,8},{10,11... | collective-permute-start | bytes 393224 | tf_op jit(solution)/shard_map/ppermute | solution.py:165
  18.4 4.1 %collective-permute-start.4 = (f32[256,128]{1,0:T(8,128)S(1)}, f32[256,128]{1,0:T(8,128)S(1)}, u32[]{:S(2)}, u32[]{:S(2)}) collective-permute-start(f32[256,128]{1,0:T(8,128)S(1)} %get-tuple-element.21), channel_id=1, source_target_pairs={{0,1},{1,0},{2,3},{3,2},{4,5},{5,4},{6,7},{7,6},{8,9},{9,8},{10,11... | collective-permute-start | bytes 393224 | tf_op jit(solution)/shard_map/ppermute | solution.py:165
  19.4 6.9 %collective-permute-start.3 = (f32[256,128]{1,0:T(8,128)S(1)}, f32[256,128]{1,0:T(8,128)S(1)}, u32[]{:S(2)}, u32[]{:S(2)}) collective-permute-start(f32[256,128]{1,0:T(8,128)S(1)} %add.24), channel_id=1, source_target_pairs={{2,0},{3,1},{0,2},{1,3},{6,4},{7,5},{4,6},{5,7},{10,8},{11,9},{8,1... | collective-permute-start | bytes 393224 | tf_op jit(solution)/shard_map/ppermute | solution.py:171
  26.4 7.1 %collective-permute-start.8 = (f32[256,128]{1,0:T(8,128)S(1)}, f32[256,128]{1,0:T(8,128)S(1)}, u32[]{:S(2)}, u32[]{:S(2)}) collective-permute-start(f32[256,128]{1,0:T(8,128)S(1)} %fusion), channel_id=1, source_target_pairs={{3,0},{1,5},{2,10},{0,15},{7,4},{5,9},{6,14},{4,3},{11,8},{9,13},{... | collective-permute-start | bytes 393224 | tf_op jit(solution)/shard_map/ppermute | solution.py:155
  30.0 5.3 %collective-permute-start.7 = (f32[256,128]{1,0:T(8,128)S(1)}, f32[256,128]{1,0:T(8,128)S(1)}, u32[]{:S(2)}, u32[]{:S(2)}) collective-permute-start(f32[256,128]{1,0:T(8,128)S(1)} %fusion), channel_id=1, source_target_pairs={{2,0},{0,5},{3,10},{1,15},{6,4},{4,9},{7,14},{5,3},{10,8},{8,13},{... | collective-permute-start | bytes 393224 | tf_op jit(solution)/shard_map/ppermute | solution.py:155
  30.0 8.2 %collective-permute-start.6 = (f32[256,128]{1,0:T(8,128)S(1)}, f32[256,128]{1,0:T(8,128)S(1)}, u32[]{:S(2)}, u32[]{:S(2)}) collective-permute-start(f32[256,128]{1,0:T(8,128)S(1)} %fusion), channel_id=1, source_target_pairs={{1,0},{3,5},{0,10},{2,15},{5,4},{7,9},{4,14},{6,3},{9,8},{11,13},{... | collective-permute-start | bytes 393224 | tf_op jit(solution)/shard_map/ppermute | solution.py:155
  30.5 7.7 %collective-permute-start.5 = (f32[256,128]{1,0:T(8,128)S(1)}, f32[256,128]{1,0:T(8,128)S(1)}, u32[]{:S(2)}, u32[]{:S(2)}) collective-permute-start(f32[256,128]{1,0:T(8,128)S(1)} %fusion), channel_id=1, source_target_pairs={{0,0},{2,5},{1,10},{3,15},{4,4},{6,9},{5,14},{7,3},{8,8},{10,13},{... | collective-permute-start | bytes 393224 | tf_op jit(solution)/shard_map/ppermute | solution.py:155
  39.3 4.0 %collective-permute-start.9 = (f32[256,128]{1,0:T(8,128)S(1)}, f32[256,128]{1,0:T(8,128)S(1)}, u32[]{:S(2)}, u32[]{:S(2)}) collective-permute-start(f32[256,128]{1,0:T(8,128)S(1)} %get-tuple-element.24), channel_id=1, source_target_pairs={{0,1},{1,0},{2,3},{3,2},{4,5},{5,4},{6,7},{7,6},{8,9},{9,8},{10,11... | collective-permute-start | bytes 393224 | tf_op jit(solution)/shard_map/ppermute | solution.py:165
  42.3 3.5 %collective-permute-start.11 = (f32[256,128]{1,0:T(8,128)S(1)}, f32[256,128]{1,0:T(8,128)S(1)}, u32[]{:S(2)}, u32[]{:S(2)}) collective-permute-start(f32[256,128]{1,0:T(8,128)S(1)} %get-tuple-element.26), channel_id=1, source_target_pairs={{0,1},{1,0},{2,3},{3,2},{4,5},{5,4},{6,7},{7,6},{8,9},{9,8},{10,11... | collective-permute-start | bytes 393224 | tf_op jit(solution)/shard_map/ppermute | solution.py:165
  43.3 6.3 %collective-permute-start.10 = (f32[256,128]{1,0:T(8,128)S(1)}, f32[256,128]{1,0:T(8,128)S(1)}, u32[]{:S(2)}, u32[]{:S(2)}) collective-permute-start(f32[256,128]{1,0:T(8,128)S(1)} %add.28), channel_id=1, source_target_pairs={{2,0},{3,1},{0,2},{1,3},{6,4},{7,5},{4,6},{5,7},{10,8},{11,9},{8,1... | collective-permute-start | bytes 393224 | tf_op jit(solution)/shard_map/ppermute | solution.py:171

commit v5 on v3

--- a/solution.py
+++ b/solution.py
@@ -20,7 +20,7 @@
 
 def source_team(team, turn, team_count):
     if team_count == 4:
-        return (2 * (team % 2) + team // 2) ^ (3 - turn)
+        return (2 * (team % 2) + team // 2) ^ (0, 2, 1, 3)[turn]
     return (team + turn) % team_count
 
 

time: 52.2 us -> 49.5 us (0.948)
  starting transfers between devices: 25.9 us -> 21.3 us
  waiting for transfers between devices: 18.8 us -> 20.6 us
    ppermute x6, starting transfers between devices: 15.6 us -> 11 us  [fetch(): return lax.ppermute(value, ('blk', 'rep'), pairs)]
    ppermute x6, waiting for transfers between devices: 9.14 us -> 11.2 us  [fetch(): return lax.ppermute(value, ('blk', 'rep'), pairs)]
    ppermute x2, starting transfers between devices: 8.48 us -> 6.72 us  [from_column(): return lax.ppermute(value, 'rep', pairs)]
    ppermute x4, starting transfers between devices: 1.79 us -> 3.54 us  [from_mate(): lax.ppermute(value, 'rep', [(team, team ^ 1) for team in range(team_count)])]
where the time goes in v5:
time: 49.5 us; the launch traced here: 49.3 us
  starting transfers between devices  21.3 us (43%)
  waiting for transfers between devices  20.6 us (42%)
  Pallas kernels  2.9 us (6%)
  local copies, waits for them, and re-layouts  2.83 us (6%)
  other arithmetic  0.88 us (2%)
  between operations  0.73 us (1%)
    ppermute x6, waiting for transfers between devices, fetch(): return lax.ppermute(value, ('blk', 'rep'), pairs)  11.2 us
    ppermute x6, starting transfers between devices, fetch(): return lax.ppermute(value, ('blk', 'rep'), pairs)  11 us
    ppermute x2, waiting for transfers between devices, from_column(): return lax.ppermute(value, 'rep', pairs)  7.61 us
    ppermute x2, starting transfers between devices, from_column(): return lax.ppermute(value, 'rep', pairs)  6.72 us
    ppermute x4, starting transfers between devices, from_mate(): lax.ppermute(value, 'rep', [(team, team ^ 1) for team in range(team_count)])  3.54 us
    unnamed x10, local copies, waits for them, and re-layouts  2.83 us
    pallas_call x2, Pallas kernels, arc_step(): pl.pallas_call(functools.partial(arc_kernel, team_count=team_count, piece...  2.33 us
    ppermute x4, waiting for transfers between devices, from_mate(): lax.ppermute(value, 'rep', [(team, team ^ 1) for team in range(team_count)])  1.82 us
  transfers between devices with their start and end apart: 12, of which 8 were waited for; matrix products, arithmetic and copies ran while one was open for 0% of the time, Pallas kernels for 1%

profile of v5, /device:TPU:0, one launch (start us, length us, event | category | flops | bytes accessed | tf_op | source)
XLA Modules:
  0.0 49.3 jit_solution(5520410972424159627)
XLA Ops:
  0.0 5.4 %collective-permute-start.1 = (f32[1024,128]{1,0:T(8,128)}, f32[1024,128]{1,0:T(8,128)S(1)}, u32[]{:S(2)}, u32[]{:S(2)}) collective-permute-start(f32[1024,128]{1,0:T(8,128)} %embeddings_ref.1), channel_id=1, source_target_pairs={{3,0},{1,5},{2,10},{0,15},{7,4},{5,9},{6,14},{4,3},{11,8},{9,13},{... | collective-permute-start | bytes 1572872 | tf_op jit(solution)/shard_map/ppermute | solution.py:155
  5.4 0.8 %collective-permute-start = (s32[8,128]{1,0:T(8,128)}, s32[8,128]{1,0:T(8,128)S(1)}, u32[]{:S(2)}, u32[]{:S(2)}) collective-permute-start(s32[8,128]{1,0:T(8,128)} %bitcast.12), channel_id=1, source_target_pairs={{3,0},{1,5},{2,10},{0,15},{7,4},{5,9},{6,14},{4,3},{11,8},{9,13},{... | collective-permute-start | bytes 12296 | tf_op jit(solution)/shard_map/ppermute | solution.py:155
  6.9 0.6 %copy-done.3 = s32[1,1,1,24]{3,2,1,0:T(1,128)S(1)} copy-done((s32[1,1,1,24]{3,2,1,0:T(1,128)S(1)}, s32[1,1,1,24]{3,2,1,0:T(1,128)}, u32[]{:S(2)}) %copy-start.3) | copy-done | bytes 120
  7.5 0.0 copy-done.4
  7.6 0.1 add_bitcast_fusion.info_ref
  7.6 1.1 %copy-done = bf16[1,1,1,24,128,128]{5,4,3,2,1,0:T(8,128)(2,1)S(1)} copy-done((bf16[1,1,1,24,128,128]{5,4,3,2,1,0:T(8,128)(2,1)S(1)}, bf16[1,1,1,24,128,128]{5,4,3,2,1,0:T(8,128)(2,1)}, u32[]{:S(2)}) %copy-start) | copy-done | bytes 786456
  8.8 1.0 %copy-done.1 = f32[1024,128]{1,0:T(8,128)S(1)} copy-done((f32[1024,128]{1,0:T(8,128)S(1)}, f32[1024,128]{1,0:T(8,128)}, u32[]{:S(2)}) %copy-start.1) | copy-done | bytes 524312
  9.8 0.6 %shard_map.64 = (bf16[1,24,128,128]{3,2,1,0:T(8,128)(2,1)S(1)}, f32[256,128]{1,0:T(8,128)S(1)}, f32[256,128]{1,0:T(8,128)S(1)}) custom-call(s32[8,128]{1,0:T(8,128)S(1)} %bitcast.13, f32[1024,128]{1,0:T(8,128)S(1)} %copy-done.1, bf16[1,24,128,128]{3,2,1,0:T(8,128)(2,1)S(1)} %bitcast.11), custom_call_target="tpu_custom_call" | custom-call | flops 131072 | bytes 524288 | tf_op jit(solution)/shard_map/pallas_call | solution.py:53
  10.4 4.2 %collective-permute-done.refs_0_ = s32[8,128]{1,0:T(8,128)S(1)} collective-permute-done((s32[8,128]{1,0:T(8,128)}, s32[8,128]{1,0:T(8,128)S(1)}, u32[]{:S(2)}, u32[]{:S(2)}) %collective-permute-start) | collective-permute-done | bytes 4128 | tf_op jit(solution)/shard_map/ppermute | solution.py:155
  14.6 1.2 %shard_map.65 = (f32[256,128]{1,0:T(8,128)S(1)}, f32[256,128]{1,0:T(8,128)S(1)}, f32[256,128]{1,0:T(8,128)S(1)}, f32[256,128]{1,0:T(8,128)S(1)}) custom-call(s32[49]{0:T(128)S(1)} %add_bitcast_fusion.info_ref, bf16[24,128,128]{2,1,0:T(8,128)(2,1)S(1)} %bitcast.9, s32[8,128]{1,0:T(8,128)S(1)} %collective-permute-done.refs_0_, ...), custom_call_target="tpu_custom_call" | custom-call | flops 201326592 | bytes 1048576 | tf_op jit(solution)/shard_map/pallas_call | solution.py:124
  15.8 0.8 %collective-permute-start.2 = (f32[256,128]{1,0:T(8,128)S(1)}, f32[256,128]{1,0:T(8,128)S(1)}, u32[]{:S(2)}, u32[]{:S(2)}) collective-permute-start(f32[256,128]{1,0:T(8,128)S(1)} %get-tuple-element.19), channel_id=1, source_target_pairs={{0,1},{1,0},{2,3},{3,2},{4,5},{5,4},{6,7},{7,6},{8,9},{9,8},{10,11... | collective-permute-start | bytes 393224 | tf_op jit(solution)/shard_map/ppermute | solution.py:165
  16.6 0.1 collective-permute-start.4
  16.7 0.9 %collective-permute-done.2 = f32[256,128]{1,0:T(8,128)S(1)} collective-permute-done((f32[256,128]{1,0:T(8,128)S(1)}, f32[256,128]{1,0:T(8,128)S(1)}, u32[]{:S(2)}, u32[]{:S(2)}) %collective-permute-start.2) | collective-permute-done | bytes 131104 | tf_op jit(solution)/shard_map/ppermute | solution.py:165
  17.6 4.0 %collective-permute-start.3 = (f32[256,128]{1,0:T(8,128)S(1)}, f32[256,128]{1,0:T(8,128)S(1)}, u32[]{:S(2)}, u32[]{:S(2)}) collective-permute-start(f32[256,128]{1,0:T(8,128)S(1)} %add.24), channel_id=1, source_target_pairs={{2,0},{3,1},{0,2},{1,3},{6,4},{7,5},{4,6},{5,7},{10,8},{11,9},{8,1... | collective-permute-start | bytes 393224 | tf_op jit(solution)/shard_map/ppermute | solution.py:171
  21.6 0.0 collective-permute-done.4
  21.6 3.8 %collective-permute-done.3 = f32[256,128]{1,0:T(8,128)S(1)} collective-permute-done((f32[256,128]{1,0:T(8,128)S(1)}, f32[256,128]{1,0:T(8,128)S(1)}, u32[]{:S(2)}, u32[]{:S(2)}) %collective-permute-start.3) | collective-permute-done | bytes 131104 | tf_op jit(solution)/shard_map/ppermute | solution.py:171
  25.5 3.6 %collective-permute-start.8 = (f32[256,128]{1,0:T(8,128)S(1)}, f32[256,128]{1,0:T(8,128)S(1)}, u32[]{:S(2)}, u32[]{:S(2)}) collective-permute-start(f32[256,128]{1,0:T(8,128)S(1)} %fusion), channel_id=1, source_target_pairs={{3,0},{1,5},{2,10},{0,15},{7,4},{5,9},{6,14},{4,3},{11,8},{9,13},{... | collective-permute-start | bytes 393224 | tf_op jit(solution)/shard_map/ppermute | solution.py:155
  29.1 0.5 %collective-permute-start.7 = (f32[256,128]{1,0:T(8,128)S(1)}, f32[256,128]{1,0:T(8,128)S(1)}, u32[]{:S(2)}, u32[]{:S(2)}) collective-permute-start(f32[256,128]{1,0:T(8,128)S(1)} %fusion), channel_id=1, source_target_pairs={{1,0},{3,5},{0,10},{2,15},{5,4},{7,9},{4,14},{6,3},{9,8},{11,13},{... | collective-permute-start | bytes 393224 | tf_op jit(solution)/shard_map/ppermute | solution.py:155
  29.6 0.0 collective-permute-start.6
  29.6 0.7 %collective-permute-start.5 = (f32[256,128]{1,0:T(8,128)S(1)}, f32[256,128]{1,0:T(8,128)S(1)}, u32[]{:S(2)}, u32[]{:S(2)}) collective-permute-start(f32[256,128]{1,0:T(8,128)S(1)} %fusion), channel_id=1, source_target_pairs={{0,0},{2,5},{1,10},{3,15},{4,4},{6,9},{5,14},{7,3},{8,8},{10,13},{... | collective-permute-start | bytes 393224 | tf_op jit(solution)/shard_map/ppermute | solution.py:155
  30.3 2.3 %collective-permute-done.8.refs_3_ = f32[256,128]{1,0:T(8,128)S(1)} collective-permute-done((f32[256,128]{1,0:T(8,128)S(1)}, f32[256,128]{1,0:T(8,128)S(1)}, u32[]{:S(2)}, u32[]{:S(2)}) %collective-permute-start.8) | collective-permute-done | bytes 131104 | tf_op jit(solution)/shard_map/ppermute | solution.py:155
  32.6 2.7 %collective-permute-done.7.refs_2_ = f32[256,128]{1,0:T(8,128)S(1)} collective-permute-done((f32[256,128]{1,0:T(8,128)S(1)}, f32[256,128]{1,0:T(8,128)S(1)}, u32[]{:S(2)}, u32[]{:S(2)}) %collective-permute-start.7) | collective-permute-done | bytes 131104 | tf_op jit(solution)/shard_map/ppermute | solution.py:155
  35.3 2.0 %collective-permute-done.6.refs_1_ = f32[256,128]{1,0:T(8,128)S(1)} collective-permute-done((f32[256,128]{1,0:T(8,128)S(1)}, f32[256,128]{1,0:T(8,128)S(1)}, u32[]{:S(2)}, u32[]{:S(2)}) %collective-permute-start.6) | collective-permute-done | bytes 131104 | tf_op jit(solution)/shard_map/ppermute | solution.py:155
  37.2 0.0 collective-permute-done.5.refs_0_
  37.3 1.2 %shard_map.66 = (f32[256,128]{1,0:T(8,128)S(1)}, f32[256,128]{1,0:T(8,128)S(1)}, f32[256,128]{1,0:T(8,128)S(1)}, f32[256,128]{1,0:T(8,128)S(1)}) custom-call(s32[49]{0:T(128)S(1)} %add_bitcast_fusion.info_ref, bf16[24,128,128]{2,1,0:T(8,128)(2,1)S(1)} %bitcast.10, f32[256,128]{1,0:T(8,128)S(1)} %collective-permute-done.5.refs_0_, ...), custom_call_target="tpu_custom_call" | custom-call | flops 201326592 | bytes 1048576 | tf_op jit(solution)/shard_map/pallas_call | solution.py:124
  38.4 2.6 %collective-permute-start.9 = (f32[256,128]{1,0:T(8,128)S(1)}, f32[256,128]{1,0:T(8,128)S(1)}, u32[]{:S(2)}, u32[]{:S(2)}) collective-permute-start(f32[256,128]{1,0:T(8,128)S(1)} %get-tuple-element.24), channel_id=1, source_target_pairs={{0,1},{1,0},{2,3},{3,2},{4,5},{5,4},{6,7},{7,6},{8,9},{9,8},{10,11... | collective-permute-start | bytes 393224 | tf_op jit(solution)/shard_map/ppermute | solution.py:165
  41.0 0.1 collective-permute-start.11
  41.1 0.9 %collective-permute-done.9 = f32[256,128]{1,0:T(8,128)S(1)} collective-permute-done((f32[256,128]{1,0:T(8,128)S(1)}, f32[256,128]{1,0:T(8,128)S(1)}, u32[]{:S(2)}, u32[]{:S(2)}) %collective-permute-start.9) | collective-permute-done | bytes 131104 | tf_op jit(solution)/shard_map/ppermute | solution.py:165
  42.0 2.7 %collective-permute-start.10 = (f32[256,128]{1,0:T(8,128)S(1)}, f32[256,128]{1,0:T(8,128)S(1)}, u32[]{:S(2)}, u32[]{:S(2)}) collective-permute-start(f32[256,128]{1,0:T(8,128)S(1)} %add.28), channel_id=1, source_target_pairs={{2,0},{3,1},{0,2},{1,3},{6,4},{7,5},{4,6},{5,7},{10,8},{11,9},{8,1... | collective-permute-start | bytes 393224 | tf_op jit(solution)/shard_map/ppermute | solution.py:171
  44.7 0.0 collective-permute-done.11
  44.7 3.8 %collective-permute-done.10 = f32[256,128]{1,0:T(8,128)S(1)} collective-permute-done((f32[256,128]{1,0:T(8,128)S(1)}, f32[256,128]{1,0:T(8,128)S(1)}, u32[]{:S(2)}, u32[]{:S(2)}) %collective-permute-start.10) | collective-permute-done | bytes 131104 | tf_op jit(solution)/shard_map/ppermute | solution.py:171
  48.5 0.7 %add_multiply_fusion = f32[256,128]{1,0:T(8,128)} fusion(f32[256,128]{1,0:T(8,128)S(1)} %get-tuple-element.22, f32[256,128]{1,0:T(8,128)S(1)} %collective-permute-done.10, f32[256,128]{1,0:T(8,128)S(1)} %get-tuple-element.25, f32[256,128]{1,0:T(8,128)S(1)} %collective-permute-done.11, f32[256,128]{1,0:T(8,128)S(1)} %get-tuple-element.16, ...), kind=kLoop, calls=%fused_computation | loop fusion | flops 294912 | bytes 1179648 | tf_op jit(solution)/shard_map/div | solution.py:212
  (10 shorter events, 0.1 us)
Async XLA Ops:
  0.0 14.6 %collective-permute-start.1 = (f32[1024,128]{1,0:T(8,128)}, f32[1024,128]{1,0:T(8,128)S(1)}, u32[]{:S(2)}, u32[]{:S(2)}) collective-permute-start(f32[1024,128]{1,0:T(8,128)} %embeddings_ref.1), channel_id=1, source_target_pairs={{3,0},{1,5},{2,10},{0,15},{7,4},{5,9},{6,14},{4,3},{11,8},{9,13},{... | collective-permute-start | bytes 1572872 | tf_op jit(solution)/shard_map/ppermute | solution.py:155
  5.4 9.2 %collective-permute-start = (s32[8,128]{1,0:T(8,128)}, s32[8,128]{1,0:T(8,128)S(1)}, u32[]{:S(2)}, u32[]{:S(2)}) collective-permute-start(s32[8,128]{1,0:T(8,128)} %bitcast.12), channel_id=1, source_target_pairs={{3,0},{1,5},{2,10},{0,15},{7,4},{5,9},{6,14},{4,3},{11,8},{9,13},{... | collective-permute-start | bytes 12296 | tf_op jit(solution)/shard_map/ppermute | solution.py:155
  6.9 0.7 %copy-start.3 = (s32[1,1,1,24]{3,2,1,0:T(1,128)S(1)}, s32[1,1,1,24]{3,2,1,0:T(1,128)}, u32[]{:S(2)}) copy-start(s32[1,1,1,24]{3,2,1,0:T(1,128)} %param.10) | copy-start | bytes 292
  6.9 0.7 %copy-start.4 = (s32[1,1,1,24]{3,2,1,0:T(1,128)S(1)}, s32[1,1,1,24]{3,2,1,0:T(1,128)}, u32[]{:S(2)}) copy-start(s32[1,1,1,24]{3,2,1,0:T(1,128)} %param.9) | copy-start | bytes 292
  6.9 0.7 %copy-start.2 = (s32[1024]{0:T(1024)S(1)}, s32[1024]{0:T(1024)}, u32[]{:S(2)}) copy-start(s32[1024]{0:T(1024)} %param.7) | copy-start | bytes 12292
  7.6 1.1 %copy-start = (bf16[1,1,1,24,128,128]{5,4,3,2,1,0:T(8,128)(2,1)S(1)}, bf16[1,1,1,24,128,128]{5,4,3,2,1,0:T(8,128)(2,1)}, u32[]{:S(2)}) copy-start(bf16[1,1,1,24,128,128]{5,4,3,2,1,0:T(8,128)(2,1)} %param.8) | copy-start | bytes 2359300
  8.8 1.0 %copy-start.1 = (f32[1024,128]{1,0:T(8,128)S(1)}, f32[1024,128]{1,0:T(8,128)}, u32[]{:S(2)}) copy-start(f32[1024,128]{1,0:T(8,128)} %embeddings_ref.1) | copy-start | bytes 1572868
  15.8 1.8 %collective-permute-start.2 = (f32[256,128]{1,0:T(8,128)S(1)}, f32[256,128]{1,0:T(8,128)S(1)}, u32[]{:S(2)}, u32[]{:S(2)}) collective-permute-start(f32[256,128]{1,0:T(8,128)S(1)} %get-tuple-element.19), channel_id=1, source_target_pairs={{0,1},{1,0},{2,3},{3,2},{4,5},{5,4},{6,7},{7,6},{8,9},{9,8},{10,11... | collective-permute-start | bytes 393224 | tf_op jit(solution)/shard_map/ppermute | solution.py:165
  16.6 5.0 %collective-permute-start.4 = (f32[256,128]{1,0:T(8,128)S(1)}, f32[256,128]{1,0:T(8,128)S(1)}, u32[]{:S(2)}, u32[]{:S(2)}) collective-permute-start(f32[256,128]{1,0:T(8,128)S(1)} %get-tuple-element.21), channel_id=1, source_target_pairs={{0,1},{1,0},{2,3},{3,2},{4,5},{5,4},{6,7},{7,6},{8,9},{9,8},{10,11... | collective-permute-start | bytes 393224 | tf_op jit(solution)/shard_map/ppermute | solution.py:165
  17.6 7.8 %collective-permute-start.3 = (f32[256,128]{1,0:T(8,128)S(1)}, f32[256,128]{1,0:T(8,128)S(1)}, u32[]{:S(2)}, u32[]{:S(2)}) collective-permute-start(f32[256,128]{1,0:T(8,128)S(1)} %add.24), channel_id=1, source_target_pairs={{2,0},{3,1},{0,2},{1,3},{6,4},{7,5},{4,6},{5,7},{10,8},{11,9},{8,1... | collective-permute-start | bytes 393224 | tf_op jit(solution)/shard_map/ppermute | solution.py:171
  25.5 7.1 %collective-permute-start.8 = (f32[256,128]{1,0:T(8,128)S(1)}, f32[256,128]{1,0:T(8,128)S(1)}, u32[]{:S(2)}, u32[]{:S(2)}) collective-permute-start(f32[256,128]{1,0:T(8,128)S(1)} %fusion), channel_id=1, source_target_pairs={{3,0},{1,5},{2,10},{0,15},{7,4},{5,9},{6,14},{4,3},{11,8},{9,13},{... | collective-permute-start | bytes 393224 | tf_op jit(solution)/shard_map/ppermute | solution.py:155
  29.1 6.2 %collective-permute-start.7 = (f32[256,128]{1,0:T(8,128)S(1)}, f32[256,128]{1,0:T(8,128)S(1)}, u32[]{:S(2)}, u32[]{:S(2)}) collective-permute-start(f32[256,128]{1,0:T(8,128)S(1)} %fusion), channel_id=1, source_target_pairs={{1,0},{3,5},{0,10},{2,15},{5,4},{7,9},{4,14},{6,3},{9,8},{11,13},{... | collective-permute-start | bytes 393224 | tf_op jit(solution)/shard_map/ppermute | solution.py:155
  29.6 7.6 %collective-permute-start.6 = (f32[256,128]{1,0:T(8,128)S(1)}, f32[256,128]{1,0:T(8,128)S(1)}, u32[]{:S(2)}, u32[]{:S(2)}) collective-permute-start(f32[256,128]{1,0:T(8,128)S(1)} %fusion), channel_id=1, source_target_pairs={{2,0},{0,5},{3,10},{1,15},{6,4},{4,9},{7,14},{5,3},{10,8},{8,13},{... | collective-permute-start | bytes 393224 | tf_op jit(solution)/shard_map/ppermute | solution.py:155
  29.6 7.6 %collective-permute-start.5 = (f32[256,128]{1,0:T(8,128)S(1)}, f32[256,128]{1,0:T(8,128)S(1)}, u32[]{:S(2)}, u32[]{:S(2)}) collective-permute-start(f32[256,128]{1,0:T(8,128)S(1)} %fusion), channel_id=1, source_target_pairs={{0,0},{2,5},{1,10},{3,15},{4,4},{6,9},{5,14},{7,3},{8,8},{10,13},{... | collective-permute-start | bytes 393224 | tf_op jit(solution)/shard_map/ppermute | solution.py:155
  38.4 3.6 %collective-permute-start.9 = (f32[256,128]{1,0:T(8,128)S(1)}, f32[256,128]{1,0:T(8,128)S(1)}, u32[]{:S(2)}, u32[]{:S(2)}) collective-permute-start(f32[256,128]{1,0:T(8,128)S(1)} %get-tuple-element.24), channel_id=1, source_target_pairs={{0,1},{1,0},{2,3},{3,2},{4,5},{5,4},{6,7},{7,6},{8,9},{9,8},{10,11... | collective-permute-start | bytes 393224 | tf_op jit(solution)/shard_map/ppermute | solution.py:165
  41.0 3.7 %collective-permute-start.11 = (f32[256,128]{1,0:T(8,128)S(1)}, f32[256,128]{1,0:T(8,128)S(1)}, u32[]{:S(2)}, u32[]{:S(2)}) collective-permute-start(f32[256,128]{1,0:T(8,128)S(1)} %get-tuple-element.26), channel_id=1, source_target_pairs={{0,1},{1,0},{2,3},{3,2},{4,5},{5,4},{6,7},{7,6},{8,9},{9,8},{10,11... | collective-permute-start | bytes 393224 | tf_op jit(solution)/shard_map/ppermute | solution.py:165
  42.0 6.5 %collective-permute-start.10 = (f32[256,128]{1,0:T(8,128)S(1)}, f32[256,128]{1,0:T(8,128)S(1)}, u32[]{:S(2)}, u32[]{:S(2)}) collective-permute-start(f32[256,128]{1,0:T(8,128)S(1)} %add.28), channel_id=1, source_target_pairs={{2,0},{3,1},{0,2},{1,3},{6,4},{7,5},{4,6},{5,7},{10,8},{11,9},{8,1... | collective-permute-start | bytes 393224 | tf_op jit(solution)/shard_map/ppermute | solution.py:171

commit v6 on v5

--- a/solution.py
+++ b/solution.py
@@ -67,14 +67,12 @@
     columns = team_count // 2
     pieces, refs = refs[:piece_count], refs[piece_count:]
     partials, refs = refs[:partial_count], refs[partial_count:]
-    outs, (table_ref, split_ref, sums_ref, sem) = refs[:team_count], refs[team_count:]
+    outs, (split_ref, sums_ref) = refs[:team_count], refs[team_count:]
     team_index = lax.axis_index("rep")
     slot_total, tile_size, _ = tiles_ref.shape
     panel_rows, width = split_ref.shape[0], split_ref.shape[1] // 2
     share_rows = panel_rows // team_count
     block_count = panel_rows // tile_size
-    table_copy = pltpu.make_async_copy(info_ref, table_ref, sem)
-    table_copy.start()
 
     def split(value, at):
         high = value.astype(jnp.bfloat16)
@@ -92,16 +90,15 @@
             owner = source_team(team_index, k, team_count)
             split(pieces[k][...], pl.ds(pl.multiple_of(owner * share_rows, share_rows), share_rows))
     sums_ref[...] = jnp.zeros_like(sums_ref)
-    table_copy.wait()
-    live_count = table_ref[0]
+    live_count = info_ref[0, 0]
     for j in range(slot_total):
-        source = pl.multiple_of(table_ref[1 + slot_total + j] * tile_size, tile_size)
+        source = pl.multiple_of(info_ref[1 + slot_total + j, 0] * tile_size, tile_size)
         product = jnp.dot(
             tiles_ref[j],
             split_ref[pl.ds(source, tile_size), :],
             preferred_element_type=jnp.float32,
         )
-        row = jnp.where(j < live_count, table_ref[1 + j], block_count)
+        row = jnp.where(j < live_count, info_ref[1 + j, 0], block_count)
         at = pl.ds(pl.multiple_of(row * tile_size, tile_size), tile_size)
         sums_ref[at, :] += product[:, :width] + product[:, width:]
 
@@ -130,13 +127,11 @@
             partial_count=len(partials),
         ),
         out_shape=[share] * team_count,
-        in_specs=[ANY] + [VMEM] * (len(operands) - 1),
+        in_specs=[VMEM] * len(operands),
         out_specs=[VMEM] * team_count,
         scratch_shapes=[
-            pltpu.SMEM(info.shape, info.dtype),
             pltpu.VMEM((panel_rows, 2 * width), jnp.bfloat16),
             pltpu.VMEM((panel_rows + tile_size, width), jnp.float32),
-            pltpu.SemaphoreType.DMA,
         ],
         compiler_params=pltpu.CompilerParams(vmem_limit_bytes=VMEM_LIMIT),
         cost_estimate=pl.CostEstimate(
@@ -193,6 +188,7 @@
     pieces = [fetch(degrees, lambda team: spread[team], arc_length), panel]
     tiles, own, norm_scale = prepare(degrees, embeddings, tile_values[0, 0])
     info = jnp.concatenate([slot_counts[0, 0][:, None], tile_rows[0, 0], tile_columns[0, 0]], axis=1)
+    info = jnp.broadcast_to(info[:, :, None], (*info.shape, embeddings.shape[1]))
 
     combined = own
     for layer in range(LAYERS):

time: 49.5 us -> 49 us (0.990)
  Pallas kernels: 2.9 us -> 2.33 us
    pallas_call x2, Pallas kernels: 2.33 us -> 1.76 us  [arc_step(): pl.pallas_call(functools.partial(arc_kernel, team_count=team_count, piece...]
where the time goes in v6:
time: 49 us; the launch traced here: 48.8 us
  starting transfers between devices  21.3 us (43%)
  waiting for transfers between devices  20.6 us (42%)
  local copies, waits for them, and re-layouts  2.9 us (6%)
  Pallas kernels  2.33 us (5%)
  other arithmetic  0.88 us (2%)
  between operations  0.73 us (1%)
    ppermute x6, waiting for transfers between devices, fetch(): return lax.ppermute(value, ('blk', 'rep'), pairs)  11.2 us
    ppermute x6, starting transfers between devices, fetch(): return lax.ppermute(value, ('blk', 'rep'), pairs)  11 us
    ppermute x2, waiting for transfers between devices, from_column(): return lax.ppermute(value, 'rep', pairs)  7.61 us
    ppermute x2, starting transfers between devices, from_column(): return lax.ppermute(value, 'rep', pairs)  6.71 us
    ppermute x4, starting transfers between devices, from_mate(): lax.ppermute(value, 'rep', [(team, team ^ 1) for team in range(team_count)])  3.54 us
    unnamed x10, local copies, waits for them, and re-layouts  2.83 us
    ppermute x4, waiting for transfers between devices, from_mate(): lax.ppermute(value, 'rep', [(team, team ^ 1) for team in range(team_count)])  1.82 us
    pallas_call x2, Pallas kernels, arc_step(): pl.pallas_call(functools.partial(arc_kernel, team_count=team_count, piece...  1.76 us
  transfers between devices with their start and end apart: 12, of which 8 were waited for; matrix products, arithmetic and copies ran while one was open for 0% of the time, Pallas kernels for 1%

profile of v6, /device:TPU:0, one launch (start us, length us, event | category | flops | bytes accessed | tf_op | source)
XLA Modules:
  0.0 48.8 jit_solution(7681637608469101803)
XLA Ops:
  0.0 5.4 %collective-permute-start.1 = (f32[1024,128]{1,0:T(8,128)}, f32[1024,128]{1,0:T(8,128)S(1)}, u32[]{:S(2)}, u32[]{:S(2)}) collective-permute-start(f32[1024,128]{1,0:T(8,128)} %embeddings_ref.1), channel_id=1, source_target_pairs={{3,0},{1,5},{2,10},{0,15},{7,4},{5,9},{6,14},{4,3},{11,8},{9,13},{... | collective-permute-start | bytes 1572872 | tf_op jit(solution)/shard_map/ppermute | solution.py:150
  5.4 0.8 %collective-permute-start = (s32[8,128]{1,0:T(8,128)}, s32[8,128]{1,0:T(8,128)S(1)}, u32[]{:S(2)}, u32[]{:S(2)}) collective-permute-start(s32[8,128]{1,0:T(8,128)} %bitcast.12), channel_id=1, source_target_pairs={{3,0},{1,5},{2,10},{0,15},{7,4},{5,9},{6,14},{4,3},{11,8},{9,13},{... | collective-permute-start | bytes 12296 | tf_op jit(solution)/shard_map/ppermute | solution.py:150
  6.9 0.6 %copy-done.3 = s32[1,1,1,24]{3,2,1,0:T(1,128)S(1)} copy-done((s32[1,1,1,24]{3,2,1,0:T(1,128)S(1)}, s32[1,1,1,24]{3,2,1,0:T(1,128)}, u32[]{:S(2)}) %copy-start.3) | copy-done | bytes 120
  7.5 0.0 copy-done.4
  7.6 0.1 add_bitcast_fusion
  7.6 1.1 %copy-done = bf16[1,1,1,24,128,128]{5,4,3,2,1,0:T(8,128)(2,1)S(1)} copy-done((bf16[1,1,1,24,128,128]{5,4,3,2,1,0:T(8,128)(2,1)S(1)}, bf16[1,1,1,24,128,128]{5,4,3,2,1,0:T(8,128)(2,1)}, u32[]{:S(2)}) %copy-start) | copy-done | bytes 786456
  8.8 1.0 %copy-done.1 = f32[1024,128]{1,0:T(8,128)S(1)} copy-done((f32[1024,128]{1,0:T(8,128)S(1)}, f32[1024,128]{1,0:T(8,128)}, u32[]{:S(2)}) %copy-start.1) | copy-done | bytes 524312
  9.8 0.6 %shard_map.64 = (bf16[1,24,128,128]{3,2,1,0:T(8,128)(2,1)S(1)}, f32[256,128]{1,0:T(8,128)S(1)}, f32[256,128]{1,0:T(8,128)S(1)}) custom-call(s32[8,128]{1,0:T(8,128)S(1)} %bitcast.13, f32[1024,128]{1,0:T(8,128)S(1)} %copy-done.1, bf16[1,24,128,128]{3,2,1,0:T(8,128)(2,1)S(1)} %bitcast.11), custom_call_target="tpu_custom_call" | custom-call | flops 131072 | bytes 524288 | tf_op jit(solution)/shard_map/pallas_call | solution.py:53
  10.4 4.2 %collective-permute-done.refs_0_ = s32[8,128]{1,0:T(8,128)S(1)} collective-permute-done((s32[8,128]{1,0:T(8,128)}, s32[8,128]{1,0:T(8,128)S(1)}, u32[]{:S(2)}, u32[]{:S(2)}) %collective-permute-start) | collective-permute-done | bytes 4128 | tf_op jit(solution)/shard_map/ppermute | solution.py:150
  14.6 0.0 collective-permute-done.1.refs_1_
  14.6 0.1 squeeze.20.info_ref
  14.7 1.0 %shard_map.65 = (f32[256,128]{1,0:T(8,128)S(1)}, f32[256,128]{1,0:T(8,128)S(1)}, f32[256,128]{1,0:T(8,128)S(1)}, f32[256,128]{1,0:T(8,128)S(1)}) custom-call(s32[49,128]{1,0:T(8,128)S(1)} %squeeze.20.info_ref, bf16[24,128,128]{2,1,0:T(8,128)(2,1)S(1)} %bitcast.9, s32[8,128]{1,0:T(8,128)S(1)} %collective-permute-done.refs_0_, ...), custom_call_target="tpu_custom_call" | custom-call | flops 201326592 | bytes 1048576 | tf_op jit(solution)/shard_map/pallas_call | solution.py:121
  15.7 0.8 %collective-permute-start.2 = (f32[256,128]{1,0:T(8,128)S(1)}, f32[256,128]{1,0:T(8,128)S(1)}, u32[]{:S(2)}, u32[]{:S(2)}) collective-permute-start(f32[256,128]{1,0:T(8,128)S(1)} %get-tuple-element.19), channel_id=1, source_target_pairs={{0,1},{1,0},{2,3},{3,2},{4,5},{5,4},{6,7},{7,6},{8,9},{9,8},{10,11... | collective-permute-start | bytes 393224 | tf_op jit(solution)/shard_map/ppermute | solution.py:160
  16.5 0.1 collective-permute-start.4
  16.6 0.9 %collective-permute-done.2 = f32[256,128]{1,0:T(8,128)S(1)} collective-permute-done((f32[256,128]{1,0:T(8,128)S(1)}, f32[256,128]{1,0:T(8,128)S(1)}, u32[]{:S(2)}, u32[]{:S(2)}) %collective-permute-start.2) | collective-permute-done | bytes 131104 | tf_op jit(solution)/shard_map/ppermute | solution.py:160
  17.5 4.0 %collective-permute-start.3 = (f32[256,128]{1,0:T(8,128)S(1)}, f32[256,128]{1,0:T(8,128)S(1)}, u32[]{:S(2)}, u32[]{:S(2)}) collective-permute-start(f32[256,128]{1,0:T(8,128)S(1)} %add.24), channel_id=1, source_target_pairs={{2,0},{3,1},{0,2},{1,3},{6,4},{7,5},{4,6},{5,7},{10,8},{11,9},{8,1... | collective-permute-start | bytes 393224 | tf_op jit(solution)/shard_map/ppermute | solution.py:166
  21.5 0.0 collective-permute-done.4
  21.5 3.8 %collective-permute-done.3 = f32[256,128]{1,0:T(8,128)S(1)} collective-permute-done((f32[256,128]{1,0:T(8,128)S(1)}, f32[256,128]{1,0:T(8,128)S(1)}, u32[]{:S(2)}, u32[]{:S(2)}) %collective-permute-start.3) | collective-permute-done | bytes 131104 | tf_op jit(solution)/shard_map/ppermute | solution.py:166
  25.4 3.6 %collective-permute-start.8 = (f32[256,128]{1,0:T(8,128)S(1)}, f32[256,128]{1,0:T(8,128)S(1)}, u32[]{:S(2)}, u32[]{:S(2)}) collective-permute-start(f32[256,128]{1,0:T(8,128)S(1)} %fusion), channel_id=1, source_target_pairs={{3,0},{1,5},{2,10},{0,15},{7,4},{5,9},{6,14},{4,3},{11,8},{9,13},{... | collective-permute-start | bytes 393224 | tf_op jit(solution)/shard_map/ppermute | solution.py:150
  29.0 0.5 %collective-permute-start.7 = (f32[256,128]{1,0:T(8,128)S(1)}, f32[256,128]{1,0:T(8,128)S(1)}, u32[]{:S(2)}, u32[]{:S(2)}) collective-permute-start(f32[256,128]{1,0:T(8,128)S(1)} %fusion), channel_id=1, source_target_pairs={{1,0},{3,5},{0,10},{2,15},{5,4},{7,9},{4,14},{6,3},{9,8},{11,13},{... | collective-permute-start | bytes 393224 | tf_op jit(solution)/shard_map/ppermute | solution.py:150
  29.5 0.0 collective-permute-start.6
  29.5 0.7 %collective-permute-start.5 = (f32[256,128]{1,0:T(8,128)S(1)}, f32[256,128]{1,0:T(8,128)S(1)}, u32[]{:S(2)}, u32[]{:S(2)}) collective-permute-start(f32[256,128]{1,0:T(8,128)S(1)} %fusion), channel_id=1, source_target_pairs={{0,0},{2,5},{1,10},{3,15},{4,4},{6,9},{5,14},{7,3},{8,8},{10,13},{... | collective-permute-start | bytes 393224 | tf_op jit(solution)/shard_map/ppermute | solution.py:150
  30.2 2.3 %collective-permute-done.8.refs_3_ = f32[256,128]{1,0:T(8,128)S(1)} collective-permute-done((f32[256,128]{1,0:T(8,128)S(1)}, f32[256,128]{1,0:T(8,128)S(1)}, u32[]{:S(2)}, u32[]{:S(2)}) %collective-permute-start.8) | collective-permute-done | bytes 131104 | tf_op jit(solution)/shard_map/ppermute | solution.py:150
  32.5 2.7 %collective-permute-done.7.refs_2_ = f32[256,128]{1,0:T(8,128)S(1)} collective-permute-done((f32[256,128]{1,0:T(8,128)S(1)}, f32[256,128]{1,0:T(8,128)S(1)}, u32[]{:S(2)}, u32[]{:S(2)}) %collective-permute-start.7) | collective-permute-done | bytes 131104 | tf_op jit(solution)/shard_map/ppermute | solution.py:150
  35.2 2.0 %collective-permute-done.6.refs_1_ = f32[256,128]{1,0:T(8,128)S(1)} collective-permute-done((f32[256,128]{1,0:T(8,128)S(1)}, f32[256,128]{1,0:T(8,128)S(1)}, u32[]{:S(2)}, u32[]{:S(2)}) %collective-permute-start.6) | collective-permute-done | bytes 131104 | tf_op jit(solution)/shard_map/ppermute | solution.py:150
  37.2 0.8 %shard_map.66 = (f32[256,128]{1,0:T(8,128)S(1)}, f32[256,128]{1,0:T(8,128)S(1)}, f32[256,128]{1,0:T(8,128)S(1)}, f32[256,128]{1,0:T(8,128)S(1)}) custom-call(s32[49,128]{1,0:T(8,128)S(1)} %squeeze.20.info_ref, bf16[24,128,128]{2,1,0:T(8,128)(2,1)S(1)} %bitcast.10, f32[256,128]{1,0:T(8,128)S(1)} %collective-permute-done.5.refs_0_, ...), custom_call_target="tpu_custom_call" | custom-call | flops 201326592 | bytes 1048576 | tf_op jit(solution)/shard_map/pallas_call | solution.py:121
  37.9 2.6 %collective-permute-start.9 = (f32[256,128]{1,0:T(8,128)S(1)}, f32[256,128]{1,0:T(8,128)S(1)}, u32[]{:S(2)}, u32[]{:S(2)}) collective-permute-start(f32[256,128]{1,0:T(8,128)S(1)} %get-tuple-element.24), channel_id=1, source_target_pairs={{0,1},{1,0},{2,3},{3,2},{4,5},{5,4},{6,7},{7,6},{8,9},{9,8},{10,11... | collective-permute-start | bytes 393224 | tf_op jit(solution)/shard_map/ppermute | solution.py:160
  40.5 0.1 collective-permute-start.11
  40.6 0.9 %collective-permute-done.9 = f32[256,128]{1,0:T(8,128)S(1)} collective-permute-done((f32[256,128]{1,0:T(8,128)S(1)}, f32[256,128]{1,0:T(8,128)S(1)}, u32[]{:S(2)}, u32[]{:S(2)}) %collective-permute-start.9) | collective-permute-done | bytes 131104 | tf_op jit(solution)/shard_map/ppermute | solution.py:160
  41.5 2.7 %collective-permute-start.10 = (f32[256,128]{1,0:T(8,128)S(1)}, f32[256,128]{1,0:T(8,128)S(1)}, u32[]{:S(2)}, u32[]{:S(2)}) collective-permute-start(f32[256,128]{1,0:T(8,128)S(1)} %add.28), channel_id=1, source_target_pairs={{2,0},{3,1},{0,2},{1,3},{6,4},{7,5},{4,6},{5,7},{10,8},{11,9},{8,1... | collective-permute-start | bytes 393224 | tf_op jit(solution)/shard_map/ppermute | solution.py:166
  44.2 3.8 %collective-permute-done.10 = f32[256,128]{1,0:T(8,128)S(1)} collective-permute-done((f32[256,128]{1,0:T(8,128)S(1)}, f32[256,128]{1,0:T(8,128)S(1)}, u32[]{:S(2)}, u32[]{:S(2)}) %collective-permute-start.10) | collective-permute-done | bytes 131104 | tf_op jit(solution)/shard_map/ppermute | solution.py:166
  48.0 0.7 %add_multiply_fusion = f32[256,128]{1,0:T(8,128)} fusion(f32[256,128]{1,0:T(8,128)S(1)} %get-tuple-element.22, f32[256,128]{1,0:T(8,128)S(1)} %collective-permute-done.10, f32[256,128]{1,0:T(8,128)S(1)} %get-tuple-element.25, f32[256,128]{1,0:T(8,128)S(1)} %collective-permute-done.11, f32[256,128]{1,0:T(8,128)S(1)} %get-tuple-element.16, ...), kind=kLoop, calls=%fused_computation | loop fusion | flops 294912 | bytes 1179648 | tf_op jit(solution)/shard_map/div | solution.py:208
  (11 shorter events, 0.1 us)
Async XLA Ops:
  0.0 14.6 %collective-permute-start.1 = (f32[1024,128]{1,0:T(8,128)}, f32[1024,128]{1,0:T(8,128)S(1)}, u32[]{:S(2)}, u32[]{:S(2)}) collective-permute-start(f32[1024,128]{1,0:T(8,128)} %embeddings_ref.1), channel_id=1, source_target_pairs={{3,0},{1,5},{2,10},{0,15},{7,4},{5,9},{6,14},{4,3},{11,8},{9,13},{... | collective-permute-start | bytes 1572872 | tf_op jit(solution)/shard_map/ppermute | solution.py:150
  5.4 9.2 %collective-permute-start = (s32[8,128]{1,0:T(8,128)}, s32[8,128]{1,0:T(8,128)S(1)}, u32[]{:S(2)}, u32[]{:S(2)}) collective-permute-start(s32[8,128]{1,0:T(8,128)} %bitcast.12), channel_id=1, source_target_pairs={{3,0},{1,5},{2,10},{0,15},{7,4},{5,9},{6,14},{4,3},{11,8},{9,13},{... | collective-permute-start | bytes 12296 | tf_op jit(solution)/shard_map/ppermute | solution.py:150
  6.9 0.7 %copy-start.3 = (s32[1,1,1,24]{3,2,1,0:T(1,128)S(1)}, s32[1,1,1,24]{3,2,1,0:T(1,128)}, u32[]{:S(2)}) copy-start(s32[1,1,1,24]{3,2,1,0:T(1,128)} %param.10) | copy-start | bytes 292
  6.9 0.7 %copy-start.4 = (s32[1,1,1,24]{3,2,1,0:T(1,128)S(1)}, s32[1,1,1,24]{3,2,1,0:T(1,128)}, u32[]{:S(2)}) copy-start(s32[1,1,1,24]{3,2,1,0:T(1,128)} %param.9) | copy-start | bytes 292
  6.9 0.7 %copy-start.2 = (s32[1024]{0:T(1024)S(1)}, s32[1024]{0:T(1024)}, u32[]{:S(2)}) copy-start(s32[1024]{0:T(1024)} %param.7) | copy-start | bytes 12292
  7.6 1.1 %copy-start = (bf16[1,1,1,24,128,128]{5,4,3,2,1,0:T(8,128)(2,1)S(1)}, bf16[1,1,1,24,128,128]{5,4,3,2,1,0:T(8,128)(2,1)}, u32[]{:S(2)}) copy-start(bf16[1,1,1,24,128,128]{5,4,3,2,1,0:T(8,128)(2,1)} %param.8) | copy-start | bytes 2359300
  8.8 1.0 %copy-start.1 = (f32[1024,128]{1,0:T(8,128)S(1)}, f32[1024,128]{1,0:T(8,128)}, u32[]{:S(2)}) copy-start(f32[1024,128]{1,0:T(8,128)} %embeddings_ref.1) | copy-start | bytes 1572868
  15.7 1.8 %collective-permute-start.2 = (f32[256,128]{1,0:T(8,128)S(1)}, f32[256,128]{1,0:T(8,128)S(1)}, u32[]{:S(2)}, u32[]{:S(2)}) collective-permute-start(f32[256,128]{1,0:T(8,128)S(1)} %get-tuple-element.19), channel_id=1, source_target_pairs={{0,1},{1,0},{2,3},{3,2},{4,5},{5,4},{6,7},{7,6},{8,9},{9,8},{10,11... | collective-permute-start | bytes 393224 | tf_op jit(solution)/shard_map/ppermute | solution.py:160
  16.5 5.0 %collective-permute-start.4 = (f32[256,128]{1,0:T(8,128)S(1)}, f32[256,128]{1,0:T(8,128)S(1)}, u32[]{:S(2)}, u32[]{:S(2)}) collective-permute-start(f32[256,128]{1,0:T(8,128)S(1)} %get-tuple-element.21), channel_id=1, source_target_pairs={{0,1},{1,0},{2,3},{3,2},{4,5},{5,4},{6,7},{7,6},{8,9},{9,8},{10,11... | collective-permute-start | bytes 393224 | tf_op jit(solution)/shard_map/ppermute | solution.py:160
  17.5 7.8 %collective-permute-start.3 = (f32[256,128]{1,0:T(8,128)S(1)}, f32[256,128]{1,0:T(8,128)S(1)}, u32[]{:S(2)}, u32[]{:S(2)}) collective-permute-start(f32[256,128]{1,0:T(8,128)S(1)} %add.24), channel_id=1, source_target_pairs={{2,0},{3,1},{0,2},{1,3},{6,4},{7,5},{4,6},{5,7},{10,8},{11,9},{8,1... | collective-permute-start | bytes 393224 | tf_op jit(solution)/shard_map/ppermute | solution.py:166
  25.4 7.1 %collective-permute-start.8 = (f32[256,128]{1,0:T(8,128)S(1)}, f32[256,128]{1,0:T(8,128)S(1)}, u32[]{:S(2)}, u32[]{:S(2)}) collective-permute-start(f32[256,128]{1,0:T(8,128)S(1)} %fusion), channel_id=1, source_target_pairs={{3,0},{1,5},{2,10},{0,15},{7,4},{5,9},{6,14},{4,3},{11,8},{9,13},{... | collective-permute-start | bytes 393224 | tf_op jit(solution)/shard_map/ppermute | solution.py:150
  29.0 6.2 %collective-permute-start.7 = (f32[256,128]{1,0:T(8,128)S(1)}, f32[256,128]{1,0:T(8,128)S(1)}, u32[]{:S(2)}, u32[]{:S(2)}) collective-permute-start(f32[256,128]{1,0:T(8,128)S(1)} %fusion), channel_id=1, source_target_pairs={{1,0},{3,5},{0,10},{2,15},{5,4},{7,9},{4,14},{6,3},{9,8},{11,13},{... | collective-permute-start | bytes 393224 | tf_op jit(solution)/shard_map/ppermute | solution.py:150
  29.5 7.6 %collective-permute-start.6 = (f32[256,128]{1,0:T(8,128)S(1)}, f32[256,128]{1,0:T(8,128)S(1)}, u32[]{:S(2)}, u32[]{:S(2)}) collective-permute-start(f32[256,128]{1,0:T(8,128)S(1)} %fusion), channel_id=1, source_target_pairs={{2,0},{0,5},{3,10},{1,15},{6,4},{4,9},{7,14},{5,3},{10,8},{8,13},{... | collective-permute-start | bytes 393224 | tf_op jit(solution)/shard_map/ppermute | solution.py:150
  29.5 7.6 %collective-permute-start.5 = (f32[256,128]{1,0:T(8,128)S(1)}, f32[256,128]{1,0:T(8,128)S(1)}, u32[]{:S(2)}, u32[]{:S(2)}) collective-permute-start(f32[256,128]{1,0:T(8,128)S(1)} %fusion), channel_id=1, source_target_pairs={{0,0},{2,5},{1,10},{3,15},{4,4},{6,9},{5,14},{7,3},{8,8},{10,13},{... | collective-permute-start | bytes 393224 | tf_op jit(solution)/shard_map/ppermute | solution.py:150
  37.9 3.6 %collective-permute-start.9 = (f32[256,128]{1,0:T(8,128)S(1)}, f32[256,128]{1,0:T(8,128)S(1)}, u32[]{:S(2)}, u32[]{:S(2)}) collective-permute-start(f32[256,128]{1,0:T(8,128)S(1)} %get-tuple-element.24), channel_id=1, source_target_pairs={{0,1},{1,0},{2,3},{3,2},{4,5},{5,4},{6,7},{7,6},{8,9},{9,8},{10,11... | collective-permute-start | bytes 393224 | tf_op jit(solution)/shard_map/ppermute | solution.py:160
  40.5 3.7 %collective-permute-start.11 = (f32[256,128]{1,0:T(8,128)S(1)}, f32[256,128]{1,0:T(8,128)S(1)}, u32[]{:S(2)}, u32[]{:S(2)}) collective-permute-start(f32[256,128]{1,0:T(8,128)S(1)} %get-tuple-element.26), channel_id=1, source_target_pairs={{0,1},{1,0},{2,3},{3,2},{4,5},{5,4},{6,7},{7,6},{8,9},{9,8},{10,11... | collective-permute-start | bytes 393224 | tf_op jit(solution)/shard_map/ppermute | solution.py:160
  41.5 6.5 %collective-permute-start.10 = (f32[256,128]{1,0:T(8,128)S(1)}, f32[256,128]{1,0:T(8,128)S(1)}, u32[]{:S(2)}, u32[]{:S(2)}) collective-permute-start(f32[256,128]{1,0:T(8,128)S(1)} %add.28), channel_id=1, source_target_pairs={{2,0},{3,1},{0,2},{1,3},{6,4},{7,5},{4,6},{5,7},{10,8},{11,9},{8,1... | collective-permute-start | bytes 393224 | tf_op jit(solution)/shard_map/ppermute | solution.py:166

commit v7 on v6

--- a/solution.py
+++ b/solution.py
@@ -20,7 +20,7 @@
 
 def source_team(team, turn, team_count):
     if team_count == 4:
-        return (2 * (team % 2) + team // 2) ^ (0, 2, 1, 3)[turn]
+        return (3 * (team % 2)) ^ (team // 2) ^ turn
     return (team + turn) % team_count
 
 
@@ -28,7 +28,10 @@
     return jnp.transpose(lax.rsqrt(degrees.astype(jnp.float32)))
 
 
-def prepare_kernel(degrees_ref, embeddings_ref, tiles_ref, held_tiles_ref, own_ref, norm_ref, panel_ref, sems):
+def prepare_kernel(
+    degrees_ref, embeddings_ref, tiles_ref, after_ref, held_tiles_ref, own_ref, norm_ref, panel_ref, sems
+):
+    del after_ref
     share_rows, width = own_ref.shape
     block_count, tile_size = degrees_ref.shape
     team_index = lax.axis_index("rep")
@@ -47,20 +50,20 @@
     tiles_copy.wait()
 
 
-def prepare(degrees, embeddings, tile_values):
+def prepare(degrees, embeddings, tile_values, after):
     panel_rows, width = embeddings.shape
     share = jax.ShapeDtypeStruct((panel_rows // lax.axis_size("rep"), width), jnp.float32)
     return pl.pallas_call(
         prepare_kernel,
         out_shape=[jax.ShapeDtypeStruct(tile_values.shape, tile_values.dtype), share, share],
-        in_specs=[VMEM, ANY, ANY],
+        in_specs=[VMEM, ANY, ANY, ANY],
         out_specs=[VMEM] * 3,
         scratch_shapes=[pltpu.VMEM((panel_rows, width), jnp.float32), pltpu.SemaphoreType.DMA((2,))],
         compiler_params=pltpu.CompilerParams(vmem_limit_bytes=VMEM_LIMIT),
         cost_estimate=pl.CostEstimate(
             flops=panel_rows * width, bytes_accessed=4 * panel_rows * width, transcendentals=0
         ),
-    )(degrees, embeddings, tile_values)
+    )(degrees, embeddings, tile_values, after)
 
 
 def arc_kernel(info_ref, tiles_ref, *refs, team_count, piece_count, scaled, partial_count):
@@ -186,9 +189,9 @@
 
     panel = fetch(embeddings, lambda team: spread[team], arc_length)
     pieces = [fetch(degrees, lambda team: spread[team], arc_length), panel]
-    tiles, own, norm_scale = prepare(degrees, embeddings, tile_values[0, 0])
     info = jnp.concatenate([slot_counts[0, 0][:, None], tile_rows[0, 0], tile_columns[0, 0]], axis=1)
     info = jnp.broadcast_to(info[:, :, None], (*info.shape, embeddings.shape[1]))
+    tiles, own, norm_scale = prepare(degrees, embeddings, tile_values[0, 0], info)
 
     combined = own
     for layer in range(LAYERS):

time: 49 us -> 49.6 us (1.012)
  waiting for transfers between devices: 20.6 us -> 18.2 us
  starting transfers between devices: 21.3 us -> 23.6 us
  local copies, waits for them, and re-layouts: 2.9 us -> 3.59 us
    ppermute x6, waiting for transfers between devices: 11.2 us -> 7.82 us  [fetch(): return lax.ppermute(value, ('blk', 'rep'), pairs)]
    ppermute x4, starting transfers between devices: 3.54 us -> 6.85 us  [from_mate(): lax.ppermute(value, 'rep', [(team, team ^ 1) for team in range(team_count)])]
    ppermute x2, starting transfers between devices: 6.71 us -> 5.1 us  [from_column(): return lax.ppermute(value, 'rep', pairs)]
    ppermute x2, waiting for transfers between devices: 7.61 us -> 8.55 us  [from_column(): return lax.ppermute(value, 'rep', pairs)]
    ppermute x6, starting transfers between devices: 11 us -> 11.7 us  [fetch(): return lax.ppermute(value, ('blk', 'rep'), pairs)]
    unnamed x10, local copies, waits for them, and re-layouts: 2.83 us -> 3.44 us
  transfers between devices with their start and end apart: 12 -> 12, of which waited for: 8 -> 7; matrix products, arithmetic and copies ran while one was open for 0% -> 0% of each run, Pallas kernels for 1% -> 1%
where the time goes in v7:
time: 49.6 us; the launch traced here: 49.3 us
  starting transfers between devices  23.6 us (48%)
  waiting for transfers between devices  18.2 us (37%)
  local copies, waits for them, and re-layouts  3.59 us (7%)
  Pallas kernels  2.32 us (5%)
  other arithmetic  0.85 us (2%)
  between operations  0.74 us (1%)
    ppermute x6, starting transfers between devices, fetch(): return lax.ppermute(value, ('blk', 'rep'), pairs)  11.7 us
    ppermute x2, waiting for transfers between devices, from_column(): return lax.ppermute(value, 'rep', pairs)  8.55 us
    ppermute x6, waiting for transfers between devices, fetch(): return lax.ppermute(value, ('blk', 'rep'), pairs)  7.82 us
    ppermute x4, starting transfers between devices, from_mate(): lax.ppermute(value, 'rep', [(team, team ^ 1) for team in range(team_count)])  6.85 us
    ppermute x2, starting transfers between devices, from_column(): return lax.ppermute(value, 'rep', pairs)  5.1 us
    unnamed x10, local copies, waits for them, and re-layouts  3.44 us
    ppermute x4, waiting for transfers between devices, from_mate(): lax.ppermute(value, 'rep', [(team, team ^ 1) for team in range(team_count)])  1.82 us
    pallas_call x2, Pallas kernels, arc_step(): pl.pallas_call(functools.partial(arc_kernel, team_count=team_count, piece...  1.74 us
  transfers between devices with their start and end apart: 12, of which 7 were waited for; matrix products, arithmetic and copies ran while one was open for 0% of the time, Pallas kernels for 1%

profile of v7, /device:TPU:0, one launch (start us, length us, event | category | flops | bytes accessed | tf_op | source)
XLA Modules:
  0.0 49.3 jit_solution(3299039302867983986)
XLA Ops:
  0.0 5.4 %collective-permute-start.1 = (f32[1024,128]{1,0:T(8,128)}, f32[1024,128]{1,0:T(8,128)S(1)}, u32[]{:S(2)}, u32[]{:S(2)}) collective-permute-start(f32[1024,128]{1,0:T(8,128)} %embeddings_ref.1), channel_id=1, source_target_pairs={{3,0},{1,5},{2,10},{0,15},{7,4},{5,9},{6,14},{4,3},{11,8},{9,13},{... | collective-permute-start | bytes 1572872 | tf_op jit(solution)/shard_map/ppermute | solution.py:153
  5.4 0.8 %collective-permute-start = (s32[8,128]{1,0:T(8,128)}, s32[8,128]{1,0:T(8,128)S(1)}, u32[]{:S(2)}, u32[]{:S(2)}) collective-permute-start(s32[8,128]{1,0:T(8,128)} %bitcast.12), channel_id=1, source_target_pairs={{3,0},{1,5},{2,10},{0,15},{7,4},{5,9},{6,14},{4,3},{11,8},{9,13},{... | collective-permute-start | bytes 12296 | tf_op jit(solution)/shard_map/ppermute | solution.py:153
  6.9 0.6 %copy-done.3 = s32[1,1,1,24]{3,2,1,0:T(1,128)S(1)} copy-done((s32[1,1,1,24]{3,2,1,0:T(1,128)S(1)}, s32[1,1,1,24]{3,2,1,0:T(1,128)}, u32[]{:S(2)}) %copy-start.3) | copy-done | bytes 120
  7.5 0.0 copy-done.4
  7.6 0.1 add_bitcast_fusion
  7.6 0.1 broadcast_in_dim.9.after_ref
  7.7 0.6 %copy-done.2 = s32[1024]{0:T(1024)S(1)} copy-done((s32[1024]{0:T(1024)S(1)}, s32[1024]{0:T(1024)}, u32[]{:S(2)}) %copy-start.2) | copy-done | bytes 4120
  8.3 1.1 %copy-done = bf16[1,1,1,24,128,128]{5,4,3,2,1,0:T(8,128)(2,1)S(1)} copy-done((bf16[1,1,1,24,128,128]{5,4,3,2,1,0:T(8,128)(2,1)S(1)}, bf16[1,1,1,24,128,128]{5,4,3,2,1,0:T(8,128)(2,1)}, u32[]{:S(2)}) %copy-start) | copy-done | bytes 786456
  9.5 1.0 %copy-done.1 = f32[1024,128]{1,0:T(8,128)S(1)} copy-done((f32[1024,128]{1,0:T(8,128)S(1)}, f32[1024,128]{1,0:T(8,128)}, u32[]{:S(2)}) %copy-start.1) | copy-done | bytes 524312
  10.5 0.6 %shard_map.64 = (bf16[1,24,128,128]{3,2,1,0:T(8,128)(2,1)S(1)}, f32[256,128]{1,0:T(8,128)S(1)}, f32[256,128]{1,0:T(8,128)S(1)}) custom-call(s32[8,128]{1,0:T(8,128)S(1)} %bitcast.13, f32[1024,128]{1,0:T(8,128)S(1)} %copy-done.1, bf16[1,24,128,128]{3,2,1,0:T(8,128)(2,1)S(1)} %bitcast.11, s32[1,49,128]{2,1,0:T(8,128)S(1)} %broadcast_in_dim.9.after_ref), custom_call_target="tpu_custom_call" | custom-call | flops 131072 | bytes 524288 | tf_op jit(solution)/shard_map/pallas_call | solution.py:56
  11.1 3.5 %collective-permute-done.refs_0_ = s32[8,128]{1,0:T(8,128)S(1)} collective-permute-done((s32[8,128]{1,0:T(8,128)}, s32[8,128]{1,0:T(8,128)S(1)}, u32[]{:S(2)}, u32[]{:S(2)}) %collective-permute-start) | collective-permute-done | bytes 4128 | tf_op jit(solution)/shard_map/ppermute | solution.py:153
  14.6 0.1 squeeze.20.info_ref
  14.7 1.0 %shard_map.65 = (f32[256,128]{1,0:T(8,128)S(1)}, f32[256,128]{1,0:T(8,128)S(1)}, f32[256,128]{1,0:T(8,128)S(1)}, f32[256,128]{1,0:T(8,128)S(1)}) custom-call(s32[49,128]{1,0:T(8,128)S(1)} %squeeze.20.info_ref, bf16[24,128,128]{2,1,0:T(8,128)(2,1)S(1)} %bitcast.9, s32[8,128]{1,0:T(8,128)S(1)} %collective-permute-done.refs_0_, ...), custom_call_target="tpu_custom_call" | custom-call | flops 201326592 | bytes 1048576 | tf_op jit(solution)/shard_map/pallas_call | solution.py:124
  15.7 0.8 %collective-permute-start.2 = (f32[256,128]{1,0:T(8,128)S(1)}, f32[256,128]{1,0:T(8,128)S(1)}, u32[]{:S(2)}, u32[]{:S(2)}) collective-permute-start(f32[256,128]{1,0:T(8,128)S(1)} %get-tuple-element.19), channel_id=1, source_target_pairs={{0,1},{1,0},{2,3},{3,2},{4,5},{5,4},{6,7},{7,6},{8,9},{9,8},{10,11... | collective-permute-start | bytes 393224 | tf_op jit(solution)/shard_map/ppermute | solution.py:163
  16.5 0.1 collective-permute-start.4
  16.6 0.9 %collective-permute-done.2 = f32[256,128]{1,0:T(8,128)S(1)} collective-permute-done((f32[256,128]{1,0:T(8,128)S(1)}, f32[256,128]{1,0:T(8,128)S(1)}, u32[]{:S(2)}, u32[]{:S(2)}) %collective-permute-start.2) | collective-permute-done | bytes 131104 | tf_op jit(solution)/shard_map/ppermute | solution.py:163
  17.5 4.0 %collective-permute-start.3 = (f32[256,128]{1,0:T(8,128)S(1)}, f32[256,128]{1,0:T(8,128)S(1)}, u32[]{:S(2)}, u32[]{:S(2)}) collective-permute-start(f32[256,128]{1,0:T(8,128)S(1)} %add.24), channel_id=1, source_target_pairs={{2,0},{3,1},{0,2},{1,3},{6,4},{7,5},{4,6},{5,7},{10,8},{11,9},{8,1... | collective-permute-start | bytes 393224 | tf_op jit(solution)/shard_map/ppermute | solution.py:169
  21.5 0.0 collective-permute-done.4
  21.5 3.8 %collective-permute-done.3 = f32[256,128]{1,0:T(8,128)S(1)} collective-permute-done((f32[256,128]{1,0:T(8,128)S(1)}, f32[256,128]{1,0:T(8,128)S(1)}, u32[]{:S(2)}, u32[]{:S(2)}) %collective-permute-start.3) | collective-permute-done | bytes 131104 | tf_op jit(solution)/shard_map/ppermute | solution.py:169
  25.3 0.1 collective-permute-start.8
  25.4 4.7 %collective-permute-start.7 = (f32[256,128]{1,0:T(8,128)S(1)}, f32[256,128]{1,0:T(8,128)S(1)}, u32[]{:S(2)}, u32[]{:S(2)}) collective-permute-start(f32[256,128]{1,0:T(8,128)S(1)} %fusion), channel_id=1, source_target_pairs={{2,0},{1,5},{3,10},{0,15},{6,4},{5,9},{7,14},{4,3},{10,8},{9,13},{... | collective-permute-start | bytes 393224 | tf_op jit(solution)/shard_map/ppermute | solution.py:153
  30.1 0.1 collective-permute-start.6
  30.2 0.7 %collective-permute-start.5 = (f32[256,128]{1,0:T(8,128)S(1)}, f32[256,128]{1,0:T(8,128)S(1)}, u32[]{:S(2)}, u32[]{:S(2)}) collective-permute-start(f32[256,128]{1,0:T(8,128)S(1)} %fusion), channel_id=1, source_target_pairs={{0,0},{3,5},{1,10},{2,15},{4,4},{7,9},{5,14},{6,3},{8,8},{11,13},{... | collective-permute-start | bytes 393224 | tf_op jit(solution)/shard_map/ppermute | solution.py:153
  30.8 2.9 %collective-permute-done.7.refs_2_ = f32[256,128]{1,0:T(8,128)S(1)} collective-permute-done((f32[256,128]{1,0:T(8,128)S(1)}, f32[256,128]{1,0:T(8,128)S(1)}, u32[]{:S(2)}, u32[]{:S(2)}) %collective-permute-start.7) | collective-permute-done | bytes 131104 | tf_op jit(solution)/shard_map/ppermute | solution.py:153
  33.7 1.4 %collective-permute-done.6.refs_1_ = f32[256,128]{1,0:T(8,128)S(1)} collective-permute-done((f32[256,128]{1,0:T(8,128)S(1)}, f32[256,128]{1,0:T(8,128)S(1)}, u32[]{:S(2)}, u32[]{:S(2)}) %collective-permute-start.6) | collective-permute-done | bytes 131104 | tf_op jit(solution)/shard_map/ppermute | solution.py:153
  35.1 0.8 %shard_map.66 = (f32[256,128]{1,0:T(8,128)S(1)}, f32[256,128]{1,0:T(8,128)S(1)}, f32[256,128]{1,0:T(8,128)S(1)}, f32[256,128]{1,0:T(8,128)S(1)}) custom-call(s32[49,128]{1,0:T(8,128)S(1)} %squeeze.20.info_ref, bf16[24,128,128]{2,1,0:T(8,128)(2,1)S(1)} %bitcast.10, f32[256,128]{1,0:T(8,128)S(1)} %collective-permute-done.5.refs_0_, ...), custom_call_target="tpu_custom_call" | custom-call | flops 201326592 | bytes 1048576 | tf_op jit(solution)/shard_map/pallas_call | solution.py:124
  35.9 5.9 %collective-permute-start.9 = (f32[256,128]{1,0:T(8,128)S(1)}, f32[256,128]{1,0:T(8,128)S(1)}, u32[]{:S(2)}, u32[]{:S(2)}) collective-permute-start(f32[256,128]{1,0:T(8,128)S(1)} %get-tuple-element.24), channel_id=1, source_target_pairs={{0,1},{1,0},{2,3},{3,2},{4,5},{5,4},{6,7},{7,6},{8,9},{9,8},{10,11... | collective-permute-start | bytes 393224 | tf_op jit(solution)/shard_map/ppermute | solution.py:163
  41.8 0.1 collective-permute-start.11
  41.9 0.9 %collective-permute-done.9 = f32[256,128]{1,0:T(8,128)S(1)} collective-permute-done((f32[256,128]{1,0:T(8,128)S(1)}, f32[256,128]{1,0:T(8,128)S(1)}, u32[]{:S(2)}, u32[]{:S(2)}) %collective-permute-start.9) | collective-permute-done | bytes 131104 | tf_op jit(solution)/shard_map/ppermute | solution.py:163
  42.8 1.1 %collective-permute-start.10 = (f32[256,128]{1,0:T(8,128)S(1)}, f32[256,128]{1,0:T(8,128)S(1)}, u32[]{:S(2)}, u32[]{:S(2)}) collective-permute-start(f32[256,128]{1,0:T(8,128)S(1)} %add.28), channel_id=1, source_target_pairs={{2,0},{3,1},{0,2},{1,3},{6,4},{7,5},{4,6},{5,7},{10,8},{11,9},{8,1... | collective-permute-start | bytes 393224 | tf_op jit(solution)/shard_map/ppermute | solution.py:169
  43.9 4.7 %collective-permute-done.10 = f32[256,128]{1,0:T(8,128)S(1)} collective-permute-done((f32[256,128]{1,0:T(8,128)S(1)}, f32[256,128]{1,0:T(8,128)S(1)}, u32[]{:S(2)}, u32[]{:S(2)}) %collective-permute-start.10) | collective-permute-done | bytes 131104 | tf_op jit(solution)/shard_map/ppermute | solution.py:169
  48.6 0.7 %add_multiply_fusion = f32[256,128]{1,0:T(8,128)} fusion(f32[256,128]{1,0:T(8,128)S(1)} %get-tuple-element.22, f32[256,128]{1,0:T(8,128)S(1)} %collective-permute-done.10, f32[256,128]{1,0:T(8,128)S(1)} %get-tuple-element.25, f32[256,128]{1,0:T(8,128)S(1)} %collective-permute-done.11, f32[256,128]{1,0:T(8,128)S(1)} %get-tuple-element.16, ...), kind=kLoop, calls=%fused_computation | loop fusion | flops 294912 | bytes 1179648 | tf_op jit(solution)/shard_map/div | solution.py:211
  (12 shorter events, 0.1 us)
Async XLA Ops:
  0.0 14.6 %collective-permute-start.1 = (f32[1024,128]{1,0:T(8,128)}, f32[1024,128]{1,0:T(8,128)S(1)}, u32[]{:S(2)}, u32[]{:S(2)}) collective-permute-start(f32[1024,128]{1,0:T(8,128)} %embeddings_ref.1), channel_id=1, source_target_pairs={{3,0},{1,5},{2,10},{0,15},{7,4},{5,9},{6,14},{4,3},{11,8},{9,13},{... | collective-permute-start | bytes 1572872 | tf_op jit(solution)/shard_map/ppermute | solution.py:153
  5.4 9.2 %collective-permute-start = (s32[8,128]{1,0:T(8,128)}, s32[8,128]{1,0:T(8,128)S(1)}, u32[]{:S(2)}, u32[]{:S(2)}) collective-permute-start(s32[8,128]{1,0:T(8,128)} %bitcast.12), channel_id=1, source_target_pairs={{3,0},{1,5},{2,10},{0,15},{7,4},{5,9},{6,14},{4,3},{11,8},{9,13},{... | collective-permute-start | bytes 12296 | tf_op jit(solution)/shard_map/ppermute | solution.py:153
  6.9 0.7 %copy-start.3 = (s32[1,1,1,24]{3,2,1,0:T(1,128)S(1)}, s32[1,1,1,24]{3,2,1,0:T(1,128)}, u32[]{:S(2)}) copy-start(s32[1,1,1,24]{3,2,1,0:T(1,128)} %param.10) | copy-start | bytes 292
  6.9 0.7 %copy-start.4 = (s32[1,1,1,24]{3,2,1,0:T(1,128)S(1)}, s32[1,1,1,24]{3,2,1,0:T(1,128)}, u32[]{:S(2)}) copy-start(s32[1,1,1,24]{3,2,1,0:T(1,128)} %param.9) | copy-start | bytes 292
  7.6 0.7 %copy-start.2 = (s32[1024]{0:T(1024)S(1)}, s32[1024]{0:T(1024)}, u32[]{:S(2)}) copy-start(s32[1024]{0:T(1024)} %param.7) | copy-start | bytes 12292
  8.3 1.1 %copy-start = (bf16[1,1,1,24,128,128]{5,4,3,2,1,0:T(8,128)(2,1)S(1)}, bf16[1,1,1,24,128,128]{5,4,3,2,1,0:T(8,128)(2,1)}, u32[]{:S(2)}) copy-start(bf16[1,1,1,24,128,128]{5,4,3,2,1,0:T(8,128)(2,1)} %param.8) | copy-start | bytes 2359300
  9.5 1.0 %copy-start.1 = (f32[1024,128]{1,0:T(8,128)S(1)}, f32[1024,128]{1,0:T(8,128)}, u32[]{:S(2)}) copy-start(f32[1024,128]{1,0:T(8,128)} %embeddings_ref.1) | copy-start | bytes 1572868
  15.7 1.8 %collective-permute-start.2 = (f32[256,128]{1,0:T(8,128)S(1)}, f32[256,128]{1,0:T(8,128)S(1)}, u32[]{:S(2)}, u32[]{:S(2)}) collective-permute-start(f32[256,128]{1,0:T(8,128)S(1)} %get-tuple-element.19), channel_id=1, source_target_pairs={{0,1},{1,0},{2,3},{3,2},{4,5},{5,4},{6,7},{7,6},{8,9},{9,8},{10,11... | collective-permute-start | bytes 393224 | tf_op jit(solution)/shard_map/ppermute | solution.py:163
  16.5 5.0 %collective-permute-start.4 = (f32[256,128]{1,0:T(8,128)S(1)}, f32[256,128]{1,0:T(8,128)S(1)}, u32[]{:S(2)}, u32[]{:S(2)}) collective-permute-start(f32[256,128]{1,0:T(8,128)S(1)} %get-tuple-element.21), channel_id=1, source_target_pairs={{0,1},{1,0},{2,3},{3,2},{4,5},{5,4},{6,7},{7,6},{8,9},{9,8},{10,11... | collective-permute-start | bytes 393224 | tf_op jit(solution)/shard_map/ppermute | solution.py:163
  17.5 7.8 %collective-permute-start.3 = (f32[256,128]{1,0:T(8,128)S(1)}, f32[256,128]{1,0:T(8,128)S(1)}, u32[]{:S(2)}, u32[]{:S(2)}) collective-permute-start(f32[256,128]{1,0:T(8,128)S(1)} %add.24), channel_id=1, source_target_pairs={{2,0},{3,1},{0,2},{1,3},{6,4},{7,5},{4,6},{5,7},{10,8},{11,9},{8,1... | collective-permute-start | bytes 393224 | tf_op jit(solution)/shard_map/ppermute | solution.py:169
  25.3 5.5 %collective-permute-start.8 = (f32[256,128]{1,0:T(8,128)S(1)}, f32[256,128]{1,0:T(8,128)S(1)}, u32[]{:S(2)}, u32[]{:S(2)}) collective-permute-start(f32[256,128]{1,0:T(8,128)S(1)} %fusion), channel_id=1, source_target_pairs={{3,0},{0,5},{2,10},{1,15},{7,4},{4,9},{6,14},{5,3},{11,8},{8,13},{... | collective-permute-start | bytes 393224 | tf_op jit(solution)/shard_map/ppermute | solution.py:153
  25.4 8.3 %collective-permute-start.7 = (f32[256,128]{1,0:T(8,128)S(1)}, f32[256,128]{1,0:T(8,128)S(1)}, u32[]{:S(2)}, u32[]{:S(2)}) collective-permute-start(f32[256,128]{1,0:T(8,128)S(1)} %fusion), channel_id=1, source_target_pairs={{2,0},{1,5},{3,10},{0,15},{6,4},{5,9},{7,14},{4,3},{10,8},{9,13},{... | collective-permute-start | bytes 393224 | tf_op jit(solution)/shard_map/ppermute | solution.py:153
  30.1 5.0 %collective-permute-start.6 = (f32[256,128]{1,0:T(8,128)S(1)}, f32[256,128]{1,0:T(8,128)S(1)}, u32[]{:S(2)}, u32[]{:S(2)}) collective-permute-start(f32[256,128]{1,0:T(8,128)S(1)} %fusion), channel_id=1, source_target_pairs={{1,0},{2,5},{0,10},{3,15},{5,4},{6,9},{4,14},{7,3},{9,8},{10,13},{... | collective-permute-start | bytes 393224 | tf_op jit(solution)/shard_map/ppermute | solution.py:153
  30.2 5.0 %collective-permute-start.5 = (f32[256,128]{1,0:T(8,128)S(1)}, f32[256,128]{1,0:T(8,128)S(1)}, u32[]{:S(2)}, u32[]{:S(2)}) collective-permute-start(f32[256,128]{1,0:T(8,128)S(1)} %fusion), channel_id=1, source_target_pairs={{0,0},{3,5},{1,10},{2,15},{4,4},{7,9},{5,14},{6,3},{8,8},{11,13},{... | collective-permute-start | bytes 393224 | tf_op jit(solution)/shard_map/ppermute | solution.py:153
  35.9 6.9 %collective-permute-start.9 = (f32[256,128]{1,0:T(8,128)S(1)}, f32[256,128]{1,0:T(8,128)S(1)}, u32[]{:S(2)}, u32[]{:S(2)}) collective-permute-start(f32[256,128]{1,0:T(8,128)S(1)} %get-tuple-element.24), channel_id=1, source_target_pairs={{0,1},{1,0},{2,3},{3,2},{4,5},{5,4},{6,7},{7,6},{8,9},{9,8},{10,11... | collective-permute-start | bytes 393224 | tf_op jit(solution)/shard_map/ppermute | solution.py:163
  41.8 2.1 %collective-permute-start.11 = (f32[256,128]{1,0:T(8,128)S(1)}, f32[256,128]{1,0:T(8,128)S(1)}, u32[]{:S(2)}, u32[]{:S(2)}) collective-permute-start(f32[256,128]{1,0:T(8,128)S(1)} %get-tuple-element.26), channel_id=1, source_target_pairs={{0,1},{1,0},{2,3},{3,2},{4,5},{5,4},{6,7},{7,6},{8,9},{9,8},{10,11... | collective-permute-start | bytes 393224 | tf_op jit(solution)/shard_map/ppermute | solution.py:163
  42.8 5.8 %collective-permute-start.10 = (f32[256,128]{1,0:T(8,128)S(1)}, f32[256,128]{1,0:T(8,128)S(1)}, u32[]{:S(2)}, u32[]{:S(2)}) collective-permute-start(f32[256,128]{1,0:T(8,128)S(1)} %add.28), channel_id=1, source_target_pairs={{2,0},{3,1},{0,2},{1,3},{6,4},{7,5},{4,6},{5,7},{10,8},{11,9},{8,1... | collective-permute-start | bytes 393224 | tf_op jit(solution)/shard_map/ppermute | solution.py:169

commit v8 on v7

--- a/solution.py
+++ b/solution.py
@@ -20,7 +20,7 @@
 
 def source_team(team, turn, team_count):
     if team_count == 4:
-        return (3 * (team % 2)) ^ (team // 2) ^ turn
+        return (3 * (team % 2)) ^ (team // 2) ^ (2, 1, 0, 3)[turn]
     return (team + turn) % team_count
 
 

time: 49.6 us -> 50.6 us (1.020)
  starting transfers between devices: 23.6 us -> 26 us
  waiting for transfers between devices: 18.2 us -> 16.8 us
    ppermute x6, starting transfers between devices: 11.7 us -> 16.1 us  [fetch(): return lax.ppermute(value, ('blk', 'rep'), pairs)]
    ppermute x4, starting transfers between devices: 6.85 us -> 2.94 us  [from_mate(): lax.ppermute(value, 'rep', [(team, team ^ 1) for team in range(team_count)])]
    ppermute x2, starting transfers between devices: 5.1 us -> 7.01 us  [from_column(): return lax.ppermute(value, 'rep', pairs)]
    ppermute x2, waiting for transfers between devices: 8.55 us -> 7.81 us  [from_column(): return lax.ppermute(value, 'rep', pairs)]
    ppermute x6, waiting for transfers between devices: 7.82 us -> 7.17 us  [fetch(): return lax.ppermute(value, ('blk', 'rep'), pairs)]
where the time goes in v8:
time: 50.6 us; the launch traced here: 50.3 us
  starting transfers between devices  26 us (51%)
  waiting for transfers between devices  16.8 us (33%)
  local copies, waits for them, and re-layouts  3.59 us (7%)
  Pallas kernels  2.32 us (5%)
  other arithmetic  0.85 us (2%)
  between operations  0.73 us (1%)
    ppermute x6, starting transfers between devices, fetch(): return lax.ppermute(value, ('blk', 'rep'), pairs)  16.1 us
    ppermute x2, waiting for transfers between devices, from_column(): return lax.ppermute(value, 'rep', pairs)  7.81 us
    ppermute x6, waiting for transfers between devices, fetch(): return lax.ppermute(value, ('blk', 'rep'), pairs)  7.17 us
    ppermute x2, starting transfers between devices, from_column(): return lax.ppermute(value, 'rep', pairs)  7.01 us
    unnamed x10, local copies, waits for them, and re-layouts  3.44 us
    ppermute x4, starting transfers between devices, from_mate(): lax.ppermute(value, 'rep', [(team, team ^ 1) for team in range(team_count)])  2.94 us
    ppermute x4, waiting for transfers between devices, from_mate(): lax.ppermute(value, 'rep', [(team, team ^ 1) for team in range(team_count)])  1.82 us
    pallas_call x2, Pallas kernels, arc_step(): pl.pallas_call(functools.partial(arc_kernel, team_count=team_count, piece...  1.74 us
  transfers between devices with their start and end apart: 12, of which 7 were waited for; matrix products, arithmetic and copies ran while one was open for 0% of the time, Pallas kernels for 1%

profile of v8, /device:TPU:0, one launch (start us, length us, event | category | flops | bytes accessed | tf_op | source)
XLA Modules:
  0.0 50.3 jit_solution(18012808535033526890)
XLA Ops:
  0.0 5.4 %collective-permute-start.1 = (f32[1024,128]{1,0:T(8,128)}, f32[1024,128]{1,0:T(8,128)S(1)}, u32[]{:S(2)}, u32[]{:S(2)}) collective-permute-start(f32[1024,128]{1,0:T(8,128)} %embeddings_ref.1), channel_id=1, source_target_pairs={{3,0},{1,5},{2,10},{0,15},{7,4},{5,9},{6,14},{4,3},{11,8},{9,13},{... | collective-permute-start | bytes 1572872 | tf_op jit(solution)/shard_map/ppermute | solution.py:153
  5.4 0.8 %collective-permute-start = (s32[8,128]{1,0:T(8,128)}, s32[8,128]{1,0:T(8,128)S(1)}, u32[]{:S(2)}, u32[]{:S(2)}) collective-permute-start(s32[8,128]{1,0:T(8,128)} %bitcast.12), channel_id=1, source_target_pairs={{3,0},{1,5},{2,10},{0,15},{7,4},{5,9},{6,14},{4,3},{11,8},{9,13},{... | collective-permute-start | bytes 12296 | tf_op jit(solution)/shard_map/ppermute | solution.py:153
  6.9 0.6 %copy-done.3 = s32[1,1,1,24]{3,2,1,0:T(1,128)S(1)} copy-done((s32[1,1,1,24]{3,2,1,0:T(1,128)S(1)}, s32[1,1,1,24]{3,2,1,0:T(1,128)}, u32[]{:S(2)}) %copy-start.3) | copy-done | bytes 120
  7.5 0.0 copy-done.4
  7.6 0.1 add_bitcast_fusion
  7.6 0.1 broadcast_in_dim.9.after_ref
  7.7 0.6 %copy-done.2 = s32[1024]{0:T(1024)S(1)} copy-done((s32[1024]{0:T(1024)S(1)}, s32[1024]{0:T(1024)}, u32[]{:S(2)}) %copy-start.2) | copy-done | bytes 4120
  8.3 1.1 %copy-done = bf16[1,1,1,24,128,128]{5,4,3,2,1,0:T(8,128)(2,1)S(1)} copy-done((bf16[1,1,1,24,128,128]{5,4,3,2,1,0:T(8,128)(2,1)S(1)}, bf16[1,1,1,24,128,128]{5,4,3,2,1,0:T(8,128)(2,1)}, u32[]{:S(2)}) %copy-start) | copy-done | bytes 786456
  9.5 1.0 %copy-done.1 = f32[1024,128]{1,0:T(8,128)S(1)} copy-done((f32[1024,128]{1,0:T(8,128)S(1)}, f32[1024,128]{1,0:T(8,128)}, u32[]{:S(2)}) %copy-start.1) | copy-done | bytes 524312
  10.5 0.6 %shard_map.64 = (bf16[1,24,128,128]{3,2,1,0:T(8,128)(2,1)S(1)}, f32[256,128]{1,0:T(8,128)S(1)}, f32[256,128]{1,0:T(8,128)S(1)}) custom-call(s32[8,128]{1,0:T(8,128)S(1)} %bitcast.13, f32[1024,128]{1,0:T(8,128)S(1)} %copy-done.1, bf16[1,24,128,128]{3,2,1,0:T(8,128)(2,1)S(1)} %bitcast.11, s32[1,49,128]{2,1,0:T(8,128)S(1)} %broadcast_in_dim.9.after_ref), custom_call_target="tpu_custom_call" | custom-call | flops 131072 | bytes 524288 | tf_op jit(solution)/shard_map/pallas_call | solution.py:56
  11.1 3.5 %collective-permute-done.refs_0_ = s32[8,128]{1,0:T(8,128)S(1)} collective-permute-done((s32[8,128]{1,0:T(8,128)}, s32[8,128]{1,0:T(8,128)S(1)}, u32[]{:S(2)}, u32[]{:S(2)}) %collective-permute-start) | collective-permute-done | bytes 4128 | tf_op jit(solution)/shard_map/ppermute | solution.py:153
  14.6 0.0 collective-permute-done.1.refs_1_
  14.6 0.1 squeeze.20.info_ref
  14.7 1.0 %shard_map.65 = (f32[256,128]{1,0:T(8,128)S(1)}, f32[256,128]{1,0:T(8,128)S(1)}, f32[256,128]{1,0:T(8,128)S(1)}, f32[256,128]{1,0:T(8,128)S(1)}) custom-call(s32[49,128]{1,0:T(8,128)S(1)} %squeeze.20.info_ref, bf16[24,128,128]{2,1,0:T(8,128)(2,1)S(1)} %bitcast.9, s32[8,128]{1,0:T(8,128)S(1)} %collective-permute-done.refs_0_, ...), custom_call_target="tpu_custom_call" | custom-call | flops 201326592 | bytes 1048576 | tf_op jit(solution)/shard_map/pallas_call | solution.py:124
  15.7 0.8 %collective-permute-start.2 = (f32[256,128]{1,0:T(8,128)S(1)}, f32[256,128]{1,0:T(8,128)S(1)}, u32[]{:S(2)}, u32[]{:S(2)}) collective-permute-start(f32[256,128]{1,0:T(8,128)S(1)} %get-tuple-element.19), channel_id=1, source_target_pairs={{0,1},{1,0},{2,3},{3,2},{4,5},{5,4},{6,7},{7,6},{8,9},{9,8},{10,11... | collective-permute-start | bytes 393224 | tf_op jit(solution)/shard_map/ppermute | solution.py:163
  16.5 0.1 collective-permute-start.4
  16.6 0.9 %collective-permute-done.2 = f32[256,128]{1,0:T(8,128)S(1)} collective-permute-done((f32[256,128]{1,0:T(8,128)S(1)}, f32[256,128]{1,0:T(8,128)S(1)}, u32[]{:S(2)}, u32[]{:S(2)}) %collective-permute-start.2) | collective-permute-done | bytes 131104 | tf_op jit(solution)/shard_map/ppermute | solution.py:163
  17.5 4.0 %collective-permute-start.3 = (f32[256,128]{1,0:T(8,128)S(1)}, f32[256,128]{1,0:T(8,128)S(1)}, u32[]{:S(2)}, u32[]{:S(2)}) collective-permute-start(f32[256,128]{1,0:T(8,128)S(1)} %add.24), channel_id=1, source_target_pairs={{2,0},{3,1},{0,2},{1,3},{6,4},{7,5},{4,6},{5,7},{10,8},{11,9},{8,1... | collective-permute-start | bytes 393224 | tf_op jit(solution)/shard_map/ppermute | solution.py:169
  21.5 3.8 %collective-permute-done.3 = f32[256,128]{1,0:T(8,128)S(1)} collective-permute-done((f32[256,128]{1,0:T(8,128)S(1)}, f32[256,128]{1,0:T(8,128)S(1)}, u32[]{:S(2)}, u32[]{:S(2)}) %collective-permute-start.3) | collective-permute-done | bytes 131104 | tf_op jit(solution)/shard_map/ppermute | solution.py:169
  25.3 0.1 collective-permute-start.8
  25.4 0.7 %collective-permute-start.7 = (f32[256,128]{1,0:T(8,128)S(1)}, f32[256,128]{1,0:T(8,128)S(1)}, u32[]{:S(2)}, u32[]{:S(2)}) collective-permute-start(f32[256,128]{1,0:T(8,128)S(1)} %fusion), channel_id=1, source_target_pairs={{0,0},{3,5},{1,10},{2,15},{4,4},{7,9},{5,14},{6,3},{8,8},{11,13},{... | collective-permute-start | bytes 393224 | tf_op jit(solution)/shard_map/ppermute | solution.py:153
  26.1 5.4 %collective-permute-start.6 = (f32[256,128]{1,0:T(8,128)S(1)}, f32[256,128]{1,0:T(8,128)S(1)}, u32[]{:S(2)}, u32[]{:S(2)}) collective-permute-start(f32[256,128]{1,0:T(8,128)S(1)} %fusion), channel_id=1, source_target_pairs={{1,0},{2,5},{0,10},{3,15},{5,4},{6,9},{4,14},{7,3},{9,8},{10,13},{... | collective-permute-start | bytes 393224 | tf_op jit(solution)/shard_map/ppermute | solution.py:153
  31.5 3.7 %collective-permute-start.5 = (f32[256,128]{1,0:T(8,128)S(1)}, f32[256,128]{1,0:T(8,128)S(1)}, u32[]{:S(2)}, u32[]{:S(2)}) collective-permute-start(f32[256,128]{1,0:T(8,128)S(1)} %fusion), channel_id=1, source_target_pairs={{2,0},{1,5},{3,10},{0,15},{6,4},{5,9},{7,14},{4,3},{10,8},{9,13},{... | collective-permute-start | bytes 393224 | tf_op jit(solution)/shard_map/ppermute | solution.py:153
  35.2 0.2 collective-permute-done.6.refs_1_
  35.4 3.5 %collective-permute-done.5.refs_0_ = f32[256,128]{1,0:T(8,128)S(1)} collective-permute-done((f32[256,128]{1,0:T(8,128)S(1)}, f32[256,128]{1,0:T(8,128)S(1)}, u32[]{:S(2)}, u32[]{:S(2)}) %collective-permute-start.5) | collective-permute-done | bytes 131104 | tf_op jit(solution)/shard_map/ppermute | solution.py:153
  38.8 0.8 %shard_map.66 = (f32[256,128]{1,0:T(8,128)S(1)}, f32[256,128]{1,0:T(8,128)S(1)}, f32[256,128]{1,0:T(8,128)S(1)}, f32[256,128]{1,0:T(8,128)S(1)}) custom-call(s32[49,128]{1,0:T(8,128)S(1)} %squeeze.20.info_ref, bf16[24,128,128]{2,1,0:T(8,128)(2,1)S(1)} %bitcast.10, f32[256,128]{1,0:T(8,128)S(1)} %collective-permute-done.5.refs_0_, ...), custom_call_target="tpu_custom_call" | custom-call | flops 201326592 | bytes 1048576 | tf_op jit(solution)/shard_map/pallas_call | solution.py:124
  39.6 2.0 %collective-permute-start.9 = (f32[256,128]{1,0:T(8,128)S(1)}, f32[256,128]{1,0:T(8,128)S(1)}, u32[]{:S(2)}, u32[]{:S(2)}) collective-permute-start(f32[256,128]{1,0:T(8,128)S(1)} %get-tuple-element.24), channel_id=1, source_target_pairs={{0,1},{1,0},{2,3},{3,2},{4,5},{5,4},{6,7},{7,6},{8,9},{9,8},{10,11... | collective-permute-start | bytes 393224 | tf_op jit(solution)/shard_map/ppermute | solution.py:163
  41.6 0.1 collective-permute-start.11
  41.7 0.9 %collective-permute-done.9 = f32[256,128]{1,0:T(8,128)S(1)} collective-permute-done((f32[256,128]{1,0:T(8,128)S(1)}, f32[256,128]{1,0:T(8,128)S(1)}, u32[]{:S(2)}, u32[]{:S(2)}) %collective-permute-start.9) | collective-permute-done | bytes 131104 | tf_op jit(solution)/shard_map/ppermute | solution.py:163
  42.6 3.0 %collective-permute-start.10 = (f32[256,128]{1,0:T(8,128)S(1)}, f32[256,128]{1,0:T(8,128)S(1)}, u32[]{:S(2)}, u32[]{:S(2)}) collective-permute-start(f32[256,128]{1,0:T(8,128)S(1)} %add.28), channel_id=1, source_target_pairs={{2,0},{3,1},{0,2},{1,3},{6,4},{7,5},{4,6},{5,7},{10,8},{11,9},{8,1... | collective-permute-start | bytes 393224 | tf_op jit(solution)/shard_map/ppermute | solution.py:169
  45.6 4.0 %collective-permute-done.10 = f32[256,128]{1,0:T(8,128)S(1)} collective-permute-done((f32[256,128]{1,0:T(8,128)S(1)}, f32[256,128]{1,0:T(8,128)S(1)}, u32[]{:S(2)}, u32[]{:S(2)}) %collective-permute-start.10) | collective-permute-done | bytes 131104 | tf_op jit(solution)/shard_map/ppermute | solution.py:169
  49.6 0.7 %add_multiply_fusion = f32[256,128]{1,0:T(8,128)} fusion(f32[256,128]{1,0:T(8,128)S(1)} %get-tuple-element.22, f32[256,128]{1,0:T(8,128)S(1)} %collective-permute-done.10, f32[256,128]{1,0:T(8,128)S(1)} %get-tuple-element.25, f32[256,128]{1,0:T(8,128)S(1)} %collective-permute-done.11, f32[256,128]{1,0:T(8,128)S(1)} %get-tuple-element.16, ...), kind=kLoop, calls=%fused_computation | loop fusion | flops 294912 | bytes 1179648 | tf_op jit(solution)/shard_map/div | solution.py:211
  (12 shorter events, 0.1 us)
Async XLA Ops:
  0.0 14.6 %collective-permute-start.1 = (f32[1024,128]{1,0:T(8,128)}, f32[1024,128]{1,0:T(8,128)S(1)}, u32[]{:S(2)}, u32[]{:S(2)}) collective-permute-start(f32[1024,128]{1,0:T(8,128)} %embeddings_ref.1), channel_id=1, source_target_pairs={{3,0},{1,5},{2,10},{0,15},{7,4},{5,9},{6,14},{4,3},{11,8},{9,13},{... | collective-permute-start | bytes 1572872 | tf_op jit(solution)/shard_map/ppermute | solution.py:153
  5.4 9.2 %collective-permute-start = (s32[8,128]{1,0:T(8,128)}, s32[8,128]{1,0:T(8,128)S(1)}, u32[]{:S(2)}, u32[]{:S(2)}) collective-permute-start(s32[8,128]{1,0:T(8,128)} %bitcast.12), channel_id=1, source_target_pairs={{3,0},{1,5},{2,10},{0,15},{7,4},{5,9},{6,14},{4,3},{11,8},{9,13},{... | collective-permute-start | bytes 12296 | tf_op jit(solution)/shard_map/ppermute | solution.py:153
  6.9 0.7 %copy-start.3 = (s32[1,1,1,24]{3,2,1,0:T(1,128)S(1)}, s32[1,1,1,24]{3,2,1,0:T(1,128)}, u32[]{:S(2)}) copy-start(s32[1,1,1,24]{3,2,1,0:T(1,128)} %param.10) | copy-start | bytes 292
  6.9 0.7 %copy-start.4 = (s32[1,1,1,24]{3,2,1,0:T(1,128)S(1)}, s32[1,1,1,24]{3,2,1,0:T(1,128)}, u32[]{:S(2)}) copy-start(s32[1,1,1,24]{3,2,1,0:T(1,128)} %param.9) | copy-start | bytes 292
  7.6 0.7 %copy-start.2 = (s32[1024]{0:T(1024)S(1)}, s32[1024]{0:T(1024)}, u32[]{:S(2)}) copy-start(s32[1024]{0:T(1024)} %param.7) | copy-start | bytes 12292
  8.3 1.1 %copy-start = (bf16[1,1,1,24,128,128]{5,4,3,2,1,0:T(8,128)(2,1)S(1)}, bf16[1,1,1,24,128,128]{5,4,3,2,1,0:T(8,128)(2,1)}, u32[]{:S(2)}) copy-start(bf16[1,1,1,24,128,128]{5,4,3,2,1,0:T(8,128)(2,1)} %param.8) | copy-start | bytes 2359300
  9.5 1.0 %copy-start.1 = (f32[1024,128]{1,0:T(8,128)S(1)}, f32[1024,128]{1,0:T(8,128)}, u32[]{:S(2)}) copy-start(f32[1024,128]{1,0:T(8,128)} %embeddings_ref.1) | copy-start | bytes 1572868
  15.7 1.8 %collective-permute-start.2 = (f32[256,128]{1,0:T(8,128)S(1)}, f32[256,128]{1,0:T(8,128)S(1)}, u32[]{:S(2)}, u32[]{:S(2)}) collective-permute-start(f32[256,128]{1,0:T(8,128)S(1)} %get-tuple-element.19), channel_id=1, source_target_pairs={{0,1},{1,0},{2,3},{3,2},{4,5},{5,4},{6,7},{7,6},{8,9},{9,8},{10,11... | collective-permute-start | bytes 393224 | tf_op jit(solution)/shard_map/ppermute | solution.py:163
  16.5 5.0 %collective-permute-start.4 = (f32[256,128]{1,0:T(8,128)S(1)}, f32[256,128]{1,0:T(8,128)S(1)}, u32[]{:S(2)}, u32[]{:S(2)}) collective-permute-start(f32[256,128]{1,0:T(8,128)S(1)} %get-tuple-element.21), channel_id=1, source_target_pairs={{0,1},{1,0},{2,3},{3,2},{4,5},{5,4},{6,7},{7,6},{8,9},{9,8},{10,11... | collective-permute-start | bytes 393224 | tf_op jit(solution)/shard_map/ppermute | solution.py:163
  17.5 7.8 %collective-permute-start.3 = (f32[256,128]{1,0:T(8,128)S(1)}, f32[256,128]{1,0:T(8,128)S(1)}, u32[]{:S(2)}, u32[]{:S(2)}) collective-permute-start(f32[256,128]{1,0:T(8,128)S(1)} %add.24), channel_id=1, source_target_pairs={{2,0},{3,1},{0,2},{1,3},{6,4},{7,5},{4,6},{5,7},{10,8},{11,9},{8,1... | collective-permute-start | bytes 393224 | tf_op jit(solution)/shard_map/ppermute | solution.py:169
  25.3 9.9 %collective-permute-start.8 = (f32[256,128]{1,0:T(8,128)S(1)}, f32[256,128]{1,0:T(8,128)S(1)}, u32[]{:S(2)}, u32[]{:S(2)}) collective-permute-start(f32[256,128]{1,0:T(8,128)S(1)} %fusion), channel_id=1, source_target_pairs={{3,0},{0,5},{2,10},{1,15},{7,4},{4,9},{6,14},{5,3},{11,8},{8,13},{... | collective-permute-start | bytes 393224 | tf_op jit(solution)/shard_map/ppermute | solution.py:153
  25.4 9.8 %collective-permute-start.7 = (f32[256,128]{1,0:T(8,128)S(1)}, f32[256,128]{1,0:T(8,128)S(1)}, u32[]{:S(2)}, u32[]{:S(2)}) collective-permute-start(f32[256,128]{1,0:T(8,128)S(1)} %fusion), channel_id=1, source_target_pairs={{0,0},{3,5},{1,10},{2,15},{4,4},{7,9},{5,14},{6,3},{8,8},{11,13},{... | collective-permute-start | bytes 393224 | tf_op jit(solution)/shard_map/ppermute | solution.py:153
  26.1 9.3 %collective-permute-start.6 = (f32[256,128]{1,0:T(8,128)S(1)}, f32[256,128]{1,0:T(8,128)S(1)}, u32[]{:S(2)}, u32[]{:S(2)}) collective-permute-start(f32[256,128]{1,0:T(8,128)S(1)} %fusion), channel_id=1, source_target_pairs={{1,0},{2,5},{0,10},{3,15},{5,4},{6,9},{4,14},{7,3},{9,8},{10,13},{... | collective-permute-start | bytes 393224 | tf_op jit(solution)/shard_map/ppermute | solution.py:153
  31.5 7.3 %collective-permute-start.5 = (f32[256,128]{1,0:T(8,128)S(1)}, f32[256,128]{1,0:T(8,128)S(1)}, u32[]{:S(2)}, u32[]{:S(2)}) collective-permute-start(f32[256,128]{1,0:T(8,128)S(1)} %fusion), channel_id=1, source_target_pairs={{2,0},{1,5},{3,10},{0,15},{6,4},{5,9},{7,14},{4,3},{10,8},{9,13},{... | collective-permute-start | bytes 393224 | tf_op jit(solution)/shard_map/ppermute | solution.py:153
  39.6 3.0 %collective-permute-start.9 = (f32[256,128]{1,0:T(8,128)S(1)}, f32[256,128]{1,0:T(8,128)S(1)}, u32[]{:S(2)}, u32[]{:S(2)}) collective-permute-start(f32[256,128]{1,0:T(8,128)S(1)} %get-tuple-element.24), channel_id=1, source_target_pairs={{0,1},{1,0},{2,3},{3,2},{4,5},{5,4},{6,7},{7,6},{8,9},{9,8},{10,11... | collective-permute-start | bytes 393224 | tf_op jit(solution)/shard_map/ppermute | solution.py:163
  41.6 4.0 %collective-permute-start.11 = (f32[256,128]{1,0:T(8,128)S(1)}, f32[256,128]{1,0:T(8,128)S(1)}, u32[]{:S(2)}, u32[]{:S(2)}) collective-permute-start(f32[256,128]{1,0:T(8,128)S(1)} %get-tuple-element.26), channel_id=1, source_target_pairs={{0,1},{1,0},{2,3},{3,2},{4,5},{5,4},{6,7},{7,6},{8,9},{9,8},{10,11... | collective-permute-start | bytes 393224 | tf_op jit(solution)/shard_map/ppermute | solution.py:163
  42.6 7.0 %collective-permute-start.10 = (f32[256,128]{1,0:T(8,128)S(1)}, f32[256,128]{1,0:T(8,128)S(1)}, u32[]{:S(2)}, u32[]{:S(2)}) collective-permute-start(f32[256,128]{1,0:T(8,128)S(1)} %add.28), channel_id=1, source_target_pairs={{2,0},{3,1},{0,2},{1,3},{6,4},{7,5},{4,6},{5,7},{10,8},{11,9},{8,1... | collective-permute-start | bytes 393224 | tf_op jit(solution)/shard_map/ppermute | solution.py:169

commit v9 on v8

--- a/solution.py
+++ b/solution.py
@@ -20,7 +20,7 @@
 
 def source_team(team, turn, team_count):
     if team_count == 4:
-        return (3 * (team % 2)) ^ (team // 2) ^ (2, 1, 0, 3)[turn]
+        return (2 * (team % 2) + team // 2) ^ (2, 0, 1, 3)[turn]
     return (team + turn) % team_count
 
 
@@ -143,6 +143,21 @@
     )(*operands)
 
 
+def hold_kernel(value_ref, after_ref, out_ref):
+    del value_ref, after_ref, out_ref
+
+
+def hold(value, after):
+    return pl.pallas_call(
+        hold_kernel,
+        out_shape=jax.ShapeDtypeStruct(value.shape, value.dtype),
+        in_specs=[ANY, ANY],
+        out_specs=ANY,
+        input_output_aliases={0: 0},
+        compiler_params=pltpu.CompilerParams(vmem_limit_bytes=VMEM_LIMIT),
+    )(value, after)
+
+
 def fetch(value, source_team, arc_length):
     cycle, team_count = lax.axis_size("blk"), lax.axis_size("rep")
     pairs = []
@@ -171,12 +186,16 @@
 
 def team_sum(sums):
     columns = len(sums) // 2
-    total = None
-    for distance in [*range(1, columns), 0]:
-        at = (columns - distance) % columns
+    own, give = sums[0], sums[columns]
+    others = []
+    for distance in range(1, columns):
+        at = columns - distance
         share = sums[at] + from_mate(sums[columns + at])
-        share = from_column(share, distance) if distance else share
-        total = share if total is None else total + share
+        give = hold(give, share)
+        others.append(from_column(share, distance))
+    total = own + from_mate(give)
+    for other in others:
+        total = total + other
     return total
 
 
@@ -191,7 +210,8 @@
     pieces = [fetch(degrees, lambda team: spread[team], arc_length), panel]
     info = jnp.concatenate([slot_counts[0, 0][:, None], tile_rows[0, 0], tile_columns[0, 0]], axis=1)
     info = jnp.broadcast_to(info[:, :, None], (*info.shape, embeddings.shape[1]))
-    tiles, own, norm_scale = prepare(degrees, embeddings, tile_values[0, 0], info)
+    info = [info[at] for at in range(arc_length)]
+    tiles, own, norm_scale = prepare(degrees, embeddings, tile_values[0, 0], info[0])
 
     combined = own
     for layer in range(LAYERS):

time: 50.6 us -> 50.5 us (level)
  waiting for transfers between devices: 16.8 us -> 18.1 us
  starting transfers between devices: 26 us -> 24.8 us
    ppermute x6, starting transfers between devices: 16.1 us -> 13.3 us  [fetch(): return lax.ppermute(value, ('blk', 'rep'), pairs)]
    ppermute x4, starting transfers between devices: 2.94 us -> 4.44 us  [from_mate(): lax.ppermute(value, 'rep', [(team, team ^ 1) for team in range(team_count)])]
    ppermute x6, waiting for transfers between devices: 7.17 us -> 8.12 us  [fetch(): return lax.ppermute(value, ('blk', 'rep'), pairs)]
where the time goes in v9:
time: 50.5 us; the launch traced here: 50.3 us
  starting transfers between devices  24.8 us (49%)
  waiting for transfers between devices  18.1 us (36%)
  local copies, waits for them, and re-layouts  3.52 us (7%)
  Pallas kernels  2.32 us (5%)
  other arithmetic  0.85 us (2%)
  between operations  0.74 us (1%)
    ppermute x6, starting transfers between devices, fetch(): return lax.ppermute(value, ('blk', 'rep'), pairs)  13.3 us
    ppermute x6, waiting for transfers between devices, fetch(): return lax.ppermute(value, ('blk', 'rep'), pairs)  8.12 us
    ppermute x2, waiting for transfers between devices, from_column(): return lax.ppermute(value, 'rep', pairs)  8.01 us
    ppermute x2, starting transfers between devices, from_column(): return lax.ppermute(value, 'rep', pairs)  7.03 us
    ppermute x4, starting transfers between devices, from_mate(): lax.ppermute(value, 'rep', [(team, team ^ 1) for team in range(team_count)])  4.44 us
    unnamed x10, local copies, waits for them, and re-layouts  3.44 us
    ppermute x4, waiting for transfers between devices, from_mate(): lax.ppermute(value, 'rep', [(team, team ^ 1) for team in range(team_count)])  1.98 us
    pallas_call x2, Pallas kernels, arc_step(): pl.pallas_call(functools.partial(arc_kernel, team_count=team_count, piece...  1.74 us
  transfers between devices with their start and end apart: 12, of which 7 were waited for; matrix products, arithmetic and copies ran while one was open for 0% of the time, Pallas kernels for 1%

profile of v9, /device:TPU:0, one launch (start us, length us, event | category | flops | bytes accessed | tf_op | source)
XLA Modules:
  0.0 50.3 jit_solution(17941103081973568221)
XLA Ops:
  0.0 5.4 %collective-permute-start.1 = (f32[1024,128]{1,0:T(8,128)}, f32[1024,128]{1,0:T(8,128)S(1)}, u32[]{:S(2)}, u32[]{:S(2)}) collective-permute-start(f32[1024,128]{1,0:T(8,128)} %embeddings_ref.1), channel_id=1, source_target_pairs={{3,0},{1,5},{2,10},{0,15},{7,4},{5,9},{6,14},{4,3},{11,8},{9,13},{... | collective-permute-start | bytes 1572872 | tf_op jit(solution)/shard_map/ppermute | solution.py:168
  5.4 0.8 %collective-permute-start = (s32[8,128]{1,0:T(8,128)}, s32[8,128]{1,0:T(8,128)S(1)}, u32[]{:S(2)}, u32[]{:S(2)}) collective-permute-start(s32[8,128]{1,0:T(8,128)} %bitcast.12), channel_id=1, source_target_pairs={{3,0},{1,5},{2,10},{0,15},{7,4},{5,9},{6,14},{4,3},{11,8},{9,13},{... | collective-permute-start | bytes 12296 | tf_op jit(solution)/shard_map/ppermute | solution.py:168
  6.9 0.6 %copy-done.3 = s32[1,1,1,24]{3,2,1,0:T(1,128)S(1)} copy-done((s32[1,1,1,24]{3,2,1,0:T(1,128)S(1)}, s32[1,1,1,24]{3,2,1,0:T(1,128)}, u32[]{:S(2)}) %copy-start.3) | copy-done | bytes 120
  7.5 0.0 copy-done.4
  7.6 0.1 add_bitcast_fusion
  7.6 0.1 squeeze.19.after_ref.info_ref
  7.7 0.6 %copy-done.2 = s32[1024]{0:T(1024)S(1)} copy-done((s32[1024]{0:T(1024)S(1)}, s32[1024]{0:T(1024)}, u32[]{:S(2)}) %copy-start.2) | copy-done | bytes 4120
  8.3 1.1 %copy-done = bf16[1,1,1,24,128,128]{5,4,3,2,1,0:T(8,128)(2,1)S(1)} copy-done((bf16[1,1,1,24,128,128]{5,4,3,2,1,0:T(8,128)(2,1)S(1)}, bf16[1,1,1,24,128,128]{5,4,3,2,1,0:T(8,128)(2,1)}, u32[]{:S(2)}) %copy-start) | copy-done | bytes 786456
  9.5 1.0 %copy-done.1 = f32[1024,128]{1,0:T(8,128)S(1)} copy-done((f32[1024,128]{1,0:T(8,128)S(1)}, f32[1024,128]{1,0:T(8,128)}, u32[]{:S(2)}) %copy-start.1) | copy-done | bytes 524312
  10.5 0.6 %shard_map.64 = (bf16[1,24,128,128]{3,2,1,0:T(8,128)(2,1)S(1)}, f32[256,128]{1,0:T(8,128)S(1)}, f32[256,128]{1,0:T(8,128)S(1)}) custom-call(s32[8,128]{1,0:T(8,128)S(1)} %bitcast.13, f32[1024,128]{1,0:T(8,128)S(1)} %copy-done.1, bf16[1,24,128,128]{3,2,1,0:T(8,128)(2,1)S(1)} %bitcast.11, s32[49,128]{1,0:T(8,128)S(1)} %squeeze.19.after_ref.info_ref), custom_call_target="tpu_custom_call" | custom-call | flops 131072 | bytes 524288 | tf_op jit(solution)/shard_map/pallas_call | solution.py:56
  11.1 3.5 %collective-permute-done.refs_0_ = s32[8,128]{1,0:T(8,128)S(1)} collective-permute-done((s32[8,128]{1,0:T(8,128)}, s32[8,128]{1,0:T(8,128)S(1)}, u32[]{:S(2)}, u32[]{:S(2)}) %collective-permute-start) | collective-permute-done | bytes 4128 | tf_op jit(solution)/shard_map/ppermute | solution.py:168
  14.6 0.0 collective-permute-done.1.refs_1_
  14.6 1.0 %shard_map.65 = (f32[256,128]{1,0:T(8,128)S(1)}, f32[256,128]{1,0:T(8,128)S(1)}, f32[256,128]{1,0:T(8,128)S(1)}, f32[256,128]{1,0:T(8,128)S(1)}) custom-call(s32[49,128]{1,0:T(8,128)S(1)} %squeeze.19.after_ref.info_ref, bf16[24,128,128]{2,1,0:T(8,128)(2,1)S(1)} %bitcast.9, s32[8,128]{1,0:T(8,128)S(1)} %collective-permute-done.refs_0_, ...), custom_call_target="tpu_custom_call" | custom-call | flops 201326592 | bytes 1048576 | tf_op jit(solution)/shard_map/pallas_call | solution.py:124
  15.6 0.8 %collective-permute-start.2 = (f32[256,128]{1,0:T(8,128)S(1)}, f32[256,128]{1,0:T(8,128)S(1)}, u32[]{:S(2)}, u32[]{:S(2)}) collective-permute-start(f32[256,128]{1,0:T(8,128)S(1)} %get-tuple-element.21), channel_id=1, source_target_pairs={{0,1},{1,0},{2,3},{3,2},{4,5},{5,4},{6,7},{7,6},{8,9},{9,8},{10,11... | collective-permute-start | bytes 393224 | tf_op jit(solution)/shard_map/ppermute | solution.py:178
  16.4 1.0 %collective-permute-done.2 = f32[256,128]{1,0:T(8,128)S(1)} collective-permute-done((f32[256,128]{1,0:T(8,128)S(1)}, f32[256,128]{1,0:T(8,128)S(1)}, u32[]{:S(2)}, u32[]{:S(2)}) %collective-permute-start.2) | collective-permute-done | bytes 131104 | tf_op jit(solution)/shard_map/ppermute | solution.py:178
  17.4 0.4 collective-permute-start.3
  17.8 3.7 %collective-permute-start.4 = (f32[256,128]{1,0:T(8,128)S(1)}, f32[256,128]{1,0:T(8,128)S(1)}, u32[]{:S(2)}, u32[]{:S(2)}) collective-permute-start(f32[256,128]{1,0:T(8,128)S(1)} %add.24.after_ref), channel_id=1, source_target_pairs={{2,0},{3,1},{0,2},{1,3},{6,4},{7,5},{4,6},{5,7},{10,8},{11,9},{8,1... | collective-permute-start | bytes 393224 | tf_op jit(solution)/shard_map/ppermute | solution.py:184
  21.6 0.0 collective-permute-done.3
  21.6 4.0 %collective-permute-done.4 = f32[256,128]{1,0:T(8,128)S(1)} collective-permute-done((f32[256,128]{1,0:T(8,128)S(1)}, f32[256,128]{1,0:T(8,128)S(1)}, u32[]{:S(2)}, u32[]{:S(2)}) %collective-permute-start.4) | collective-permute-done | bytes 131104 | tf_op jit(solution)/shard_map/ppermute | solution.py:184
  25.6 3.9 %collective-permute-start.8 = (f32[256,128]{1,0:T(8,128)S(1)}, f32[256,128]{1,0:T(8,128)S(1)}, u32[]{:S(2)}, u32[]{:S(2)}) collective-permute-start(f32[256,128]{1,0:T(8,128)S(1)} %fusion), channel_id=1, source_target_pairs={{3,0},{1,5},{2,10},{0,15},{7,4},{5,9},{6,14},{4,3},{11,8},{9,13},{... | collective-permute-start | bytes 393224 | tf_op jit(solution)/shard_map/ppermute | solution.py:168
  29.5 0.3 collective-permute-start.7
  29.8 0.7 %collective-permute-start.6 = (f32[256,128]{1,0:T(8,128)S(1)}, f32[256,128]{1,0:T(8,128)S(1)}, u32[]{:S(2)}, u32[]{:S(2)}) collective-permute-start(f32[256,128]{1,0:T(8,128)S(1)} %fusion), channel_id=1, source_target_pairs={{0,0},{2,5},{1,10},{3,15},{4,4},{6,9},{5,14},{7,3},{8,8},{10,13},{... | collective-permute-start | bytes 393224 | tf_op jit(solution)/shard_map/ppermute | solution.py:168
  30.5 2.2 %collective-permute-start.5 = (f32[256,128]{1,0:T(8,128)S(1)}, f32[256,128]{1,0:T(8,128)S(1)}, u32[]{:S(2)}, u32[]{:S(2)}) collective-permute-start(f32[256,128]{1,0:T(8,128)S(1)} %fusion), channel_id=1, source_target_pairs={{2,0},{0,5},{3,10},{1,15},{6,4},{4,9},{7,14},{5,3},{10,8},{8,13},{... | collective-permute-start | bytes 393224 | tf_op jit(solution)/shard_map/ppermute | solution.py:168
  32.7 1.8 %collective-permute-done.7.refs_2_ = f32[256,128]{1,0:T(8,128)S(1)} collective-permute-done((f32[256,128]{1,0:T(8,128)S(1)}, f32[256,128]{1,0:T(8,128)S(1)}, u32[]{:S(2)}, u32[]{:S(2)}) %collective-permute-start.7) | collective-permute-done | bytes 131104 | tf_op jit(solution)/shard_map/ppermute | solution.py:168
  34.5 2.8 %collective-permute-done.5.refs_0_ = f32[256,128]{1,0:T(8,128)S(1)} collective-permute-done((f32[256,128]{1,0:T(8,128)S(1)}, f32[256,128]{1,0:T(8,128)S(1)}, u32[]{:S(2)}, u32[]{:S(2)}) %collective-permute-start.5) | collective-permute-done | bytes 131104 | tf_op jit(solution)/shard_map/ppermute | solution.py:168
  37.3 0.8 %shard_map.67 = (f32[256,128]{1,0:T(8,128)S(1)}, f32[256,128]{1,0:T(8,128)S(1)}, f32[256,128]{1,0:T(8,128)S(1)}, f32[256,128]{1,0:T(8,128)S(1)}) custom-call(s32[49,128]{1,0:T(8,128)S(1)} %squeeze.19.after_ref.info_ref, bf16[24,128,128]{2,1,0:T(8,128)(2,1)S(1)} %bitcast.10, f32[256,128]{1,0:T(8,128)S(1)} %collective-permute-done.5.refs_0_, ...), custom_call_target="tpu_custom_call" | custom-call | flops 201326592 | bytes 1048576 | tf_op jit(solution)/shard_map/pallas_call | solution.py:124
  38.1 2.8 %collective-permute-start.9 = (f32[256,128]{1,0:T(8,128)S(1)}, f32[256,128]{1,0:T(8,128)S(1)}, u32[]{:S(2)}, u32[]{:S(2)}) collective-permute-start(f32[256,128]{1,0:T(8,128)S(1)} %get-tuple-element.26), channel_id=1, source_target_pairs={{0,1},{1,0},{2,3},{3,2},{4,5},{5,4},{6,7},{7,6},{8,9},{9,8},{10,11... | collective-permute-start | bytes 393224 | tf_op jit(solution)/shard_map/ppermute | solution.py:178
  40.8 1.0 %collective-permute-done.9 = f32[256,128]{1,0:T(8,128)S(1)} collective-permute-done((f32[256,128]{1,0:T(8,128)S(1)}, f32[256,128]{1,0:T(8,128)S(1)}, u32[]{:S(2)}, u32[]{:S(2)}) %collective-permute-start.9) | collective-permute-done | bytes 131104 | tf_op jit(solution)/shard_map/ppermute | solution.py:178
  41.9 0.4 collective-permute-start.10
  42.3 3.3 %collective-permute-start.11 = (f32[256,128]{1,0:T(8,128)S(1)}, f32[256,128]{1,0:T(8,128)S(1)}, u32[]{:S(2)}, u32[]{:S(2)}) collective-permute-start(f32[256,128]{1,0:T(8,128)S(1)} %add.28.after_ref), channel_id=1, source_target_pairs={{2,0},{3,1},{0,2},{1,3},{6,4},{7,5},{4,6},{5,7},{10,8},{11,9},{8,1... | collective-permute-start | bytes 393224 | tf_op jit(solution)/shard_map/ppermute | solution.py:184
  45.6 4.0 %collective-permute-done.11 = f32[256,128]{1,0:T(8,128)S(1)} collective-permute-done((f32[256,128]{1,0:T(8,128)S(1)}, f32[256,128]{1,0:T(8,128)S(1)}, u32[]{:S(2)}, u32[]{:S(2)}) %collective-permute-start.11) | collective-permute-done | bytes 131104 | tf_op jit(solution)/shard_map/ppermute | solution.py:184
  49.6 0.7 %add_multiply_fusion = f32[256,128]{1,0:T(8,128)} fusion(f32[256,128]{1,0:T(8,128)S(1)} %get-tuple-element.22, f32[256,128]{1,0:T(8,128)S(1)} %collective-permute-done.11, f32[256,128]{1,0:T(8,128)S(1)} %get-tuple-element.23, f32[256,128]{1,0:T(8,128)S(1)} %collective-permute-done.10, f32[256,128]{1,0:T(8,128)S(1)} %get-tuple-element.16, ...), kind=kLoop, calls=%fused_computation | loop fusion | flops 294912 | bytes 1179648 | tf_op jit(solution)/shard_map/div | solution.py:231
  (13 shorter events, 0.1 us)
Async XLA Ops:
  0.0 14.6 %collective-permute-start.1 = (f32[1024,128]{1,0:T(8,128)}, f32[1024,128]{1,0:T(8,128)S(1)}, u32[]{:S(2)}, u32[]{:S(2)}) collective-permute-start(f32[1024,128]{1,0:T(8,128)} %embeddings_ref.1), channel_id=1, source_target_pairs={{3,0},{1,5},{2,10},{0,15},{7,4},{5,9},{6,14},{4,3},{11,8},{9,13},{... | collective-permute-start | bytes 1572872 | tf_op jit(solution)/shard_map/ppermute | solution.py:168
  5.4 9.2 %collective-permute-start = (s32[8,128]{1,0:T(8,128)}, s32[8,128]{1,0:T(8,128)S(1)}, u32[]{:S(2)}, u32[]{:S(2)}) collective-permute-start(s32[8,128]{1,0:T(8,128)} %bitcast.12), channel_id=1, source_target_pairs={{3,0},{1,5},{2,10},{0,15},{7,4},{5,9},{6,14},{4,3},{11,8},{9,13},{... | collective-permute-start | bytes 12296 | tf_op jit(solution)/shard_map/ppermute | solution.py:168
  6.9 0.7 %copy-start.3 = (s32[1,1,1,24]{3,2,1,0:T(1,128)S(1)}, s32[1,1,1,24]{3,2,1,0:T(1,128)}, u32[]{:S(2)}) copy-start(s32[1,1,1,24]{3,2,1,0:T(1,128)} %param.10) | copy-start | bytes 292
  6.9 0.7 %copy-start.4 = (s32[1,1,1,24]{3,2,1,0:T(1,128)S(1)}, s32[1,1,1,24]{3,2,1,0:T(1,128)}, u32[]{:S(2)}) copy-start(s32[1,1,1,24]{3,2,1,0:T(1,128)} %param.9) | copy-start | bytes 292
  7.6 0.7 %copy-start.2 = (s32[1024]{0:T(1024)S(1)}, s32[1024]{0:T(1024)}, u32[]{:S(2)}) copy-start(s32[1024]{0:T(1024)} %param.7) | copy-start | bytes 12292
  8.3 1.1 %copy-start = (bf16[1,1,1,24,128,128]{5,4,3,2,1,0:T(8,128)(2,1)S(1)}, bf16[1,1,1,24,128,128]{5,4,3,2,1,0:T(8,128)(2,1)}, u32[]{:S(2)}) copy-start(bf16[1,1,1,24,128,128]{5,4,3,2,1,0:T(8,128)(2,1)} %param.8) | copy-start | bytes 2359300
  9.5 1.0 %copy-start.1 = (f32[1024,128]{1,0:T(8,128)S(1)}, f32[1024,128]{1,0:T(8,128)}, u32[]{:S(2)}) copy-start(f32[1024,128]{1,0:T(8,128)} %embeddings_ref.1) | copy-start | bytes 1572868
  15.6 1.8 %collective-permute-start.2 = (f32[256,128]{1,0:T(8,128)S(1)}, f32[256,128]{1,0:T(8,128)S(1)}, u32[]{:S(2)}, u32[]{:S(2)}) collective-permute-start(f32[256,128]{1,0:T(8,128)S(1)} %get-tuple-element.21), channel_id=1, source_target_pairs={{0,1},{1,0},{2,3},{3,2},{4,5},{5,4},{6,7},{7,6},{8,9},{9,8},{10,11... | collective-permute-start | bytes 393224 | tf_op jit(solution)/shard_map/ppermute | solution.py:178
  17.4 4.2 %collective-permute-start.3 = (f32[256,128]{1,0:T(8,128)S(1)}, f32[256,128]{1,0:T(8,128)S(1)}, u32[]{:S(2)}, u32[]{:S(2)}) collective-permute-start(f32[256,128]{1,0:T(8,128)S(1)} %shard_map.66), channel_id=1, source_target_pairs={{0,1},{1,0},{2,3},{3,2},{4,5},{5,4},{6,7},{7,6},{8,9},{9,8},{10,11... | collective-permute-start | bytes 393224 | tf_op jit(solution)/shard_map/ppermute | solution.py:178
  17.8 7.8 %collective-permute-start.4 = (f32[256,128]{1,0:T(8,128)S(1)}, f32[256,128]{1,0:T(8,128)S(1)}, u32[]{:S(2)}, u32[]{:S(2)}) collective-permute-start(f32[256,128]{1,0:T(8,128)S(1)} %add.24.after_ref), channel_id=1, source_target_pairs={{2,0},{3,1},{0,2},{1,3},{6,4},{7,5},{4,6},{5,7},{10,8},{11,9},{8,1... | collective-permute-start | bytes 393224 | tf_op jit(solution)/shard_map/ppermute | solution.py:184
  25.6 7.1 %collective-permute-start.8 = (f32[256,128]{1,0:T(8,128)S(1)}, f32[256,128]{1,0:T(8,128)S(1)}, u32[]{:S(2)}, u32[]{:S(2)}) collective-permute-start(f32[256,128]{1,0:T(8,128)S(1)} %fusion), channel_id=1, source_target_pairs={{3,0},{1,5},{2,10},{0,15},{7,4},{5,9},{6,14},{4,3},{11,8},{9,13},{... | collective-permute-start | bytes 393224 | tf_op jit(solution)/shard_map/ppermute | solution.py:168
  29.5 5.0 %collective-permute-start.7 = (f32[256,128]{1,0:T(8,128)S(1)}, f32[256,128]{1,0:T(8,128)S(1)}, u32[]{:S(2)}, u32[]{:S(2)}) collective-permute-start(f32[256,128]{1,0:T(8,128)S(1)} %fusion), channel_id=1, source_target_pairs={{1,0},{3,5},{0,10},{2,15},{5,4},{7,9},{4,14},{6,3},{9,8},{11,13},{... | collective-permute-start | bytes 393224 | tf_op jit(solution)/shard_map/ppermute | solution.py:168
  29.8 4.7 %collective-permute-start.6 = (f32[256,128]{1,0:T(8,128)S(1)}, f32[256,128]{1,0:T(8,128)S(1)}, u32[]{:S(2)}, u32[]{:S(2)}) collective-permute-start(f32[256,128]{1,0:T(8,128)S(1)} %fusion), channel_id=1, source_target_pairs={{0,0},{2,5},{1,10},{3,15},{4,4},{6,9},{5,14},{7,3},{8,8},{10,13},{... | collective-permute-start | bytes 393224 | tf_op jit(solution)/shard_map/ppermute | solution.py:168
  30.5 6.8 %collective-permute-start.5 = (f32[256,128]{1,0:T(8,128)S(1)}, f32[256,128]{1,0:T(8,128)S(1)}, u32[]{:S(2)}, u32[]{:S(2)}) collective-permute-start(f32[256,128]{1,0:T(8,128)S(1)} %fusion), channel_id=1, source_target_pairs={{2,0},{0,5},{3,10},{1,15},{6,4},{4,9},{7,14},{5,3},{10,8},{8,13},{... | collective-permute-start | bytes 393224 | tf_op jit(solution)/shard_map/ppermute | solution.py:168
  38.1 3.8 %collective-permute-start.9 = (f32[256,128]{1,0:T(8,128)S(1)}, f32[256,128]{1,0:T(8,128)S(1)}, u32[]{:S(2)}, u32[]{:S(2)}) collective-permute-start(f32[256,128]{1,0:T(8,128)S(1)} %get-tuple-element.26), channel_id=1, source_target_pairs={{0,1},{1,0},{2,3},{3,2},{4,5},{5,4},{6,7},{7,6},{8,9},{9,8},{10,11... | collective-permute-start | bytes 393224 | tf_op jit(solution)/shard_map/ppermute | solution.py:178
  41.9 3.7 %collective-permute-start.10 = (f32[256,128]{1,0:T(8,128)S(1)}, f32[256,128]{1,0:T(8,128)S(1)}, u32[]{:S(2)}, u32[]{:S(2)}) collective-permute-start(f32[256,128]{1,0:T(8,128)S(1)} %shard_map.68), channel_id=1, source_target_pairs={{0,1},{1,0},{2,3},{3,2},{4,5},{5,4},{6,7},{7,6},{8,9},{9,8},{10,11... | collective-permute-start | bytes 393224 | tf_op jit(solution)/shard_map/ppermute | solution.py:178
  42.3 7.3 %collective-permute-start.11 = (f32[256,128]{1,0:T(8,128)S(1)}, f32[256,128]{1,0:T(8,128)S(1)}, u32[]{:S(2)}, u32[]{:S(2)}) collective-permute-start(f32[256,128]{1,0:T(8,128)S(1)} %add.28.after_ref), channel_id=1, source_target_pairs={{2,0},{3,1},{0,2},{1,3},{6,4},{7,5},{4,6},{5,7},{10,8},{11,9},{8,1... | collective-permute-start | bytes 393224 | tf_op jit(solution)/shard_map/ppermute | solution.py:184

commit v10 on v6

--- a/solution.py
+++ b/solution.py
@@ -20,7 +20,7 @@
 
 def source_team(team, turn, team_count):
     if team_count == 4:
-        return (2 * (team % 2) + team // 2) ^ (0, 2, 1, 3)[turn]
+        return (2 * (team % 2) + team // 2) ^ (0, 2, 3, 1)[turn]
     return (team + turn) % team_count
 
 

time: 49 us -> 50.1 us (1.022)
  starting transfers between devices: 21.3 us -> 24.8 us
  waiting for transfers between devices: 20.6 us -> 18.3 us
    ppermute x4, starting transfers between devices: 3.54 us -> 6.73 us  [from_mate(): lax.ppermute(value, 'rep', [(team, team ^ 1) for team in range(team_count)])]
    ppermute x6, waiting for transfers between devices: 11.2 us -> 8.84 us  [fetch(): return lax.ppermute(value, ('blk', 'rep'), pairs)]
    ppermute x2, starting transfers between devices: 6.71 us -> 7.38 us  [from_column(): return lax.ppermute(value, 'rep', pairs)]
  transfers between devices with their start and end apart: 12 -> 12, of which waited for: 8 -> 7; matrix products, arithmetic and copies ran while one was open for 0% -> 0% of each run, Pallas kernels for 1% -> 1%
where the time goes in v10:
time: 50.1 us; the launch traced here: 49.9 us
  starting transfers between devices  24.8 us (50%)
  waiting for transfers between devices  18.3 us (37%)
  local copies, waits for them, and re-layouts  2.9 us (6%)
  Pallas kernels  2.33 us (5%)
  other arithmetic  0.88 us (2%)
  between operations  0.74 us (1%)
    ppermute x6, starting transfers between devices, fetch(): return lax.ppermute(value, ('blk', 'rep'), pairs)  10.6 us
    ppermute x6, waiting for transfers between devices, fetch(): return lax.ppermute(value, ('blk', 'rep'), pairs)  8.84 us
    ppermute x2, waiting for transfers between devices, from_column(): return lax.ppermute(value, 'rep', pairs)  7.61 us
    ppermute x2, starting transfers between devices, from_column(): return lax.ppermute(value, 'rep', pairs)  7.38 us
    ppermute x4, starting transfers between devices, from_mate(): lax.ppermute(value, 'rep', [(team, team ^ 1) for team in range(team_count)])  6.73 us
    unnamed x10, local copies, waits for them, and re-layouts  2.83 us
    ppermute x4, waiting for transfers between devices, from_mate(): lax.ppermute(value, 'rep', [(team, team ^ 1) for team in range(team_count)])  1.82 us
    pallas_call x2, Pallas kernels, arc_step(): pl.pallas_call(functools.partial(arc_kernel, team_count=team_count, piece...  1.76 us
  transfers between devices with their start and end apart: 12, of which 7 were waited for; matrix products, arithmetic and copies ran while one was open for 0% of the time, Pallas kernels for 1%

profile of v10, /device:TPU:0, one launch (start us, length us, event | category | flops | bytes accessed | tf_op | source)
XLA Modules:
  0.0 49.9 jit_solution(11497488791523276419)
XLA Ops:
  0.0 5.4 %collective-permute-start.1 = (f32[1024,128]{1,0:T(8,128)}, f32[1024,128]{1,0:T(8,128)S(1)}, u32[]{:S(2)}, u32[]{:S(2)}) collective-permute-start(f32[1024,128]{1,0:T(8,128)} %embeddings_ref.1), channel_id=1, source_target_pairs={{3,0},{1,5},{2,10},{0,15},{7,4},{5,9},{6,14},{4,3},{11,8},{9,13},{... | collective-permute-start | bytes 1572872 | tf_op jit(solution)/shard_map/ppermute | solution.py:150
  5.4 0.8 %collective-permute-start = (s32[8,128]{1,0:T(8,128)}, s32[8,128]{1,0:T(8,128)S(1)}, u32[]{:S(2)}, u32[]{:S(2)}) collective-permute-start(s32[8,128]{1,0:T(8,128)} %bitcast.12), channel_id=1, source_target_pairs={{3,0},{1,5},{2,10},{0,15},{7,4},{5,9},{6,14},{4,3},{11,8},{9,13},{... | collective-permute-start | bytes 12296 | tf_op jit(solution)/shard_map/ppermute | solution.py:150
  6.9 0.6 %copy-done.3 = s32[1,1,1,24]{3,2,1,0:T(1,128)S(1)} copy-done((s32[1,1,1,24]{3,2,1,0:T(1,128)S(1)}, s32[1,1,1,24]{3,2,1,0:T(1,128)}, u32[]{:S(2)}) %copy-start.3) | copy-done | bytes 120
  7.5 0.0 copy-done.4
  7.6 0.1 add_bitcast_fusion
  7.6 1.1 %copy-done = bf16[1,1,1,24,128,128]{5,4,3,2,1,0:T(8,128)(2,1)S(1)} copy-done((bf16[1,1,1,24,128,128]{5,4,3,2,1,0:T(8,128)(2,1)S(1)}, bf16[1,1,1,24,128,128]{5,4,3,2,1,0:T(8,128)(2,1)}, u32[]{:S(2)}) %copy-start) | copy-done | bytes 786456
  8.8 1.0 %copy-done.1 = f32[1024,128]{1,0:T(8,128)S(1)} copy-done((f32[1024,128]{1,0:T(8,128)S(1)}, f32[1024,128]{1,0:T(8,128)}, u32[]{:S(2)}) %copy-start.1) | copy-done | bytes 524312
  9.8 0.6 %shard_map.64 = (bf16[1,24,128,128]{3,2,1,0:T(8,128)(2,1)S(1)}, f32[256,128]{1,0:T(8,128)S(1)}, f32[256,128]{1,0:T(8,128)S(1)}) custom-call(s32[8,128]{1,0:T(8,128)S(1)} %bitcast.13, f32[1024,128]{1,0:T(8,128)S(1)} %copy-done.1, bf16[1,24,128,128]{3,2,1,0:T(8,128)(2,1)S(1)} %bitcast.11), custom_call_target="tpu_custom_call" | custom-call | flops 131072 | bytes 524288 | tf_op jit(solution)/shard_map/pallas_call | solution.py:53
  10.4 4.2 %collective-permute-done.refs_0_ = s32[8,128]{1,0:T(8,128)S(1)} collective-permute-done((s32[8,128]{1,0:T(8,128)}, s32[8,128]{1,0:T(8,128)S(1)}, u32[]{:S(2)}, u32[]{:S(2)}) %collective-permute-start) | collective-permute-done | bytes 4128 | tf_op jit(solution)/shard_map/ppermute | solution.py:150
  14.6 0.0 collective-permute-done.1.refs_1_
  14.6 0.1 squeeze.20.info_ref
  14.7 1.0 %shard_map.65 = (f32[256,128]{1,0:T(8,128)S(1)}, f32[256,128]{1,0:T(8,128)S(1)}, f32[256,128]{1,0:T(8,128)S(1)}, f32[256,128]{1,0:T(8,128)S(1)}) custom-call(s32[49,128]{1,0:T(8,128)S(1)} %squeeze.20.info_ref, bf16[24,128,128]{2,1,0:T(8,128)(2,1)S(1)} %bitcast.9, s32[8,128]{1,0:T(8,128)S(1)} %collective-permute-done.refs_0_, ...), custom_call_target="tpu_custom_call" | custom-call | flops 201326592 | bytes 1048576 | tf_op jit(solution)/shard_map/pallas_call | solution.py:121
  15.7 0.8 %collective-permute-start.2 = (f32[256,128]{1,0:T(8,128)S(1)}, f32[256,128]{1,0:T(8,128)S(1)}, u32[]{:S(2)}, u32[]{:S(2)}) collective-permute-start(f32[256,128]{1,0:T(8,128)S(1)} %get-tuple-element.19), channel_id=1, source_target_pairs={{0,1},{1,0},{2,3},{3,2},{4,5},{5,4},{6,7},{7,6},{8,9},{9,8},{10,11... | collective-permute-start | bytes 393224 | tf_op jit(solution)/shard_map/ppermute | solution.py:160
  16.5 0.1 collective-permute-start.4
  16.6 0.9 %collective-permute-done.2 = f32[256,128]{1,0:T(8,128)S(1)} collective-permute-done((f32[256,128]{1,0:T(8,128)S(1)}, f32[256,128]{1,0:T(8,128)S(1)}, u32[]{:S(2)}, u32[]{:S(2)}) %collective-permute-start.2) | collective-permute-done | bytes 131104 | tf_op jit(solution)/shard_map/ppermute | solution.py:160
  17.5 4.0 %collective-permute-start.3 = (f32[256,128]{1,0:T(8,128)S(1)}, f32[256,128]{1,0:T(8,128)S(1)}, u32[]{:S(2)}, u32[]{:S(2)}) collective-permute-start(f32[256,128]{1,0:T(8,128)S(1)} %add.24), channel_id=1, source_target_pairs={{2,0},{3,1},{0,2},{1,3},{6,4},{7,5},{4,6},{5,7},{10,8},{11,9},{8,1... | collective-permute-start | bytes 393224 | tf_op jit(solution)/shard_map/ppermute | solution.py:166
  21.5 0.0 collective-permute-done.4
  21.5 3.8 %collective-permute-done.3 = f32[256,128]{1,0:T(8,128)S(1)} collective-permute-done((f32[256,128]{1,0:T(8,128)S(1)}, f32[256,128]{1,0:T(8,128)S(1)}, u32[]{:S(2)}, u32[]{:S(2)}) %collective-permute-start.3) | collective-permute-done | bytes 131104 | tf_op jit(solution)/shard_map/ppermute | solution.py:166
  25.4 1.3 %collective-permute-start.8 = (f32[256,128]{1,0:T(8,128)S(1)}, f32[256,128]{1,0:T(8,128)S(1)}, u32[]{:S(2)}, u32[]{:S(2)}) collective-permute-start(f32[256,128]{1,0:T(8,128)S(1)} %fusion), channel_id=1, source_target_pairs={{1,0},{3,5},{0,10},{2,15},{5,4},{7,9},{4,14},{6,3},{9,8},{11,13},{... | collective-permute-start | bytes 393224 | tf_op jit(solution)/shard_map/ppermute | solution.py:150
  26.6 2.5 %collective-permute-start.7 = (f32[256,128]{1,0:T(8,128)S(1)}, f32[256,128]{1,0:T(8,128)S(1)}, u32[]{:S(2)}, u32[]{:S(2)}) collective-permute-start(f32[256,128]{1,0:T(8,128)S(1)} %fusion), channel_id=1, source_target_pairs={{3,0},{1,5},{2,10},{0,15},{7,4},{5,9},{6,14},{4,3},{11,8},{9,13},{... | collective-permute-start | bytes 393224 | tf_op jit(solution)/shard_map/ppermute | solution.py:150
  29.1 0.7 %collective-permute-start.5 = (f32[256,128]{1,0:T(8,128)S(1)}, f32[256,128]{1,0:T(8,128)S(1)}, u32[]{:S(2)}, u32[]{:S(2)}) collective-permute-start(f32[256,128]{1,0:T(8,128)S(1)} %fusion), channel_id=1, source_target_pairs={{0,0},{2,5},{1,10},{3,15},{4,4},{6,9},{5,14},{7,3},{8,8},{10,13},{... | collective-permute-start | bytes 393224 | tf_op jit(solution)/shard_map/ppermute | solution.py:150
  29.8 2.6 %collective-permute-done.7.refs_2_ = f32[256,128]{1,0:T(8,128)S(1)} collective-permute-done((f32[256,128]{1,0:T(8,128)S(1)}, f32[256,128]{1,0:T(8,128)S(1)}, u32[]{:S(2)}, u32[]{:S(2)}) %collective-permute-start.7) | collective-permute-done | bytes 131104 | tf_op jit(solution)/shard_map/ppermute | solution.py:150
  32.4 2.0 %collective-permute-done.6.refs_1_ = f32[256,128]{1,0:T(8,128)S(1)} collective-permute-done((f32[256,128]{1,0:T(8,128)S(1)}, f32[256,128]{1,0:T(8,128)S(1)}, u32[]{:S(2)}, u32[]{:S(2)}) %collective-permute-start.6) | collective-permute-done | bytes 131104 | tf_op jit(solution)/shard_map/ppermute | solution.py:150
  34.4 0.0 collective-permute-done.5.refs_0_
  34.4 0.8 %shard_map.66 = (f32[256,128]{1,0:T(8,128)S(1)}, f32[256,128]{1,0:T(8,128)S(1)}, f32[256,128]{1,0:T(8,128)S(1)}, f32[256,128]{1,0:T(8,128)S(1)}) custom-call(s32[49,128]{1,0:T(8,128)S(1)} %squeeze.20.info_ref, bf16[24,128,128]{2,1,0:T(8,128)(2,1)S(1)} %bitcast.10, f32[256,128]{1,0:T(8,128)S(1)} %collective-permute-done.5.refs_0_, ...), custom_call_target="tpu_custom_call" | custom-call | flops 201326592 | bytes 1048576 | tf_op jit(solution)/shard_map/pallas_call | solution.py:121
  35.2 5.8 %collective-permute-start.9 = (f32[256,128]{1,0:T(8,128)S(1)}, f32[256,128]{1,0:T(8,128)S(1)}, u32[]{:S(2)}, u32[]{:S(2)}) collective-permute-start(f32[256,128]{1,0:T(8,128)S(1)} %get-tuple-element.24), channel_id=1, source_target_pairs={{0,1},{1,0},{2,3},{3,2},{4,5},{5,4},{6,7},{7,6},{8,9},{9,8},{10,11... | collective-permute-start | bytes 393224 | tf_op jit(solution)/shard_map/ppermute | solution.py:160
  41.0 0.1 collective-permute-start.11
  41.0 0.9 %collective-permute-done.9 = f32[256,128]{1,0:T(8,128)S(1)} collective-permute-done((f32[256,128]{1,0:T(8,128)S(1)}, f32[256,128]{1,0:T(8,128)S(1)}, u32[]{:S(2)}, u32[]{:S(2)}) %collective-permute-start.9) | collective-permute-done | bytes 131104 | tf_op jit(solution)/shard_map/ppermute | solution.py:160
  42.0 3.4 %collective-permute-start.10 = (f32[256,128]{1,0:T(8,128)S(1)}, f32[256,128]{1,0:T(8,128)S(1)}, u32[]{:S(2)}, u32[]{:S(2)}) collective-permute-start(f32[256,128]{1,0:T(8,128)S(1)} %add.28), channel_id=1, source_target_pairs={{2,0},{3,1},{0,2},{1,3},{6,4},{7,5},{4,6},{5,7},{10,8},{11,9},{8,1... | collective-permute-start | bytes 393224 | tf_op jit(solution)/shard_map/ppermute | solution.py:166
  45.3 0.0 collective-permute-done.11
  45.3 3.8 %collective-permute-done.10 = f32[256,128]{1,0:T(8,128)S(1)} collective-permute-done((f32[256,128]{1,0:T(8,128)S(1)}, f32[256,128]{1,0:T(8,128)S(1)}, u32[]{:S(2)}, u32[]{:S(2)}) %collective-permute-start.10) | collective-permute-done | bytes 131104 | tf_op jit(solution)/shard_map/ppermute | solution.py:166
  49.1 0.7 %add_multiply_fusion = f32[256,128]{1,0:T(8,128)} fusion(f32[256,128]{1,0:T(8,128)S(1)} %get-tuple-element.22, f32[256,128]{1,0:T(8,128)S(1)} %collective-permute-done.10, f32[256,128]{1,0:T(8,128)S(1)} %get-tuple-element.25, f32[256,128]{1,0:T(8,128)S(1)} %collective-permute-done.11, f32[256,128]{1,0:T(8,128)S(1)} %get-tuple-element.16, ...), kind=kLoop, calls=%fused_computation | loop fusion | flops 294912 | bytes 1179648 | tf_op jit(solution)/shard_map/div | solution.py:208
  (11 shorter events, 0.1 us)
Async XLA Ops:
  0.0 14.6 %collective-permute-start.1 = (f32[1024,128]{1,0:T(8,128)}, f32[1024,128]{1,0:T(8,128)S(1)}, u32[]{:S(2)}, u32[]{:S(2)}) collective-permute-start(f32[1024,128]{1,0:T(8,128)} %embeddings_ref.1), channel_id=1, source_target_pairs={{3,0},{1,5},{2,10},{0,15},{7,4},{5,9},{6,14},{4,3},{11,8},{9,13},{... | collective-permute-start | bytes 1572872 | tf_op jit(solution)/shard_map/ppermute | solution.py:150
  5.4 9.2 %collective-permute-start = (s32[8,128]{1,0:T(8,128)}, s32[8,128]{1,0:T(8,128)S(1)}, u32[]{:S(2)}, u32[]{:S(2)}) collective-permute-start(s32[8,128]{1,0:T(8,128)} %bitcast.12), channel_id=1, source_target_pairs={{3,0},{1,5},{2,10},{0,15},{7,4},{5,9},{6,14},{4,3},{11,8},{9,13},{... | collective-permute-start | bytes 12296 | tf_op jit(solution)/shard_map/ppermute | solution.py:150
  6.9 0.7 %copy-start.3 = (s32[1,1,1,24]{3,2,1,0:T(1,128)S(1)}, s32[1,1,1,24]{3,2,1,0:T(1,128)}, u32[]{:S(2)}) copy-start(s32[1,1,1,24]{3,2,1,0:T(1,128)} %param.10) | copy-start | bytes 292
  6.9 0.7 %copy-start.4 = (s32[1,1,1,24]{3,2,1,0:T(1,128)S(1)}, s32[1,1,1,24]{3,2,1,0:T(1,128)}, u32[]{:S(2)}) copy-start(s32[1,1,1,24]{3,2,1,0:T(1,128)} %param.9) | copy-start | bytes 292
  6.9 0.7 %copy-start.2 = (s32[1024]{0:T(1024)S(1)}, s32[1024]{0:T(1024)}, u32[]{:S(2)}) copy-start(s32[1024]{0:T(1024)} %param.7) | copy-start | bytes 12292
  7.6 1.1 %copy-start = (bf16[1,1,1,24,128,128]{5,4,3,2,1,0:T(8,128)(2,1)S(1)}, bf16[1,1,1,24,128,128]{5,4,3,2,1,0:T(8,128)(2,1)}, u32[]{:S(2)}) copy-start(bf16[1,1,1,24,128,128]{5,4,3,2,1,0:T(8,128)(2,1)} %param.8) | copy-start | bytes 2359300
  8.8 1.0 %copy-start.1 = (f32[1024,128]{1,0:T(8,128)S(1)}, f32[1024,128]{1,0:T(8,128)}, u32[]{:S(2)}) copy-start(f32[1024,128]{1,0:T(8,128)} %embeddings_ref.1) | copy-start | bytes 1572868
  15.7 1.8 %collective-permute-start.2 = (f32[256,128]{1,0:T(8,128)S(1)}, f32[256,128]{1,0:T(8,128)S(1)}, u32[]{:S(2)}, u32[]{:S(2)}) collective-permute-start(f32[256,128]{1,0:T(8,128)S(1)} %get-tuple-element.19), channel_id=1, source_target_pairs={{0,1},{1,0},{2,3},{3,2},{4,5},{5,4},{6,7},{7,6},{8,9},{9,8},{10,11... | collective-permute-start | bytes 393224 | tf_op jit(solution)/shard_map/ppermute | solution.py:160
  16.5 5.0 %collective-permute-start.4 = (f32[256,128]{1,0:T(8,128)S(1)}, f32[256,128]{1,0:T(8,128)S(1)}, u32[]{:S(2)}, u32[]{:S(2)}) collective-permute-start(f32[256,128]{1,0:T(8,128)S(1)} %get-tuple-element.21), channel_id=1, source_target_pairs={{0,1},{1,0},{2,3},{3,2},{4,5},{5,4},{6,7},{7,6},{8,9},{9,8},{10,11... | collective-permute-start | bytes 393224 | tf_op jit(solution)/shard_map/ppermute | solution.py:160
  17.5 7.8 %collective-permute-start.3 = (f32[256,128]{1,0:T(8,128)S(1)}, f32[256,128]{1,0:T(8,128)S(1)}, u32[]{:S(2)}, u32[]{:S(2)}) collective-permute-start(f32[256,128]{1,0:T(8,128)S(1)} %add.24), channel_id=1, source_target_pairs={{2,0},{3,1},{0,2},{1,3},{6,4},{7,5},{4,6},{5,7},{10,8},{11,9},{8,1... | collective-permute-start | bytes 393224 | tf_op jit(solution)/shard_map/ppermute | solution.py:166
  25.4 4.4 %collective-permute-start.8 = (f32[256,128]{1,0:T(8,128)S(1)}, f32[256,128]{1,0:T(8,128)S(1)}, u32[]{:S(2)}, u32[]{:S(2)}) collective-permute-start(f32[256,128]{1,0:T(8,128)S(1)} %fusion), channel_id=1, source_target_pairs={{1,0},{3,5},{0,10},{2,15},{5,4},{7,9},{4,14},{6,3},{9,8},{11,13},{... | collective-permute-start | bytes 393224 | tf_op jit(solution)/shard_map/ppermute | solution.py:150
  26.6 5.8 %collective-permute-start.7 = (f32[256,128]{1,0:T(8,128)S(1)}, f32[256,128]{1,0:T(8,128)S(1)}, u32[]{:S(2)}, u32[]{:S(2)}) collective-permute-start(f32[256,128]{1,0:T(8,128)S(1)} %fusion), channel_id=1, source_target_pairs={{3,0},{1,5},{2,10},{0,15},{7,4},{5,9},{6,14},{4,3},{11,8},{9,13},{... | collective-permute-start | bytes 393224 | tf_op jit(solution)/shard_map/ppermute | solution.py:150
  29.1 5.3 %collective-permute-start.6 = (f32[256,128]{1,0:T(8,128)S(1)}, f32[256,128]{1,0:T(8,128)S(1)}, u32[]{:S(2)}, u32[]{:S(2)}) collective-permute-start(f32[256,128]{1,0:T(8,128)S(1)} %fusion), channel_id=1, source_target_pairs={{2,0},{0,5},{3,10},{1,15},{6,4},{4,9},{7,14},{5,3},{10,8},{8,13},{... | collective-permute-start | bytes 393224 | tf_op jit(solution)/shard_map/ppermute | solution.py:150
  29.1 5.3 %collective-permute-start.5 = (f32[256,128]{1,0:T(8,128)S(1)}, f32[256,128]{1,0:T(8,128)S(1)}, u32[]{:S(2)}, u32[]{:S(2)}) collective-permute-start(f32[256,128]{1,0:T(8,128)S(1)} %fusion), channel_id=1, source_target_pairs={{0,0},{2,5},{1,10},{3,15},{4,4},{6,9},{5,14},{7,3},{8,8},{10,13},{... | collective-permute-start | bytes 393224 | tf_op jit(solution)/shard_map/ppermute | solution.py:150
  35.2 6.8 %collective-permute-start.9 = (f32[256,128]{1,0:T(8,128)S(1)}, f32[256,128]{1,0:T(8,128)S(1)}, u32[]{:S(2)}, u32[]{:S(2)}) collective-permute-start(f32[256,128]{1,0:T(8,128)S(1)} %get-tuple-element.24), channel_id=1, source_target_pairs={{0,1},{1,0},{2,3},{3,2},{4,5},{5,4},{6,7},{7,6},{8,9},{9,8},{10,11... | collective-permute-start | bytes 393224 | tf_op jit(solution)/shard_map/ppermute | solution.py:160
  41.0 4.4 %collective-permute-start.11 = (f32[256,128]{1,0:T(8,128)S(1)}, f32[256,128]{1,0:T(8,128)S(1)}, u32[]{:S(2)}, u32[]{:S(2)}) collective-permute-start(f32[256,128]{1,0:T(8,128)S(1)} %get-tuple-element.26), channel_id=1, source_target_pairs={{0,1},{1,0},{2,3},{3,2},{4,5},{5,4},{6,7},{7,6},{8,9},{9,8},{10,11... | collective-permute-start | bytes 393224 | tf_op jit(solution)/shard_map/ppermute | solution.py:160
  42.0 7.2 %collective-permute-start.10 = (f32[256,128]{1,0:T(8,128)S(1)}, f32[256,128]{1,0:T(8,128)S(1)}, u32[]{:S(2)}, u32[]{:S(2)}) collective-permute-start(f32[256,128]{1,0:T(8,128)S(1)} %add.28), channel_id=1, source_target_pairs={{2,0},{3,1},{0,2},{1,3},{6,4},{7,5},{4,6},{5,7},{10,8},{11,9},{8,1... | collective-permute-start | bytes 393224 | tf_op jit(solution)/shard_map/ppermute | solution.py:166

commit v11 on v10

--- a/solution.py
+++ b/solution.py
@@ -18,9 +18,11 @@
     return 2 * lax.rem(team_index // 2 + column, columns) + lax.rem(team_index, 2)
 
 
-def source_team(team, turn, team_count):
+def source_team(shard, team, turn, team_count):
     if team_count == 4:
-        return (2 * (team % 2) + team // 2) ^ (0, 2, 3, 1)[turn]
+        row, late_row = (0, 2, 1, 3)[turn], (2, 0, 1, 3)[turn]
+        swap = (shard == 2) * (row ^ late_row)
+        return (2 * (team % 2) + team // 2) ^ row ^ swap
     return (team + turn) % team_count
 
 
@@ -63,7 +65,7 @@
     )(degrees, embeddings, tile_values)
 
 
-def arc_kernel(info_ref, tiles_ref, *refs, team_count, piece_count, scaled, partial_count):
+def arc_kernel(info_ref, tiles_ref, *refs, team_count, arc_length, arc_slot, piece_count, scaled, partial_count):
     columns = team_count // 2
     pieces, refs = refs[:piece_count], refs[piece_count:]
     partials, refs = refs[:partial_count], refs[partial_count:]
@@ -86,8 +88,10 @@
             at = pl.ds(block * tile_size, tile_size)
             split(panel_ref[at, :] * norms[:, block : block + 1], at)
     else:
+        cycle = lax.axis_size("blk")
+        shard = lax.rem(lax.axis_index("blk") + cycle - lax.rem(team_index * arc_length + arc_slot, cycle), cycle)
         for k in range(piece_count):
-            owner = source_team(team_index, k, team_count)
+            owner = source_team(shard, team_index, k, team_count)
             split(pieces[k][...], pl.ds(pl.multiple_of(owner * share_rows, share_rows), share_rows))
     sums_ref[...] = jnp.zeros_like(sums_ref)
     live_count = info_ref[0, 0]
@@ -111,7 +115,7 @@
             outs[at][...] = value + partials[at][...] if partials else value
 
 
-def arc_step(info, tiles, pieces, partials, scaled):
+def arc_step(info, tiles, pieces, partials, scaled, arc_length, arc_slot):
     team_count = lax.axis_size("rep")
     panel_rows = pieces[1].shape[0] if scaled else sum(piece.shape[0] for piece in pieces)
     width = pieces[1].shape[1]
@@ -122,6 +126,8 @@
         functools.partial(
             arc_kernel,
             team_count=team_count,
+            arc_length=arc_length,
+            arc_slot=arc_slot,
             piece_count=len(pieces),
             scaled=scaled,
             partial_count=len(partials),
@@ -140,13 +146,13 @@
     )(*operands)
 
 
-def fetch(value, source_team, arc_length):
+def fetch(value, source, arc_length):
     cycle, team_count = lax.axis_size("blk"), lax.axis_size("rep")
     pairs = []
     for shard in range(cycle):
         for team in range(team_count):
             to_shard = (shard + team * arc_length) % cycle
-            pairs.append((shard * team_count + source_team(team), to_shard * team_count + team))
+            pairs.append((shard * team_count + source(shard, team), to_shard * team_count + team))
     return lax.ppermute(value, ("blk", "rep"), pairs)
 
 
@@ -184,8 +190,8 @@
     spread = (3, 1, 2, 0) if team_count == 4 else tuple(range(team_count))
     degrees = degrees.reshape(panel_rows // tile_size, tile_size)
 
-    panel = fetch(embeddings, lambda team: spread[team], arc_length)
-    pieces = [fetch(degrees, lambda team: spread[team], arc_length), panel]
+    panel = fetch(embeddings, lambda shard, team: spread[team], arc_length)
+    pieces = [fetch(degrees, lambda shard, team: spread[team], arc_length), panel]
     tiles, own, norm_scale = prepare(degrees, embeddings, tile_values[0, 0])
     info = jnp.concatenate([slot_counts[0, 0][:, None], tile_rows[0, 0], tile_columns[0, 0]], axis=1)
     info = jnp.broadcast_to(info[:, :, None], (*info.shape, embeddings.shape[1]))
@@ -194,7 +200,7 @@
     for layer in range(LAYERS):
         sums = ()
         for arc_slot in range(arc_length):
-            sums = arc_step(info[arc_slot], tiles[arc_slot], pieces, sums, layer == 0)
+            sums = arc_step(info[arc_slot], tiles[arc_slot], pieces, sums, layer == 0, arc_length, arc_slot)
             if arc_slot + 1 < arc_length:
                 pieces = [next_shard(piece) for piece in pieces]
         current = team_sum(sums) * norm_scale
@@ -202,7 +208,7 @@
         if layer + 1 < LAYERS:
             source = current * norm_scale
             pieces = [
-                fetch(source, lambda team, k=k: source_team(team, k, team_count), arc_length)
+                fetch(source, lambda shard, team, k=k: source_team(shard, team, k, team_count), arc_length)
                 for k in range(team_count)
             ]
     return combined / (LAYERS + 1.0)

time: 50.1 us -> 50 us (level)
    ppermute x6, starting transfers between devices: 10.6 us -> 13 us  [fetch(): return lax.ppermute(value, ('blk', 'rep'), pairs)]
    ppermute x2, starting transfers between devices: 7.38 us -> 6.1 us  [from_column(): return lax.ppermute(value, 'rep', pairs)]
    ppermute x4, starting transfers between devices: 6.73 us -> 5.85 us  [from_mate(): lax.ppermute(value, 'rep', [(team, team ^ 1) for team in range(team_count)])]
where the time goes in v11:
time: 50 us; the launch traced here: 49.7 us
  starting transfers between devices  24.9 us (50%)
  waiting for transfers between devices  17.9 us (36%)
  local copies, waits for them, and re-layouts  2.9 us (6%)
  Pallas kernels  2.36 us (5%)
  other arithmetic  0.88 us (2%)
  between operations  0.74 us (1%)
    ppermute x6, starting transfers between devices, fetch(): return lax.ppermute(value, ('blk', 'rep'), pairs)  13 us
    ppermute x6, waiting for transfers between devices, fetch(): return lax.ppermute(value, ('blk', 'rep'), pairs)  8.47 us
    ppermute x2, waiting for transfers between devices, from_column(): return lax.ppermute(value, 'rep', pairs)  7.61 us
    ppermute x2, starting transfers between devices, from_column(): return lax.ppermute(value, 'rep', pairs)  6.1 us
    ppermute x4, starting transfers between devices, from_mate(): lax.ppermute(value, 'rep', [(team, team ^ 1) for team in range(team_count)])  5.85 us
    unnamed x10, local copies, waits for them, and re-layouts  2.83 us
    ppermute x4, waiting for transfers between devices, from_mate(): lax.ppermute(value, 'rep', [(team, team ^ 1) for team in range(team_count)])  1.82 us
    pallas_call x2, Pallas kernels, arc_step(): pl.pallas_call(functools.partial(arc_kernel, team_count=team_count, arc_l...  1.79 us
  transfers between devices with their start and end apart: 12, of which 7 were waited for; matrix products, arithmetic and copies ran while one was open for 0% of the time, Pallas kernels for 1%

profile of v11, /device:TPU:0, one launch (start us, length us, event | category | flops | bytes accessed | tf_op | source)
XLA Modules:
  0.0 49.7 jit_solution(14025356619535560913)
XLA Ops:
  0.0 5.4 %collective-permute-start.1 = (f32[1024,128]{1,0:T(8,128)}, f32[1024,128]{1,0:T(8,128)S(1)}, u32[]{:S(2)}, u32[]{:S(2)}) collective-permute-start(f32[1024,128]{1,0:T(8,128)} %embeddings_ref.1), channel_id=1, source_target_pairs={{3,0},{1,5},{2,10},{0,15},{7,4},{5,9},{6,14},{4,3},{11,8},{9,13},{... | collective-permute-start | bytes 1572872 | tf_op jit(solution)/shard_map/ppermute | solution.py:156
  5.4 0.8 %collective-permute-start = (s32[8,128]{1,0:T(8,128)}, s32[8,128]{1,0:T(8,128)S(1)}, u32[]{:S(2)}, u32[]{:S(2)}) collective-permute-start(s32[8,128]{1,0:T(8,128)} %bitcast.12), channel_id=1, source_target_pairs={{3,0},{1,5},{2,10},{0,15},{7,4},{5,9},{6,14},{4,3},{11,8},{9,13},{... | collective-permute-start | bytes 12296 | tf_op jit(solution)/shard_map/ppermute | solution.py:156
  6.9 0.6 %copy-done.3 = s32[1,1,1,24]{3,2,1,0:T(1,128)S(1)} copy-done((s32[1,1,1,24]{3,2,1,0:T(1,128)S(1)}, s32[1,1,1,24]{3,2,1,0:T(1,128)}, u32[]{:S(2)}) %copy-start.3) | copy-done | bytes 120
  7.5 0.0 copy-done.4
  7.6 0.1 add_bitcast_fusion
  7.6 1.1 %copy-done = bf16[1,1,1,24,128,128]{5,4,3,2,1,0:T(8,128)(2,1)S(1)} copy-done((bf16[1,1,1,24,128,128]{5,4,3,2,1,0:T(8,128)(2,1)S(1)}, bf16[1,1,1,24,128,128]{5,4,3,2,1,0:T(8,128)(2,1)}, u32[]{:S(2)}) %copy-start) | copy-done | bytes 786456
  8.8 1.0 %copy-done.1 = f32[1024,128]{1,0:T(8,128)S(1)} copy-done((f32[1024,128]{1,0:T(8,128)S(1)}, f32[1024,128]{1,0:T(8,128)}, u32[]{:S(2)}) %copy-start.1) | copy-done | bytes 524312
  9.8 0.6 %shard_map.64 = (bf16[1,24,128,128]{3,2,1,0:T(8,128)(2,1)S(1)}, f32[256,128]{1,0:T(8,128)S(1)}, f32[256,128]{1,0:T(8,128)S(1)}) custom-call(s32[8,128]{1,0:T(8,128)S(1)} %bitcast.13, f32[1024,128]{1,0:T(8,128)S(1)} %copy-done.1, bf16[1,24,128,128]{3,2,1,0:T(8,128)(2,1)S(1)} %bitcast.11), custom_call_target="tpu_custom_call" | custom-call | flops 131072 | bytes 524288 | tf_op jit(solution)/shard_map/pallas_call | solution.py:55
  10.4 4.2 %collective-permute-done.refs_0_ = s32[8,128]{1,0:T(8,128)S(1)} collective-permute-done((s32[8,128]{1,0:T(8,128)}, s32[8,128]{1,0:T(8,128)S(1)}, u32[]{:S(2)}, u32[]{:S(2)}) %collective-permute-start) | collective-permute-done | bytes 4128 | tf_op jit(solution)/shard_map/ppermute | solution.py:156
  14.6 0.1 squeeze.20.info_ref
  14.7 1.0 %shard_map.65 = (f32[256,128]{1,0:T(8,128)S(1)}, f32[256,128]{1,0:T(8,128)S(1)}, f32[256,128]{1,0:T(8,128)S(1)}, f32[256,128]{1,0:T(8,128)S(1)}) custom-call(s32[49,128]{1,0:T(8,128)S(1)} %squeeze.20.info_ref, bf16[24,128,128]{2,1,0:T(8,128)(2,1)S(1)} %bitcast.9, s32[8,128]{1,0:T(8,128)S(1)} %collective-permute-done.refs_0_, ...), custom_call_target="tpu_custom_call" | custom-call | flops 201326592 | bytes 1048576 | tf_op jit(solution)/shard_map/pallas_call | solution.py:125
  15.7 0.8 %collective-permute-start.2 = (f32[256,128]{1,0:T(8,128)S(1)}, f32[256,128]{1,0:T(8,128)S(1)}, u32[]{:S(2)}, u32[]{:S(2)}) collective-permute-start(f32[256,128]{1,0:T(8,128)S(1)} %get-tuple-element.19), channel_id=1, source_target_pairs={{0,1},{1,0},{2,3},{3,2},{4,5},{5,4},{6,7},{7,6},{8,9},{9,8},{10,11... | collective-permute-start | bytes 393224 | tf_op jit(solution)/shard_map/ppermute | solution.py:166
  16.5 0.1 collective-permute-start.4
  16.6 0.9 %collective-permute-done.2 = f32[256,128]{1,0:T(8,128)S(1)} collective-permute-done((f32[256,128]{1,0:T(8,128)S(1)}, f32[256,128]{1,0:T(8,128)S(1)}, u32[]{:S(2)}, u32[]{:S(2)}) %collective-permute-start.2) | collective-permute-done | bytes 131104 | tf_op jit(solution)/shard_map/ppermute | solution.py:166
  17.5 4.0 %collective-permute-start.3 = (f32[256,128]{1,0:T(8,128)S(1)}, f32[256,128]{1,0:T(8,128)S(1)}, u32[]{:S(2)}, u32[]{:S(2)}) collective-permute-start(f32[256,128]{1,0:T(8,128)S(1)} %add.24), channel_id=1, source_target_pairs={{2,0},{3,1},{0,2},{1,3},{6,4},{7,5},{4,6},{5,7},{10,8},{11,9},{8,1... | collective-permute-start | bytes 393224 | tf_op jit(solution)/shard_map/ppermute | solution.py:172
  21.5 0.0 collective-permute-done.4
  21.5 3.8 %collective-permute-done.3 = f32[256,128]{1,0:T(8,128)S(1)} collective-permute-done((f32[256,128]{1,0:T(8,128)S(1)}, f32[256,128]{1,0:T(8,128)S(1)}, u32[]{:S(2)}, u32[]{:S(2)}) %collective-permute-start.3) | collective-permute-done | bytes 131104 | tf_op jit(solution)/shard_map/ppermute | solution.py:172
  25.4 3.6 %collective-permute-start.8 = (f32[256,128]{1,0:T(8,128)S(1)}, f32[256,128]{1,0:T(8,128)S(1)}, u32[]{:S(2)}, u32[]{:S(2)}) collective-permute-start(f32[256,128]{1,0:T(8,128)S(1)} %fusion), channel_id=1, source_target_pairs={{3,0},{1,5},{2,10},{0,15},{7,4},{5,9},{6,14},{4,3},{11,8},{9,13},{... | collective-permute-start | bytes 393224 | tf_op jit(solution)/shard_map/ppermute | solution.py:156
  29.0 0.5 %collective-permute-start.7 = (f32[256,128]{1,0:T(8,128)S(1)}, f32[256,128]{1,0:T(8,128)S(1)}, u32[]{:S(2)}, u32[]{:S(2)}) collective-permute-start(f32[256,128]{1,0:T(8,128)S(1)} %fusion), channel_id=1, source_target_pairs={{1,0},{3,5},{0,10},{2,15},{5,4},{7,9},{4,14},{6,3},{9,8},{11,13},{... | collective-permute-start | bytes 393224 | tf_op jit(solution)/shard_map/ppermute | solution.py:156
  29.5 1.9 %collective-permute-start.6 = (f32[256,128]{1,0:T(8,128)S(1)}, f32[256,128]{1,0:T(8,128)S(1)}, u32[]{:S(2)}, u32[]{:S(2)}) collective-permute-start(f32[256,128]{1,0:T(8,128)S(1)} %fusion), channel_id=1, source_target_pairs={{2,0},{0,5},{3,10},{1,15},{6,4},{4,9},{7,14},{5,3},{8,8},{10,13},{... | collective-permute-start | bytes 393224 | tf_op jit(solution)/shard_map/ppermute | solution.py:156
  31.4 0.7 %collective-permute-start.5 = (f32[256,128]{1,0:T(8,128)S(1)}, f32[256,128]{1,0:T(8,128)S(1)}, u32[]{:S(2)}, u32[]{:S(2)}) collective-permute-start(f32[256,128]{1,0:T(8,128)S(1)} %fusion), channel_id=1, source_target_pairs={{0,0},{2,5},{1,10},{3,15},{4,4},{6,9},{5,14},{7,3},{10,8},{8,13},{... | collective-permute-start | bytes 393224 | tf_op jit(solution)/shard_map/ppermute | solution.py:156
  32.1 0.0 collective-permute-done.8.refs_3_
  32.1 1.2 %collective-permute-done.7.refs_2_ = f32[256,128]{1,0:T(8,128)S(1)} collective-permute-done((f32[256,128]{1,0:T(8,128)S(1)}, f32[256,128]{1,0:T(8,128)S(1)}, u32[]{:S(2)}, u32[]{:S(2)}) %collective-permute-start.7) | collective-permute-done | bytes 131104 | tf_op jit(solution)/shard_map/ppermute | solution.py:156
  33.3 3.0 %collective-permute-done.6.refs_1_ = f32[256,128]{1,0:T(8,128)S(1)} collective-permute-done((f32[256,128]{1,0:T(8,128)S(1)}, f32[256,128]{1,0:T(8,128)S(1)}, u32[]{:S(2)}, u32[]{:S(2)}) %collective-permute-start.6) | collective-permute-done | bytes 131104 | tf_op jit(solution)/shard_map/ppermute | solution.py:156
  36.4 0.0 collective-permute-done.5.refs_0_
  36.4 0.8 %shard_map.66 = (f32[256,128]{1,0:T(8,128)S(1)}, f32[256,128]{1,0:T(8,128)S(1)}, f32[256,128]{1,0:T(8,128)S(1)}, f32[256,128]{1,0:T(8,128)S(1)}) custom-call(s32[49,128]{1,0:T(8,128)S(1)} %squeeze.20.info_ref, bf16[24,128,128]{2,1,0:T(8,128)(2,1)S(1)} %bitcast.10, f32[256,128]{1,0:T(8,128)S(1)} %collective-permute-done.5.refs_0_, ...), custom_call_target="tpu_custom_call" | custom-call | flops 201326592 | bytes 1048576 | tf_op jit(solution)/shard_map/pallas_call | solution.py:125
  37.2 4.9 %collective-permute-start.9 = (f32[256,128]{1,0:T(8,128)S(1)}, f32[256,128]{1,0:T(8,128)S(1)}, u32[]{:S(2)}, u32[]{:S(2)}) collective-permute-start(f32[256,128]{1,0:T(8,128)S(1)} %get-tuple-element.24), channel_id=1, source_target_pairs={{0,1},{1,0},{2,3},{3,2},{4,5},{5,4},{6,7},{7,6},{8,9},{9,8},{10,11... | collective-permute-start | bytes 393224 | tf_op jit(solution)/shard_map/ppermute | solution.py:166
  42.1 0.1 collective-permute-start.11
  42.1 0.9 %collective-permute-done.9 = f32[256,128]{1,0:T(8,128)S(1)} collective-permute-done((f32[256,128]{1,0:T(8,128)S(1)}, f32[256,128]{1,0:T(8,128)S(1)}, u32[]{:S(2)}, u32[]{:S(2)}) %collective-permute-start.9) | collective-permute-done | bytes 131104 | tf_op jit(solution)/shard_map/ppermute | solution.py:166
  43.1 2.1 %collective-permute-start.10 = (f32[256,128]{1,0:T(8,128)S(1)}, f32[256,128]{1,0:T(8,128)S(1)}, u32[]{:S(2)}, u32[]{:S(2)}) collective-permute-start(f32[256,128]{1,0:T(8,128)S(1)} %add.28), channel_id=1, source_target_pairs={{2,0},{3,1},{0,2},{1,3},{6,4},{7,5},{4,6},{5,7},{10,8},{11,9},{8,1... | collective-permute-start | bytes 393224 | tf_op jit(solution)/shard_map/ppermute | solution.py:172
  45.2 3.8 %collective-permute-done.10 = f32[256,128]{1,0:T(8,128)S(1)} collective-permute-done((f32[256,128]{1,0:T(8,128)S(1)}, f32[256,128]{1,0:T(8,128)S(1)}, u32[]{:S(2)}, u32[]{:S(2)}) %collective-permute-start.10) | collective-permute-done | bytes 131104 | tf_op jit(solution)/shard_map/ppermute | solution.py:172
  49.0 0.7 %add_multiply_fusion = f32[256,128]{1,0:T(8,128)} fusion(f32[256,128]{1,0:T(8,128)S(1)} %get-tuple-element.22, f32[256,128]{1,0:T(8,128)S(1)} %collective-permute-done.10, f32[256,128]{1,0:T(8,128)S(1)} %get-tuple-element.25, f32[256,128]{1,0:T(8,128)S(1)} %collective-permute-done.11, f32[256,128]{1,0:T(8,128)S(1)} %get-tuple-element.16, ...), kind=kLoop, calls=%fused_computation | loop fusion | flops 294912 | bytes 1179648 | tf_op jit(solution)/shard_map/div | solution.py:214
  (11 shorter events, 0.1 us)
Async XLA Ops:
  0.0 14.6 %collective-permute-start.1 = (f32[1024,128]{1,0:T(8,128)}, f32[1024,128]{1,0:T(8,128)S(1)}, u32[]{:S(2)}, u32[]{:S(2)}) collective-permute-start(f32[1024,128]{1,0:T(8,128)} %embeddings_ref.1), channel_id=1, source_target_pairs={{3,0},{1,5},{2,10},{0,15},{7,4},{5,9},{6,14},{4,3},{11,8},{9,13},{... | collective-permute-start | bytes 1572872 | tf_op jit(solution)/shard_map/ppermute | solution.py:156
  5.4 9.2 %collective-permute-start = (s32[8,128]{1,0:T(8,128)}, s32[8,128]{1,0:T(8,128)S(1)}, u32[]{:S(2)}, u32[]{:S(2)}) collective-permute-start(s32[8,128]{1,0:T(8,128)} %bitcast.12), channel_id=1, source_target_pairs={{3,0},{1,5},{2,10},{0,15},{7,4},{5,9},{6,14},{4,3},{11,8},{9,13},{... | collective-permute-start | bytes 12296 | tf_op jit(solution)/shard_map/ppermute | solution.py:156
  6.9 0.7 %copy-start.3 = (s32[1,1,1,24]{3,2,1,0:T(1,128)S(1)}, s32[1,1,1,24]{3,2,1,0:T(1,128)}, u32[]{:S(2)}) copy-start(s32[1,1,1,24]{3,2,1,0:T(1,128)} %param.10) | copy-start | bytes 292
  6.9 0.7 %copy-start.4 = (s32[1,1,1,24]{3,2,1,0:T(1,128)S(1)}, s32[1,1,1,24]{3,2,1,0:T(1,128)}, u32[]{:S(2)}) copy-start(s32[1,1,1,24]{3,2,1,0:T(1,128)} %param.9) | copy-start | bytes 292
  6.9 0.7 %copy-start.2 = (s32[1024]{0:T(1024)S(1)}, s32[1024]{0:T(1024)}, u32[]{:S(2)}) copy-start(s32[1024]{0:T(1024)} %param.7) | copy-start | bytes 12292
  7.6 1.1 %copy-start = (bf16[1,1,1,24,128,128]{5,4,3,2,1,0:T(8,128)(2,1)S(1)}, bf16[1,1,1,24,128,128]{5,4,3,2,1,0:T(8,128)(2,1)}, u32[]{:S(2)}) copy-start(bf16[1,1,1,24,128,128]{5,4,3,2,1,0:T(8,128)(2,1)} %param.8) | copy-start | bytes 2359300
  8.8 1.0 %copy-start.1 = (f32[1024,128]{1,0:T(8,128)S(1)}, f32[1024,128]{1,0:T(8,128)}, u32[]{:S(2)}) copy-start(f32[1024,128]{1,0:T(8,128)} %embeddings_ref.1) | copy-start | bytes 1572868
  15.7 1.8 %collective-permute-start.2 = (f32[256,128]{1,0:T(8,128)S(1)}, f32[256,128]{1,0:T(8,128)S(1)}, u32[]{:S(2)}, u32[]{:S(2)}) collective-permute-start(f32[256,128]{1,0:T(8,128)S(1)} %get-tuple-element.19), channel_id=1, source_target_pairs={{0,1},{1,0},{2,3},{3,2},{4,5},{5,4},{6,7},{7,6},{8,9},{9,8},{10,11... | collective-permute-start | bytes 393224 | tf_op jit(solution)/shard_map/ppermute | solution.py:166
  16.5 5.0 %collective-permute-start.4 = (f32[256,128]{1,0:T(8,128)S(1)}, f32[256,128]{1,0:T(8,128)S(1)}, u32[]{:S(2)}, u32[]{:S(2)}) collective-permute-start(f32[256,128]{1,0:T(8,128)S(1)} %get-tuple-element.21), channel_id=1, source_target_pairs={{0,1},{1,0},{2,3},{3,2},{4,5},{5,4},{6,7},{7,6},{8,9},{9,8},{10,11... | collective-permute-start | bytes 393224 | tf_op jit(solution)/shard_map/ppermute | solution.py:166
  17.5 7.8 %collective-permute-start.3 = (f32[256,128]{1,0:T(8,128)S(1)}, f32[256,128]{1,0:T(8,128)S(1)}, u32[]{:S(2)}, u32[]{:S(2)}) collective-permute-start(f32[256,128]{1,0:T(8,128)S(1)} %add.24), channel_id=1, source_target_pairs={{2,0},{3,1},{0,2},{1,3},{6,4},{7,5},{4,6},{5,7},{10,8},{11,9},{8,1... | collective-permute-start | bytes 393224 | tf_op jit(solution)/shard_map/ppermute | solution.py:172
  25.4 6.7 %collective-permute-start.8 = (f32[256,128]{1,0:T(8,128)S(1)}, f32[256,128]{1,0:T(8,128)S(1)}, u32[]{:S(2)}, u32[]{:S(2)}) collective-permute-start(f32[256,128]{1,0:T(8,128)S(1)} %fusion), channel_id=1, source_target_pairs={{3,0},{1,5},{2,10},{0,15},{7,4},{5,9},{6,14},{4,3},{11,8},{9,13},{... | collective-permute-start | bytes 393224 | tf_op jit(solution)/shard_map/ppermute | solution.py:156
  29.0 4.3 %collective-permute-start.7 = (f32[256,128]{1,0:T(8,128)S(1)}, f32[256,128]{1,0:T(8,128)S(1)}, u32[]{:S(2)}, u32[]{:S(2)}) collective-permute-start(f32[256,128]{1,0:T(8,128)S(1)} %fusion), channel_id=1, source_target_pairs={{1,0},{3,5},{0,10},{2,15},{5,4},{7,9},{4,14},{6,3},{9,8},{11,13},{... | collective-permute-start | bytes 393224 | tf_op jit(solution)/shard_map/ppermute | solution.py:156
  29.5 6.8 %collective-permute-start.6 = (f32[256,128]{1,0:T(8,128)S(1)}, f32[256,128]{1,0:T(8,128)S(1)}, u32[]{:S(2)}, u32[]{:S(2)}) collective-permute-start(f32[256,128]{1,0:T(8,128)S(1)} %fusion), channel_id=1, source_target_pairs={{2,0},{0,5},{3,10},{1,15},{6,4},{4,9},{7,14},{5,3},{8,8},{10,13},{... | collective-permute-start | bytes 393224 | tf_op jit(solution)/shard_map/ppermute | solution.py:156
  31.4 4.9 %collective-permute-start.5 = (f32[256,128]{1,0:T(8,128)S(1)}, f32[256,128]{1,0:T(8,128)S(1)}, u32[]{:S(2)}, u32[]{:S(2)}) collective-permute-start(f32[256,128]{1,0:T(8,128)S(1)} %fusion), channel_id=1, source_target_pairs={{0,0},{2,5},{1,10},{3,15},{4,4},{6,9},{5,14},{7,3},{10,8},{8,13},{... | collective-permute-start | bytes 393224 | tf_op jit(solution)/shard_map/ppermute | solution.py:156
  37.2 5.9 %collective-permute-start.9 = (f32[256,128]{1,0:T(8,128)S(1)}, f32[256,128]{1,0:T(8,128)S(1)}, u32[]{:S(2)}, u32[]{:S(2)}) collective-permute-start(f32[256,128]{1,0:T(8,128)S(1)} %get-tuple-element.24), channel_id=1, source_target_pairs={{0,1},{1,0},{2,3},{3,2},{4,5},{5,4},{6,7},{7,6},{8,9},{9,8},{10,11... | collective-permute-start | bytes 393224 | tf_op jit(solution)/shard_map/ppermute | solution.py:166
  42.1 3.1 %collective-permute-start.11 = (f32[256,128]{1,0:T(8,128)S(1)}, f32[256,128]{1,0:T(8,128)S(1)}, u32[]{:S(2)}, u32[]{:S(2)}) collective-permute-start(f32[256,128]{1,0:T(8,128)S(1)} %get-tuple-element.26), channel_id=1, source_target_pairs={{0,1},{1,0},{2,3},{3,2},{4,5},{5,4},{6,7},{7,6},{8,9},{9,8},{10,11... | collective-permute-start | bytes 393224 | tf_op jit(solution)/shard_map/ppermute | solution.py:166
  43.1 5.9 %collective-permute-start.10 = (f32[256,128]{1,0:T(8,128)S(1)}, f32[256,128]{1,0:T(8,128)S(1)}, u32[]{:S(2)}, u32[]{:S(2)}) collective-permute-start(f32[256,128]{1,0:T(8,128)S(1)} %add.28), channel_id=1, source_target_pairs={{2,0},{3,1},{0,2},{1,3},{6,4},{7,5},{4,6},{5,7},{10,8},{11,9},{8,1... | collective-permute-start | bytes 393224 | tf_op jit(solution)/shard_map/ppermute | solution.py:172

commit v12 on v8

--- a/solution.py
+++ b/solution.py
@@ -20,7 +20,7 @@
 
 def source_team(team, turn, team_count):
     if team_count == 4:
-        return (3 * (team % 2)) ^ (team // 2) ^ (2, 1, 0, 3)[turn]
+        return (2 * (team % 2) + team // 2) ^ (0, 2, 1, 3)[turn]
     return (team + turn) % team_count
 
 
@@ -169,15 +169,41 @@
     return lax.ppermute(value, "rep", pairs)
 
 
-def team_sum(sums):
+def team_terms(sums):
     columns = len(sums) // 2
-    total = None
-    for distance in [*range(1, columns), 0]:
-        at = (columns - distance) % columns
-        share = sums[at] + from_mate(sums[columns + at])
-        share = from_column(share, distance) if distance else share
-        total = share if total is None else total + share
-    return total
+    others = []
+    for distance in range(1, columns):
+        at = columns - distance
+        others.append(from_column(sums[at] + from_mate(sums[columns + at]), distance))
+    return [sums[0], from_mate(sums[columns]), *others]
+
+
+def finish_kernel(base_ref, norm_ref, *refs, layer_count):
+    *terms, out_hbm, held_ref, sems = refs
+    pieces = sems.shape[0]
+    rows = held_ref.shape[0] // pieces
+    copies = []
+    for piece in range(pieces):
+        at = pl.ds(piece * rows, rows)
+        total = terms[0][at, :]
+        for term_ref in terms[1:]:
+            total = total + term_ref[at, :]
+        held_ref[at, :] = (base_ref[at, :] + total * norm_ref[at, :]) / layer_count
+        copies.append(pltpu.make_async_copy(held_ref.at[at, :], out_hbm.at[at, :], sems.at[piece]))
+        copies[-1].start()
+    for copy in copies:
+        copy.wait()
+
+
+def finish(base, norm_scale, terms):
+    return pl.pallas_call(
+        functools.partial(finish_kernel, layer_count=LAYERS + 1.0),
+        out_shape=jax.ShapeDtypeStruct(base.shape, jnp.float32),
+        in_specs=[VMEM] * (2 + len(terms)),
+        out_specs=ANY,
+        scratch_shapes=[pltpu.VMEM(base.shape, jnp.float32), pltpu.SemaphoreType.DMA((2,))],
+        compiler_params=pltpu.CompilerParams(vmem_limit_bytes=VMEM_LIMIT),
+    )(base, norm_scale, *terms)
 
 
 def per_device(embeddings, degrees, tile_values, tile_rows, tile_columns, slot_counts):
@@ -191,7 +217,8 @@
     pieces = [fetch(degrees, lambda team: spread[team], arc_length), panel]
     info = jnp.concatenate([slot_counts[0, 0][:, None], tile_rows[0, 0], tile_columns[0, 0]], axis=1)
     info = jnp.broadcast_to(info[:, :, None], (*info.shape, embeddings.shape[1]))
-    tiles, own, norm_scale = prepare(degrees, embeddings, tile_values[0, 0], info)
+    info = [info[at] for at in range(arc_length)]
+    tiles, own, norm_scale = prepare(degrees, embeddings, tile_values[0, 0], info[0])
 
     combined = own
     for layer in range(LAYERS):
@@ -200,15 +227,16 @@
             sums = arc_step(info[arc_slot], tiles[arc_slot], pieces, sums, layer == 0)
             if arc_slot + 1 < arc_length:
                 pieces = [next_shard(piece) for piece in pieces]
-        current = team_sum(sums) * norm_scale
+        terms = team_terms(sums)
+        if layer + 1 == LAYERS:
+            return finish(combined, norm_scale, terms)
+        current = functools.reduce(jnp.add, terms) * norm_scale
         combined = combined + current
-        if layer + 1 < LAYERS:
-            source = current * norm_scale
-            pieces = [
-                fetch(source, lambda team, k=k: source_team(team, k, team_count), arc_length)
-                for k in range(team_count)
-            ]
-    return combined / (LAYERS + 1.0)
+        source = current * norm_scale
+        pieces = [
+            fetch(source, lambda team, k=k: source_team(team, k, team_count), arc_length)
+            for k in range(team_count)
+        ]
 
 
 def solution(mesh):

time: 50.6 us -> 48.9 us (0.966)
  starting transfers between devices: 26 us -> 21.3 us
  waiting for transfers between devices: 16.8 us -> 19.9 us
  Pallas kernels: 2.32 us -> 3.01 us
  other arithmetic: 0.85 us -> 0.16 us
    ppermute x6, starting transfers between devices: 16.1 us -> 11 us  [fetch(): return lax.ppermute(value, ('blk', 'rep'), pairs)]
    ppermute x6, waiting for transfers between devices: 7.17 us -> 10.5 us  [fetch(): return lax.ppermute(value, ('blk', 'rep'), pairs)]
    div x1 -> x0, other arithmetic: 0.71 us -> none  [per_device(): return combined / (LAYERS + 1.0)]
    pallas_call x0 -> x1, Pallas kernels: none -> 0.7 us  [finish(): pl.pallas_call(functools.partial(finish_kernel, layer_count=LAYERS + 1.0)...]
    ppermute x4, starting transfers between devices: 2.94 us -> 3.54 us  [from_mate(): lax.ppermute(value, 'rep', [(team, team ^ 1) for team in range(team_count)])]
  transfers between devices with their start and end apart: 12 -> 12, of which waited for: 7 -> 8; matrix products, arithmetic and copies ran while one was open for 0% -> 0% of each run, Pallas kernels for 1% -> 1%
where the time goes in v12:
time: 48.9 us; the launch traced here: 48.6 us
  starting transfers between devices  21.3 us (44%)
  waiting for transfers between devices  19.9 us (41%)
  local copies, waits for them, and re-layouts  3.52 us (7%)
  Pallas kernels  3.01 us (6%)
  between operations  0.72 us (1%)
    ppermute x6, starting transfers between devices, fetch(): return lax.ppermute(value, ('blk', 'rep'), pairs)  11 us
    ppermute x6, waiting for transfers between devices, fetch(): return lax.ppermute(value, ('blk', 'rep'), pairs)  10.5 us
    ppermute x2, waiting for transfers between devices, from_column(): return lax.ppermute(value, 'rep', pairs)  7.61 us
    ppermute x2, starting transfers between devices, from_column(): return lax.ppermute(value, 'rep', pairs)  6.72 us
    ppermute x4, starting transfers between devices, from_mate(): lax.ppermute(value, 'rep', [(team, team ^ 1) for team in range(team_count)])  3.54 us
    unnamed x10, local copies, waits for them, and re-layouts  3.44 us
    ppermute x4, waiting for transfers between devices, from_mate(): lax.ppermute(value, 'rep', [(team, team ^ 1) for team in range(team_count)])  1.82 us
    pallas_call x2, Pallas kernels, arc_step(): pl.pallas_call(functools.partial(arc_kernel, team_count=team_count, piece...  1.74 us
  transfers between devices with their start and end apart: 12, of which 8 were waited for; matrix products, arithmetic and copies ran while one was open for 0% of the time, Pallas kernels for 1%

profile of v12, /device:TPU:0, one launch (start us, length us, event | category | flops | bytes accessed | tf_op | source)
XLA Modules:
  0.0 48.6 jit_solution(18022597802044917166)
XLA Ops:
  0.0 5.4 %collective-permute-start.1 = (f32[1024,128]{1,0:T(8,128)}, f32[1024,128]{1,0:T(8,128)S(1)}, u32[]{:S(2)}, u32[]{:S(2)}) collective-permute-start(f32[1024,128]{1,0:T(8,128)} %embeddings_ref.1), channel_id=1, source_target_pairs={{3,0},{1,5},{2,10},{0,15},{7,4},{5,9},{6,14},{4,3},{11,8},{9,13},{... | collective-permute-start | bytes 1572872 | tf_op jit(solution)/shard_map/ppermute | solution.py:153
  5.4 0.8 %collective-permute-start = (s32[8,128]{1,0:T(8,128)}, s32[8,128]{1,0:T(8,128)S(1)}, u32[]{:S(2)}, u32[]{:S(2)}) collective-permute-start(s32[8,128]{1,0:T(8,128)} %bitcast.12), channel_id=1, source_target_pairs={{3,0},{1,5},{2,10},{0,15},{7,4},{5,9},{6,14},{4,3},{11,8},{9,13},{... | collective-permute-start | bytes 12296 | tf_op jit(solution)/shard_map/ppermute | solution.py:153
  6.9 0.6 %copy-done.3 = s32[1,1,1,24]{3,2,1,0:T(1,128)S(1)} copy-done((s32[1,1,1,24]{3,2,1,0:T(1,128)S(1)}, s32[1,1,1,24]{3,2,1,0:T(1,128)}, u32[]{:S(2)}) %copy-start.3) | copy-done | bytes 120
  7.5 0.0 copy-done.4
  7.6 0.1 add_bitcast_fusion
  7.6 0.1 squeeze.19.after_ref.info_ref
  7.7 0.6 %copy-done.2 = s32[1024]{0:T(1024)S(1)} copy-done((s32[1024]{0:T(1024)S(1)}, s32[1024]{0:T(1024)}, u32[]{:S(2)}) %copy-start.2) | copy-done | bytes 4120
  8.3 1.1 %copy-done = bf16[1,1,1,24,128,128]{5,4,3,2,1,0:T(8,128)(2,1)S(1)} copy-done((bf16[1,1,1,24,128,128]{5,4,3,2,1,0:T(8,128)(2,1)S(1)}, bf16[1,1,1,24,128,128]{5,4,3,2,1,0:T(8,128)(2,1)}, u32[]{:S(2)}) %copy-start) | copy-done | bytes 786456
  9.5 1.0 %copy-done.1 = f32[1024,128]{1,0:T(8,128)S(1)} copy-done((f32[1024,128]{1,0:T(8,128)S(1)}, f32[1024,128]{1,0:T(8,128)}, u32[]{:S(2)}) %copy-start.1) | copy-done | bytes 524312
  10.5 0.6 %shard_map.64 = (bf16[1,24,128,128]{3,2,1,0:T(8,128)(2,1)S(1)}, f32[256,128]{1,0:T(8,128)S(1)}, f32[256,128]{1,0:T(8,128)S(1)}) custom-call(s32[8,128]{1,0:T(8,128)S(1)} %bitcast.13, f32[1024,128]{1,0:T(8,128)S(1)} %copy-done.1, bf16[1,24,128,128]{3,2,1,0:T(8,128)(2,1)S(1)} %bitcast.11, s32[49,128]{1,0:T(8,128)S(1)} %squeeze.19.after_ref.info_ref), custom_call_target="tpu_custom_call" | custom-call | flops 131072 | bytes 524288 | tf_op jit(solution)/shard_map/pallas_call | solution.py:56
  11.1 3.5 %collective-permute-done.refs_0_ = s32[8,128]{1,0:T(8,128)S(1)} collective-permute-done((s32[8,128]{1,0:T(8,128)}, s32[8,128]{1,0:T(8,128)S(1)}, u32[]{:S(2)}, u32[]{:S(2)}) %collective-permute-start) | collective-permute-done | bytes 4128 | tf_op jit(solution)/shard_map/ppermute | solution.py:153
  14.6 1.0 %shard_map.65 = (f32[256,128]{1,0:T(8,128)S(1)}, f32[256,128]{1,0:T(8,128)S(1)}, f32[256,128]{1,0:T(8,128)S(1)}, f32[256,128]{1,0:T(8,128)S(1)}) custom-call(s32[49,128]{1,0:T(8,128)S(1)} %squeeze.19.after_ref.info_ref, bf16[24,128,128]{2,1,0:T(8,128)(2,1)S(1)} %bitcast.9, s32[8,128]{1,0:T(8,128)S(1)} %collective-permute-done.refs_0_, ...), custom_call_target="tpu_custom_call" | custom-call | flops 201326592 | bytes 1048576 | tf_op jit(solution)/shard_map/pallas_call | solution.py:124
  15.6 0.8 %collective-permute-start.3 = (f32[256,128]{1,0:T(8,128)S(1)}, f32[256,128]{1,0:T(8,128)S(1)}, u32[]{:S(2)}, u32[]{:S(2)}) collective-permute-start(f32[256,128]{1,0:T(8,128)S(1)} %get-tuple-element.21), channel_id=1, source_target_pairs={{0,1},{1,0},{2,3},{3,2},{4,5},{5,4},{6,7},{7,6},{8,9},{9,8},{10,11... | collective-permute-start | bytes 393224 | tf_op jit(solution)/shard_map/ppermute | solution.py:163
  16.4 0.1 collective-permute-start.2
  16.5 0.9 %collective-permute-done.3 = f32[256,128]{1,0:T(8,128)S(1)} collective-permute-done((f32[256,128]{1,0:T(8,128)S(1)}, f32[256,128]{1,0:T(8,128)S(1)}, u32[]{:S(2)}, u32[]{:S(2)}) %collective-permute-start.3) | collective-permute-done | bytes 131104 | tf_op jit(solution)/shard_map/ppermute | solution.py:163
  17.4 4.0 %collective-permute-start.4 = (f32[256,128]{1,0:T(8,128)S(1)}, f32[256,128]{1,0:T(8,128)S(1)}, u32[]{:S(2)}, u32[]{:S(2)}) collective-permute-start(f32[256,128]{1,0:T(8,128)S(1)} %add.16), channel_id=1, source_target_pairs={{2,0},{3,1},{0,2},{1,3},{6,4},{7,5},{4,6},{5,7},{10,8},{11,9},{8,1... | collective-permute-start | bytes 393224 | tf_op jit(solution)/shard_map/ppermute | solution.py:169
  21.4 0.0 collective-permute-done.2
  21.4 3.8 %collective-permute-done.4 = f32[256,128]{1,0:T(8,128)S(1)} collective-permute-done((f32[256,128]{1,0:T(8,128)S(1)}, f32[256,128]{1,0:T(8,128)S(1)}, u32[]{:S(2)}, u32[]{:S(2)}) %collective-permute-start.4) | collective-permute-done | bytes 131104 | tf_op jit(solution)/shard_map/ppermute | solution.py:169
  25.3 3.6 %collective-permute-start.8 = (f32[256,128]{1,0:T(8,128)S(1)}, f32[256,128]{1,0:T(8,128)S(1)}, u32[]{:S(2)}, u32[]{:S(2)}) collective-permute-start(f32[256,128]{1,0:T(8,128)S(1)} %get-tuple-element.27), channel_id=1, source_target_pairs={{3,0},{1,5},{2,10},{0,15},{7,4},{5,9},{6,14},{4,3},{11,8},{9,13},{... | collective-permute-start | bytes 393224 | tf_op jit(solution)/shard_map/ppermute | solution.py:153
  28.9 0.5 %collective-permute-start.7 = (f32[256,128]{1,0:T(8,128)S(1)}, f32[256,128]{1,0:T(8,128)S(1)}, u32[]{:S(2)}, u32[]{:S(2)}) collective-permute-start(f32[256,128]{1,0:T(8,128)S(1)} %get-tuple-element.27), channel_id=1, source_target_pairs={{1,0},{3,5},{0,10},{2,15},{5,4},{7,9},{4,14},{6,3},{9,8},{11,13},{... | collective-permute-start | bytes 393224 | tf_op jit(solution)/shard_map/ppermute | solution.py:153
  29.4 0.0 collective-permute-start.6
  29.4 0.7 %collective-permute-start.5 = (f32[256,128]{1,0:T(8,128)S(1)}, f32[256,128]{1,0:T(8,128)S(1)}, u32[]{:S(2)}, u32[]{:S(2)}) collective-permute-start(f32[256,128]{1,0:T(8,128)S(1)} %get-tuple-element.27), channel_id=1, source_target_pairs={{0,0},{2,5},{1,10},{3,15},{4,4},{6,9},{5,14},{7,3},{8,8},{10,13},{... | collective-permute-start | bytes 393224 | tf_op jit(solution)/shard_map/ppermute | solution.py:153
  30.1 2.3 %collective-permute-done.8.refs_3_ = f32[256,128]{1,0:T(8,128)S(1)} collective-permute-done((f32[256,128]{1,0:T(8,128)S(1)}, f32[256,128]{1,0:T(8,128)S(1)}, u32[]{:S(2)}, u32[]{:S(2)}) %collective-permute-start.8) | collective-permute-done | bytes 131104 | tf_op jit(solution)/shard_map/ppermute | solution.py:153
  32.4 2.7 %collective-permute-done.7.refs_2_ = f32[256,128]{1,0:T(8,128)S(1)} collective-permute-done((f32[256,128]{1,0:T(8,128)S(1)}, f32[256,128]{1,0:T(8,128)S(1)}, u32[]{:S(2)}, u32[]{:S(2)}) %collective-permute-start.7) | collective-permute-done | bytes 131104 | tf_op jit(solution)/shard_map/ppermute | solution.py:153
  35.1 2.0 %collective-permute-done.6.refs_1_ = f32[256,128]{1,0:T(8,128)S(1)} collective-permute-done((f32[256,128]{1,0:T(8,128)S(1)}, f32[256,128]{1,0:T(8,128)S(1)}, u32[]{:S(2)}, u32[]{:S(2)}) %collective-permute-start.6) | collective-permute-done | bytes 131104 | tf_op jit(solution)/shard_map/ppermute | solution.py:153
  37.1 0.8 %shard_map.66 = (f32[256,128]{1,0:T(8,128)S(1)}, f32[256,128]{1,0:T(8,128)S(1)}, f32[256,128]{1,0:T(8,128)S(1)}, f32[256,128]{1,0:T(8,128)S(1)}) custom-call(s32[49,128]{1,0:T(8,128)S(1)} %squeeze.19.after_ref.info_ref, bf16[24,128,128]{2,1,0:T(8,128)(2,1)S(1)} %bitcast.10, f32[256,128]{1,0:T(8,128)S(1)} %collective-permute-done.5.refs_0_, ...), custom_call_target="tpu_custom_call" | custom-call | flops 201326592 | bytes 1048576 | tf_op jit(solution)/shard_map/pallas_call | solution.py:124
  37.8 2.6 %collective-permute-start.10 = (f32[256,128]{1,0:T(8,128)S(1)}, f32[256,128]{1,0:T(8,128)S(1)}, u32[]{:S(2)}, u32[]{:S(2)}) collective-permute-start(f32[256,128]{1,0:T(8,128)S(1)} %get-tuple-element.26), channel_id=1, source_target_pairs={{0,1},{1,0},{2,3},{3,2},{4,5},{5,4},{6,7},{7,6},{8,9},{9,8},{10,11... | collective-permute-start | bytes 393224 | tf_op jit(solution)/shard_map/ppermute | solution.py:163
  40.4 0.1 collective-permute-start.9
  40.5 0.9 %collective-permute-done.10 = f32[256,128]{1,0:T(8,128)S(1)} collective-permute-done((f32[256,128]{1,0:T(8,128)S(1)}, f32[256,128]{1,0:T(8,128)S(1)}, u32[]{:S(2)}, u32[]{:S(2)}) %collective-permute-start.10) | collective-permute-done | bytes 131104 | tf_op jit(solution)/shard_map/ppermute | solution.py:163
  41.4 2.7 %collective-permute-start.11 = (f32[256,128]{1,0:T(8,128)S(1)}, f32[256,128]{1,0:T(8,128)S(1)}, u32[]{:S(2)}, u32[]{:S(2)}) collective-permute-start(f32[256,128]{1,0:T(8,128)S(1)} %add.19), channel_id=1, source_target_pairs={{2,0},{3,1},{0,2},{1,3},{6,4},{7,5},{4,6},{5,7},{10,8},{11,9},{8,1... | collective-permute-start | bytes 393224 | tf_op jit(solution)/shard_map/ppermute | solution.py:169
  44.1 3.8 %collective-permute-done.11.refs_2_ = f32[256,128]{1,0:T(8,128)S(1)} collective-permute-done((f32[256,128]{1,0:T(8,128)S(1)}, f32[256,128]{1,0:T(8,128)S(1)}, u32[]{:S(2)}, u32[]{:S(2)}) %collective-permute-start.11) | collective-permute-done | bytes 131104 | tf_op jit(solution)/shard_map/ppermute | solution.py:169
  47.9 0.7 %shard_map.67 = f32[256,128]{1,0:T(8,128)} custom-call(f32[256,128]{1,0:T(8,128)S(1)} %get-tuple-element.28.base_ref, f32[256,128]{1,0:T(8,128)S(1)} %get-tuple-element.22.norm_ref, f32[256,128]{1,0:T(8,128)S(1)} %get-tuple-element.23.refs_0_, f32[256,128]{1,0:T(8,128)S(1)} %collective-permute-done.9.refs_1_, f32[256,128]{1,0:T(8,128)S(1)} %collective-permute-done.11.refs_2_), custom_call_target="tpu_custom_call" | custom-call | tf_op jit(solution)/shard_map/pallas_call | solution.py:199
  (11 shorter events, 0.1 us)
Async XLA Ops:
  0.0 14.6 %collective-permute-start.1 = (f32[1024,128]{1,0:T(8,128)}, f32[1024,128]{1,0:T(8,128)S(1)}, u32[]{:S(2)}, u32[]{:S(2)}) collective-permute-start(f32[1024,128]{1,0:T(8,128)} %embeddings_ref.1), channel_id=1, source_target_pairs={{3,0},{1,5},{2,10},{0,15},{7,4},{5,9},{6,14},{4,3},{11,8},{9,13},{... | collective-permute-start | bytes 1572872 | tf_op jit(solution)/shard_map/ppermute | solution.py:153
  5.4 9.2 %collective-permute-start = (s32[8,128]{1,0:T(8,128)}, s32[8,128]{1,0:T(8,128)S(1)}, u32[]{:S(2)}, u32[]{:S(2)}) collective-permute-start(s32[8,128]{1,0:T(8,128)} %bitcast.12), channel_id=1, source_target_pairs={{3,0},{1,5},{2,10},{0,15},{7,4},{5,9},{6,14},{4,3},{11,8},{9,13},{... | collective-permute-start | bytes 12296 | tf_op jit(solution)/shard_map/ppermute | solution.py:153
  6.9 0.7 %copy-start.3 = (s32[1,1,1,24]{3,2,1,0:T(1,128)S(1)}, s32[1,1,1,24]{3,2,1,0:T(1,128)}, u32[]{:S(2)}) copy-start(s32[1,1,1,24]{3,2,1,0:T(1,128)} %param.10) | copy-start | bytes 292
  6.9 0.7 %copy-start.4 = (s32[1,1,1,24]{3,2,1,0:T(1,128)S(1)}, s32[1,1,1,24]{3,2,1,0:T(1,128)}, u32[]{:S(2)}) copy-start(s32[1,1,1,24]{3,2,1,0:T(1,128)} %param.9) | copy-start | bytes 292
  7.6 0.7 %copy-start.2 = (s32[1024]{0:T(1024)S(1)}, s32[1024]{0:T(1024)}, u32[]{:S(2)}) copy-start(s32[1024]{0:T(1024)} %param.7) | copy-start | bytes 12292
  8.3 1.1 %copy-start = (bf16[1,1,1,24,128,128]{5,4,3,2,1,0:T(8,128)(2,1)S(1)}, bf16[1,1,1,24,128,128]{5,4,3,2,1,0:T(8,128)(2,1)}, u32[]{:S(2)}) copy-start(bf16[1,1,1,24,128,128]{5,4,3,2,1,0:T(8,128)(2,1)} %param.8) | copy-start | bytes 2359300
  9.5 1.0 %copy-start.1 = (f32[1024,128]{1,0:T(8,128)S(1)}, f32[1024,128]{1,0:T(8,128)}, u32[]{:S(2)}) copy-start(f32[1024,128]{1,0:T(8,128)} %embeddings_ref.1) | copy-start | bytes 1572868
  15.6 1.8 %collective-permute-start.3 = (f32[256,128]{1,0:T(8,128)S(1)}, f32[256,128]{1,0:T(8,128)S(1)}, u32[]{:S(2)}, u32[]{:S(2)}) collective-permute-start(f32[256,128]{1,0:T(8,128)S(1)} %get-tuple-element.21), channel_id=1, source_target_pairs={{0,1},{1,0},{2,3},{3,2},{4,5},{5,4},{6,7},{7,6},{8,9},{9,8},{10,11... | collective-permute-start | bytes 393224 | tf_op jit(solution)/shard_map/ppermute | solution.py:163
  16.4 5.0 %collective-permute-start.2 = (f32[256,128]{1,0:T(8,128)S(1)}, f32[256,128]{1,0:T(8,128)S(1)}, u32[]{:S(2)}, u32[]{:S(2)}) collective-permute-start(f32[256,128]{1,0:T(8,128)S(1)} %get-tuple-element.19), channel_id=1, source_target_pairs={{0,1},{1,0},{2,3},{3,2},{4,5},{5,4},{6,7},{7,6},{8,9},{9,8},{10,11... | collective-permute-start | bytes 393224 | tf_op jit(solution)/shard_map/ppermute | solution.py:163
  17.4 7.8 %collective-permute-start.4 = (f32[256,128]{1,0:T(8,128)S(1)}, f32[256,128]{1,0:T(8,128)S(1)}, u32[]{:S(2)}, u32[]{:S(2)}) collective-permute-start(f32[256,128]{1,0:T(8,128)S(1)} %add.16), channel_id=1, source_target_pairs={{2,0},{3,1},{0,2},{1,3},{6,4},{7,5},{4,6},{5,7},{10,8},{11,9},{8,1... | collective-permute-start | bytes 393224 | tf_op jit(solution)/shard_map/ppermute | solution.py:169
  25.3 7.1 %collective-permute-start.8 = (f32[256,128]{1,0:T(8,128)S(1)}, f32[256,128]{1,0:T(8,128)S(1)}, u32[]{:S(2)}, u32[]{:S(2)}) collective-permute-start(f32[256,128]{1,0:T(8,128)S(1)} %get-tuple-element.27), channel_id=1, source_target_pairs={{3,0},{1,5},{2,10},{0,15},{7,4},{5,9},{6,14},{4,3},{11,8},{9,13},{... | collective-permute-start | bytes 393224 | tf_op jit(solution)/shard_map/ppermute | solution.py:153
  28.9 6.2 %collective-permute-start.7 = (f32[256,128]{1,0:T(8,128)S(1)}, f32[256,128]{1,0:T(8,128)S(1)}, u32[]{:S(2)}, u32[]{:S(2)}) collective-permute-start(f32[256,128]{1,0:T(8,128)S(1)} %get-tuple-element.27), channel_id=1, source_target_pairs={{1,0},{3,5},{0,10},{2,15},{5,4},{7,9},{4,14},{6,3},{9,8},{11,13},{... | collective-permute-start | bytes 393224 | tf_op jit(solution)/shard_map/ppermute | solution.py:153
  29.4 7.6 %collective-permute-start.6 = (f32[256,128]{1,0:T(8,128)S(1)}, f32[256,128]{1,0:T(8,128)S(1)}, u32[]{:S(2)}, u32[]{:S(2)}) collective-permute-start(f32[256,128]{1,0:T(8,128)S(1)} %get-tuple-element.27), channel_id=1, source_target_pairs={{2,0},{0,5},{3,10},{1,15},{6,4},{4,9},{7,14},{5,3},{10,8},{8,13},{... | collective-permute-start | bytes 393224 | tf_op jit(solution)/shard_map/ppermute | solution.py:153
  29.4 7.6 %collective-permute-start.5 = (f32[256,128]{1,0:T(8,128)S(1)}, f32[256,128]{1,0:T(8,128)S(1)}, u32[]{:S(2)}, u32[]{:S(2)}) collective-permute-start(f32[256,128]{1,0:T(8,128)S(1)} %get-tuple-element.27), channel_id=1, source_target_pairs={{0,0},{2,5},{1,10},{3,15},{4,4},{6,9},{5,14},{7,3},{8,8},{10,13},{... | collective-permute-start | bytes 393224 | tf_op jit(solution)/shard_map/ppermute | solution.py:153
  37.8 3.6 %collective-permute-start.10 = (f32[256,128]{1,0:T(8,128)S(1)}, f32[256,128]{1,0:T(8,128)S(1)}, u32[]{:S(2)}, u32[]{:S(2)}) collective-permute-start(f32[256,128]{1,0:T(8,128)S(1)} %get-tuple-element.26), channel_id=1, source_target_pairs={{0,1},{1,0},{2,3},{3,2},{4,5},{5,4},{6,7},{7,6},{8,9},{9,8},{10,11... | collective-permute-start | bytes 393224 | tf_op jit(solution)/shard_map/ppermute | solution.py:163
  40.4 3.7 %collective-permute-start.9 = (f32[256,128]{1,0:T(8,128)S(1)}, f32[256,128]{1,0:T(8,128)S(1)}, u32[]{:S(2)}, u32[]{:S(2)}) collective-permute-start(f32[256,128]{1,0:T(8,128)S(1)} %get-tuple-element.24), channel_id=1, source_target_pairs={{0,1},{1,0},{2,3},{3,2},{4,5},{5,4},{6,7},{7,6},{8,9},{9,8},{10,11... | collective-permute-start | bytes 393224 | tf_op jit(solution)/shard_map/ppermute | solution.py:163
  41.4 6.5 %collective-permute-start.11 = (f32[256,128]{1,0:T(8,128)S(1)}, f32[256,128]{1,0:T(8,128)S(1)}, u32[]{:S(2)}, u32[]{:S(2)}) collective-permute-start(f32[256,128]{1,0:T(8,128)S(1)} %add.19), channel_id=1, source_target_pairs={{2,0},{3,1},{0,2},{1,3},{6,4},{7,5},{4,6},{5,7},{10,8},{11,9},{8,1... | collective-permute-start | bytes 393224 | tf_op jit(solution)/shard_map/ppermute | solution.py:169

commit v13 on v12

--- a/solution.py
+++ b/solution.py
@@ -20,7 +20,7 @@
 
 def source_team(team, turn, team_count):
     if team_count == 4:
-        return (2 * (team % 2) + team // 2) ^ (0, 2, 1, 3)[turn]
+        return (2 * (team % 2) + team // 2) ^ (0, 1, 3, 2)[turn]
     return (team + turn) % team_count
 
 

time: 48.9 us -> 50.2 us (1.027)
  starting transfers between devices: 21.3 us -> 24.1 us
  waiting for transfers between devices: 19.9 us -> 18.5 us
    ppermute x4, starting transfers between devices: 3.54 us -> 5.25 us  [from_mate(): lax.ppermute(value, 'rep', [(team, team ^ 1) for team in range(team_count)])]
    ppermute x6, waiting for transfers between devices: 10.5 us -> 9.04 us  [fetch(): return lax.ppermute(value, ('blk', 'rep'), pairs)]
    ppermute x2, starting transfers between devices: 6.72 us -> 7.5 us  [from_column(): return lax.ppermute(value, 'rep', pairs)]
where the time goes in v13:
time: 50.2 us; the launch traced here: 50 us
  starting transfers between devices  24.1 us (48%)
  waiting for transfers between devices  18.5 us (37%)
  local copies, waits for them, and re-layouts  3.52 us (7%)
  Pallas kernels  3.01 us (6%)
  between operations  0.73 us (1%)
    ppermute x6, starting transfers between devices, fetch(): return lax.ppermute(value, ('blk', 'rep'), pairs)  11.3 us
    ppermute x6, waiting for transfers between devices, fetch(): return lax.ppermute(value, ('blk', 'rep'), pairs)  9.04 us
    ppermute x2, waiting for transfers between devices, from_column(): return lax.ppermute(value, 'rep', pairs)  7.61 us
    ppermute x2, starting transfers between devices, from_column(): return lax.ppermute(value, 'rep', pairs)  7.5 us
    ppermute x4, starting transfers between devices, from_mate(): lax.ppermute(value, 'rep', [(team, team ^ 1) for team in range(team_count)])  5.25 us
    unnamed x10, local copies, waits for them, and re-layouts  3.44 us
    ppermute x4, waiting for transfers between devices, from_mate(): lax.ppermute(value, 'rep', [(team, team ^ 1) for team in range(team_count)])  1.82 us
    pallas_call x2, Pallas kernels, arc_step(): pl.pallas_call(functools.partial(arc_kernel, team_count=team_count, piece...  1.73 us
  transfers between devices with their start and end apart: 12, of which 8 were waited for; matrix products, arithmetic and copies ran while one was open for 0% of the time, Pallas kernels for 1%

profile of v13, /device:TPU:0, one launch (start us, length us, event | category | flops | bytes accessed | tf_op | source)
XLA Modules:
  0.0 50.0 jit_solution(7786856219317528614)
XLA Ops:
  0.0 5.4 %collective-permute-start.1 = (f32[1024,128]{1,0:T(8,128)}, f32[1024,128]{1,0:T(8,128)S(1)}, u32[]{:S(2)}, u32[]{:S(2)}) collective-permute-start(f32[1024,128]{1,0:T(8,128)} %embeddings_ref.1), channel_id=1, source_target_pairs={{3,0},{1,5},{2,10},{0,15},{7,4},{5,9},{6,14},{4,3},{11,8},{9,13},{... | collective-permute-start | bytes 1572872 | tf_op jit(solution)/shard_map/ppermute | solution.py:153
  5.4 0.8 %collective-permute-start = (s32[8,128]{1,0:T(8,128)}, s32[8,128]{1,0:T(8,128)S(1)}, u32[]{:S(2)}, u32[]{:S(2)}) collective-permute-start(s32[8,128]{1,0:T(8,128)} %bitcast.12), channel_id=1, source_target_pairs={{3,0},{1,5},{2,10},{0,15},{7,4},{5,9},{6,14},{4,3},{11,8},{9,13},{... | collective-permute-start | bytes 12296 | tf_op jit(solution)/shard_map/ppermute | solution.py:153
  6.9 0.6 %copy-done.3 = s32[1,1,1,24]{3,2,1,0:T(1,128)S(1)} copy-done((s32[1,1,1,24]{3,2,1,0:T(1,128)S(1)}, s32[1,1,1,24]{3,2,1,0:T(1,128)}, u32[]{:S(2)}) %copy-start.3) | copy-done | bytes 120
  7.5 0.0 copy-done.4
  7.6 0.1 add_bitcast_fusion
  7.6 0.1 squeeze.19.after_ref.info_ref
  7.7 0.6 %copy-done.2 = s32[1024]{0:T(1024)S(1)} copy-done((s32[1024]{0:T(1024)S(1)}, s32[1024]{0:T(1024)}, u32[]{:S(2)}) %copy-start.2) | copy-done | bytes 4120
  8.3 1.1 %copy-done = bf16[1,1,1,24,128,128]{5,4,3,2,1,0:T(8,128)(2,1)S(1)} copy-done((bf16[1,1,1,24,128,128]{5,4,3,2,1,0:T(8,128)(2,1)S(1)}, bf16[1,1,1,24,128,128]{5,4,3,2,1,0:T(8,128)(2,1)}, u32[]{:S(2)}) %copy-start) | copy-done | bytes 786456
  9.5 1.0 %copy-done.1 = f32[1024,128]{1,0:T(8,128)S(1)} copy-done((f32[1024,128]{1,0:T(8,128)S(1)}, f32[1024,128]{1,0:T(8,128)}, u32[]{:S(2)}) %copy-start.1) | copy-done | bytes 524312
  10.5 0.6 %shard_map.64 = (bf16[1,24,128,128]{3,2,1,0:T(8,128)(2,1)S(1)}, f32[256,128]{1,0:T(8,128)S(1)}, f32[256,128]{1,0:T(8,128)S(1)}) custom-call(s32[8,128]{1,0:T(8,128)S(1)} %bitcast.13, f32[1024,128]{1,0:T(8,128)S(1)} %copy-done.1, bf16[1,24,128,128]{3,2,1,0:T(8,128)(2,1)S(1)} %bitcast.11, s32[49,128]{1,0:T(8,128)S(1)} %squeeze.19.after_ref.info_ref), custom_call_target="tpu_custom_call" | custom-call | flops 131072 | bytes 524288 | tf_op jit(solution)/shard_map/pallas_call | solution.py:56
  11.1 3.5 %collective-permute-done.refs_0_ = s32[8,128]{1,0:T(8,128)S(1)} collective-permute-done((s32[8,128]{1,0:T(8,128)}, s32[8,128]{1,0:T(8,128)S(1)}, u32[]{:S(2)}, u32[]{:S(2)}) %collective-permute-start) | collective-permute-done | bytes 4128 | tf_op jit(solution)/shard_map/ppermute | solution.py:153
  14.6 1.0 %shard_map.65 = (f32[256,128]{1,0:T(8,128)S(1)}, f32[256,128]{1,0:T(8,128)S(1)}, f32[256,128]{1,0:T(8,128)S(1)}, f32[256,128]{1,0:T(8,128)S(1)}) custom-call(s32[49,128]{1,0:T(8,128)S(1)} %squeeze.19.after_ref.info_ref, bf16[24,128,128]{2,1,0:T(8,128)(2,1)S(1)} %bitcast.9, s32[8,128]{1,0:T(8,128)S(1)} %collective-permute-done.refs_0_, ...), custom_call_target="tpu_custom_call" | custom-call | flops 201326592 | bytes 1048576 | tf_op jit(solution)/shard_map/pallas_call | solution.py:124
  15.6 0.8 %collective-permute-start.3 = (f32[256,128]{1,0:T(8,128)S(1)}, f32[256,128]{1,0:T(8,128)S(1)}, u32[]{:S(2)}, u32[]{:S(2)}) collective-permute-start(f32[256,128]{1,0:T(8,128)S(1)} %get-tuple-element.21), channel_id=1, source_target_pairs={{0,1},{1,0},{2,3},{3,2},{4,5},{5,4},{6,7},{7,6},{8,9},{9,8},{10,11... | collective-permute-start | bytes 393224 | tf_op jit(solution)/shard_map/ppermute | solution.py:163
  16.4 0.1 collective-permute-start.2
  16.5 0.9 %collective-permute-done.3 = f32[256,128]{1,0:T(8,128)S(1)} collective-permute-done((f32[256,128]{1,0:T(8,128)S(1)}, f32[256,128]{1,0:T(8,128)S(1)}, u32[]{:S(2)}, u32[]{:S(2)}) %collective-permute-start.3) | collective-permute-done | bytes 131104 | tf_op jit(solution)/shard_map/ppermute | solution.py:163
  17.4 4.0 %collective-permute-start.4 = (f32[256,128]{1,0:T(8,128)S(1)}, f32[256,128]{1,0:T(8,128)S(1)}, u32[]{:S(2)}, u32[]{:S(2)}) collective-permute-start(f32[256,128]{1,0:T(8,128)S(1)} %add.16), channel_id=1, source_target_pairs={{2,0},{3,1},{0,2},{1,3},{6,4},{7,5},{4,6},{5,7},{10,8},{11,9},{8,1... | collective-permute-start | bytes 393224 | tf_op jit(solution)/shard_map/ppermute | solution.py:169
  21.4 0.0 collective-permute-done.2
  21.4 3.8 %collective-permute-done.4 = f32[256,128]{1,0:T(8,128)S(1)} collective-permute-done((f32[256,128]{1,0:T(8,128)S(1)}, f32[256,128]{1,0:T(8,128)S(1)}, u32[]{:S(2)}, u32[]{:S(2)}) %collective-permute-start.4) | collective-permute-done | bytes 131104 | tf_op jit(solution)/shard_map/ppermute | solution.py:169
  25.3 0.1 collective-permute-start.8
  25.4 4.0 %collective-permute-start.7 = (f32[256,128]{1,0:T(8,128)S(1)}, f32[256,128]{1,0:T(8,128)S(1)}, u32[]{:S(2)}, u32[]{:S(2)}) collective-permute-start(f32[256,128]{1,0:T(8,128)S(1)} %get-tuple-element.27), channel_id=1, source_target_pairs={{3,0},{1,5},{2,10},{0,15},{7,4},{5,9},{6,14},{4,3},{11,8},{9,13},{... | collective-permute-start | bytes 393224 | tf_op jit(solution)/shard_map/ppermute | solution.py:153
  29.3 0.4 collective-permute-start.6
  29.7 0.7 %collective-permute-start.5 = (f32[256,128]{1,0:T(8,128)S(1)}, f32[256,128]{1,0:T(8,128)S(1)}, u32[]{:S(2)}, u32[]{:S(2)}) collective-permute-start(f32[256,128]{1,0:T(8,128)S(1)} %get-tuple-element.27), channel_id=1, source_target_pairs={{0,0},{2,5},{1,10},{3,15},{4,4},{6,9},{5,14},{7,3},{8,8},{10,13},{... | collective-permute-start | bytes 393224 | tf_op jit(solution)/shard_map/ppermute | solution.py:153
  30.4 0.8 %collective-permute-done.8.refs_3_ = f32[256,128]{1,0:T(8,128)S(1)} collective-permute-done((f32[256,128]{1,0:T(8,128)S(1)}, f32[256,128]{1,0:T(8,128)S(1)}, u32[]{:S(2)}, u32[]{:S(2)}) %collective-permute-start.8) | collective-permute-done | bytes 131104 | tf_op jit(solution)/shard_map/ppermute | solution.py:153
  31.2 2.0 %collective-permute-done.7.refs_2_ = f32[256,128]{1,0:T(8,128)S(1)} collective-permute-done((f32[256,128]{1,0:T(8,128)S(1)}, f32[256,128]{1,0:T(8,128)S(1)}, u32[]{:S(2)}, u32[]{:S(2)}) %collective-permute-start.7) | collective-permute-done | bytes 131104 | tf_op jit(solution)/shard_map/ppermute | solution.py:153
  33.2 2.7 %collective-permute-done.6.refs_1_ = f32[256,128]{1,0:T(8,128)S(1)} collective-permute-done((f32[256,128]{1,0:T(8,128)S(1)}, f32[256,128]{1,0:T(8,128)S(1)}, u32[]{:S(2)}, u32[]{:S(2)}) %collective-permute-start.6) | collective-permute-done | bytes 131104 | tf_op jit(solution)/shard_map/ppermute | solution.py:153
  35.9 0.8 %shard_map.66 = (f32[256,128]{1,0:T(8,128)S(1)}, f32[256,128]{1,0:T(8,128)S(1)}, f32[256,128]{1,0:T(8,128)S(1)}, f32[256,128]{1,0:T(8,128)S(1)}) custom-call(s32[49,128]{1,0:T(8,128)S(1)} %squeeze.19.after_ref.info_ref, bf16[24,128,128]{2,1,0:T(8,128)(2,1)S(1)} %bitcast.10, f32[256,128]{1,0:T(8,128)S(1)} %collective-permute-done.5.refs_0_, ...), custom_call_target="tpu_custom_call" | custom-call | flops 201326592 | bytes 1048576 | tf_op jit(solution)/shard_map/pallas_call | solution.py:124
  36.7 4.3 %collective-permute-start.10 = (f32[256,128]{1,0:T(8,128)S(1)}, f32[256,128]{1,0:T(8,128)S(1)}, u32[]{:S(2)}, u32[]{:S(2)}) collective-permute-start(f32[256,128]{1,0:T(8,128)S(1)} %get-tuple-element.26), channel_id=1, source_target_pairs={{0,1},{1,0},{2,3},{3,2},{4,5},{5,4},{6,7},{7,6},{8,9},{9,8},{10,11... | collective-permute-start | bytes 393224 | tf_op jit(solution)/shard_map/ppermute | solution.py:163
  41.0 0.1 collective-permute-start.9
  41.0 0.9 %collective-permute-done.10 = f32[256,128]{1,0:T(8,128)S(1)} collective-permute-done((f32[256,128]{1,0:T(8,128)S(1)}, f32[256,128]{1,0:T(8,128)S(1)}, u32[]{:S(2)}, u32[]{:S(2)}) %collective-permute-start.10) | collective-permute-done | bytes 131104 | tf_op jit(solution)/shard_map/ppermute | solution.py:163
  42.0 3.5 %collective-permute-start.11 = (f32[256,128]{1,0:T(8,128)S(1)}, f32[256,128]{1,0:T(8,128)S(1)}, u32[]{:S(2)}, u32[]{:S(2)}) collective-permute-start(f32[256,128]{1,0:T(8,128)S(1)} %add.19), channel_id=1, source_target_pairs={{2,0},{3,1},{0,2},{1,3},{6,4},{7,5},{4,6},{5,7},{10,8},{11,9},{8,1... | collective-permute-start | bytes 393224 | tf_op jit(solution)/shard_map/ppermute | solution.py:169
  45.5 3.8 %collective-permute-done.11.refs_2_ = f32[256,128]{1,0:T(8,128)S(1)} collective-permute-done((f32[256,128]{1,0:T(8,128)S(1)}, f32[256,128]{1,0:T(8,128)S(1)}, u32[]{:S(2)}, u32[]{:S(2)}) %collective-permute-start.11) | collective-permute-done | bytes 131104 | tf_op jit(solution)/shard_map/ppermute | solution.py:169
  49.3 0.7 %shard_map.67 = f32[256,128]{1,0:T(8,128)} custom-call(f32[256,128]{1,0:T(8,128)S(1)} %get-tuple-element.28.base_ref, f32[256,128]{1,0:T(8,128)S(1)} %get-tuple-element.22.norm_ref, f32[256,128]{1,0:T(8,128)S(1)} %get-tuple-element.23.refs_0_, f32[256,128]{1,0:T(8,128)S(1)} %collective-permute-done.9.refs_1_, f32[256,128]{1,0:T(8,128)S(1)} %collective-permute-done.11.refs_2_), custom_call_target="tpu_custom_call" | custom-call | tf_op jit(solution)/shard_map/pallas_call | solution.py:199
  (11 shorter events, 0.1 us)
Async XLA Ops:
  0.0 14.6 %collective-permute-start.1 = (f32[1024,128]{1,0:T(8,128)}, f32[1024,128]{1,0:T(8,128)S(1)}, u32[]{:S(2)}, u32[]{:S(2)}) collective-permute-start(f32[1024,128]{1,0:T(8,128)} %embeddings_ref.1), channel_id=1, source_target_pairs={{3,0},{1,5},{2,10},{0,15},{7,4},{5,9},{6,14},{4,3},{11,8},{9,13},{... | collective-permute-start | bytes 1572872 | tf_op jit(solution)/shard_map/ppermute | solution.py:153
  5.4 9.2 %collective-permute-start = (s32[8,128]{1,0:T(8,128)}, s32[8,128]{1,0:T(8,128)S(1)}, u32[]{:S(2)}, u32[]{:S(2)}) collective-permute-start(s32[8,128]{1,0:T(8,128)} %bitcast.12), channel_id=1, source_target_pairs={{3,0},{1,5},{2,10},{0,15},{7,4},{5,9},{6,14},{4,3},{11,8},{9,13},{... | collective-permute-start | bytes 12296 | tf_op jit(solution)/shard_map/ppermute | solution.py:153
  6.9 0.7 %copy-start.3 = (s32[1,1,1,24]{3,2,1,0:T(1,128)S(1)}, s32[1,1,1,24]{3,2,1,0:T(1,128)}, u32[]{:S(2)}) copy-start(s32[1,1,1,24]{3,2,1,0:T(1,128)} %param.10) | copy-start | bytes 292
  6.9 0.7 %copy-start.4 = (s32[1,1,1,24]{3,2,1,0:T(1,128)S(1)}, s32[1,1,1,24]{3,2,1,0:T(1,128)}, u32[]{:S(2)}) copy-start(s32[1,1,1,24]{3,2,1,0:T(1,128)} %param.9) | copy-start | bytes 292
  7.6 0.7 %copy-start.2 = (s32[1024]{0:T(1024)S(1)}, s32[1024]{0:T(1024)}, u32[]{:S(2)}) copy-start(s32[1024]{0:T(1024)} %param.7) | copy-start | bytes 12292
  8.3 1.1 %copy-start = (bf16[1,1,1,24,128,128]{5,4,3,2,1,0:T(8,128)(2,1)S(1)}, bf16[1,1,1,24,128,128]{5,4,3,2,1,0:T(8,128)(2,1)}, u32[]{:S(2)}) copy-start(bf16[1,1,1,24,128,128]{5,4,3,2,1,0:T(8,128)(2,1)} %param.8) | copy-start | bytes 2359300
  9.5 1.0 %copy-start.1 = (f32[1024,128]{1,0:T(8,128)S(1)}, f32[1024,128]{1,0:T(8,128)}, u32[]{:S(2)}) copy-start(f32[1024,128]{1,0:T(8,128)} %embeddings_ref.1) | copy-start | bytes 1572868
  15.6 1.8 %collective-permute-start.3 = (f32[256,128]{1,0:T(8,128)S(1)}, f32[256,128]{1,0:T(8,128)S(1)}, u32[]{:S(2)}, u32[]{:S(2)}) collective-permute-start(f32[256,128]{1,0:T(8,128)S(1)} %get-tuple-element.21), channel_id=1, source_target_pairs={{0,1},{1,0},{2,3},{3,2},{4,5},{5,4},{6,7},{7,6},{8,9},{9,8},{10,11... | collective-permute-start | bytes 393224 | tf_op jit(solution)/shard_map/ppermute | solution.py:163
  16.4 5.0 %collective-permute-start.2 = (f32[256,128]{1,0:T(8,128)S(1)}, f32[256,128]{1,0:T(8,128)S(1)}, u32[]{:S(2)}, u32[]{:S(2)}) collective-permute-start(f32[256,128]{1,0:T(8,128)S(1)} %get-tuple-element.19), channel_id=1, source_target_pairs={{0,1},{1,0},{2,3},{3,2},{4,5},{5,4},{6,7},{7,6},{8,9},{9,8},{10,11... | collective-permute-start | bytes 393224 | tf_op jit(solution)/shard_map/ppermute | solution.py:163
  17.4 7.8 %collective-permute-start.4 = (f32[256,128]{1,0:T(8,128)S(1)}, f32[256,128]{1,0:T(8,128)S(1)}, u32[]{:S(2)}, u32[]{:S(2)}) collective-permute-start(f32[256,128]{1,0:T(8,128)S(1)} %add.16), channel_id=1, source_target_pairs={{2,0},{3,1},{0,2},{1,3},{6,4},{7,5},{4,6},{5,7},{10,8},{11,9},{8,1... | collective-permute-start | bytes 393224 | tf_op jit(solution)/shard_map/ppermute | solution.py:169
  25.3 5.9 %collective-permute-start.8 = (f32[256,128]{1,0:T(8,128)S(1)}, f32[256,128]{1,0:T(8,128)S(1)}, u32[]{:S(2)}, u32[]{:S(2)}) collective-permute-start(f32[256,128]{1,0:T(8,128)S(1)} %get-tuple-element.27), channel_id=1, source_target_pairs={{2,0},{0,5},{3,10},{1,15},{6,4},{4,9},{7,14},{5,3},{10,8},{8,13},{... | collective-permute-start | bytes 393224 | tf_op jit(solution)/shard_map/ppermute | solution.py:153
  25.4 7.9 %collective-permute-start.7 = (f32[256,128]{1,0:T(8,128)S(1)}, f32[256,128]{1,0:T(8,128)S(1)}, u32[]{:S(2)}, u32[]{:S(2)}) collective-permute-start(f32[256,128]{1,0:T(8,128)S(1)} %get-tuple-element.27), channel_id=1, source_target_pairs={{3,0},{1,5},{2,10},{0,15},{7,4},{5,9},{6,14},{4,3},{11,8},{9,13},{... | collective-permute-start | bytes 393224 | tf_op jit(solution)/shard_map/ppermute | solution.py:153
  29.3 6.6 %collective-permute-start.6 = (f32[256,128]{1,0:T(8,128)S(1)}, f32[256,128]{1,0:T(8,128)S(1)}, u32[]{:S(2)}, u32[]{:S(2)}) collective-permute-start(f32[256,128]{1,0:T(8,128)S(1)} %get-tuple-element.27), channel_id=1, source_target_pairs={{1,0},{3,5},{0,10},{2,15},{5,4},{7,9},{4,14},{6,3},{9,8},{11,13},{... | collective-permute-start | bytes 393224 | tf_op jit(solution)/shard_map/ppermute | solution.py:153
  29.7 6.2 %collective-permute-start.5 = (f32[256,128]{1,0:T(8,128)S(1)}, f32[256,128]{1,0:T(8,128)S(1)}, u32[]{:S(2)}, u32[]{:S(2)}) collective-permute-start(f32[256,128]{1,0:T(8,128)S(1)} %get-tuple-element.27), channel_id=1, source_target_pairs={{0,0},{2,5},{1,10},{3,15},{4,4},{6,9},{5,14},{7,3},{8,8},{10,13},{... | collective-permute-start | bytes 393224 | tf_op jit(solution)/shard_map/ppermute | solution.py:153
  36.7 5.3 %collective-permute-start.10 = (f32[256,128]{1,0:T(8,128)S(1)}, f32[256,128]{1,0:T(8,128)S(1)}, u32[]{:S(2)}, u32[]{:S(2)}) collective-permute-start(f32[256,128]{1,0:T(8,128)S(1)} %get-tuple-element.26), channel_id=1, source_target_pairs={{0,1},{1,0},{2,3},{3,2},{4,5},{5,4},{6,7},{7,6},{8,9},{9,8},{10,11... | collective-permute-start | bytes 393224 | tf_op jit(solution)/shard_map/ppermute | solution.py:163
  41.0 4.5 %collective-permute-start.9 = (f32[256,128]{1,0:T(8,128)S(1)}, f32[256,128]{1,0:T(8,128)S(1)}, u32[]{:S(2)}, u32[]{:S(2)}) collective-permute-start(f32[256,128]{1,0:T(8,128)S(1)} %get-tuple-element.24), channel_id=1, source_target_pairs={{0,1},{1,0},{2,3},{3,2},{4,5},{5,4},{6,7},{7,6},{8,9},{9,8},{10,11... | collective-permute-start | bytes 393224 | tf_op jit(solution)/shard_map/ppermute | solution.py:163
  42.0 7.3 %collective-permute-start.11 = (f32[256,128]{1,0:T(8,128)S(1)}, f32[256,128]{1,0:T(8,128)S(1)}, u32[]{:S(2)}, u32[]{:S(2)}) collective-permute-start(f32[256,128]{1,0:T(8,128)S(1)} %add.19), channel_id=1, source_target_pairs={{2,0},{3,1},{0,2},{1,3},{6,4},{7,5},{4,6},{5,7},{10,8},{11,9},{8,1... | collective-permute-start | bytes 393224 | tf_op jit(solution)/shard_map/ppermute | solution.py:169

commit v14 on v13

--- a/solution.py
+++ b/solution.py
@@ -18,9 +18,10 @@
     return 2 * lax.rem(team_index // 2 + column, columns) + lax.rem(team_index, 2)
 
 
-def source_team(team, turn, team_count):
+def source_team(shard, team, turn, cycle, team_count):
     if team_count == 4:
-        return (2 * (team % 2) + team // 2) ^ (0, 1, 3, 2)[turn]
+        lower, upper = (0, 1, 3, 2)[turn], (3, 1, 0, 2)[turn]
+        return (2 * (team % 2) + team // 2) ^ lower ^ ((shard >= cycle // 2) * (lower ^ upper))
     return (team + turn) % team_count
 
 
@@ -66,7 +67,7 @@
     )(degrees, embeddings, tile_values, after)
 
 
-def arc_kernel(info_ref, tiles_ref, *refs, team_count, piece_count, scaled, partial_count):
+def arc_kernel(info_ref, tiles_ref, *refs, team_count, arc_length, arc_slot, piece_count, scaled, partial_count):
     columns = team_count // 2
     pieces, refs = refs[:piece_count], refs[piece_count:]
     partials, refs = refs[:partial_count], refs[partial_count:]
@@ -89,8 +90,10 @@
             at = pl.ds(block * tile_size, tile_size)
             split(panel_ref[at, :] * norms[:, block : block + 1], at)
     else:
+        cycle = lax.axis_size("blk")
+        shard = lax.rem(lax.axis_index("blk") + cycle - lax.rem(team_index * arc_length + arc_slot, cycle), cycle)
         for k in range(piece_count):
-            owner = source_team(team_index, k, team_count)
+            owner = source_team(shard, team_index, k, cycle, team_count)
             split(pieces[k][...], pl.ds(pl.multiple_of(owner * share_rows, share_rows), share_rows))
     sums_ref[...] = jnp.zeros_like(sums_ref)
     live_count = info_ref[0, 0]
@@ -114,7 +117,7 @@
             outs[at][...] = value + partials[at][...] if partials else value
 
 
-def arc_step(info, tiles, pieces, partials, scaled):
+def arc_step(info, tiles, pieces, partials, scaled, arc_length, arc_slot):
     team_count = lax.axis_size("rep")
     panel_rows = pieces[1].shape[0] if scaled else sum(piece.shape[0] for piece in pieces)
     width = pieces[1].shape[1]
@@ -125,6 +128,8 @@
         functools.partial(
             arc_kernel,
             team_count=team_count,
+            arc_length=arc_length,
+            arc_slot=arc_slot,
             piece_count=len(pieces),
             scaled=scaled,
             partial_count=len(partials),
@@ -143,13 +148,13 @@
     )(*operands)
 
 
-def fetch(value, source_team, arc_length):
+def fetch(value, source, arc_length):
     cycle, team_count = lax.axis_size("blk"), lax.axis_size("rep")
     pairs = []
     for shard in range(cycle):
         for team in range(team_count):
             to_shard = (shard + team * arc_length) % cycle
-            pairs.append((shard * team_count + source_team(team), to_shard * team_count + team))
+            pairs.append((shard * team_count + source(shard, team), to_shard * team_count + team))
     return lax.ppermute(value, ("blk", "rep"), pairs)
 
 
@@ -209,12 +214,12 @@
 def per_device(embeddings, degrees, tile_values, tile_rows, tile_columns, slot_counts):
     arc_length, _, tile_size, _ = tile_values.shape[2:]
     panel_rows = embeddings.shape[0]
-    team_count = lax.axis_size("rep")
+    cycle, team_count = lax.axis_size("blk"), lax.axis_size("rep")
     spread = (3, 1, 2, 0) if team_count == 4 else tuple(range(team_count))
     degrees = degrees.reshape(panel_rows // tile_size, tile_size)
 
-    panel = fetch(embeddings, lambda team: spread[team], arc_length)
-    pieces = [fetch(degrees, lambda team: spread[team], arc_length), panel]
+    panel = fetch(embeddings, lambda shard, team: spread[team], arc_length)
+    pieces = [fetch(degrees, lambda shard, team: spread[team], arc_length), panel]
     info = jnp.concatenate([slot_counts[0, 0][:, None], tile_rows[0, 0], tile_columns[0, 0]], axis=1)
     info = jnp.broadcast_to(info[:, :, None], (*info.shape, embeddings.shape[1]))
     info = [info[at] for at in range(arc_length)]
@@ -224,7 +229,7 @@
     for layer in range(LAYERS):
         sums = ()
         for arc_slot in range(arc_length):
-            sums = arc_step(info[arc_slot], tiles[arc_slot], pieces, sums, layer == 0)
+            sums = arc_step(info[arc_slot], tiles[arc_slot], pieces, sums, layer == 0, arc_length, arc_slot)
             if arc_slot + 1 < arc_length:
                 pieces = [next_shard(piece) for piece in pieces]
         terms = team_terms(sums)
@@ -234,7 +239,7 @@
         combined = combined + current
         source = current * norm_scale
         pieces = [
-            fetch(source, lambda team, k=k: source_team(team, k, team_count), arc_length)
+            fetch(source, lambda shard, team, k=k: source_team(shard, team, k, cycle, team_count), arc_length)
             for k in range(team_count)
         ]
 

time: 50.2 us -> 50.7 us (level)
  starting transfers between devices: 24.1 us -> 26.6 us
  waiting for transfers between devices: 18.5 us -> 16.3 us
    ppermute x6, waiting for transfers between devices: 9.04 us -> 6.88 us  [fetch(): return lax.ppermute(value, ('blk', 'rep'), pairs)]
    ppermute x6, starting transfers between devices: 11.3 us -> 13.1 us  [fetch(): return lax.ppermute(value, ('blk', 'rep'), pairs)]
    ppermute x4, starting transfers between devices: 5.25 us -> 5.87 us  [from_mate(): lax.ppermute(value, 'rep', [(team, team ^ 1) for team in range(team_count)])]
  transfers between devices with their start and end apart: 12 -> 12, of which waited for: 8 -> 7; matrix products, arithmetic and copies ran while one was open for 0% -> 0% of each run, Pallas kernels for 1% -> 1%
where the time goes in v14:
time: 50.7 us; the launch traced here: 50.4 us
  starting transfers between devices  26.6 us (52%)
  waiting for transfers between devices  16.3 us (32%)
  local copies, waits for them, and re-layouts  3.52 us (7%)
  Pallas kernels  3.04 us (6%)
  between operations  0.74 us (1%)
    ppermute x6, starting transfers between devices, fetch(): return lax.ppermute(value, ('blk', 'rep'), pairs)  13.1 us
    ppermute x2, starting transfers between devices, from_column(): return lax.ppermute(value, 'rep', pairs)  7.63 us
    ppermute x2, waiting for transfers between devices, from_column(): return lax.ppermute(value, 'rep', pairs)  7.61 us
    ppermute x6, waiting for transfers between devices, fetch(): return lax.ppermute(value, ('blk', 'rep'), pairs)  6.88 us
    ppermute x4, starting transfers between devices, from_mate(): lax.ppermute(value, 'rep', [(team, team ^ 1) for team in range(team_count)])  5.87 us
    unnamed x10, local copies, waits for them, and re-layouts  3.44 us
    ppermute x4, waiting for transfers between devices, from_mate(): lax.ppermute(value, 'rep', [(team, team ^ 1) for team in range(team_count)])  1.82 us
    pallas_call x2, Pallas kernels, arc_step(): pl.pallas_call(functools.partial(arc_kernel, team_count=team_count, arc_l...  1.77 us
  transfers between devices with their start and end apart: 12, of which 7 were waited for; matrix products, arithmetic and copies ran while one was open for 0% of the time, Pallas kernels for 1%

profile of v14, /device:TPU:0, one launch (start us, length us, event | category | flops | bytes accessed | tf_op | source)
XLA Modules:
  0.0 50.4 jit_solution(13614540949056153792)
XLA Ops:
  0.0 5.4 %collective-permute-start.1 = (f32[1024,128]{1,0:T(8,128)}, f32[1024,128]{1,0:T(8,128)S(1)}, u32[]{:S(2)}, u32[]{:S(2)}) collective-permute-start(f32[1024,128]{1,0:T(8,128)} %embeddings_ref.1), channel_id=1, source_target_pairs={{3,0},{1,5},{2,10},{0,15},{7,4},{5,9},{6,14},{4,3},{11,8},{9,13},{... | collective-permute-start | bytes 1572872 | tf_op jit(solution)/shard_map/ppermute | solution.py:158
  5.4 0.8 %collective-permute-start = (s32[8,128]{1,0:T(8,128)}, s32[8,128]{1,0:T(8,128)S(1)}, u32[]{:S(2)}, u32[]{:S(2)}) collective-permute-start(s32[8,128]{1,0:T(8,128)} %bitcast.12), channel_id=1, source_target_pairs={{3,0},{1,5},{2,10},{0,15},{7,4},{5,9},{6,14},{4,3},{11,8},{9,13},{... | collective-permute-start | bytes 12296 | tf_op jit(solution)/shard_map/ppermute | solution.py:158
  6.9 0.6 %copy-done.3 = s32[1,1,1,24]{3,2,1,0:T(1,128)S(1)} copy-done((s32[1,1,1,24]{3,2,1,0:T(1,128)S(1)}, s32[1,1,1,24]{3,2,1,0:T(1,128)}, u32[]{:S(2)}) %copy-start.3) | copy-done | bytes 120
  7.5 0.0 copy-done.4
  7.6 0.1 add_bitcast_fusion
  7.6 0.1 squeeze.19.after_ref.info_ref
  7.7 0.6 %copy-done.2 = s32[1024]{0:T(1024)S(1)} copy-done((s32[1024]{0:T(1024)S(1)}, s32[1024]{0:T(1024)}, u32[]{:S(2)}) %copy-start.2) | copy-done | bytes 4120
  8.3 1.1 %copy-done = bf16[1,1,1,24,128,128]{5,4,3,2,1,0:T(8,128)(2,1)S(1)} copy-done((bf16[1,1,1,24,128,128]{5,4,3,2,1,0:T(8,128)(2,1)S(1)}, bf16[1,1,1,24,128,128]{5,4,3,2,1,0:T(8,128)(2,1)}, u32[]{:S(2)}) %copy-start) | copy-done | bytes 786456
  9.5 1.0 %copy-done.1 = f32[1024,128]{1,0:T(8,128)S(1)} copy-done((f32[1024,128]{1,0:T(8,128)S(1)}, f32[1024,128]{1,0:T(8,128)}, u32[]{:S(2)}) %copy-start.1) | copy-done | bytes 524312
  10.5 0.6 %shard_map.64 = (bf16[1,24,128,128]{3,2,1,0:T(8,128)(2,1)S(1)}, f32[256,128]{1,0:T(8,128)S(1)}, f32[256,128]{1,0:T(8,128)S(1)}) custom-call(s32[8,128]{1,0:T(8,128)S(1)} %bitcast.13, f32[1024,128]{1,0:T(8,128)S(1)} %copy-done.1, bf16[1,24,128,128]{3,2,1,0:T(8,128)(2,1)S(1)} %bitcast.11, s32[49,128]{1,0:T(8,128)S(1)} %squeeze.19.after_ref.info_ref), custom_call_target="tpu_custom_call" | custom-call | flops 131072 | bytes 524288 | tf_op jit(solution)/shard_map/pallas_call | solution.py:57
  11.1 3.5 %collective-permute-done.refs_0_ = s32[8,128]{1,0:T(8,128)S(1)} collective-permute-done((s32[8,128]{1,0:T(8,128)}, s32[8,128]{1,0:T(8,128)S(1)}, u32[]{:S(2)}, u32[]{:S(2)}) %collective-permute-start) | collective-permute-done | bytes 4128 | tf_op jit(solution)/shard_map/ppermute | solution.py:158
  14.6 1.0 %shard_map.65 = (f32[256,128]{1,0:T(8,128)S(1)}, f32[256,128]{1,0:T(8,128)S(1)}, f32[256,128]{1,0:T(8,128)S(1)}, f32[256,128]{1,0:T(8,128)S(1)}) custom-call(s32[49,128]{1,0:T(8,128)S(1)} %squeeze.19.after_ref.info_ref, bf16[24,128,128]{2,1,0:T(8,128)(2,1)S(1)} %bitcast.9, s32[8,128]{1,0:T(8,128)S(1)} %collective-permute-done.refs_0_, ...), custom_call_target="tpu_custom_call" | custom-call | flops 201326592 | bytes 1048576 | tf_op jit(solution)/shard_map/pallas_call | solution.py:127
  15.6 0.8 %collective-permute-start.3 = (f32[256,128]{1,0:T(8,128)S(1)}, f32[256,128]{1,0:T(8,128)S(1)}, u32[]{:S(2)}, u32[]{:S(2)}) collective-permute-start(f32[256,128]{1,0:T(8,128)S(1)} %get-tuple-element.21), channel_id=1, source_target_pairs={{0,1},{1,0},{2,3},{3,2},{4,5},{5,4},{6,7},{7,6},{8,9},{9,8},{10,11... | collective-permute-start | bytes 393224 | tf_op jit(solution)/shard_map/ppermute | solution.py:168
  16.4 0.1 collective-permute-start.2
  16.5 0.9 %collective-permute-done.3 = f32[256,128]{1,0:T(8,128)S(1)} collective-permute-done((f32[256,128]{1,0:T(8,128)S(1)}, f32[256,128]{1,0:T(8,128)S(1)}, u32[]{:S(2)}, u32[]{:S(2)}) %collective-permute-start.3) | collective-permute-done | bytes 131104 | tf_op jit(solution)/shard_map/ppermute | solution.py:168
  17.4 4.0 %collective-permute-start.4 = (f32[256,128]{1,0:T(8,128)S(1)}, f32[256,128]{1,0:T(8,128)S(1)}, u32[]{:S(2)}, u32[]{:S(2)}) collective-permute-start(f32[256,128]{1,0:T(8,128)S(1)} %add.16), channel_id=1, source_target_pairs={{2,0},{3,1},{0,2},{1,3},{6,4},{7,5},{4,6},{5,7},{10,8},{11,9},{8,1... | collective-permute-start | bytes 393224 | tf_op jit(solution)/shard_map/ppermute | solution.py:174
  21.4 3.8 %collective-permute-done.4 = f32[256,128]{1,0:T(8,128)S(1)} collective-permute-done((f32[256,128]{1,0:T(8,128)S(1)}, f32[256,128]{1,0:T(8,128)S(1)}, u32[]{:S(2)}, u32[]{:S(2)}) %collective-permute-start.4) | collective-permute-done | bytes 131104 | tf_op jit(solution)/shard_map/ppermute | solution.py:174
  25.3 0.1 collective-permute-start.8
  25.4 5.9 %collective-permute-start.7 = (f32[256,128]{1,0:T(8,128)S(1)}, f32[256,128]{1,0:T(8,128)S(1)}, u32[]{:S(2)}, u32[]{:S(2)}) collective-permute-start(f32[256,128]{1,0:T(8,128)S(1)} %get-tuple-element.27), channel_id=1, source_target_pairs={{3,0},{1,5},{2,10},{0,15},{7,4},{5,9},{6,14},{4,3},{8,8},{10,13},{... | collective-permute-start | bytes 393224 | tf_op jit(solution)/shard_map/ppermute | solution.py:158
  31.2 0.3 collective-permute-start.6
  31.5 0.7 %collective-permute-start.5 = (f32[256,128]{1,0:T(8,128)S(1)}, f32[256,128]{1,0:T(8,128)S(1)}, u32[]{:S(2)}, u32[]{:S(2)}) collective-permute-start(f32[256,128]{1,0:T(8,128)S(1)} %get-tuple-element.27), channel_id=1, source_target_pairs={{0,0},{2,5},{1,10},{3,15},{4,4},{6,9},{5,14},{7,3},{11,8},{9,13},{... | collective-permute-start | bytes 393224 | tf_op jit(solution)/shard_map/ppermute | solution.py:158
  32.2 1.9 %collective-permute-done.7.refs_2_ = f32[256,128]{1,0:T(8,128)S(1)} collective-permute-done((f32[256,128]{1,0:T(8,128)S(1)}, f32[256,128]{1,0:T(8,128)S(1)}, u32[]{:S(2)}, u32[]{:S(2)}) %collective-permute-start.7) | collective-permute-done | bytes 131104 | tf_op jit(solution)/shard_map/ppermute | solution.py:158
  34.1 1.4 %collective-permute-done.6.refs_1_ = f32[256,128]{1,0:T(8,128)S(1)} collective-permute-done((f32[256,128]{1,0:T(8,128)S(1)}, f32[256,128]{1,0:T(8,128)S(1)}, u32[]{:S(2)}, u32[]{:S(2)}) %collective-permute-start.6) | collective-permute-done | bytes 131104 | tf_op jit(solution)/shard_map/ppermute | solution.py:158
  35.5 0.0 collective-permute-done.5.refs_0_
  35.5 0.8 %shard_map.66 = (f32[256,128]{1,0:T(8,128)S(1)}, f32[256,128]{1,0:T(8,128)S(1)}, f32[256,128]{1,0:T(8,128)S(1)}, f32[256,128]{1,0:T(8,128)S(1)}) custom-call(s32[49,128]{1,0:T(8,128)S(1)} %squeeze.19.after_ref.info_ref, bf16[24,128,128]{2,1,0:T(8,128)(2,1)S(1)} %bitcast.10, f32[256,128]{1,0:T(8,128)S(1)} %collective-permute-done.5.refs_0_, ...), custom_call_target="tpu_custom_call" | custom-call | flops 201326592 | bytes 1048576 | tf_op jit(solution)/shard_map/pallas_call | solution.py:127
  36.3 4.9 %collective-permute-start.10 = (f32[256,128]{1,0:T(8,128)S(1)}, f32[256,128]{1,0:T(8,128)S(1)}, u32[]{:S(2)}, u32[]{:S(2)}) collective-permute-start(f32[256,128]{1,0:T(8,128)S(1)} %get-tuple-element.26), channel_id=1, source_target_pairs={{0,1},{1,0},{2,3},{3,2},{4,5},{5,4},{6,7},{7,6},{8,9},{9,8},{10,11... | collective-permute-start | bytes 393224 | tf_op jit(solution)/shard_map/ppermute | solution.py:168
  41.3 0.1 collective-permute-start.9
  41.3 0.9 %collective-permute-done.10 = f32[256,128]{1,0:T(8,128)S(1)} collective-permute-done((f32[256,128]{1,0:T(8,128)S(1)}, f32[256,128]{1,0:T(8,128)S(1)}, u32[]{:S(2)}, u32[]{:S(2)}) %collective-permute-start.10) | collective-permute-done | bytes 131104 | tf_op jit(solution)/shard_map/ppermute | solution.py:168
  42.3 3.6 %collective-permute-start.11 = (f32[256,128]{1,0:T(8,128)S(1)}, f32[256,128]{1,0:T(8,128)S(1)}, u32[]{:S(2)}, u32[]{:S(2)}) collective-permute-start(f32[256,128]{1,0:T(8,128)S(1)} %add.19), channel_id=1, source_target_pairs={{2,0},{3,1},{0,2},{1,3},{6,4},{7,5},{4,6},{5,7},{10,8},{11,9},{8,1... | collective-permute-start | bytes 393224 | tf_op jit(solution)/shard_map/ppermute | solution.py:174
  45.9 0.0 collective-permute-done.9.refs_1_
  45.9 3.8 %collective-permute-done.11.refs_2_ = f32[256,128]{1,0:T(8,128)S(1)} collective-permute-done((f32[256,128]{1,0:T(8,128)S(1)}, f32[256,128]{1,0:T(8,128)S(1)}, u32[]{:S(2)}, u32[]{:S(2)}) %collective-permute-start.11) | collective-permute-done | bytes 131104 | tf_op jit(solution)/shard_map/ppermute | solution.py:174
  49.7 0.7 %shard_map.67 = f32[256,128]{1,0:T(8,128)} custom-call(f32[256,128]{1,0:T(8,128)S(1)} %get-tuple-element.28.base_ref, f32[256,128]{1,0:T(8,128)S(1)} %get-tuple-element.22.norm_ref, f32[256,128]{1,0:T(8,128)S(1)} %get-tuple-element.23.refs_0_, f32[256,128]{1,0:T(8,128)S(1)} %collective-permute-done.9.refs_1_, f32[256,128]{1,0:T(8,128)S(1)} %collective-permute-done.11.refs_2_), custom_call_target="tpu_custom_call" | custom-call | tf_op jit(solution)/shard_map/pallas_call | solution.py:204
  (11 shorter events, 0.1 us)
Async XLA Ops:
  0.0 14.6 %collective-permute-start.1 = (f32[1024,128]{1,0:T(8,128)}, f32[1024,128]{1,0:T(8,128)S(1)}, u32[]{:S(2)}, u32[]{:S(2)}) collective-permute-start(f32[1024,128]{1,0:T(8,128)} %embeddings_ref.1), channel_id=1, source_target_pairs={{3,0},{1,5},{2,10},{0,15},{7,4},{5,9},{6,14},{4,3},{11,8},{9,13},{... | collective-permute-start | bytes 1572872 | tf_op jit(solution)/shard_map/ppermute | solution.py:158
  5.4 9.2 %collective-permute-start = (s32[8,128]{1,0:T(8,128)}, s32[8,128]{1,0:T(8,128)S(1)}, u32[]{:S(2)}, u32[]{:S(2)}) collective-permute-start(s32[8,128]{1,0:T(8,128)} %bitcast.12), channel_id=1, source_target_pairs={{3,0},{1,5},{2,10},{0,15},{7,4},{5,9},{6,14},{4,3},{11,8},{9,13},{... | collective-permute-start | bytes 12296 | tf_op jit(solution)/shard_map/ppermute | solution.py:158
  6.9 0.7 %copy-start.3 = (s32[1,1,1,24]{3,2,1,0:T(1,128)S(1)}, s32[1,1,1,24]{3,2,1,0:T(1,128)}, u32[]{:S(2)}) copy-start(s32[1,1,1,24]{3,2,1,0:T(1,128)} %param.10) | copy-start | bytes 292
  6.9 0.7 %copy-start.4 = (s32[1,1,1,24]{3,2,1,0:T(1,128)S(1)}, s32[1,1,1,24]{3,2,1,0:T(1,128)}, u32[]{:S(2)}) copy-start(s32[1,1,1,24]{3,2,1,0:T(1,128)} %param.9) | copy-start | bytes 292
  7.6 0.7 %copy-start.2 = (s32[1024]{0:T(1024)S(1)}, s32[1024]{0:T(1024)}, u32[]{:S(2)}) copy-start(s32[1024]{0:T(1024)} %param.7) | copy-start | bytes 12292
  8.3 1.1 %copy-start = (bf16[1,1,1,24,128,128]{5,4,3,2,1,0:T(8,128)(2,1)S(1)}, bf16[1,1,1,24,128,128]{5,4,3,2,1,0:T(8,128)(2,1)}, u32[]{:S(2)}) copy-start(bf16[1,1,1,24,128,128]{5,4,3,2,1,0:T(8,128)(2,1)} %param.8) | copy-start | bytes 2359300
  9.5 1.0 %copy-start.1 = (f32[1024,128]{1,0:T(8,128)S(1)}, f32[1024,128]{1,0:T(8,128)}, u32[]{:S(2)}) copy-start(f32[1024,128]{1,0:T(8,128)} %embeddings_ref.1) | copy-start | bytes 1572868
  15.6 1.8 %collective-permute-start.3 = (f32[256,128]{1,0:T(8,128)S(1)}, f32[256,128]{1,0:T(8,128)S(1)}, u32[]{:S(2)}, u32[]{:S(2)}) collective-permute-start(f32[256,128]{1,0:T(8,128)S(1)} %get-tuple-element.21), channel_id=1, source_target_pairs={{0,1},{1,0},{2,3},{3,2},{4,5},{5,4},{6,7},{7,6},{8,9},{9,8},{10,11... | collective-permute-start | bytes 393224 | tf_op jit(solution)/shard_map/ppermute | solution.py:168
  16.4 5.0 %collective-permute-start.2 = (f32[256,128]{1,0:T(8,128)S(1)}, f32[256,128]{1,0:T(8,128)S(1)}, u32[]{:S(2)}, u32[]{:S(2)}) collective-permute-start(f32[256,128]{1,0:T(8,128)S(1)} %get-tuple-element.19), channel_id=1, source_target_pairs={{0,1},{1,0},{2,3},{3,2},{4,5},{5,4},{6,7},{7,6},{8,9},{9,8},{10,11... | collective-permute-start | bytes 393224 | tf_op jit(solution)/shard_map/ppermute | solution.py:168
  17.4 7.8 %collective-permute-start.4 = (f32[256,128]{1,0:T(8,128)S(1)}, f32[256,128]{1,0:T(8,128)S(1)}, u32[]{:S(2)}, u32[]{:S(2)}) collective-permute-start(f32[256,128]{1,0:T(8,128)S(1)} %add.16), channel_id=1, source_target_pairs={{2,0},{3,1},{0,2},{1,3},{6,4},{7,5},{4,6},{5,7},{10,8},{11,9},{8,1... | collective-permute-start | bytes 393224 | tf_op jit(solution)/shard_map/ppermute | solution.py:174
  25.3 6.9 %collective-permute-start.8 = (f32[256,128]{1,0:T(8,128)S(1)}, f32[256,128]{1,0:T(8,128)S(1)}, u32[]{:S(2)}, u32[]{:S(2)}) collective-permute-start(f32[256,128]{1,0:T(8,128)S(1)} %get-tuple-element.27), channel_id=1, source_target_pairs={{2,0},{0,5},{3,10},{1,15},{6,4},{4,9},{7,14},{5,3},{10,8},{8,13},{... | collective-permute-start | bytes 393224 | tf_op jit(solution)/shard_map/ppermute | solution.py:158
  25.4 8.8 %collective-permute-start.7 = (f32[256,128]{1,0:T(8,128)S(1)}, f32[256,128]{1,0:T(8,128)S(1)}, u32[]{:S(2)}, u32[]{:S(2)}) collective-permute-start(f32[256,128]{1,0:T(8,128)S(1)} %get-tuple-element.27), channel_id=1, source_target_pairs={{3,0},{1,5},{2,10},{0,15},{7,4},{5,9},{6,14},{4,3},{8,8},{10,13},{... | collective-permute-start | bytes 393224 | tf_op jit(solution)/shard_map/ppermute | solution.py:158
  31.2 4.3 %collective-permute-start.6 = (f32[256,128]{1,0:T(8,128)S(1)}, f32[256,128]{1,0:T(8,128)S(1)}, u32[]{:S(2)}, u32[]{:S(2)}) collective-permute-start(f32[256,128]{1,0:T(8,128)S(1)} %get-tuple-element.27), channel_id=1, source_target_pairs={{1,0},{3,5},{0,10},{2,15},{5,4},{7,9},{4,14},{6,3},{9,8},{11,13},{... | collective-permute-start | bytes 393224 | tf_op jit(solution)/shard_map/ppermute | solution.py:158
  31.5 4.0 %collective-permute-start.5 = (f32[256,128]{1,0:T(8,128)S(1)}, f32[256,128]{1,0:T(8,128)S(1)}, u32[]{:S(2)}, u32[]{:S(2)}) collective-permute-start(f32[256,128]{1,0:T(8,128)S(1)} %get-tuple-element.27), channel_id=1, source_target_pairs={{0,0},{2,5},{1,10},{3,15},{4,4},{6,9},{5,14},{7,3},{11,8},{9,13},{... | collective-permute-start | bytes 393224 | tf_op jit(solution)/shard_map/ppermute | solution.py:158
  36.3 5.9 %collective-permute-start.10 = (f32[256,128]{1,0:T(8,128)S(1)}, f32[256,128]{1,0:T(8,128)S(1)}, u32[]{:S(2)}, u32[]{:S(2)}) collective-permute-start(f32[256,128]{1,0:T(8,128)S(1)} %get-tuple-element.26), channel_id=1, source_target_pairs={{0,1},{1,0},{2,3},{3,2},{4,5},{5,4},{6,7},{7,6},{8,9},{9,8},{10,11... | collective-permute-start | bytes 393224 | tf_op jit(solution)/shard_map/ppermute | solution.py:168
  41.3 4.6 %collective-permute-start.9 = (f32[256,128]{1,0:T(8,128)S(1)}, f32[256,128]{1,0:T(8,128)S(1)}, u32[]{:S(2)}, u32[]{:S(2)}) collective-permute-start(f32[256,128]{1,0:T(8,128)S(1)} %get-tuple-element.24), channel_id=1, source_target_pairs={{0,1},{1,0},{2,3},{3,2},{4,5},{5,4},{6,7},{7,6},{8,9},{9,8},{10,11... | collective-permute-start | bytes 393224 | tf_op jit(solution)/shard_map/ppermute | solution.py:168
  42.3 7.4 %collective-permute-start.11 = (f32[256,128]{1,0:T(8,128)S(1)}, f32[256,128]{1,0:T(8,128)S(1)}, u32[]{:S(2)}, u32[]{:S(2)}) collective-permute-start(f32[256,128]{1,0:T(8,128)S(1)} %add.19), channel_id=1, source_target_pairs={{2,0},{3,1},{0,2},{1,3},{6,4},{7,5},{4,6},{5,7},{10,8},{11,9},{8,1... | collective-permute-start | bytes 393224 | tf_op jit(solution)/shard_map/ppermute | solution.py:174

commit v15 on v12

--- a/solution.py
+++ b/solution.py
@@ -214,7 +214,8 @@
     degrees = degrees.reshape(panel_rows // tile_size, tile_size)
 
     panel = fetch(embeddings, lambda team: spread[team], arc_length)
-    pieces = [fetch(degrees, lambda team: spread[team], arc_length), panel]
+    beside = (1, 3, 0, 2) if team_count == 4 else tuple((team + 1) % team_count for team in range(team_count))
+    pieces = [fetch(degrees, lambda team: beside[team], arc_length), panel]
     info = jnp.concatenate([slot_counts[0, 0][:, None], tile_rows[0, 0], tile_columns[0, 0]], axis=1)
     info = jnp.broadcast_to(info[:, :, None], (*info.shape, embeddings.shape[1]))
     info = [info[at] for at in range(arc_length)]

time: 48.9 us -> 48.9 us (level)
  starting transfers between devices: 21.3 us -> 20.5 us
  waiting for transfers between devices: 19.9 us -> 20.7 us
    ppermute x6, starting transfers between devices: 11 us -> 10.2 us  [fetch(): return lax.ppermute(value, ('blk', 'rep'), pairs)]
    ppermute x6, waiting for transfers between devices: 10.5 us -> 11.3 us  [fetch(): return lax.ppermute(value, ('blk', 'rep'), pairs)]
where the time goes in v15:
time: 48.9 us; the launch traced here: 48.6 us
  waiting for transfers between devices  20.7 us (42%)
  starting transfers between devices  20.5 us (42%)
  local copies, waits for them, and re-layouts  3.52 us (7%)
  Pallas kernels  3.01 us (6%)
  between operations  0.72 us (1%)
    ppermute x6, waiting for transfers between devices, fetch(): return lax.ppermute(value, ('blk', 'rep'), pairs)  11.3 us
    ppermute x6, starting transfers between devices, fetch(): return lax.ppermute(value, ('blk', 'rep'), pairs)  10.2 us
    ppermute x2, waiting for transfers between devices, from_column(): return lax.ppermute(value, 'rep', pairs)  7.61 us
    ppermute x2, starting transfers between devices, from_column(): return lax.ppermute(value, 'rep', pairs)  6.81 us
    ppermute x4, starting transfers between devices, from_mate(): lax.ppermute(value, 'rep', [(team, team ^ 1) for team in range(team_count)])  3.45 us
    unnamed x10, local copies, waits for them, and re-layouts  3.44 us
    ppermute x4, waiting for transfers between devices, from_mate(): lax.ppermute(value, 'rep', [(team, team ^ 1) for team in range(team_count)])  1.82 us
    pallas_call x2, Pallas kernels, arc_step(): pl.pallas_call(functools.partial(arc_kernel, team_count=team_count, piece...  1.74 us
  transfers between devices with their start and end apart: 12, of which 8 were waited for; matrix products, arithmetic and copies ran while one was open for 0% of the time, Pallas kernels for 1%

profile of v15, /device:TPU:0, one launch (start us, length us, event | category | flops | bytes accessed | tf_op | source)
XLA Modules:
  0.0 48.6 jit_solution(9522415942301835590)
XLA Ops:
  0.0 5.4 %collective-permute-start.1 = (f32[1024,128]{1,0:T(8,128)}, f32[1024,128]{1,0:T(8,128)S(1)}, u32[]{:S(2)}, u32[]{:S(2)}) collective-permute-start(f32[1024,128]{1,0:T(8,128)} %embeddings_ref.1), channel_id=1, source_target_pairs={{3,0},{1,5},{2,10},{0,15},{7,4},{5,9},{6,14},{4,3},{11,8},{9,13},{... | collective-permute-start | bytes 1572872 | tf_op jit(solution)/shard_map/ppermute | solution.py:153
  6.1 0.6 %copy-done.3 = s32[1,1,1,24]{3,2,1,0:T(1,128)S(1)} copy-done((s32[1,1,1,24]{3,2,1,0:T(1,128)S(1)}, s32[1,1,1,24]{3,2,1,0:T(1,128)}, u32[]{:S(2)}) %copy-start.3) | copy-done | bytes 120
  6.7 0.0 copy-done.4
  6.7 0.1 add_bitcast_fusion
  6.8 0.1 squeeze.19.after_ref.info_ref
  6.9 0.6 %copy-done.2 = s32[1024]{0:T(1024)S(1)} copy-done((s32[1024]{0:T(1024)S(1)}, s32[1024]{0:T(1024)}, u32[]{:S(2)}) %copy-start.2) | copy-done | bytes 4120
  7.5 1.1 %copy-done = bf16[1,1,1,24,128,128]{5,4,3,2,1,0:T(8,128)(2,1)S(1)} copy-done((bf16[1,1,1,24,128,128]{5,4,3,2,1,0:T(8,128)(2,1)S(1)}, bf16[1,1,1,24,128,128]{5,4,3,2,1,0:T(8,128)(2,1)}, u32[]{:S(2)}) %copy-start) | copy-done | bytes 786456
  8.6 1.0 %copy-done.1 = f32[1024,128]{1,0:T(8,128)S(1)} copy-done((f32[1024,128]{1,0:T(8,128)S(1)}, f32[1024,128]{1,0:T(8,128)}, u32[]{:S(2)}) %copy-start.1) | copy-done | bytes 524312
  9.7 0.6 %shard_map.64 = (bf16[1,24,128,128]{3,2,1,0:T(8,128)(2,1)S(1)}, f32[256,128]{1,0:T(8,128)S(1)}, f32[256,128]{1,0:T(8,128)S(1)}) custom-call(s32[8,128]{1,0:T(8,128)S(1)} %bitcast.13, f32[1024,128]{1,0:T(8,128)S(1)} %copy-done.1, bf16[1,24,128,128]{3,2,1,0:T(8,128)(2,1)S(1)} %bitcast.11, s32[49,128]{1,0:T(8,128)S(1)} %squeeze.19.after_ref.info_ref), custom_call_target="tpu_custom_call" | custom-call | flops 131072 | bytes 524288 | tf_op jit(solution)/shard_map/pallas_call | solution.py:56
  10.3 4.3 %collective-permute-done.refs_0_ = s32[8,128]{1,0:T(8,128)S(1)} collective-permute-done((s32[8,128]{1,0:T(8,128)}, s32[8,128]{1,0:T(8,128)S(1)}, u32[]{:S(2)}, u32[]{:S(2)}) %collective-permute-start) | collective-permute-done | bytes 4128 | tf_op jit(solution)/shard_map/ppermute | solution.py:153
  14.6 0.0 collective-permute-done.1.refs_1_
  14.6 1.0 %shard_map.65 = (f32[256,128]{1,0:T(8,128)S(1)}, f32[256,128]{1,0:T(8,128)S(1)}, f32[256,128]{1,0:T(8,128)S(1)}, f32[256,128]{1,0:T(8,128)S(1)}) custom-call(s32[49,128]{1,0:T(8,128)S(1)} %squeeze.19.after_ref.info_ref, bf16[24,128,128]{2,1,0:T(8,128)(2,1)S(1)} %bitcast.9, s32[8,128]{1,0:T(8,128)S(1)} %collective-permute-done.refs_0_, ...), custom_call_target="tpu_custom_call" | custom-call | flops 201326592 | bytes 1048576 | tf_op jit(solution)/shard_map/pallas_call | solution.py:124
  15.6 0.8 %collective-permute-start.3 = (f32[256,128]{1,0:T(8,128)S(1)}, f32[256,128]{1,0:T(8,128)S(1)}, u32[]{:S(2)}, u32[]{:S(2)}) collective-permute-start(f32[256,128]{1,0:T(8,128)S(1)} %get-tuple-element.21), channel_id=1, source_target_pairs={{0,1},{1,0},{2,3},{3,2},{4,5},{5,4},{6,7},{7,6},{8,9},{9,8},{10,11... | collective-permute-start | bytes 393224 | tf_op jit(solution)/shard_map/ppermute | solution.py:163
  16.3 0.1 collective-permute-start.2
  16.4 0.9 %collective-permute-done.3 = f32[256,128]{1,0:T(8,128)S(1)} collective-permute-done((f32[256,128]{1,0:T(8,128)S(1)}, f32[256,128]{1,0:T(8,128)S(1)}, u32[]{:S(2)}, u32[]{:S(2)}) %collective-permute-start.3) | collective-permute-done | bytes 131104 | tf_op jit(solution)/shard_map/ppermute | solution.py:163
  17.3 4.1 %collective-permute-start.4 = (f32[256,128]{1,0:T(8,128)S(1)}, f32[256,128]{1,0:T(8,128)S(1)}, u32[]{:S(2)}, u32[]{:S(2)}) collective-permute-start(f32[256,128]{1,0:T(8,128)S(1)} %add.16), channel_id=1, source_target_pairs={{2,0},{3,1},{0,2},{1,3},{6,4},{7,5},{4,6},{5,7},{10,8},{11,9},{8,1... | collective-permute-start | bytes 393224 | tf_op jit(solution)/shard_map/ppermute | solution.py:169
  21.4 0.0 collective-permute-done.2
  21.4 3.8 %collective-permute-done.4 = f32[256,128]{1,0:T(8,128)S(1)} collective-permute-done((f32[256,128]{1,0:T(8,128)S(1)}, f32[256,128]{1,0:T(8,128)S(1)}, u32[]{:S(2)}, u32[]{:S(2)}) %collective-permute-start.4) | collective-permute-done | bytes 131104 | tf_op jit(solution)/shard_map/ppermute | solution.py:169
  25.2 3.6 %collective-permute-start.8 = (f32[256,128]{1,0:T(8,128)S(1)}, f32[256,128]{1,0:T(8,128)S(1)}, u32[]{:S(2)}, u32[]{:S(2)}) collective-permute-start(f32[256,128]{1,0:T(8,128)S(1)} %get-tuple-element.27), channel_id=1, source_target_pairs={{3,0},{1,5},{2,10},{0,15},{7,4},{5,9},{6,14},{4,3},{11,8},{9,13},{... | collective-permute-start | bytes 393224 | tf_op jit(solution)/shard_map/ppermute | solution.py:153
  28.9 0.5 %collective-permute-start.7 = (f32[256,128]{1,0:T(8,128)S(1)}, f32[256,128]{1,0:T(8,128)S(1)}, u32[]{:S(2)}, u32[]{:S(2)}) collective-permute-start(f32[256,128]{1,0:T(8,128)S(1)} %get-tuple-element.27), channel_id=1, source_target_pairs={{1,0},{3,5},{0,10},{2,15},{5,4},{7,9},{4,14},{6,3},{9,8},{11,13},{... | collective-permute-start | bytes 393224 | tf_op jit(solution)/shard_map/ppermute | solution.py:153
  29.4 0.0 collective-permute-start.6
  29.4 0.7 %collective-permute-start.5 = (f32[256,128]{1,0:T(8,128)S(1)}, f32[256,128]{1,0:T(8,128)S(1)}, u32[]{:S(2)}, u32[]{:S(2)}) collective-permute-start(f32[256,128]{1,0:T(8,128)S(1)} %get-tuple-element.27), channel_id=1, source_target_pairs={{0,0},{2,5},{1,10},{3,15},{4,4},{6,9},{5,14},{7,3},{8,8},{10,13},{... | collective-permute-start | bytes 393224 | tf_op jit(solution)/shard_map/ppermute | solution.py:153
  30.1 2.3 %collective-permute-done.8.refs_3_ = f32[256,128]{1,0:T(8,128)S(1)} collective-permute-done((f32[256,128]{1,0:T(8,128)S(1)}, f32[256,128]{1,0:T(8,128)S(1)}, u32[]{:S(2)}, u32[]{:S(2)}) %collective-permute-start.8) | collective-permute-done | bytes 131104 | tf_op jit(solution)/shard_map/ppermute | solution.py:153
  32.4 2.2 %collective-permute-done.7.refs_2_ = f32[256,128]{1,0:T(8,128)S(1)} collective-permute-done((f32[256,128]{1,0:T(8,128)S(1)}, f32[256,128]{1,0:T(8,128)S(1)}, u32[]{:S(2)}, u32[]{:S(2)}) %collective-permute-start.7) | collective-permute-done | bytes 131104 | tf_op jit(solution)/shard_map/ppermute | solution.py:153
  34.6 2.4 %collective-permute-done.6.refs_1_ = f32[256,128]{1,0:T(8,128)S(1)} collective-permute-done((f32[256,128]{1,0:T(8,128)S(1)}, f32[256,128]{1,0:T(8,128)S(1)}, u32[]{:S(2)}, u32[]{:S(2)}) %collective-permute-start.6) | collective-permute-done | bytes 131104 | tf_op jit(solution)/shard_map/ppermute | solution.py:153
  37.1 0.8 %shard_map.66 = (f32[256,128]{1,0:T(8,128)S(1)}, f32[256,128]{1,0:T(8,128)S(1)}, f32[256,128]{1,0:T(8,128)S(1)}, f32[256,128]{1,0:T(8,128)S(1)}) custom-call(s32[49,128]{1,0:T(8,128)S(1)} %squeeze.19.after_ref.info_ref, bf16[24,128,128]{2,1,0:T(8,128)(2,1)S(1)} %bitcast.10, f32[256,128]{1,0:T(8,128)S(1)} %collective-permute-done.5.refs_0_, ...), custom_call_target="tpu_custom_call" | custom-call | flops 201326592 | bytes 1048576 | tf_op jit(solution)/shard_map/pallas_call | solution.py:124
  37.8 2.5 %collective-permute-start.10 = (f32[256,128]{1,0:T(8,128)S(1)}, f32[256,128]{1,0:T(8,128)S(1)}, u32[]{:S(2)}, u32[]{:S(2)}) collective-permute-start(f32[256,128]{1,0:T(8,128)S(1)} %get-tuple-element.26), channel_id=1, source_target_pairs={{0,1},{1,0},{2,3},{3,2},{4,5},{5,4},{6,7},{7,6},{8,9},{9,8},{10,11... | collective-permute-start | bytes 393224 | tf_op jit(solution)/shard_map/ppermute | solution.py:163
  40.4 0.1 collective-permute-start.9
  40.4 0.9 %collective-permute-done.10 = f32[256,128]{1,0:T(8,128)S(1)} collective-permute-done((f32[256,128]{1,0:T(8,128)S(1)}, f32[256,128]{1,0:T(8,128)S(1)}, u32[]{:S(2)}, u32[]{:S(2)}) %collective-permute-start.10) | collective-permute-done | bytes 131104 | tf_op jit(solution)/shard_map/ppermute | solution.py:163
  41.4 2.7 %collective-permute-start.11 = (f32[256,128]{1,0:T(8,128)S(1)}, f32[256,128]{1,0:T(8,128)S(1)}, u32[]{:S(2)}, u32[]{:S(2)}) collective-permute-start(f32[256,128]{1,0:T(8,128)S(1)} %add.19), channel_id=1, source_target_pairs={{2,0},{3,1},{0,2},{1,3},{6,4},{7,5},{4,6},{5,7},{10,8},{11,9},{8,1... | collective-permute-start | bytes 393224 | tf_op jit(solution)/shard_map/ppermute | solution.py:169
  44.1 3.8 %collective-permute-done.11.refs_2_ = f32[256,128]{1,0:T(8,128)S(1)} collective-permute-done((f32[256,128]{1,0:T(8,128)S(1)}, f32[256,128]{1,0:T(8,128)S(1)}, u32[]{:S(2)}, u32[]{:S(2)}) %collective-permute-start.11) | collective-permute-done | bytes 131104 | tf_op jit(solution)/shard_map/ppermute | solution.py:169
  47.9 0.7 %shard_map.67 = f32[256,128]{1,0:T(8,128)} custom-call(f32[256,128]{1,0:T(8,128)S(1)} %get-tuple-element.28.base_ref, f32[256,128]{1,0:T(8,128)S(1)} %get-tuple-element.22.norm_ref, f32[256,128]{1,0:T(8,128)S(1)} %get-tuple-element.23.refs_0_, f32[256,128]{1,0:T(8,128)S(1)} %collective-permute-done.9.refs_1_, f32[256,128]{1,0:T(8,128)S(1)} %collective-permute-done.11.refs_2_), custom_call_target="tpu_custom_call" | custom-call | tf_op jit(solution)/shard_map/pallas_call | solution.py:199
  (11 shorter events, 0.1 us)
Async XLA Ops:
  0.0 14.6 %collective-permute-start.1 = (f32[1024,128]{1,0:T(8,128)}, f32[1024,128]{1,0:T(8,128)S(1)}, u32[]{:S(2)}, u32[]{:S(2)}) collective-permute-start(f32[1024,128]{1,0:T(8,128)} %embeddings_ref.1), channel_id=1, source_target_pairs={{3,0},{1,5},{2,10},{0,15},{7,4},{5,9},{6,14},{4,3},{11,8},{9,13},{... | collective-permute-start | bytes 1572872 | tf_op jit(solution)/shard_map/ppermute | solution.py:153
  5.4 9.2 %collective-permute-start = (s32[8,128]{1,0:T(8,128)}, s32[8,128]{1,0:T(8,128)S(1)}, u32[]{:S(2)}, u32[]{:S(2)}) collective-permute-start(s32[8,128]{1,0:T(8,128)} %bitcast.12), channel_id=1, source_target_pairs={{1,0},{3,5},{0,10},{2,15},{5,4},{7,9},{4,14},{6,3},{9,8},{11,13},{... | collective-permute-start | bytes 12296 | tf_op jit(solution)/shard_map/ppermute | solution.py:153
  6.1 0.7 %copy-start.3 = (s32[1,1,1,24]{3,2,1,0:T(1,128)S(1)}, s32[1,1,1,24]{3,2,1,0:T(1,128)}, u32[]{:S(2)}) copy-start(s32[1,1,1,24]{3,2,1,0:T(1,128)} %param.10) | copy-start | bytes 292
  6.1 0.7 %copy-start.4 = (s32[1,1,1,24]{3,2,1,0:T(1,128)S(1)}, s32[1,1,1,24]{3,2,1,0:T(1,128)}, u32[]{:S(2)}) copy-start(s32[1,1,1,24]{3,2,1,0:T(1,128)} %param.9) | copy-start | bytes 292
  6.8 0.7 %copy-start.2 = (s32[1024]{0:T(1024)S(1)}, s32[1024]{0:T(1024)}, u32[]{:S(2)}) copy-start(s32[1024]{0:T(1024)} %param.7) | copy-start | bytes 12292
  7.5 1.1 %copy-start = (bf16[1,1,1,24,128,128]{5,4,3,2,1,0:T(8,128)(2,1)S(1)}, bf16[1,1,1,24,128,128]{5,4,3,2,1,0:T(8,128)(2,1)}, u32[]{:S(2)}) copy-start(bf16[1,1,1,24,128,128]{5,4,3,2,1,0:T(8,128)(2,1)} %param.8) | copy-start | bytes 2359300
  8.6 1.0 %copy-start.1 = (f32[1024,128]{1,0:T(8,128)S(1)}, f32[1024,128]{1,0:T(8,128)}, u32[]{:S(2)}) copy-start(f32[1024,128]{1,0:T(8,128)} %embeddings_ref.1) | copy-start | bytes 1572868
  15.6 1.7 %collective-permute-start.3 = (f32[256,128]{1,0:T(8,128)S(1)}, f32[256,128]{1,0:T(8,128)S(1)}, u32[]{:S(2)}, u32[]{:S(2)}) collective-permute-start(f32[256,128]{1,0:T(8,128)S(1)} %get-tuple-element.21), channel_id=1, source_target_pairs={{0,1},{1,0},{2,3},{3,2},{4,5},{5,4},{6,7},{7,6},{8,9},{9,8},{10,11... | collective-permute-start | bytes 393224 | tf_op jit(solution)/shard_map/ppermute | solution.py:163
  16.3 5.1 %collective-permute-start.2 = (f32[256,128]{1,0:T(8,128)S(1)}, f32[256,128]{1,0:T(8,128)S(1)}, u32[]{:S(2)}, u32[]{:S(2)}) collective-permute-start(f32[256,128]{1,0:T(8,128)S(1)} %get-tuple-element.19), channel_id=1, source_target_pairs={{0,1},{1,0},{2,3},{3,2},{4,5},{5,4},{6,7},{7,6},{8,9},{9,8},{10,11... | collective-permute-start | bytes 393224 | tf_op jit(solution)/shard_map/ppermute | solution.py:163
  17.3 7.9 %collective-permute-start.4 = (f32[256,128]{1,0:T(8,128)S(1)}, f32[256,128]{1,0:T(8,128)S(1)}, u32[]{:S(2)}, u32[]{:S(2)}) collective-permute-start(f32[256,128]{1,0:T(8,128)S(1)} %add.16), channel_id=1, source_target_pairs={{2,0},{3,1},{0,2},{1,3},{6,4},{7,5},{4,6},{5,7},{10,8},{11,9},{8,1... | collective-permute-start | bytes 393224 | tf_op jit(solution)/shard_map/ppermute | solution.py:169
  25.2 7.2 %collective-permute-start.8 = (f32[256,128]{1,0:T(8,128)S(1)}, f32[256,128]{1,0:T(8,128)S(1)}, u32[]{:S(2)}, u32[]{:S(2)}) collective-permute-start(f32[256,128]{1,0:T(8,128)S(1)} %get-tuple-element.27), channel_id=1, source_target_pairs={{3,0},{1,5},{2,10},{0,15},{7,4},{5,9},{6,14},{4,3},{11,8},{9,13},{... | collective-permute-start | bytes 393224 | tf_op jit(solution)/shard_map/ppermute | solution.py:153
  28.9 5.8 %collective-permute-start.7 = (f32[256,128]{1,0:T(8,128)S(1)}, f32[256,128]{1,0:T(8,128)S(1)}, u32[]{:S(2)}, u32[]{:S(2)}) collective-permute-start(f32[256,128]{1,0:T(8,128)S(1)} %get-tuple-element.27), channel_id=1, source_target_pairs={{1,0},{3,5},{0,10},{2,15},{5,4},{7,9},{4,14},{6,3},{9,8},{11,13},{... | collective-permute-start | bytes 393224 | tf_op jit(solution)/shard_map/ppermute | solution.py:153
  29.4 7.7 %collective-permute-start.6 = (f32[256,128]{1,0:T(8,128)S(1)}, f32[256,128]{1,0:T(8,128)S(1)}, u32[]{:S(2)}, u32[]{:S(2)}) collective-permute-start(f32[256,128]{1,0:T(8,128)S(1)} %get-tuple-element.27), channel_id=1, source_target_pairs={{2,0},{0,5},{3,10},{1,15},{6,4},{4,9},{7,14},{5,3},{10,8},{8,13},{... | collective-permute-start | bytes 393224 | tf_op jit(solution)/shard_map/ppermute | solution.py:153
  29.4 7.7 %collective-permute-start.5 = (f32[256,128]{1,0:T(8,128)S(1)}, f32[256,128]{1,0:T(8,128)S(1)}, u32[]{:S(2)}, u32[]{:S(2)}) collective-permute-start(f32[256,128]{1,0:T(8,128)S(1)} %get-tuple-element.27), channel_id=1, source_target_pairs={{0,0},{2,5},{1,10},{3,15},{4,4},{6,9},{5,14},{7,3},{8,8},{10,13},{... | collective-permute-start | bytes 393224 | tf_op jit(solution)/shard_map/ppermute | solution.py:153
  37.8 3.5 %collective-permute-start.10 = (f32[256,128]{1,0:T(8,128)S(1)}, f32[256,128]{1,0:T(8,128)S(1)}, u32[]{:S(2)}, u32[]{:S(2)}) collective-permute-start(f32[256,128]{1,0:T(8,128)S(1)} %get-tuple-element.26), channel_id=1, source_target_pairs={{0,1},{1,0},{2,3},{3,2},{4,5},{5,4},{6,7},{7,6},{8,9},{9,8},{10,11... | collective-permute-start | bytes 393224 | tf_op jit(solution)/shard_map/ppermute | solution.py:163
  40.4 3.8 %collective-permute-start.9 = (f32[256,128]{1,0:T(8,128)S(1)}, f32[256,128]{1,0:T(8,128)S(1)}, u32[]{:S(2)}, u32[]{:S(2)}) collective-permute-start(f32[256,128]{1,0:T(8,128)S(1)} %get-tuple-element.24), channel_id=1, source_target_pairs={{0,1},{1,0},{2,3},{3,2},{4,5},{5,4},{6,7},{7,6},{8,9},{9,8},{10,11... | collective-permute-start | bytes 393224 | tf_op jit(solution)/shard_map/ppermute | solution.py:163
  41.4 6.6 %collective-permute-start.11 = (f32[256,128]{1,0:T(8,128)S(1)}, f32[256,128]{1,0:T(8,128)S(1)}, u32[]{:S(2)}, u32[]{:S(2)}) collective-permute-start(f32[256,128]{1,0:T(8,128)S(1)} %add.19), channel_id=1, source_target_pairs={{2,0},{3,1},{0,2},{1,3},{6,4},{7,5},{4,6},{5,7},{10,8},{11,9},{8,1... | collective-permute-start | bytes 393224 | tf_op jit(solution)/shard_map/ppermute | solution.py:169

commit v16 on v13

--- a/solution.py
+++ b/solution.py
@@ -20,7 +20,7 @@
 
 def source_team(team, turn, team_count):
     if team_count == 4:
-        return (2 * (team % 2) + team // 2) ^ (0, 1, 3, 2)[turn]
+        return (2 * (team % 2) + team // 2) ^ (0, 3, 2, 1)[turn]
     return (team + turn) % team_count
 
 

time: 50.2 us -> 49.3 us (0.982)
  waiting for transfers between devices: 18.5 us -> 16.9 us
  starting transfers between devices: 24.1 us -> 24.7 us
    ppermute x4, starting transfers between devices: 5.25 us -> 6.87 us  [from_mate(): lax.ppermute(value, 'rep', [(team, team ^ 1) for team in range(team_count)])]
    ppermute x6, waiting for transfers between devices: 9.04 us -> 7.49 us  [fetch(): return lax.ppermute(value, ('blk', 'rep'), pairs)]
    ppermute x2, starting transfers between devices: 7.5 us -> 6.68 us  [from_column(): return lax.ppermute(value, 'rep', pairs)]
  transfers between devices with their start and end apart: 12 -> 12, of which waited for: 8 -> 7; matrix products, arithmetic and copies ran while one was open for 0% -> 0% of each run, Pallas kernels for 1% -> 1%
where the time goes in v16:
time: 49.3 us; the launch traced here: 49 us
  starting transfers between devices  24.7 us (50%)
  waiting for transfers between devices  16.9 us (34%)
  local copies, waits for them, and re-layouts  3.52 us (7%)
  Pallas kernels  3.01 us (6%)
  between operations  0.73 us (1%)
    ppermute x6, starting transfers between devices, fetch(): return lax.ppermute(value, ('blk', 'rep'), pairs)  11.2 us
    ppermute x2, waiting for transfers between devices, from_column(): return lax.ppermute(value, 'rep', pairs)  7.61 us
    ppermute x6, waiting for transfers between devices, fetch(): return lax.ppermute(value, ('blk', 'rep'), pairs)  7.49 us
    ppermute x4, starting transfers between devices, from_mate(): lax.ppermute(value, 'rep', [(team, team ^ 1) for team in range(team_count)])  6.87 us
    ppermute x2, starting transfers between devices, from_column(): return lax.ppermute(value, 'rep', pairs)  6.68 us
    unnamed x10, local copies, waits for them, and re-layouts  3.44 us
    ppermute x4, waiting for transfers between devices, from_mate(): lax.ppermute(value, 'rep', [(team, team ^ 1) for team in range(team_count)])  1.82 us
    pallas_call x2, Pallas kernels, arc_step(): pl.pallas_call(functools.partial(arc_kernel, team_count=team_count, piece...  1.73 us
  transfers between devices with their start and end apart: 12, of which 7 were waited for; matrix products, arithmetic and copies ran while one was open for 0% of the time, Pallas kernels for 1%

profile of v16, /device:TPU:0, one launch (start us, length us, event | category | flops | bytes accessed | tf_op | source)
XLA Modules:
  0.0 49.0 jit_solution(229939224520117889)
XLA Ops:
  0.0 5.4 %collective-permute-start.1 = (f32[1024,128]{1,0:T(8,128)}, f32[1024,128]{1,0:T(8,128)S(1)}, u32[]{:S(2)}, u32[]{:S(2)}) collective-permute-start(f32[1024,128]{1,0:T(8,128)} %embeddings_ref.1), channel_id=1, source_target_pairs={{3,0},{1,5},{2,10},{0,15},{7,4},{5,9},{6,14},{4,3},{11,8},{9,13},{... | collective-permute-start | bytes 1572872 | tf_op jit(solution)/shard_map/ppermute | solution.py:153
  5.4 0.8 %collective-permute-start = (s32[8,128]{1,0:T(8,128)}, s32[8,128]{1,0:T(8,128)S(1)}, u32[]{:S(2)}, u32[]{:S(2)}) collective-permute-start(s32[8,128]{1,0:T(8,128)} %bitcast.12), channel_id=1, source_target_pairs={{3,0},{1,5},{2,10},{0,15},{7,4},{5,9},{6,14},{4,3},{11,8},{9,13},{... | collective-permute-start | bytes 12296 | tf_op jit(solution)/shard_map/ppermute | solution.py:153
  6.9 0.6 %copy-done.3 = s32[1,1,1,24]{3,2,1,0:T(1,128)S(1)} copy-done((s32[1,1,1,24]{3,2,1,0:T(1,128)S(1)}, s32[1,1,1,24]{3,2,1,0:T(1,128)}, u32[]{:S(2)}) %copy-start.3) | copy-done | bytes 120
  7.5 0.0 copy-done.4
  7.6 0.1 add_bitcast_fusion
  7.6 0.1 squeeze.19.after_ref.info_ref
  7.7 0.6 %copy-done.2 = s32[1024]{0:T(1024)S(1)} copy-done((s32[1024]{0:T(1024)S(1)}, s32[1024]{0:T(1024)}, u32[]{:S(2)}) %copy-start.2) | copy-done | bytes 4120
  8.3 1.1 %copy-done = bf16[1,1,1,24,128,128]{5,4,3,2,1,0:T(8,128)(2,1)S(1)} copy-done((bf16[1,1,1,24,128,128]{5,4,3,2,1,0:T(8,128)(2,1)S(1)}, bf16[1,1,1,24,128,128]{5,4,3,2,1,0:T(8,128)(2,1)}, u32[]{:S(2)}) %copy-start) | copy-done | bytes 786456
  9.5 1.0 %copy-done.1 = f32[1024,128]{1,0:T(8,128)S(1)} copy-done((f32[1024,128]{1,0:T(8,128)S(1)}, f32[1024,128]{1,0:T(8,128)}, u32[]{:S(2)}) %copy-start.1) | copy-done | bytes 524312
  10.5 0.6 %shard_map.64 = (bf16[1,24,128,128]{3,2,1,0:T(8,128)(2,1)S(1)}, f32[256,128]{1,0:T(8,128)S(1)}, f32[256,128]{1,0:T(8,128)S(1)}) custom-call(s32[8,128]{1,0:T(8,128)S(1)} %bitcast.13, f32[1024,128]{1,0:T(8,128)S(1)} %copy-done.1, bf16[1,24,128,128]{3,2,1,0:T(8,128)(2,1)S(1)} %bitcast.11, s32[49,128]{1,0:T(8,128)S(1)} %squeeze.19.after_ref.info_ref), custom_call_target="tpu_custom_call" | custom-call | flops 131072 | bytes 524288 | tf_op jit(solution)/shard_map/pallas_call | solution.py:56
  11.1 3.5 %collective-permute-done.refs_0_ = s32[8,128]{1,0:T(8,128)S(1)} collective-permute-done((s32[8,128]{1,0:T(8,128)}, s32[8,128]{1,0:T(8,128)S(1)}, u32[]{:S(2)}, u32[]{:S(2)}) %collective-permute-start) | collective-permute-done | bytes 4128 | tf_op jit(solution)/shard_map/ppermute | solution.py:153
  14.6 0.0 collective-permute-done.1.refs_1_
  14.6 1.0 %shard_map.65 = (f32[256,128]{1,0:T(8,128)S(1)}, f32[256,128]{1,0:T(8,128)S(1)}, f32[256,128]{1,0:T(8,128)S(1)}, f32[256,128]{1,0:T(8,128)S(1)}) custom-call(s32[49,128]{1,0:T(8,128)S(1)} %squeeze.19.after_ref.info_ref, bf16[24,128,128]{2,1,0:T(8,128)(2,1)S(1)} %bitcast.9, s32[8,128]{1,0:T(8,128)S(1)} %collective-permute-done.refs_0_, ...), custom_call_target="tpu_custom_call" | custom-call | flops 201326592 | bytes 1048576 | tf_op jit(solution)/shard_map/pallas_call | solution.py:124
  15.6 0.8 %collective-permute-start.3 = (f32[256,128]{1,0:T(8,128)S(1)}, f32[256,128]{1,0:T(8,128)S(1)}, u32[]{:S(2)}, u32[]{:S(2)}) collective-permute-start(f32[256,128]{1,0:T(8,128)S(1)} %get-tuple-element.21), channel_id=1, source_target_pairs={{0,1},{1,0},{2,3},{3,2},{4,5},{5,4},{6,7},{7,6},{8,9},{9,8},{10,11... | collective-permute-start | bytes 393224 | tf_op jit(solution)/shard_map/ppermute | solution.py:163
  16.4 0.1 collective-permute-start.2
  16.5 0.9 %collective-permute-done.3 = f32[256,128]{1,0:T(8,128)S(1)} collective-permute-done((f32[256,128]{1,0:T(8,128)S(1)}, f32[256,128]{1,0:T(8,128)S(1)}, u32[]{:S(2)}, u32[]{:S(2)}) %collective-permute-start.3) | collective-permute-done | bytes 131104 | tf_op jit(solution)/shard_map/ppermute | solution.py:163
  17.4 4.0 %collective-permute-start.4 = (f32[256,128]{1,0:T(8,128)S(1)}, f32[256,128]{1,0:T(8,128)S(1)}, u32[]{:S(2)}, u32[]{:S(2)}) collective-permute-start(f32[256,128]{1,0:T(8,128)S(1)} %add.16), channel_id=1, source_target_pairs={{2,0},{3,1},{0,2},{1,3},{6,4},{7,5},{4,6},{5,7},{10,8},{11,9},{8,1... | collective-permute-start | bytes 393224 | tf_op jit(solution)/shard_map/ppermute | solution.py:169
  21.4 0.0 collective-permute-done.2
  21.4 3.8 %collective-permute-done.4 = f32[256,128]{1,0:T(8,128)S(1)} collective-permute-done((f32[256,128]{1,0:T(8,128)S(1)}, f32[256,128]{1,0:T(8,128)S(1)}, u32[]{:S(2)}, u32[]{:S(2)}) %collective-permute-start.4) | collective-permute-done | bytes 131104 | tf_op jit(solution)/shard_map/ppermute | solution.py:169
  25.3 1.3 %collective-permute-start.8 = (f32[256,128]{1,0:T(8,128)S(1)}, f32[256,128]{1,0:T(8,128)S(1)}, u32[]{:S(2)}, u32[]{:S(2)}) collective-permute-start(f32[256,128]{1,0:T(8,128)S(1)} %get-tuple-element.27), channel_id=1, source_target_pairs={{1,0},{3,5},{0,10},{2,15},{5,4},{7,9},{4,14},{6,3},{9,8},{11,13},{... | collective-permute-start | bytes 393224 | tf_op jit(solution)/shard_map/ppermute | solution.py:153
  26.6 0.0 collective-permute-start.7
  26.6 3.0 %collective-permute-start.6 = (f32[256,128]{1,0:T(8,128)S(1)}, f32[256,128]{1,0:T(8,128)S(1)}, u32[]{:S(2)}, u32[]{:S(2)}) collective-permute-start(f32[256,128]{1,0:T(8,128)S(1)} %get-tuple-element.27), channel_id=1, source_target_pairs={{3,0},{1,5},{2,10},{0,15},{7,4},{5,9},{6,14},{4,3},{11,8},{9,13},{... | collective-permute-start | bytes 393224 | tf_op jit(solution)/shard_map/ppermute | solution.py:153
  29.6 0.7 %collective-permute-start.5 = (f32[256,128]{1,0:T(8,128)S(1)}, f32[256,128]{1,0:T(8,128)S(1)}, u32[]{:S(2)}, u32[]{:S(2)}) collective-permute-start(f32[256,128]{1,0:T(8,128)S(1)} %get-tuple-element.27), channel_id=1, source_target_pairs={{0,0},{2,5},{1,10},{3,15},{4,4},{6,9},{5,14},{7,3},{8,8},{10,13},{... | collective-permute-start | bytes 393224 | tf_op jit(solution)/shard_map/ppermute | solution.py:153
  30.2 3.6 %collective-permute-done.7.refs_2_ = f32[256,128]{1,0:T(8,128)S(1)} collective-permute-done((f32[256,128]{1,0:T(8,128)S(1)}, f32[256,128]{1,0:T(8,128)S(1)}, u32[]{:S(2)}, u32[]{:S(2)}) %collective-permute-start.7) | collective-permute-done | bytes 131104 | tf_op jit(solution)/shard_map/ppermute | solution.py:153
  33.8 0.4 collective-permute-done.6.refs_1_
  34.2 0.8 %shard_map.66 = (f32[256,128]{1,0:T(8,128)S(1)}, f32[256,128]{1,0:T(8,128)S(1)}, f32[256,128]{1,0:T(8,128)S(1)}, f32[256,128]{1,0:T(8,128)S(1)}) custom-call(s32[49,128]{1,0:T(8,128)S(1)} %squeeze.19.after_ref.info_ref, bf16[24,128,128]{2,1,0:T(8,128)(2,1)S(1)} %bitcast.10, f32[256,128]{1,0:T(8,128)S(1)} %collective-permute-done.5.refs_0_, ...), custom_call_target="tpu_custom_call" | custom-call | flops 201326592 | bytes 1048576 | tf_op jit(solution)/shard_map/pallas_call | solution.py:124
  35.0 5.9 %collective-permute-start.10 = (f32[256,128]{1,0:T(8,128)S(1)}, f32[256,128]{1,0:T(8,128)S(1)}, u32[]{:S(2)}, u32[]{:S(2)}) collective-permute-start(f32[256,128]{1,0:T(8,128)S(1)} %get-tuple-element.26), channel_id=1, source_target_pairs={{0,1},{1,0},{2,3},{3,2},{4,5},{5,4},{6,7},{7,6},{8,9},{9,8},{10,11... | collective-permute-start | bytes 393224 | tf_op jit(solution)/shard_map/ppermute | solution.py:163
  40.9 0.1 collective-permute-start.9
  40.9 0.9 %collective-permute-done.10 = f32[256,128]{1,0:T(8,128)S(1)} collective-permute-done((f32[256,128]{1,0:T(8,128)S(1)}, f32[256,128]{1,0:T(8,128)S(1)}, u32[]{:S(2)}, u32[]{:S(2)}) %collective-permute-start.10) | collective-permute-done | bytes 131104 | tf_op jit(solution)/shard_map/ppermute | solution.py:163
  41.9 2.7 %collective-permute-start.11 = (f32[256,128]{1,0:T(8,128)S(1)}, f32[256,128]{1,0:T(8,128)S(1)}, u32[]{:S(2)}, u32[]{:S(2)}) collective-permute-start(f32[256,128]{1,0:T(8,128)S(1)} %add.19), channel_id=1, source_target_pairs={{2,0},{3,1},{0,2},{1,3},{6,4},{7,5},{4,6},{5,7},{10,8},{11,9},{8,1... | collective-permute-start | bytes 393224 | tf_op jit(solution)/shard_map/ppermute | solution.py:169
  44.5 3.8 %collective-permute-done.11.refs_2_ = f32[256,128]{1,0:T(8,128)S(1)} collective-permute-done((f32[256,128]{1,0:T(8,128)S(1)}, f32[256,128]{1,0:T(8,128)S(1)}, u32[]{:S(2)}, u32[]{:S(2)}) %collective-permute-start.11) | collective-permute-done | bytes 131104 | tf_op jit(solution)/shard_map/ppermute | solution.py:169
  48.4 0.7 %shard_map.67 = f32[256,128]{1,0:T(8,128)} custom-call(f32[256,128]{1,0:T(8,128)S(1)} %get-tuple-element.28.base_ref, f32[256,128]{1,0:T(8,128)S(1)} %get-tuple-element.22.norm_ref, f32[256,128]{1,0:T(8,128)S(1)} %get-tuple-element.23.refs_0_, f32[256,128]{1,0:T(8,128)S(1)} %collective-permute-done.9.refs_1_, f32[256,128]{1,0:T(8,128)S(1)} %collective-permute-done.11.refs_2_), custom_call_target="tpu_custom_call" | custom-call | tf_op jit(solution)/shard_map/pallas_call | solution.py:199
  (11 shorter events, 0.1 us)
Async XLA Ops:
  0.0 14.6 %collective-permute-start.1 = (f32[1024,128]{1,0:T(8,128)}, f32[1024,128]{1,0:T(8,128)S(1)}, u32[]{:S(2)}, u32[]{:S(2)}) collective-permute-start(f32[1024,128]{1,0:T(8,128)} %embeddings_ref.1), channel_id=1, source_target_pairs={{3,0},{1,5},{2,10},{0,15},{7,4},{5,9},{6,14},{4,3},{11,8},{9,13},{... | collective-permute-start | bytes 1572872 | tf_op jit(solution)/shard_map/ppermute | solution.py:153
  5.4 9.2 %collective-permute-start = (s32[8,128]{1,0:T(8,128)}, s32[8,128]{1,0:T(8,128)S(1)}, u32[]{:S(2)}, u32[]{:S(2)}) collective-permute-start(s32[8,128]{1,0:T(8,128)} %bitcast.12), channel_id=1, source_target_pairs={{3,0},{1,5},{2,10},{0,15},{7,4},{5,9},{6,14},{4,3},{11,8},{9,13},{... | collective-permute-start | bytes 12296 | tf_op jit(solution)/shard_map/ppermute | solution.py:153
  6.9 0.7 %copy-start.3 = (s32[1,1,1,24]{3,2,1,0:T(1,128)S(1)}, s32[1,1,1,24]{3,2,1,0:T(1,128)}, u32[]{:S(2)}) copy-start(s32[1,1,1,24]{3,2,1,0:T(1,128)} %param.10) | copy-start | bytes 292
  6.9 0.7 %copy-start.4 = (s32[1,1,1,24]{3,2,1,0:T(1,128)S(1)}, s32[1,1,1,24]{3,2,1,0:T(1,128)}, u32[]{:S(2)}) copy-start(s32[1,1,1,24]{3,2,1,0:T(1,128)} %param.9) | copy-start | bytes 292
  7.6 0.7 %copy-start.2 = (s32[1024]{0:T(1024)S(1)}, s32[1024]{0:T(1024)}, u32[]{:S(2)}) copy-start(s32[1024]{0:T(1024)} %param.7) | copy-start | bytes 12292
  8.3 1.1 %copy-start = (bf16[1,1,1,24,128,128]{5,4,3,2,1,0:T(8,128)(2,1)S(1)}, bf16[1,1,1,24,128,128]{5,4,3,2,1,0:T(8,128)(2,1)}, u32[]{:S(2)}) copy-start(bf16[1,1,1,24,128,128]{5,4,3,2,1,0:T(8,128)(2,1)} %param.8) | copy-start | bytes 2359300
  9.5 1.0 %copy-start.1 = (f32[1024,128]{1,0:T(8,128)S(1)}, f32[1024,128]{1,0:T(8,128)}, u32[]{:S(2)}) copy-start(f32[1024,128]{1,0:T(8,128)} %embeddings_ref.1) | copy-start | bytes 1572868
  15.6 1.8 %collective-permute-start.3 = (f32[256,128]{1,0:T(8,128)S(1)}, f32[256,128]{1,0:T(8,128)S(1)}, u32[]{:S(2)}, u32[]{:S(2)}) collective-permute-start(f32[256,128]{1,0:T(8,128)S(1)} %get-tuple-element.21), channel_id=1, source_target_pairs={{0,1},{1,0},{2,3},{3,2},{4,5},{5,4},{6,7},{7,6},{8,9},{9,8},{10,11... | collective-permute-start | bytes 393224 | tf_op jit(solution)/shard_map/ppermute | solution.py:163
  16.4 5.0 %collective-permute-start.2 = (f32[256,128]{1,0:T(8,128)S(1)}, f32[256,128]{1,0:T(8,128)S(1)}, u32[]{:S(2)}, u32[]{:S(2)}) collective-permute-start(f32[256,128]{1,0:T(8,128)S(1)} %get-tuple-element.19), channel_id=1, source_target_pairs={{0,1},{1,0},{2,3},{3,2},{4,5},{5,4},{6,7},{7,6},{8,9},{9,8},{10,11... | collective-permute-start | bytes 393224 | tf_op jit(solution)/shard_map/ppermute | solution.py:163
  17.4 7.8 %collective-permute-start.4 = (f32[256,128]{1,0:T(8,128)S(1)}, f32[256,128]{1,0:T(8,128)S(1)}, u32[]{:S(2)}, u32[]{:S(2)}) collective-permute-start(f32[256,128]{1,0:T(8,128)S(1)} %add.16), channel_id=1, source_target_pairs={{2,0},{3,1},{0,2},{1,3},{6,4},{7,5},{4,6},{5,7},{10,8},{11,9},{8,1... | collective-permute-start | bytes 393224 | tf_op jit(solution)/shard_map/ppermute | solution.py:169
  25.3 4.9 %collective-permute-start.8 = (f32[256,128]{1,0:T(8,128)S(1)}, f32[256,128]{1,0:T(8,128)S(1)}, u32[]{:S(2)}, u32[]{:S(2)}) collective-permute-start(f32[256,128]{1,0:T(8,128)S(1)} %get-tuple-element.27), channel_id=1, source_target_pairs={{1,0},{3,5},{0,10},{2,15},{5,4},{7,9},{4,14},{6,3},{9,8},{11,13},{... | collective-permute-start | bytes 393224 | tf_op jit(solution)/shard_map/ppermute | solution.py:153
  26.6 7.2 %collective-permute-start.7 = (f32[256,128]{1,0:T(8,128)S(1)}, f32[256,128]{1,0:T(8,128)S(1)}, u32[]{:S(2)}, u32[]{:S(2)}) collective-permute-start(f32[256,128]{1,0:T(8,128)S(1)} %get-tuple-element.27), channel_id=1, source_target_pairs={{2,0},{0,5},{3,10},{1,15},{6,4},{4,9},{7,14},{5,3},{10,8},{8,13},{... | collective-permute-start | bytes 393224 | tf_op jit(solution)/shard_map/ppermute | solution.py:153
  26.6 7.6 %collective-permute-start.6 = (f32[256,128]{1,0:T(8,128)S(1)}, f32[256,128]{1,0:T(8,128)S(1)}, u32[]{:S(2)}, u32[]{:S(2)}) collective-permute-start(f32[256,128]{1,0:T(8,128)S(1)} %get-tuple-element.27), channel_id=1, source_target_pairs={{3,0},{1,5},{2,10},{0,15},{7,4},{5,9},{6,14},{4,3},{11,8},{9,13},{... | collective-permute-start | bytes 393224 | tf_op jit(solution)/shard_map/ppermute | solution.py:153
  29.6 4.6 %collective-permute-start.5 = (f32[256,128]{1,0:T(8,128)S(1)}, f32[256,128]{1,0:T(8,128)S(1)}, u32[]{:S(2)}, u32[]{:S(2)}) collective-permute-start(f32[256,128]{1,0:T(8,128)S(1)} %get-tuple-element.27), channel_id=1, source_target_pairs={{0,0},{2,5},{1,10},{3,15},{4,4},{6,9},{5,14},{7,3},{8,8},{10,13},{... | collective-permute-start | bytes 393224 | tf_op jit(solution)/shard_map/ppermute | solution.py:153
  35.0 6.9 %collective-permute-start.10 = (f32[256,128]{1,0:T(8,128)S(1)}, f32[256,128]{1,0:T(8,128)S(1)}, u32[]{:S(2)}, u32[]{:S(2)}) collective-permute-start(f32[256,128]{1,0:T(8,128)S(1)} %get-tuple-element.26), channel_id=1, source_target_pairs={{0,1},{1,0},{2,3},{3,2},{4,5},{5,4},{6,7},{7,6},{8,9},{9,8},{10,11... | collective-permute-start | bytes 393224 | tf_op jit(solution)/shard_map/ppermute | solution.py:163
  40.9 3.7 %collective-permute-start.9 = (f32[256,128]{1,0:T(8,128)S(1)}, f32[256,128]{1,0:T(8,128)S(1)}, u32[]{:S(2)}, u32[]{:S(2)}) collective-permute-start(f32[256,128]{1,0:T(8,128)S(1)} %get-tuple-element.24), channel_id=1, source_target_pairs={{0,1},{1,0},{2,3},{3,2},{4,5},{5,4},{6,7},{7,6},{8,9},{9,8},{10,11... | collective-permute-start | bytes 393224 | tf_op jit(solution)/shard_map/ppermute | solution.py:163
  41.9 6.5 %collective-permute-start.11 = (f32[256,128]{1,0:T(8,128)S(1)}, f32[256,128]{1,0:T(8,128)S(1)}, u32[]{:S(2)}, u32[]{:S(2)}) collective-permute-start(f32[256,128]{1,0:T(8,128)S(1)} %add.19), channel_id=1, source_target_pairs={{2,0},{3,1},{0,2},{1,3},{6,4},{7,5},{4,6},{5,7},{10,8},{11,9},{8,1... | collective-permute-start | bytes 393224 | tf_op jit(solution)/shard_map/ppermute | solution.py:169

commit v17 on v16

--- a/solution.py
+++ b/solution.py
@@ -20,7 +20,7 @@
 
 def source_team(team, turn, team_count):
     if team_count == 4:
-        return (2 * (team % 2) + team // 2) ^ (0, 3, 2, 1)[turn]
+        return (2 * (team % 2) + team // 2) ^ (3, 0, 2, 1)[turn]
     return (team + turn) % team_count
 
 

time: 49.3 us -> 49.5 us (level)
  starting transfers between devices: 24.7 us -> 26 us
  waiting for transfers between devices: 16.9 us -> 15.8 us
    ppermute x6, starting transfers between devices: 11.2 us -> 15.7 us  [fetch(): return lax.ppermute(value, ('blk', 'rep'), pairs)]
    ppermute x4, starting transfers between devices: 6.87 us -> 4.01 us  [from_mate(): lax.ppermute(value, 'rep', [(team, team ^ 1) for team in range(team_count)])]
    ppermute x6, waiting for transfers between devices: 7.49 us -> 6.41 us  [fetch(): return lax.ppermute(value, ('blk', 'rep'), pairs)]
  transfers between devices with their start and end apart: 12 -> 12, of which waited for: 7 -> 6; matrix products, arithmetic and copies ran while one was open for 0% -> 0% of each run, Pallas kernels for 1% -> 1%
where the time goes in v17:
time: 49.5 us; the launch traced here: 49.2 us
  starting transfers between devices  26 us (53%)
  waiting for transfers between devices  15.8 us (32%)
  local copies, waits for them, and re-layouts  3.52 us (7%)
  Pallas kernels  3.01 us (6%)
  between operations  0.72 us (1%)
    ppermute x6, starting transfers between devices, fetch(): return lax.ppermute(value, ('blk', 'rep'), pairs)  15.7 us
    ppermute x2, waiting for transfers between devices, from_column(): return lax.ppermute(value, 'rep', pairs)  7.61 us
    ppermute x6, waiting for transfers between devices, fetch(): return lax.ppermute(value, ('blk', 'rep'), pairs)  6.41 us
    ppermute x2, starting transfers between devices, from_column(): return lax.ppermute(value, 'rep', pairs)  6.3 us
    ppermute x4, starting transfers between devices, from_mate(): lax.ppermute(value, 'rep', [(team, team ^ 1) for team in range(team_count)])  4.01 us
    unnamed x10, local copies, waits for them, and re-layouts  3.44 us
    ppermute x4, waiting for transfers between devices, from_mate(): lax.ppermute(value, 'rep', [(team, team ^ 1) for team in range(team_count)])  1.82 us
    pallas_call x2, Pallas kernels, arc_step(): pl.pallas_call(functools.partial(arc_kernel, team_count=team_count, piece...  1.74 us
  transfers between devices with their start and end apart: 12, of which 6 were waited for; matrix products, arithmetic and copies ran while one was open for 0% of the time, Pallas kernels for 1%

profile of v17, /device:TPU:0, one launch (start us, length us, event | category | flops | bytes accessed | tf_op | source)
XLA Modules:
  0.0 49.2 jit_solution(6496587853749543190)
XLA Ops:
  0.0 5.4 %collective-permute-start.1 = (f32[1024,128]{1,0:T(8,128)}, f32[1024,128]{1,0:T(8,128)S(1)}, u32[]{:S(2)}, u32[]{:S(2)}) collective-permute-start(f32[1024,128]{1,0:T(8,128)} %embeddings_ref.1), channel_id=1, source_target_pairs={{3,0},{1,5},{2,10},{0,15},{7,4},{5,9},{6,14},{4,3},{11,8},{9,13},{... | collective-permute-start | bytes 1572872 | tf_op jit(solution)/shard_map/ppermute | solution.py:153
  5.4 0.8 %collective-permute-start = (s32[8,128]{1,0:T(8,128)}, s32[8,128]{1,0:T(8,128)S(1)}, u32[]{:S(2)}, u32[]{:S(2)}) collective-permute-start(s32[8,128]{1,0:T(8,128)} %bitcast.12), channel_id=1, source_target_pairs={{3,0},{1,5},{2,10},{0,15},{7,4},{5,9},{6,14},{4,3},{11,8},{9,13},{... | collective-permute-start | bytes 12296 | tf_op jit(solution)/shard_map/ppermute | solution.py:153
  6.9 0.6 %copy-done.3 = s32[1,1,1,24]{3,2,1,0:T(1,128)S(1)} copy-done((s32[1,1,1,24]{3,2,1,0:T(1,128)S(1)}, s32[1,1,1,24]{3,2,1,0:T(1,128)}, u32[]{:S(2)}) %copy-start.3) | copy-done | bytes 120
  7.5 0.0 copy-done.4
  7.6 0.1 add_bitcast_fusion
  7.6 0.1 squeeze.19.after_ref.info_ref
  7.7 0.6 %copy-done.2 = s32[1024]{0:T(1024)S(1)} copy-done((s32[1024]{0:T(1024)S(1)}, s32[1024]{0:T(1024)}, u32[]{:S(2)}) %copy-start.2) | copy-done | bytes 4120
  8.3 1.1 %copy-done = bf16[1,1,1,24,128,128]{5,4,3,2,1,0:T(8,128)(2,1)S(1)} copy-done((bf16[1,1,1,24,128,128]{5,4,3,2,1,0:T(8,128)(2,1)S(1)}, bf16[1,1,1,24,128,128]{5,4,3,2,1,0:T(8,128)(2,1)}, u32[]{:S(2)}) %copy-start) | copy-done | bytes 786456
  9.5 1.0 %copy-done.1 = f32[1024,128]{1,0:T(8,128)S(1)} copy-done((f32[1024,128]{1,0:T(8,128)S(1)}, f32[1024,128]{1,0:T(8,128)}, u32[]{:S(2)}) %copy-start.1) | copy-done | bytes 524312
  10.5 0.6 %shard_map.64 = (bf16[1,24,128,128]{3,2,1,0:T(8,128)(2,1)S(1)}, f32[256,128]{1,0:T(8,128)S(1)}, f32[256,128]{1,0:T(8,128)S(1)}) custom-call(s32[8,128]{1,0:T(8,128)S(1)} %bitcast.13, f32[1024,128]{1,0:T(8,128)S(1)} %copy-done.1, bf16[1,24,128,128]{3,2,1,0:T(8,128)(2,1)S(1)} %bitcast.11, s32[49,128]{1,0:T(8,128)S(1)} %squeeze.19.after_ref.info_ref), custom_call_target="tpu_custom_call" | custom-call | flops 131072 | bytes 524288 | tf_op jit(solution)/shard_map/pallas_call | solution.py:56
  11.1 3.5 %collective-permute-done.refs_0_ = s32[8,128]{1,0:T(8,128)S(1)} collective-permute-done((s32[8,128]{1,0:T(8,128)}, s32[8,128]{1,0:T(8,128)S(1)}, u32[]{:S(2)}, u32[]{:S(2)}) %collective-permute-start) | collective-permute-done | bytes 4128 | tf_op jit(solution)/shard_map/ppermute | solution.py:153
  14.6 0.0 collective-permute-done.1.refs_1_
  14.6 1.0 %shard_map.65 = (f32[256,128]{1,0:T(8,128)S(1)}, f32[256,128]{1,0:T(8,128)S(1)}, f32[256,128]{1,0:T(8,128)S(1)}, f32[256,128]{1,0:T(8,128)S(1)}) custom-call(s32[49,128]{1,0:T(8,128)S(1)} %squeeze.19.after_ref.info_ref, bf16[24,128,128]{2,1,0:T(8,128)(2,1)S(1)} %bitcast.9, s32[8,128]{1,0:T(8,128)S(1)} %collective-permute-done.refs_0_, ...), custom_call_target="tpu_custom_call" | custom-call | flops 201326592 | bytes 1048576 | tf_op jit(solution)/shard_map/pallas_call | solution.py:124
  15.6 0.8 %collective-permute-start.3 = (f32[256,128]{1,0:T(8,128)S(1)}, f32[256,128]{1,0:T(8,128)S(1)}, u32[]{:S(2)}, u32[]{:S(2)}) collective-permute-start(f32[256,128]{1,0:T(8,128)S(1)} %get-tuple-element.21), channel_id=1, source_target_pairs={{0,1},{1,0},{2,3},{3,2},{4,5},{5,4},{6,7},{7,6},{8,9},{9,8},{10,11... | collective-permute-start | bytes 393224 | tf_op jit(solution)/shard_map/ppermute | solution.py:163
  16.4 0.1 collective-permute-start.2
  16.5 0.9 %collective-permute-done.3 = f32[256,128]{1,0:T(8,128)S(1)} collective-permute-done((f32[256,128]{1,0:T(8,128)S(1)}, f32[256,128]{1,0:T(8,128)S(1)}, u32[]{:S(2)}, u32[]{:S(2)}) %collective-permute-start.3) | collective-permute-done | bytes 131104 | tf_op jit(solution)/shard_map/ppermute | solution.py:163
  17.4 4.0 %collective-permute-start.4 = (f32[256,128]{1,0:T(8,128)S(1)}, f32[256,128]{1,0:T(8,128)S(1)}, u32[]{:S(2)}, u32[]{:S(2)}) collective-permute-start(f32[256,128]{1,0:T(8,128)S(1)} %add.16), channel_id=1, source_target_pairs={{2,0},{3,1},{0,2},{1,3},{6,4},{7,5},{4,6},{5,7},{10,8},{11,9},{8,1... | collective-permute-start | bytes 393224 | tf_op jit(solution)/shard_map/ppermute | solution.py:169
  21.4 0.0 collective-permute-done.2
  21.4 3.8 %collective-permute-done.4 = f32[256,128]{1,0:T(8,128)S(1)} collective-permute-done((f32[256,128]{1,0:T(8,128)S(1)}, f32[256,128]{1,0:T(8,128)S(1)}, u32[]{:S(2)}, u32[]{:S(2)}) %collective-permute-start.4) | collective-permute-done | bytes 131104 | tf_op jit(solution)/shard_map/ppermute | solution.py:169
  25.3 1.3 %collective-permute-start.8 = (f32[256,128]{1,0:T(8,128)S(1)}, f32[256,128]{1,0:T(8,128)S(1)}, u32[]{:S(2)}, u32[]{:S(2)}) collective-permute-start(f32[256,128]{1,0:T(8,128)S(1)} %get-tuple-element.27), channel_id=1, source_target_pairs={{1,0},{3,5},{0,10},{2,15},{5,4},{7,9},{4,14},{6,3},{9,8},{11,13},{... | collective-permute-start | bytes 393224 | tf_op jit(solution)/shard_map/ppermute | solution.py:153
  26.6 0.0 collective-permute-start.7
  26.6 0.7 %collective-permute-start.6 = (f32[256,128]{1,0:T(8,128)S(1)}, f32[256,128]{1,0:T(8,128)S(1)}, u32[]{:S(2)}, u32[]{:S(2)}) collective-permute-start(f32[256,128]{1,0:T(8,128)S(1)} %get-tuple-element.27), channel_id=1, source_target_pairs={{0,0},{2,5},{1,10},{3,15},{4,4},{6,9},{5,14},{7,3},{8,8},{10,13},{... | collective-permute-start | bytes 393224 | tf_op jit(solution)/shard_map/ppermute | solution.py:153
  27.2 7.5 %collective-permute-start.5 = (f32[256,128]{1,0:T(8,128)S(1)}, f32[256,128]{1,0:T(8,128)S(1)}, u32[]{:S(2)}, u32[]{:S(2)}) collective-permute-start(f32[256,128]{1,0:T(8,128)S(1)} %get-tuple-element.27), channel_id=1, source_target_pairs={{3,0},{1,5},{2,10},{0,15},{7,4},{5,9},{6,14},{4,3},{11,8},{9,13},{... | collective-permute-start | bytes 393224 | tf_op jit(solution)/shard_map/ppermute | solution.py:153
  34.7 0.0 collective-permute-done.8.refs_3_
  34.7 2.9 %collective-permute-done.5.refs_0_ = f32[256,128]{1,0:T(8,128)S(1)} collective-permute-done((f32[256,128]{1,0:T(8,128)S(1)}, f32[256,128]{1,0:T(8,128)S(1)}, u32[]{:S(2)}, u32[]{:S(2)}) %collective-permute-start.5) | collective-permute-done | bytes 131104 | tf_op jit(solution)/shard_map/ppermute | solution.py:153
  37.6 0.8 %shard_map.66 = (f32[256,128]{1,0:T(8,128)S(1)}, f32[256,128]{1,0:T(8,128)S(1)}, f32[256,128]{1,0:T(8,128)S(1)}, f32[256,128]{1,0:T(8,128)S(1)}) custom-call(s32[49,128]{1,0:T(8,128)S(1)} %squeeze.19.after_ref.info_ref, bf16[24,128,128]{2,1,0:T(8,128)(2,1)S(1)} %bitcast.10, f32[256,128]{1,0:T(8,128)S(1)} %collective-permute-done.5.refs_0_, ...), custom_call_target="tpu_custom_call" | custom-call | flops 201326592 | bytes 1048576 | tf_op jit(solution)/shard_map/pallas_call | solution.py:124
  38.4 3.1 %collective-permute-start.10 = (f32[256,128]{1,0:T(8,128)S(1)}, f32[256,128]{1,0:T(8,128)S(1)}, u32[]{:S(2)}, u32[]{:S(2)}) collective-permute-start(f32[256,128]{1,0:T(8,128)S(1)} %get-tuple-element.26), channel_id=1, source_target_pairs={{0,1},{1,0},{2,3},{3,2},{4,5},{5,4},{6,7},{7,6},{8,9},{9,8},{10,11... | collective-permute-start | bytes 393224 | tf_op jit(solution)/shard_map/ppermute | solution.py:163
  41.4 0.1 collective-permute-start.9
  41.5 0.9 %collective-permute-done.10 = f32[256,128]{1,0:T(8,128)S(1)} collective-permute-done((f32[256,128]{1,0:T(8,128)S(1)}, f32[256,128]{1,0:T(8,128)S(1)}, u32[]{:S(2)}, u32[]{:S(2)}) %collective-permute-start.10) | collective-permute-done | bytes 131104 | tf_op jit(solution)/shard_map/ppermute | solution.py:163
  42.4 2.3 %collective-permute-start.11 = (f32[256,128]{1,0:T(8,128)S(1)}, f32[256,128]{1,0:T(8,128)S(1)}, u32[]{:S(2)}, u32[]{:S(2)}) collective-permute-start(f32[256,128]{1,0:T(8,128)S(1)} %add.19), channel_id=1, source_target_pairs={{2,0},{3,1},{0,2},{1,3},{6,4},{7,5},{4,6},{5,7},{10,8},{11,9},{8,1... | collective-permute-start | bytes 393224 | tf_op jit(solution)/shard_map/ppermute | solution.py:169
  44.7 3.8 %collective-permute-done.11.refs_2_ = f32[256,128]{1,0:T(8,128)S(1)} collective-permute-done((f32[256,128]{1,0:T(8,128)S(1)}, f32[256,128]{1,0:T(8,128)S(1)}, u32[]{:S(2)}, u32[]{:S(2)}) %collective-permute-start.11) | collective-permute-done | bytes 131104 | tf_op jit(solution)/shard_map/ppermute | solution.py:169
  48.5 0.7 %shard_map.67 = f32[256,128]{1,0:T(8,128)} custom-call(f32[256,128]{1,0:T(8,128)S(1)} %get-tuple-element.28.base_ref, f32[256,128]{1,0:T(8,128)S(1)} %get-tuple-element.22.norm_ref, f32[256,128]{1,0:T(8,128)S(1)} %get-tuple-element.23.refs_0_, f32[256,128]{1,0:T(8,128)S(1)} %collective-permute-done.9.refs_1_, f32[256,128]{1,0:T(8,128)S(1)} %collective-permute-done.11.refs_2_), custom_call_target="tpu_custom_call" | custom-call | tf_op jit(solution)/shard_map/pallas_call | solution.py:199
  (11 shorter events, 0.1 us)
Async XLA Ops:
  0.0 14.6 %collective-permute-start.1 = (f32[1024,128]{1,0:T(8,128)}, f32[1024,128]{1,0:T(8,128)S(1)}, u32[]{:S(2)}, u32[]{:S(2)}) collective-permute-start(f32[1024,128]{1,0:T(8,128)} %embeddings_ref.1), channel_id=1, source_target_pairs={{3,0},{1,5},{2,10},{0,15},{7,4},{5,9},{6,14},{4,3},{11,8},{9,13},{... | collective-permute-start | bytes 1572872 | tf_op jit(solution)/shard_map/ppermute | solution.py:153
  5.4 9.2 %collective-permute-start = (s32[8,128]{1,0:T(8,128)}, s32[8,128]{1,0:T(8,128)S(1)}, u32[]{:S(2)}, u32[]{:S(2)}) collective-permute-start(s32[8,128]{1,0:T(8,128)} %bitcast.12), channel_id=1, source_target_pairs={{3,0},{1,5},{2,10},{0,15},{7,4},{5,9},{6,14},{4,3},{11,8},{9,13},{... | collective-permute-start | bytes 12296 | tf_op jit(solution)/shard_map/ppermute | solution.py:153
  6.9 0.7 %copy-start.3 = (s32[1,1,1,24]{3,2,1,0:T(1,128)S(1)}, s32[1,1,1,24]{3,2,1,0:T(1,128)}, u32[]{:S(2)}) copy-start(s32[1,1,1,24]{3,2,1,0:T(1,128)} %param.10) | copy-start | bytes 292
  6.9 0.7 %copy-start.4 = (s32[1,1,1,24]{3,2,1,0:T(1,128)S(1)}, s32[1,1,1,24]{3,2,1,0:T(1,128)}, u32[]{:S(2)}) copy-start(s32[1,1,1,24]{3,2,1,0:T(1,128)} %param.9) | copy-start | bytes 292
  7.6 0.7 %copy-start.2 = (s32[1024]{0:T(1024)S(1)}, s32[1024]{0:T(1024)}, u32[]{:S(2)}) copy-start(s32[1024]{0:T(1024)} %param.7) | copy-start | bytes 12292
  8.3 1.1 %copy-start = (bf16[1,1,1,24,128,128]{5,4,3,2,1,0:T(8,128)(2,1)S(1)}, bf16[1,1,1,24,128,128]{5,4,3,2,1,0:T(8,128)(2,1)}, u32[]{:S(2)}) copy-start(bf16[1,1,1,24,128,128]{5,4,3,2,1,0:T(8,128)(2,1)} %param.8) | copy-start | bytes 2359300
  9.5 1.0 %copy-start.1 = (f32[1024,128]{1,0:T(8,128)S(1)}, f32[1024,128]{1,0:T(8,128)}, u32[]{:S(2)}) copy-start(f32[1024,128]{1,0:T(8,128)} %embeddings_ref.1) | copy-start | bytes 1572868
  15.6 1.8 %collective-permute-start.3 = (f32[256,128]{1,0:T(8,128)S(1)}, f32[256,128]{1,0:T(8,128)S(1)}, u32[]{:S(2)}, u32[]{:S(2)}) collective-permute-start(f32[256,128]{1,0:T(8,128)S(1)} %get-tuple-element.21), channel_id=1, source_target_pairs={{0,1},{1,0},{2,3},{3,2},{4,5},{5,4},{6,7},{7,6},{8,9},{9,8},{10,11... | collective-permute-start | bytes 393224 | tf_op jit(solution)/shard_map/ppermute | solution.py:163
  16.4 5.0 %collective-permute-start.2 = (f32[256,128]{1,0:T(8,128)S(1)}, f32[256,128]{1,0:T(8,128)S(1)}, u32[]{:S(2)}, u32[]{:S(2)}) collective-permute-start(f32[256,128]{1,0:T(8,128)S(1)} %get-tuple-element.19), channel_id=1, source_target_pairs={{0,1},{1,0},{2,3},{3,2},{4,5},{5,4},{6,7},{7,6},{8,9},{9,8},{10,11... | collective-permute-start | bytes 393224 | tf_op jit(solution)/shard_map/ppermute | solution.py:163
  17.4 7.8 %collective-permute-start.4 = (f32[256,128]{1,0:T(8,128)S(1)}, f32[256,128]{1,0:T(8,128)S(1)}, u32[]{:S(2)}, u32[]{:S(2)}) collective-permute-start(f32[256,128]{1,0:T(8,128)S(1)} %add.16), channel_id=1, source_target_pairs={{2,0},{3,1},{0,2},{1,3},{6,4},{7,5},{4,6},{5,7},{10,8},{11,9},{8,1... | collective-permute-start | bytes 393224 | tf_op jit(solution)/shard_map/ppermute | solution.py:169
  25.3 9.4 %collective-permute-start.8 = (f32[256,128]{1,0:T(8,128)S(1)}, f32[256,128]{1,0:T(8,128)S(1)}, u32[]{:S(2)}, u32[]{:S(2)}) collective-permute-start(f32[256,128]{1,0:T(8,128)S(1)} %get-tuple-element.27), channel_id=1, source_target_pairs={{1,0},{3,5},{0,10},{2,15},{5,4},{7,9},{4,14},{6,3},{9,8},{11,13},{... | collective-permute-start | bytes 393224 | tf_op jit(solution)/shard_map/ppermute | solution.py:153
  26.6 8.2 %collective-permute-start.7 = (f32[256,128]{1,0:T(8,128)S(1)}, f32[256,128]{1,0:T(8,128)S(1)}, u32[]{:S(2)}, u32[]{:S(2)}) collective-permute-start(f32[256,128]{1,0:T(8,128)S(1)} %get-tuple-element.27), channel_id=1, source_target_pairs={{2,0},{0,5},{3,10},{1,15},{6,4},{4,9},{7,14},{5,3},{10,8},{8,13},{... | collective-permute-start | bytes 393224 | tf_op jit(solution)/shard_map/ppermute | solution.py:153
  26.6 8.2 %collective-permute-start.6 = (f32[256,128]{1,0:T(8,128)S(1)}, f32[256,128]{1,0:T(8,128)S(1)}, u32[]{:S(2)}, u32[]{:S(2)}) collective-permute-start(f32[256,128]{1,0:T(8,128)S(1)} %get-tuple-element.27), channel_id=1, source_target_pairs={{0,0},{2,5},{1,10},{3,15},{4,4},{6,9},{5,14},{7,3},{8,8},{10,13},{... | collective-permute-start | bytes 393224 | tf_op jit(solution)/shard_map/ppermute | solution.py:153
  27.2 10.4 %collective-permute-start.5 = (f32[256,128]{1,0:T(8,128)S(1)}, f32[256,128]{1,0:T(8,128)S(1)}, u32[]{:S(2)}, u32[]{:S(2)}) collective-permute-start(f32[256,128]{1,0:T(8,128)S(1)} %get-tuple-element.27), channel_id=1, source_target_pairs={{3,0},{1,5},{2,10},{0,15},{7,4},{5,9},{6,14},{4,3},{11,8},{9,13},{... | collective-permute-start | bytes 393224 | tf_op jit(solution)/shard_map/ppermute | solution.py:153
  38.4 4.0 %collective-permute-start.10 = (f32[256,128]{1,0:T(8,128)S(1)}, f32[256,128]{1,0:T(8,128)S(1)}, u32[]{:S(2)}, u32[]{:S(2)}) collective-permute-start(f32[256,128]{1,0:T(8,128)S(1)} %get-tuple-element.26), channel_id=1, source_target_pairs={{0,1},{1,0},{2,3},{3,2},{4,5},{5,4},{6,7},{7,6},{8,9},{9,8},{10,11... | collective-permute-start | bytes 393224 | tf_op jit(solution)/shard_map/ppermute | solution.py:163
  41.4 3.3 %collective-permute-start.9 = (f32[256,128]{1,0:T(8,128)S(1)}, f32[256,128]{1,0:T(8,128)S(1)}, u32[]{:S(2)}, u32[]{:S(2)}) collective-permute-start(f32[256,128]{1,0:T(8,128)S(1)} %get-tuple-element.24), channel_id=1, source_target_pairs={{0,1},{1,0},{2,3},{3,2},{4,5},{5,4},{6,7},{7,6},{8,9},{9,8},{10,11... | collective-permute-start | bytes 393224 | tf_op jit(solution)/shard_map/ppermute | solution.py:163
  42.4 6.1 %collective-permute-start.11 = (f32[256,128]{1,0:T(8,128)S(1)}, f32[256,128]{1,0:T(8,128)S(1)}, u32[]{:S(2)}, u32[]{:S(2)}) collective-permute-start(f32[256,128]{1,0:T(8,128)S(1)} %add.19), channel_id=1, source_target_pairs={{2,0},{3,1},{0,2},{1,3},{6,4},{7,5},{4,6},{5,7},{10,8},{11,9},{8,1... | collective-permute-start | bytes 393224 | tf_op jit(solution)/shard_map/ppermute | solution.py:169

commit v18 on v12

--- a/solution.py
+++ b/solution.py
@@ -143,13 +143,13 @@
     )(*operands)
 
 
-def fetch(value, source_team, arc_length):
+def fetch(value, source, arc_length):
     cycle, team_count = lax.axis_size("blk"), lax.axis_size("rep")
     pairs = []
     for shard in range(cycle):
         for team in range(team_count):
             to_shard = (shard + team * arc_length) % cycle
-            pairs.append((shard * team_count + source_team(team), to_shard * team_count + team))
+            pairs.append((shard * team_count + source(shard, team), to_shard * team_count + team))
     return lax.ppermute(value, ("blk", "rep"), pairs)
 
 
@@ -209,12 +209,14 @@
 def per_device(embeddings, degrees, tile_values, tile_rows, tile_columns, slot_counts):
     arc_length, _, tile_size, _ = tile_values.shape[2:]
     panel_rows = embeddings.shape[0]
-    team_count = lax.axis_size("rep")
-    spread = (3, 1, 2, 0) if team_count == 4 else tuple(range(team_count))
+    cycle, team_count = lax.axis_size("blk"), lax.axis_size("rep")
+    spread = [tuple(range(team_count))] * cycle
+    if (cycle, team_count) == (4, 4):
+        spread = [(2, 1, 0, 3), (0, 1, 2, 3), (3, 0, 2, 1), (0, 1, 2, 3)]
     degrees = degrees.reshape(panel_rows // tile_size, tile_size)
 
-    panel = fetch(embeddings, lambda team: spread[team], arc_length)
-    pieces = [fetch(degrees, lambda team: spread[team], arc_length), panel]
+    panel = fetch(embeddings, lambda shard, team: spread[shard][team], arc_length)
+    pieces = [fetch(degrees, lambda shard, team: spread[shard][team], arc_length), panel]
     info = jnp.concatenate([slot_counts[0, 0][:, None], tile_rows[0, 0], tile_columns[0, 0]], axis=1)
     info = jnp.broadcast_to(info[:, :, None], (*info.shape, embeddings.shape[1]))
     info = [info[at] for at in range(arc_length)]
@@ -234,7 +236,7 @@
         combined = combined + current
         source = current * norm_scale
         pieces = [
-            fetch(source, lambda team, k=k: source_team(team, k, team_count), arc_length)
+            fetch(source, lambda shard, team, k=k: source_team(team, k, team_count), arc_length)
             for k in range(team_count)
         ]
 

time: 48.9 us -> 50.7 us (1.037)
  starting transfers between devices: 21.3 us -> 23.6 us
    ppermute x6, starting transfers between devices: 11 us -> 14.3 us  [fetch(): return lax.ppermute(value, ('blk', 'rep'), pairs)]
    ppermute x2, starting transfers between devices: 6.72 us -> 6.12 us  [from_column(): return lax.ppermute(value, 'rep', pairs)]
where the time goes in v18:
time: 50.7 us; the launch traced here: 50.4 us
  starting transfers between devices  23.6 us (47%)
  waiting for transfers between devices  19.4 us (38%)
  local copies, waits for them, and re-layouts  3.52 us (7%)
  Pallas kernels  3.01 us (6%)
  between operations  0.74 us (1%)
    ppermute x6, starting transfers between devices, fetch(): return lax.ppermute(value, ('blk', 'rep'), pairs)  14.3 us
    ppermute x6, waiting for transfers between devices, fetch(): return lax.ppermute(value, ('blk', 'rep'), pairs)  10.1 us
    ppermute x2, waiting for transfers between devices, from_column(): return lax.ppermute(value, 'rep', pairs)  7.61 us
    ppermute x2, starting transfers between devices, from_column(): return lax.ppermute(value, 'rep', pairs)  6.12 us
    unnamed x10, local copies, waits for them, and re-layouts  3.44 us
    ppermute x4, starting transfers between devices, from_mate(): lax.ppermute(value, 'rep', [(team, team ^ 1) for team in range(team_count)])  3.18 us
    ppermute x4, waiting for transfers between devices, from_mate(): lax.ppermute(value, 'rep', [(team, team ^ 1) for team in range(team_count)])  1.75 us
    pallas_call x2, Pallas kernels, arc_step(): pl.pallas_call(functools.partial(arc_kernel, team_count=team_count, piece...  1.74 us
  transfers between devices with their start and end apart: 12, of which 8 were waited for; matrix products, arithmetic and copies ran while one was open for 0% of the time, Pallas kernels for 1%

profile of v18, /device:TPU:0, one launch (start us, length us, event | category | flops | bytes accessed | tf_op | source)
XLA Modules:
  0.0 50.4 jit_solution(12006383321713652055)
XLA Ops:
  0.0 6.9 %collective-permute-start.1 = (f32[1024,128]{1,0:T(8,128)}, f32[1024,128]{1,0:T(8,128)S(1)}, u32[]{:S(2)}, u32[]{:S(2)}) collective-permute-start(f32[1024,128]{1,0:T(8,128)} %embeddings_ref.1), channel_id=1, source_target_pairs={{2,0},{1,5},{0,10},{3,15},{4,4},{5,9},{6,14},{7,3},{11,8},{8,13},{... | collective-permute-start | bytes 1572872 | tf_op jit(solution)/shard_map/ppermute | solution.py:153
  6.9 2.2 %collective-permute-start = (s32[8,128]{1,0:T(8,128)}, s32[8,128]{1,0:T(8,128)S(1)}, u32[]{:S(2)}, u32[]{:S(2)}) collective-permute-start(s32[8,128]{1,0:T(8,128)} %bitcast.12), channel_id=1, source_target_pairs={{2,0},{1,5},{0,10},{3,15},{4,4},{5,9},{6,14},{7,3},{11,8},{8,13},{... | collective-permute-start | bytes 12296 | tf_op jit(solution)/shard_map/ppermute | solution.py:153
  9.8 0.6 %copy-done.3 = s32[1,1,1,24]{3,2,1,0:T(1,128)S(1)} copy-done((s32[1,1,1,24]{3,2,1,0:T(1,128)S(1)}, s32[1,1,1,24]{3,2,1,0:T(1,128)}, u32[]{:S(2)}) %copy-start.3) | copy-done | bytes 120
  10.4 0.0 copy-done.4
  10.4 0.1 add_bitcast_fusion
  10.5 0.1 squeeze.19.after_ref.info_ref
  10.6 0.6 %copy-done.2 = s32[1024]{0:T(1024)S(1)} copy-done((s32[1024]{0:T(1024)S(1)}, s32[1024]{0:T(1024)}, u32[]{:S(2)}) %copy-start.2) | copy-done | bytes 4120
  11.2 1.1 %copy-done = bf16[1,1,1,24,128,128]{5,4,3,2,1,0:T(8,128)(2,1)S(1)} copy-done((bf16[1,1,1,24,128,128]{5,4,3,2,1,0:T(8,128)(2,1)S(1)}, bf16[1,1,1,24,128,128]{5,4,3,2,1,0:T(8,128)(2,1)}, u32[]{:S(2)}) %copy-start) | copy-done | bytes 786456
  12.3 1.0 %copy-done.1 = f32[1024,128]{1,0:T(8,128)S(1)} copy-done((f32[1024,128]{1,0:T(8,128)S(1)}, f32[1024,128]{1,0:T(8,128)}, u32[]{:S(2)}) %copy-start.1) | copy-done | bytes 524312
  13.4 0.6 %shard_map.64 = (bf16[1,24,128,128]{3,2,1,0:T(8,128)(2,1)S(1)}, f32[256,128]{1,0:T(8,128)S(1)}, f32[256,128]{1,0:T(8,128)S(1)}) custom-call(s32[8,128]{1,0:T(8,128)S(1)} %bitcast.13, f32[1024,128]{1,0:T(8,128)S(1)} %copy-done.1, bf16[1,24,128,128]{3,2,1,0:T(8,128)(2,1)S(1)} %bitcast.11, s32[49,128]{1,0:T(8,128)S(1)} %squeeze.19.after_ref.info_ref), custom_call_target="tpu_custom_call" | custom-call | flops 131072 | bytes 524288 | tf_op jit(solution)/shard_map/pallas_call | solution.py:56
  14.0 2.5 %collective-permute-done.refs_0_ = s32[8,128]{1,0:T(8,128)S(1)} collective-permute-done((s32[8,128]{1,0:T(8,128)}, s32[8,128]{1,0:T(8,128)S(1)}, u32[]{:S(2)}, u32[]{:S(2)}) %collective-permute-start) | collective-permute-done | bytes 4128 | tf_op jit(solution)/shard_map/ppermute | solution.py:153
  16.5 1.0 %shard_map.65 = (f32[256,128]{1,0:T(8,128)S(1)}, f32[256,128]{1,0:T(8,128)S(1)}, f32[256,128]{1,0:T(8,128)S(1)}, f32[256,128]{1,0:T(8,128)S(1)}) custom-call(s32[49,128]{1,0:T(8,128)S(1)} %squeeze.19.after_ref.info_ref, bf16[24,128,128]{2,1,0:T(8,128)(2,1)S(1)} %bitcast.9, s32[8,128]{1,0:T(8,128)S(1)} %collective-permute-done.refs_0_, ...), custom_call_target="tpu_custom_call" | custom-call | flops 201326592 | bytes 1048576 | tf_op jit(solution)/shard_map/pallas_call | solution.py:124
  17.5 0.1 collective-permute-start.3
  17.6 0.5 collective-permute-start.2
  18.1 0.8 %collective-permute-done.3 = f32[256,128]{1,0:T(8,128)S(1)} collective-permute-done((f32[256,128]{1,0:T(8,128)S(1)}, f32[256,128]{1,0:T(8,128)S(1)}, u32[]{:S(2)}, u32[]{:S(2)}) %collective-permute-start.3) | collective-permute-done | bytes 131104 | tf_op jit(solution)/shard_map/ppermute | solution.py:163
  18.9 3.4 %collective-permute-start.4 = (f32[256,128]{1,0:T(8,128)S(1)}, f32[256,128]{1,0:T(8,128)S(1)}, u32[]{:S(2)}, u32[]{:S(2)}) collective-permute-start(f32[256,128]{1,0:T(8,128)S(1)} %add.16), channel_id=1, source_target_pairs={{2,0},{3,1},{0,2},{1,3},{6,4},{7,5},{4,6},{5,7},{10,8},{11,9},{8,1... | collective-permute-start | bytes 393224 | tf_op jit(solution)/shard_map/ppermute | solution.py:169
  22.3 3.8 %collective-permute-done.4 = f32[256,128]{1,0:T(8,128)S(1)} collective-permute-done((f32[256,128]{1,0:T(8,128)S(1)}, f32[256,128]{1,0:T(8,128)S(1)}, u32[]{:S(2)}, u32[]{:S(2)}) %collective-permute-start.4) | collective-permute-done | bytes 131104 | tf_op jit(solution)/shard_map/ppermute | solution.py:169
  26.2 4.5 %collective-permute-start.8 = (f32[256,128]{1,0:T(8,128)S(1)}, f32[256,128]{1,0:T(8,128)S(1)}, u32[]{:S(2)}, u32[]{:S(2)}) collective-permute-start(f32[256,128]{1,0:T(8,128)S(1)} %get-tuple-element.27), channel_id=1, source_target_pairs={{3,0},{1,5},{2,10},{0,15},{7,4},{5,9},{6,14},{4,3},{11,8},{9,13},{... | collective-permute-start | bytes 393224 | tf_op jit(solution)/shard_map/ppermute | solution.py:153
  30.7 0.0 collective-permute-start.7
  30.7 0.0 collective-permute-start.6
  30.7 0.7 %collective-permute-start.5 = (f32[256,128]{1,0:T(8,128)S(1)}, f32[256,128]{1,0:T(8,128)S(1)}, u32[]{:S(2)}, u32[]{:S(2)}) collective-permute-start(f32[256,128]{1,0:T(8,128)S(1)} %get-tuple-element.27), channel_id=1, source_target_pairs={{0,0},{2,5},{1,10},{3,15},{4,4},{6,9},{5,14},{7,3},{8,8},{10,13},{... | collective-permute-start | bytes 393224 | tf_op jit(solution)/shard_map/ppermute | solution.py:153
  31.4 2.9 %collective-permute-done.8.refs_3_ = f32[256,128]{1,0:T(8,128)S(1)} collective-permute-done((f32[256,128]{1,0:T(8,128)S(1)}, f32[256,128]{1,0:T(8,128)S(1)}, u32[]{:S(2)}, u32[]{:S(2)}) %collective-permute-start.8) | collective-permute-done | bytes 131104 | tf_op jit(solution)/shard_map/ppermute | solution.py:153
  34.2 2.1 %collective-permute-done.7.refs_2_ = f32[256,128]{1,0:T(8,128)S(1)} collective-permute-done((f32[256,128]{1,0:T(8,128)S(1)}, f32[256,128]{1,0:T(8,128)S(1)}, u32[]{:S(2)}, u32[]{:S(2)}) %collective-permute-start.7) | collective-permute-done | bytes 131104 | tf_op jit(solution)/shard_map/ppermute | solution.py:153
  36.4 2.5 %collective-permute-done.6.refs_1_ = f32[256,128]{1,0:T(8,128)S(1)} collective-permute-done((f32[256,128]{1,0:T(8,128)S(1)}, f32[256,128]{1,0:T(8,128)S(1)}, u32[]{:S(2)}, u32[]{:S(2)}) %collective-permute-start.6) | collective-permute-done | bytes 131104 | tf_op jit(solution)/shard_map/ppermute | solution.py:153
  38.9 0.0 collective-permute-done.5.refs_0_
  38.9 0.8 %shard_map.66 = (f32[256,128]{1,0:T(8,128)S(1)}, f32[256,128]{1,0:T(8,128)S(1)}, f32[256,128]{1,0:T(8,128)S(1)}, f32[256,128]{1,0:T(8,128)S(1)}) custom-call(s32[49,128]{1,0:T(8,128)S(1)} %squeeze.19.after_ref.info_ref, bf16[24,128,128]{2,1,0:T(8,128)(2,1)S(1)} %bitcast.10, f32[256,128]{1,0:T(8,128)S(1)} %collective-permute-done.5.refs_0_, ...), custom_call_target="tpu_custom_call" | custom-call | flops 201326592 | bytes 1048576 | tf_op jit(solution)/shard_map/pallas_call | solution.py:124
  39.7 2.5 %collective-permute-start.10 = (f32[256,128]{1,0:T(8,128)S(1)}, f32[256,128]{1,0:T(8,128)S(1)}, u32[]{:S(2)}, u32[]{:S(2)}) collective-permute-start(f32[256,128]{1,0:T(8,128)S(1)} %get-tuple-element.26), channel_id=1, source_target_pairs={{0,1},{1,0},{2,3},{3,2},{4,5},{5,4},{6,7},{7,6},{8,9},{9,8},{10,11... | collective-permute-start | bytes 393224 | tf_op jit(solution)/shard_map/ppermute | solution.py:163
  42.2 0.1 collective-permute-start.9
  42.3 0.9 %collective-permute-done.10 = f32[256,128]{1,0:T(8,128)S(1)} collective-permute-done((f32[256,128]{1,0:T(8,128)S(1)}, f32[256,128]{1,0:T(8,128)S(1)}, u32[]{:S(2)}, u32[]{:S(2)}) %collective-permute-start.10) | collective-permute-done | bytes 131104 | tf_op jit(solution)/shard_map/ppermute | solution.py:163
  43.2 2.7 %collective-permute-start.11 = (f32[256,128]{1,0:T(8,128)S(1)}, f32[256,128]{1,0:T(8,128)S(1)}, u32[]{:S(2)}, u32[]{:S(2)}) collective-permute-start(f32[256,128]{1,0:T(8,128)S(1)} %add.19), channel_id=1, source_target_pairs={{2,0},{3,1},{0,2},{1,3},{6,4},{7,5},{4,6},{5,7},{10,8},{11,9},{8,1... | collective-permute-start | bytes 393224 | tf_op jit(solution)/shard_map/ppermute | solution.py:169
  45.9 3.8 %collective-permute-done.11.refs_2_ = f32[256,128]{1,0:T(8,128)S(1)} collective-permute-done((f32[256,128]{1,0:T(8,128)S(1)}, f32[256,128]{1,0:T(8,128)S(1)}, u32[]{:S(2)}, u32[]{:S(2)}) %collective-permute-start.11) | collective-permute-done | bytes 131104 | tf_op jit(solution)/shard_map/ppermute | solution.py:169
  49.7 0.7 %shard_map.67 = f32[256,128]{1,0:T(8,128)} custom-call(f32[256,128]{1,0:T(8,128)S(1)} %get-tuple-element.28.base_ref, f32[256,128]{1,0:T(8,128)S(1)} %get-tuple-element.22.norm_ref, f32[256,128]{1,0:T(8,128)S(1)} %get-tuple-element.23.refs_0_, f32[256,128]{1,0:T(8,128)S(1)} %collective-permute-done.9.refs_1_, f32[256,128]{1,0:T(8,128)S(1)} %collective-permute-done.11.refs_2_), custom_call_target="tpu_custom_call" | custom-call | tf_op jit(solution)/shard_map/pallas_call | solution.py:199
  (11 shorter events, 0.1 us)
Async XLA Ops:
  0.0 16.5 %collective-permute-start.1 = (f32[1024,128]{1,0:T(8,128)}, f32[1024,128]{1,0:T(8,128)S(1)}, u32[]{:S(2)}, u32[]{:S(2)}) collective-permute-start(f32[1024,128]{1,0:T(8,128)} %embeddings_ref.1), channel_id=1, source_target_pairs={{2,0},{1,5},{0,10},{3,15},{4,4},{5,9},{6,14},{7,3},{11,8},{8,13},{... | collective-permute-start | bytes 1572872 | tf_op jit(solution)/shard_map/ppermute | solution.py:153
  6.9 9.6 %collective-permute-start = (s32[8,128]{1,0:T(8,128)}, s32[8,128]{1,0:T(8,128)S(1)}, u32[]{:S(2)}, u32[]{:S(2)}) collective-permute-start(s32[8,128]{1,0:T(8,128)} %bitcast.12), channel_id=1, source_target_pairs={{2,0},{1,5},{0,10},{3,15},{4,4},{5,9},{6,14},{7,3},{11,8},{8,13},{... | collective-permute-start | bytes 12296 | tf_op jit(solution)/shard_map/ppermute | solution.py:153
  9.8 0.7 %copy-start.3 = (s32[1,1,1,24]{3,2,1,0:T(1,128)S(1)}, s32[1,1,1,24]{3,2,1,0:T(1,128)}, u32[]{:S(2)}) copy-start(s32[1,1,1,24]{3,2,1,0:T(1,128)} %param.10) | copy-start | bytes 292
  9.8 0.7 %copy-start.4 = (s32[1,1,1,24]{3,2,1,0:T(1,128)S(1)}, s32[1,1,1,24]{3,2,1,0:T(1,128)}, u32[]{:S(2)}) copy-start(s32[1,1,1,24]{3,2,1,0:T(1,128)} %param.9) | copy-start | bytes 292
  10.5 0.7 %copy-start.2 = (s32[1024]{0:T(1024)S(1)}, s32[1024]{0:T(1024)}, u32[]{:S(2)}) copy-start(s32[1024]{0:T(1024)} %param.7) | copy-start | bytes 12292
  11.2 1.1 %copy-start = (bf16[1,1,1,24,128,128]{5,4,3,2,1,0:T(8,128)(2,1)S(1)}, bf16[1,1,1,24,128,128]{5,4,3,2,1,0:T(8,128)(2,1)}, u32[]{:S(2)}) copy-start(bf16[1,1,1,24,128,128]{5,4,3,2,1,0:T(8,128)(2,1)} %param.8) | copy-start | bytes 2359300
  12.3 1.0 %copy-start.1 = (f32[1024,128]{1,0:T(8,128)S(1)}, f32[1024,128]{1,0:T(8,128)}, u32[]{:S(2)}) copy-start(f32[1024,128]{1,0:T(8,128)} %embeddings_ref.1) | copy-start | bytes 1572868
  17.5 1.4 %collective-permute-start.3 = (f32[256,128]{1,0:T(8,128)S(1)}, f32[256,128]{1,0:T(8,128)S(1)}, u32[]{:S(2)}, u32[]{:S(2)}) collective-permute-start(f32[256,128]{1,0:T(8,128)S(1)} %get-tuple-element.21), channel_id=1, source_target_pairs={{0,1},{1,0},{2,3},{3,2},{4,5},{5,4},{6,7},{7,6},{8,9},{9,8},{10,11... | collective-permute-start | bytes 393224 | tf_op jit(solution)/shard_map/ppermute | solution.py:163
  17.6 4.8 %collective-permute-start.2 = (f32[256,128]{1,0:T(8,128)S(1)}, f32[256,128]{1,0:T(8,128)S(1)}, u32[]{:S(2)}, u32[]{:S(2)}) collective-permute-start(f32[256,128]{1,0:T(8,128)S(1)} %get-tuple-element.19), channel_id=1, source_target_pairs={{0,1},{1,0},{2,3},{3,2},{4,5},{5,4},{6,7},{7,6},{8,9},{9,8},{10,11... | collective-permute-start | bytes 393224 | tf_op jit(solution)/shard_map/ppermute | solution.py:163
  18.9 7.2 %collective-permute-start.4 = (f32[256,128]{1,0:T(8,128)S(1)}, f32[256,128]{1,0:T(8,128)S(1)}, u32[]{:S(2)}, u32[]{:S(2)}) collective-permute-start(f32[256,128]{1,0:T(8,128)S(1)} %add.16), channel_id=1, source_target_pairs={{2,0},{3,1},{0,2},{1,3},{6,4},{7,5},{4,6},{5,7},{10,8},{11,9},{8,1... | collective-permute-start | bytes 393224 | tf_op jit(solution)/shard_map/ppermute | solution.py:169
  26.2 8.0 %collective-permute-start.8 = (f32[256,128]{1,0:T(8,128)S(1)}, f32[256,128]{1,0:T(8,128)S(1)}, u32[]{:S(2)}, u32[]{:S(2)}) collective-permute-start(f32[256,128]{1,0:T(8,128)S(1)} %get-tuple-element.27), channel_id=1, source_target_pairs={{3,0},{1,5},{2,10},{0,15},{7,4},{5,9},{6,14},{4,3},{11,8},{9,13},{... | collective-permute-start | bytes 393224 | tf_op jit(solution)/shard_map/ppermute | solution.py:153
  30.7 5.7 %collective-permute-start.7 = (f32[256,128]{1,0:T(8,128)S(1)}, f32[256,128]{1,0:T(8,128)S(1)}, u32[]{:S(2)}, u32[]{:S(2)}) collective-permute-start(f32[256,128]{1,0:T(8,128)S(1)} %get-tuple-element.27), channel_id=1, source_target_pairs={{1,0},{3,5},{0,10},{2,15},{5,4},{7,9},{4,14},{6,3},{9,8},{11,13},{... | collective-permute-start | bytes 393224 | tf_op jit(solution)/shard_map/ppermute | solution.py:153
  30.7 8.2 %collective-permute-start.6 = (f32[256,128]{1,0:T(8,128)S(1)}, f32[256,128]{1,0:T(8,128)S(1)}, u32[]{:S(2)}, u32[]{:S(2)}) collective-permute-start(f32[256,128]{1,0:T(8,128)S(1)} %get-tuple-element.27), channel_id=1, source_target_pairs={{2,0},{0,5},{3,10},{1,15},{6,4},{4,9},{7,14},{5,3},{10,8},{8,13},{... | collective-permute-start | bytes 393224 | tf_op jit(solution)/shard_map/ppermute | solution.py:153
  30.7 8.2 %collective-permute-start.5 = (f32[256,128]{1,0:T(8,128)S(1)}, f32[256,128]{1,0:T(8,128)S(1)}, u32[]{:S(2)}, u32[]{:S(2)}) collective-permute-start(f32[256,128]{1,0:T(8,128)S(1)} %get-tuple-element.27), channel_id=1, source_target_pairs={{0,0},{2,5},{1,10},{3,15},{4,4},{6,9},{5,14},{7,3},{8,8},{10,13},{... | collective-permute-start | bytes 393224 | tf_op jit(solution)/shard_map/ppermute | solution.py:153
  39.7 3.5 %collective-permute-start.10 = (f32[256,128]{1,0:T(8,128)S(1)}, f32[256,128]{1,0:T(8,128)S(1)}, u32[]{:S(2)}, u32[]{:S(2)}) collective-permute-start(f32[256,128]{1,0:T(8,128)S(1)} %get-tuple-element.26), channel_id=1, source_target_pairs={{0,1},{1,0},{2,3},{3,2},{4,5},{5,4},{6,7},{7,6},{8,9},{9,8},{10,11... | collective-permute-start | bytes 393224 | tf_op jit(solution)/shard_map/ppermute | solution.py:163
  42.2 3.7 %collective-permute-start.9 = (f32[256,128]{1,0:T(8,128)S(1)}, f32[256,128]{1,0:T(8,128)S(1)}, u32[]{:S(2)}, u32[]{:S(2)}) collective-permute-start(f32[256,128]{1,0:T(8,128)S(1)} %get-tuple-element.24), channel_id=1, source_target_pairs={{0,1},{1,0},{2,3},{3,2},{4,5},{5,4},{6,7},{7,6},{8,9},{9,8},{10,11... | collective-permute-start | bytes 393224 | tf_op jit(solution)/shard_map/ppermute | solution.py:163
  43.2 6.5 %collective-permute-start.11 = (f32[256,128]{1,0:T(8,128)S(1)}, f32[256,128]{1,0:T(8,128)S(1)}, u32[]{:S(2)}, u32[]{:S(2)}) collective-permute-start(f32[256,128]{1,0:T(8,128)S(1)} %add.19), channel_id=1, source_target_pairs={{2,0},{3,1},{0,2},{1,3},{6,4},{7,5},{4,6},{5,7},{10,8},{11,9},{8,1... | collective-permute-start | bytes 393224 | tf_op jit(solution)/shard_map/ppermute | solution.py:169

commit v19 on v14

--- a/solution.py
+++ b/solution.py
@@ -18,10 +18,10 @@
     return 2 * lax.rem(team_index // 2 + column, columns) + lax.rem(team_index, 2)
 
 
-def source_team(shard, team, turn, cycle, team_count):
+def source_team(shard, team, turn, team_count):
     if team_count == 4:
-        lower, upper = (0, 1, 3, 2)[turn], (3, 1, 0, 2)[turn]
-        return (2 * (team % 2) + team // 2) ^ lower ^ ((shard >= cycle // 2) * (lower ^ upper))
+        row, first_row = (0, 2, 1, 3)[turn], (1, 2, 0, 3)[turn]
+        return (2 * (team % 2) + team // 2) ^ row ^ ((shard == 0) * (row ^ first_row))
     return (team + turn) % team_count
 
 
@@ -93,7 +93,7 @@
         cycle = lax.axis_size("blk")
         shard = lax.rem(lax.axis_index("blk") + cycle - lax.rem(team_index * arc_length + arc_slot, cycle), cycle)
         for k in range(piece_count):
-            owner = source_team(shard, team_index, k, cycle, team_count)
+            owner = source_team(shard, team_index, k, team_count)
             split(pieces[k][...], pl.ds(pl.multiple_of(owner * share_rows, share_rows), share_rows))
     sums_ref[...] = jnp.zeros_like(sums_ref)
     live_count = info_ref[0, 0]
@@ -214,7 +214,7 @@
 def per_device(embeddings, degrees, tile_values, tile_rows, tile_columns, slot_counts):
     arc_length, _, tile_size, _ = tile_values.shape[2:]
     panel_rows = embeddings.shape[0]
-    cycle, team_count = lax.axis_size("blk"), lax.axis_size("rep")
+    team_count = lax.axis_size("rep")
     spread = (3, 1, 2, 0) if team_count == 4 else tuple(range(team_count))
     degrees = degrees.reshape(panel_rows // tile_size, tile_size)
 
@@ -239,7 +239,7 @@
         combined = combined + current
         source = current * norm_scale
         pieces = [
-            fetch(source, lambda shard, team, k=k: source_team(shard, team, k, cycle, team_count), arc_length)
+            fetch(source, lambda shard, team, k=k: source_team(shard, team, k, team_count), arc_length)
             for k in range(team_count)
         ]
 

time: 50.7 us -> 50.5 us (level)
  waiting for transfers between devices: 16.3 us -> 15.5 us
  starting transfers between devices: 26.6 us -> 27.3 us
    ppermute x6, starting transfers between devices: 13.1 us -> 15.7 us  [fetch(): return lax.ppermute(value, ('blk', 'rep'), pairs)]
    ppermute x4, starting transfers between devices: 5.87 us -> 4.91 us  [from_mate(): lax.ppermute(value, 'rep', [(team, team ^ 1) for team in range(team_count)])]
    ppermute x2, starting transfers between devices: 7.63 us -> 6.68 us  [from_column(): return lax.ppermute(value, 'rep', pairs)]
    ppermute x6, waiting for transfers between devices: 6.88 us -> 6.02 us  [fetch(): return lax.ppermute(value, ('blk', 'rep'), pairs)]
where the time goes in v19:
time: 50.5 us; the launch traced here: 50.2 us
  starting transfers between devices  27.3 us (54%)
  waiting for transfers between devices  15.5 us (31%)
  local copies, waits for them, and re-layouts  3.52 us (7%)
  Pallas kernels  3.03 us (6%)
  between operations  0.75 us (1%)
    ppermute x6, starting transfers between devices, fetch(): return lax.ppermute(value, ('blk', 'rep'), pairs)  15.7 us
    ppermute x2, waiting for transfers between devices, from_column(): return lax.ppermute(value, 'rep', pairs)  7.61 us
    ppermute x2, starting transfers between devices, from_column(): return lax.ppermute(value, 'rep', pairs)  6.68 us
    ppermute x6, waiting for transfers between devices, fetch(): return lax.ppermute(value, ('blk', 'rep'), pairs)  6.02 us
    ppermute x4, starting transfers between devices, from_mate(): lax.ppermute(value, 'rep', [(team, team ^ 1) for team in range(team_count)])  4.91 us
    unnamed x10, local copies, waits for them, and re-layouts  3.44 us
    ppermute x4, waiting for transfers between devices, from_mate(): lax.ppermute(value, 'rep', [(team, team ^ 1) for team in range(team_count)])  1.82 us
    pallas_call x2, Pallas kernels, arc_step(): pl.pallas_call(functools.partial(arc_kernel, team_count=team_count, arc_l...  1.76 us
  transfers between devices with their start and end apart: 12, of which 7 were waited for; matrix products, arithmetic and copies ran while one was open for 0% of the time, Pallas kernels for 1%

profile of v19, /device:TPU:0, one launch (start us, length us, event | category | flops | bytes accessed | tf_op | source)
XLA Modules:
  0.0 50.2 jit_solution(12156377019960272603)
XLA Ops:
  0.0 5.4 %collective-permute-start.1 = (f32[1024,128]{1,0:T(8,128)}, f32[1024,128]{1,0:T(8,128)S(1)}, u32[]{:S(2)}, u32[]{:S(2)}) collective-permute-start(f32[1024,128]{1,0:T(8,128)} %embeddings_ref.1), channel_id=1, source_target_pairs={{3,0},{1,5},{2,10},{0,15},{7,4},{5,9},{6,14},{4,3},{11,8},{9,13},{... | collective-permute-start | bytes 1572872 | tf_op jit(solution)/shard_map/ppermute | solution.py:158
  5.4 0.8 %collective-permute-start = (s32[8,128]{1,0:T(8,128)}, s32[8,128]{1,0:T(8,128)S(1)}, u32[]{:S(2)}, u32[]{:S(2)}) collective-permute-start(s32[8,128]{1,0:T(8,128)} %bitcast.12), channel_id=1, source_target_pairs={{3,0},{1,5},{2,10},{0,15},{7,4},{5,9},{6,14},{4,3},{11,8},{9,13},{... | collective-permute-start | bytes 12296 | tf_op jit(solution)/shard_map/ppermute | solution.py:158
  6.9 0.6 %copy-done.3 = s32[1,1,1,24]{3,2,1,0:T(1,128)S(1)} copy-done((s32[1,1,1,24]{3,2,1,0:T(1,128)S(1)}, s32[1,1,1,24]{3,2,1,0:T(1,128)}, u32[]{:S(2)}) %copy-start.3) | copy-done | bytes 120
  7.5 0.0 copy-done.4
  7.6 0.1 add_bitcast_fusion
  7.6 0.1 squeeze.19.after_ref.info_ref
  7.7 0.6 %copy-done.2 = s32[1024]{0:T(1024)S(1)} copy-done((s32[1024]{0:T(1024)S(1)}, s32[1024]{0:T(1024)}, u32[]{:S(2)}) %copy-start.2) | copy-done | bytes 4120
  8.3 1.1 %copy-done = bf16[1,1,1,24,128,128]{5,4,3,2,1,0:T(8,128)(2,1)S(1)} copy-done((bf16[1,1,1,24,128,128]{5,4,3,2,1,0:T(8,128)(2,1)S(1)}, bf16[1,1,1,24,128,128]{5,4,3,2,1,0:T(8,128)(2,1)}, u32[]{:S(2)}) %copy-start) | copy-done | bytes 786456
  9.5 1.0 %copy-done.1 = f32[1024,128]{1,0:T(8,128)S(1)} copy-done((f32[1024,128]{1,0:T(8,128)S(1)}, f32[1024,128]{1,0:T(8,128)}, u32[]{:S(2)}) %copy-start.1) | copy-done | bytes 524312
  10.5 0.6 %shard_map.64 = (bf16[1,24,128,128]{3,2,1,0:T(8,128)(2,1)S(1)}, f32[256,128]{1,0:T(8,128)S(1)}, f32[256,128]{1,0:T(8,128)S(1)}) custom-call(s32[8,128]{1,0:T(8,128)S(1)} %bitcast.13, f32[1024,128]{1,0:T(8,128)S(1)} %copy-done.1, bf16[1,24,128,128]{3,2,1,0:T(8,128)(2,1)S(1)} %bitcast.11, s32[49,128]{1,0:T(8,128)S(1)} %squeeze.19.after_ref.info_ref), custom_call_target="tpu_custom_call" | custom-call | flops 131072 | bytes 524288 | tf_op jit(solution)/shard_map/pallas_call | solution.py:57
  11.1 3.5 %collective-permute-done.refs_0_ = s32[8,128]{1,0:T(8,128)S(1)} collective-permute-done((s32[8,128]{1,0:T(8,128)}, s32[8,128]{1,0:T(8,128)S(1)}, u32[]{:S(2)}, u32[]{:S(2)}) %collective-permute-start) | collective-permute-done | bytes 4128 | tf_op jit(solution)/shard_map/ppermute | solution.py:158
  14.6 1.0 %shard_map.65 = (f32[256,128]{1,0:T(8,128)S(1)}, f32[256,128]{1,0:T(8,128)S(1)}, f32[256,128]{1,0:T(8,128)S(1)}, f32[256,128]{1,0:T(8,128)S(1)}) custom-call(s32[49,128]{1,0:T(8,128)S(1)} %squeeze.19.after_ref.info_ref, bf16[24,128,128]{2,1,0:T(8,128)(2,1)S(1)} %bitcast.9, s32[8,128]{1,0:T(8,128)S(1)} %collective-permute-done.refs_0_, ...), custom_call_target="tpu_custom_call" | custom-call | flops 201326592 | bytes 1048576 | tf_op jit(solution)/shard_map/pallas_call | solution.py:127
  15.6 0.8 %collective-permute-start.3 = (f32[256,128]{1,0:T(8,128)S(1)}, f32[256,128]{1,0:T(8,128)S(1)}, u32[]{:S(2)}, u32[]{:S(2)}) collective-permute-start(f32[256,128]{1,0:T(8,128)S(1)} %get-tuple-element.21), channel_id=1, source_target_pairs={{0,1},{1,0},{2,3},{3,2},{4,5},{5,4},{6,7},{7,6},{8,9},{9,8},{10,11... | collective-permute-start | bytes 393224 | tf_op jit(solution)/shard_map/ppermute | solution.py:168
  16.4 0.1 collective-permute-start.2
  16.5 0.9 %collective-permute-done.3 = f32[256,128]{1,0:T(8,128)S(1)} collective-permute-done((f32[256,128]{1,0:T(8,128)S(1)}, f32[256,128]{1,0:T(8,128)S(1)}, u32[]{:S(2)}, u32[]{:S(2)}) %collective-permute-start.3) | collective-permute-done | bytes 131104 | tf_op jit(solution)/shard_map/ppermute | solution.py:168
  17.4 4.0 %collective-permute-start.4 = (f32[256,128]{1,0:T(8,128)S(1)}, f32[256,128]{1,0:T(8,128)S(1)}, u32[]{:S(2)}, u32[]{:S(2)}) collective-permute-start(f32[256,128]{1,0:T(8,128)S(1)} %add.16), channel_id=1, source_target_pairs={{2,0},{3,1},{0,2},{1,3},{6,4},{7,5},{4,6},{5,7},{10,8},{11,9},{8,1... | collective-permute-start | bytes 393224 | tf_op jit(solution)/shard_map/ppermute | solution.py:174
  21.4 0.0 collective-permute-done.2
  21.4 3.8 %collective-permute-done.4 = f32[256,128]{1,0:T(8,128)S(1)} collective-permute-done((f32[256,128]{1,0:T(8,128)S(1)}, f32[256,128]{1,0:T(8,128)S(1)}, u32[]{:S(2)}, u32[]{:S(2)}) %collective-permute-start.4) | collective-permute-done | bytes 131104 | tf_op jit(solution)/shard_map/ppermute | solution.py:174
  25.3 3.6 %collective-permute-start.8 = (f32[256,128]{1,0:T(8,128)S(1)}, f32[256,128]{1,0:T(8,128)S(1)}, u32[]{:S(2)}, u32[]{:S(2)}) collective-permute-start(f32[256,128]{1,0:T(8,128)S(1)} %get-tuple-element.27), channel_id=1, source_target_pairs={{3,0},{1,5},{2,10},{0,15},{7,4},{5,9},{6,14},{4,3},{11,8},{9,13},{... | collective-permute-start | bytes 393224 | tf_op jit(solution)/shard_map/ppermute | solution.py:158
  28.9 0.7 %collective-permute-start.7 = (f32[256,128]{1,0:T(8,128)S(1)}, f32[256,128]{1,0:T(8,128)S(1)}, u32[]{:S(2)}, u32[]{:S(2)}) collective-permute-start(f32[256,128]{1,0:T(8,128)S(1)} %get-tuple-element.27), channel_id=1, source_target_pairs={{0,0},{2,5},{1,10},{3,15},{5,4},{7,9},{4,14},{6,3},{9,8},{11,13},{... | collective-permute-start | bytes 393224 | tf_op jit(solution)/shard_map/ppermute | solution.py:158
  29.6 0.1 collective-permute-start.6
  29.7 5.1 %collective-permute-start.5 = (f32[256,128]{1,0:T(8,128)S(1)}, f32[256,128]{1,0:T(8,128)S(1)}, u32[]{:S(2)}, u32[]{:S(2)}) collective-permute-start(f32[256,128]{1,0:T(8,128)S(1)} %get-tuple-element.27), channel_id=1, source_target_pairs={{1,0},{3,5},{0,10},{2,15},{4,4},{6,9},{5,14},{7,3},{8,8},{10,13},{... | collective-permute-start | bytes 393224 | tf_op jit(solution)/shard_map/ppermute | solution.py:158
  34.8 0.0 collective-permute-done.8.refs_3_
  34.8 1.1 %collective-permute-done.6.refs_1_ = f32[256,128]{1,0:T(8,128)S(1)} collective-permute-done((f32[256,128]{1,0:T(8,128)S(1)}, f32[256,128]{1,0:T(8,128)S(1)}, u32[]{:S(2)}, u32[]{:S(2)}) %collective-permute-start.6) | collective-permute-done | bytes 131104 | tf_op jit(solution)/shard_map/ppermute | solution.py:158
  36.0 1.3 %collective-permute-done.5.refs_0_ = f32[256,128]{1,0:T(8,128)S(1)} collective-permute-done((f32[256,128]{1,0:T(8,128)S(1)}, f32[256,128]{1,0:T(8,128)S(1)}, u32[]{:S(2)}, u32[]{:S(2)}) %collective-permute-start.5) | collective-permute-done | bytes 131104 | tf_op jit(solution)/shard_map/ppermute | solution.py:158
  37.3 0.8 %shard_map.66 = (f32[256,128]{1,0:T(8,128)S(1)}, f32[256,128]{1,0:T(8,128)S(1)}, f32[256,128]{1,0:T(8,128)S(1)}, f32[256,128]{1,0:T(8,128)S(1)}) custom-call(s32[49,128]{1,0:T(8,128)S(1)} %squeeze.19.after_ref.info_ref, bf16[24,128,128]{2,1,0:T(8,128)(2,1)S(1)} %bitcast.10, f32[256,128]{1,0:T(8,128)S(1)} %collective-permute-done.5.refs_0_, ...), custom_call_target="tpu_custom_call" | custom-call | flops 201326592 | bytes 1048576 | tf_op jit(solution)/shard_map/pallas_call | solution.py:127
  38.1 3.9 %collective-permute-start.10 = (f32[256,128]{1,0:T(8,128)S(1)}, f32[256,128]{1,0:T(8,128)S(1)}, u32[]{:S(2)}, u32[]{:S(2)}) collective-permute-start(f32[256,128]{1,0:T(8,128)S(1)} %get-tuple-element.26), channel_id=1, source_target_pairs={{0,1},{1,0},{2,3},{3,2},{4,5},{5,4},{6,7},{7,6},{8,9},{9,8},{10,11... | collective-permute-start | bytes 393224 | tf_op jit(solution)/shard_map/ppermute | solution.py:168
  42.0 0.1 collective-permute-start.9
  42.1 0.9 %collective-permute-done.10 = f32[256,128]{1,0:T(8,128)S(1)} collective-permute-done((f32[256,128]{1,0:T(8,128)S(1)}, f32[256,128]{1,0:T(8,128)S(1)}, u32[]{:S(2)}, u32[]{:S(2)}) %collective-permute-start.10) | collective-permute-done | bytes 131104 | tf_op jit(solution)/shard_map/ppermute | solution.py:168
  43.0 2.7 %collective-permute-start.11 = (f32[256,128]{1,0:T(8,128)S(1)}, f32[256,128]{1,0:T(8,128)S(1)}, u32[]{:S(2)}, u32[]{:S(2)}) collective-permute-start(f32[256,128]{1,0:T(8,128)S(1)} %add.19), channel_id=1, source_target_pairs={{2,0},{3,1},{0,2},{1,3},{6,4},{7,5},{4,6},{5,7},{10,8},{11,9},{8,1... | collective-permute-start | bytes 393224 | tf_op jit(solution)/shard_map/ppermute | solution.py:174
  45.7 3.8 %collective-permute-done.11.refs_2_ = f32[256,128]{1,0:T(8,128)S(1)} collective-permute-done((f32[256,128]{1,0:T(8,128)S(1)}, f32[256,128]{1,0:T(8,128)S(1)}, u32[]{:S(2)}, u32[]{:S(2)}) %collective-permute-start.11) | collective-permute-done | bytes 131104 | tf_op jit(solution)/shard_map/ppermute | solution.py:174
  49.5 0.7 %shard_map.67 = f32[256,128]{1,0:T(8,128)} custom-call(f32[256,128]{1,0:T(8,128)S(1)} %get-tuple-element.28.base_ref, f32[256,128]{1,0:T(8,128)S(1)} %get-tuple-element.22.norm_ref, f32[256,128]{1,0:T(8,128)S(1)} %get-tuple-element.23.refs_0_, f32[256,128]{1,0:T(8,128)S(1)} %collective-permute-done.9.refs_1_, f32[256,128]{1,0:T(8,128)S(1)} %collective-permute-done.11.refs_2_), custom_call_target="tpu_custom_call" | custom-call | tf_op jit(solution)/shard_map/pallas_call | solution.py:204
  (11 shorter events, 0.1 us)
Async XLA Ops:
  0.0 14.6 %collective-permute-start.1 = (f32[1024,128]{1,0:T(8,128)}, f32[1024,128]{1,0:T(8,128)S(1)}, u32[]{:S(2)}, u32[]{:S(2)}) collective-permute-start(f32[1024,128]{1,0:T(8,128)} %embeddings_ref.1), channel_id=1, source_target_pairs={{3,0},{1,5},{2,10},{0,15},{7,4},{5,9},{6,14},{4,3},{11,8},{9,13},{... | collective-permute-start | bytes 1572872 | tf_op jit(solution)/shard_map/ppermute | solution.py:158
  5.4 9.2 %collective-permute-start = (s32[8,128]{1,0:T(8,128)}, s32[8,128]{1,0:T(8,128)S(1)}, u32[]{:S(2)}, u32[]{:S(2)}) collective-permute-start(s32[8,128]{1,0:T(8,128)} %bitcast.12), channel_id=1, source_target_pairs={{3,0},{1,5},{2,10},{0,15},{7,4},{5,9},{6,14},{4,3},{11,8},{9,13},{... | collective-permute-start | bytes 12296 | tf_op jit(solution)/shard_map/ppermute | solution.py:158
  6.9 0.7 %copy-start.3 = (s32[1,1,1,24]{3,2,1,0:T(1,128)S(1)}, s32[1,1,1,24]{3,2,1,0:T(1,128)}, u32[]{:S(2)}) copy-start(s32[1,1,1,24]{3,2,1,0:T(1,128)} %param.10) | copy-start | bytes 292
  6.9 0.7 %copy-start.4 = (s32[1,1,1,24]{3,2,1,0:T(1,128)S(1)}, s32[1,1,1,24]{3,2,1,0:T(1,128)}, u32[]{:S(2)}) copy-start(s32[1,1,1,24]{3,2,1,0:T(1,128)} %param.9) | copy-start | bytes 292
  7.6 0.7 %copy-start.2 = (s32[1024]{0:T(1024)S(1)}, s32[1024]{0:T(1024)}, u32[]{:S(2)}) copy-start(s32[1024]{0:T(1024)} %param.7) | copy-start | bytes 12292
  8.3 1.1 %copy-start = (bf16[1,1,1,24,128,128]{5,4,3,2,1,0:T(8,128)(2,1)S(1)}, bf16[1,1,1,24,128,128]{5,4,3,2,1,0:T(8,128)(2,1)}, u32[]{:S(2)}) copy-start(bf16[1,1,1,24,128,128]{5,4,3,2,1,0:T(8,128)(2,1)} %param.8) | copy-start | bytes 2359300
  9.5 1.0 %copy-start.1 = (f32[1024,128]{1,0:T(8,128)S(1)}, f32[1024,128]{1,0:T(8,128)}, u32[]{:S(2)}) copy-start(f32[1024,128]{1,0:T(8,128)} %embeddings_ref.1) | copy-start | bytes 1572868
  15.6 1.8 %collective-permute-start.3 = (f32[256,128]{1,0:T(8,128)S(1)}, f32[256,128]{1,0:T(8,128)S(1)}, u32[]{:S(2)}, u32[]{:S(2)}) collective-permute-start(f32[256,128]{1,0:T(8,128)S(1)} %get-tuple-element.21), channel_id=1, source_target_pairs={{0,1},{1,0},{2,3},{3,2},{4,5},{5,4},{6,7},{7,6},{8,9},{9,8},{10,11... | collective-permute-start | bytes 393224 | tf_op jit(solution)/shard_map/ppermute | solution.py:168
  16.4 5.0 %collective-permute-start.2 = (f32[256,128]{1,0:T(8,128)S(1)}, f32[256,128]{1,0:T(8,128)S(1)}, u32[]{:S(2)}, u32[]{:S(2)}) collective-permute-start(f32[256,128]{1,0:T(8,128)S(1)} %get-tuple-element.19), channel_id=1, source_target_pairs={{0,1},{1,0},{2,3},{3,2},{4,5},{5,4},{6,7},{7,6},{8,9},{9,8},{10,11... | collective-permute-start | bytes 393224 | tf_op jit(solution)/shard_map/ppermute | solution.py:168
  17.4 7.8 %collective-permute-start.4 = (f32[256,128]{1,0:T(8,128)S(1)}, f32[256,128]{1,0:T(8,128)S(1)}, u32[]{:S(2)}, u32[]{:S(2)}) collective-permute-start(f32[256,128]{1,0:T(8,128)S(1)} %add.16), channel_id=1, source_target_pairs={{2,0},{3,1},{0,2},{1,3},{6,4},{7,5},{4,6},{5,7},{10,8},{11,9},{8,1... | collective-permute-start | bytes 393224 | tf_op jit(solution)/shard_map/ppermute | solution.py:174
  25.3 9.5 %collective-permute-start.8 = (f32[256,128]{1,0:T(8,128)S(1)}, f32[256,128]{1,0:T(8,128)S(1)}, u32[]{:S(2)}, u32[]{:S(2)}) collective-permute-start(f32[256,128]{1,0:T(8,128)S(1)} %get-tuple-element.27), channel_id=1, source_target_pairs={{3,0},{1,5},{2,10},{0,15},{7,4},{5,9},{6,14},{4,3},{11,8},{9,13},{... | collective-permute-start | bytes 393224 | tf_op jit(solution)/shard_map/ppermute | solution.py:158
  28.9 5.9 %collective-permute-start.7 = (f32[256,128]{1,0:T(8,128)S(1)}, f32[256,128]{1,0:T(8,128)S(1)}, u32[]{:S(2)}, u32[]{:S(2)}) collective-permute-start(f32[256,128]{1,0:T(8,128)S(1)} %get-tuple-element.27), channel_id=1, source_target_pairs={{0,0},{2,5},{1,10},{3,15},{5,4},{7,9},{4,14},{6,3},{9,8},{11,13},{... | collective-permute-start | bytes 393224 | tf_op jit(solution)/shard_map/ppermute | solution.py:158
  29.6 6.4 %collective-permute-start.6 = (f32[256,128]{1,0:T(8,128)S(1)}, f32[256,128]{1,0:T(8,128)S(1)}, u32[]{:S(2)}, u32[]{:S(2)}) collective-permute-start(f32[256,128]{1,0:T(8,128)S(1)} %get-tuple-element.27), channel_id=1, source_target_pairs={{2,0},{0,5},{3,10},{1,15},{6,4},{4,9},{7,14},{5,3},{10,8},{8,13},{... | collective-permute-start | bytes 393224 | tf_op jit(solution)/shard_map/ppermute | solution.py:158
  29.7 7.6 %collective-permute-start.5 = (f32[256,128]{1,0:T(8,128)S(1)}, f32[256,128]{1,0:T(8,128)S(1)}, u32[]{:S(2)}, u32[]{:S(2)}) collective-permute-start(f32[256,128]{1,0:T(8,128)S(1)} %get-tuple-element.27), channel_id=1, source_target_pairs={{1,0},{3,5},{0,10},{2,15},{4,4},{6,9},{5,14},{7,3},{8,8},{10,13},{... | collective-permute-start | bytes 393224 | tf_op jit(solution)/shard_map/ppermute | solution.py:158
  38.1 4.9 %collective-permute-start.10 = (f32[256,128]{1,0:T(8,128)S(1)}, f32[256,128]{1,0:T(8,128)S(1)}, u32[]{:S(2)}, u32[]{:S(2)}) collective-permute-start(f32[256,128]{1,0:T(8,128)S(1)} %get-tuple-element.26), channel_id=1, source_target_pairs={{0,1},{1,0},{2,3},{3,2},{4,5},{5,4},{6,7},{7,6},{8,9},{9,8},{10,11... | collective-permute-start | bytes 393224 | tf_op jit(solution)/shard_map/ppermute | solution.py:168
  42.0 3.7 %collective-permute-start.9 = (f32[256,128]{1,0:T(8,128)S(1)}, f32[256,128]{1,0:T(8,128)S(1)}, u32[]{:S(2)}, u32[]{:S(2)}) collective-permute-start(f32[256,128]{1,0:T(8,128)S(1)} %get-tuple-element.24), channel_id=1, source_target_pairs={{0,1},{1,0},{2,3},{3,2},{4,5},{5,4},{6,7},{7,6},{8,9},{9,8},{10,11... | collective-permute-start | bytes 393224 | tf_op jit(solution)/shard_map/ppermute | solution.py:168
  43.0 6.5 %collective-permute-start.11 = (f32[256,128]{1,0:T(8,128)S(1)}, f32[256,128]{1,0:T(8,128)S(1)}, u32[]{:S(2)}, u32[]{:S(2)}) collective-permute-start(f32[256,128]{1,0:T(8,128)S(1)} %add.19), channel_id=1, source_target_pairs={{2,0},{3,1},{0,2},{1,3},{6,4},{7,5},{4,6},{5,7},{10,8},{11,9},{8,1... | collective-permute-start | bytes 393224 | tf_op jit(solution)/shard_map/ppermute | solution.py:174

commit v20 on v17

--- a/solution.py
+++ b/solution.py
@@ -20,7 +20,7 @@
 
 def source_team(team, turn, team_count):
     if team_count == 4:
-        return (2 * (team % 2) + team // 2) ^ (3, 0, 2, 1)[turn]
+        return (3 * (team % 2)) ^ (team // 2) ^ (3, 0, 1, 2)[turn]
     return (team + turn) % team_count
 
 

time: 49.5 us -> 49.3 us (level)
  starting transfers between devices: 26 us -> 25.5 us
    ppermute x6, starting transfers between devices: 15.7 us -> 13.5 us  [fetch(): return lax.ppermute(value, ('blk', 'rep'), pairs)]
    ppermute x2, starting transfers between devices: 6.3 us -> 7.35 us  [from_column(): return lax.ppermute(value, 'rep', pairs)]
    ppermute x4, starting transfers between devices: 4.01 us -> 4.7 us  [from_mate(): lax.ppermute(value, 'rep', [(team, team ^ 1) for team in range(team_count)])]
  transfers between devices with their start and end apart: 12 -> 12, of which waited for: 6 -> 7; matrix products, arithmetic and copies ran while one was open for 0% -> 0% of each run, Pallas kernels for 1% -> 1%
where the time goes in v20:
time: 49.3 us; the launch traced here: 49 us
  starting transfers between devices  25.5 us (52%)
  waiting for transfers between devices  16.1 us (33%)
  local copies, waits for them, and re-layouts  3.52 us (7%)
  Pallas kernels  3.01 us (6%)
  between operations  0.72 us (1%)
    ppermute x6, starting transfers between devices, fetch(): return lax.ppermute(value, ('blk', 'rep'), pairs)  13.5 us
    ppermute x2, waiting for transfers between devices, from_column(): return lax.ppermute(value, 'rep', pairs)  7.61 us
    ppermute x2, starting transfers between devices, from_column(): return lax.ppermute(value, 'rep', pairs)  7.35 us
    ppermute x6, waiting for transfers between devices, fetch(): return lax.ppermute(value, ('blk', 'rep'), pairs)  6.66 us
    ppermute x4, starting transfers between devices, from_mate(): lax.ppermute(value, 'rep', [(team, team ^ 1) for team in range(team_count)])  4.7 us
    unnamed x10, local copies, waits for them, and re-layouts  3.44 us
    ppermute x4, waiting for transfers between devices, from_mate(): lax.ppermute(value, 'rep', [(team, team ^ 1) for team in range(team_count)])  1.82 us
    pallas_call x2, Pallas kernels, arc_step(): pl.pallas_call(functools.partial(arc_kernel, team_count=team_count, piece...  1.74 us
  transfers between devices with their start and end apart: 12, of which 7 were waited for; matrix products, arithmetic and copies ran while one was open for 0% of the time, Pallas kernels for 1%

profile of v20, /device:TPU:0, one launch (start us, length us, event | category | flops | bytes accessed | tf_op | source)
XLA Modules:
  0.0 49.0 jit_solution(2947337290909188800)
XLA Ops:
  0.0 5.4 %collective-permute-start.1 = (f32[1024,128]{1,0:T(8,128)}, f32[1024,128]{1,0:T(8,128)S(1)}, u32[]{:S(2)}, u32[]{:S(2)}) collective-permute-start(f32[1024,128]{1,0:T(8,128)} %embeddings_ref.1), channel_id=1, source_target_pairs={{3,0},{1,5},{2,10},{0,15},{7,4},{5,9},{6,14},{4,3},{11,8},{9,13},{... | collective-permute-start | bytes 1572872 | tf_op jit(solution)/shard_map/ppermute | solution.py:153
  5.4 0.8 %collective-permute-start = (s32[8,128]{1,0:T(8,128)}, s32[8,128]{1,0:T(8,128)S(1)}, u32[]{:S(2)}, u32[]{:S(2)}) collective-permute-start(s32[8,128]{1,0:T(8,128)} %bitcast.12), channel_id=1, source_target_pairs={{3,0},{1,5},{2,10},{0,15},{7,4},{5,9},{6,14},{4,3},{11,8},{9,13},{... | collective-permute-start | bytes 12296 | tf_op jit(solution)/shard_map/ppermute | solution.py:153
  6.9 0.6 %copy-done.3 = s32[1,1,1,24]{3,2,1,0:T(1,128)S(1)} copy-done((s32[1,1,1,24]{3,2,1,0:T(1,128)S(1)}, s32[1,1,1,24]{3,2,1,0:T(1,128)}, u32[]{:S(2)}) %copy-start.3) | copy-done | bytes 120
  7.5 0.0 copy-done.4
  7.6 0.1 add_bitcast_fusion
  7.6 0.1 squeeze.19.after_ref.info_ref
  7.7 0.6 %copy-done.2 = s32[1024]{0:T(1024)S(1)} copy-done((s32[1024]{0:T(1024)S(1)}, s32[1024]{0:T(1024)}, u32[]{:S(2)}) %copy-start.2) | copy-done | bytes 4120
  8.3 1.1 %copy-done = bf16[1,1,1,24,128,128]{5,4,3,2,1,0:T(8,128)(2,1)S(1)} copy-done((bf16[1,1,1,24,128,128]{5,4,3,2,1,0:T(8,128)(2,1)S(1)}, bf16[1,1,1,24,128,128]{5,4,3,2,1,0:T(8,128)(2,1)}, u32[]{:S(2)}) %copy-start) | copy-done | bytes 786456
  9.5 1.0 %copy-done.1 = f32[1024,128]{1,0:T(8,128)S(1)} copy-done((f32[1024,128]{1,0:T(8,128)S(1)}, f32[1024,128]{1,0:T(8,128)}, u32[]{:S(2)}) %copy-start.1) | copy-done | bytes 524312
  10.5 0.6 %shard_map.64 = (bf16[1,24,128,128]{3,2,1,0:T(8,128)(2,1)S(1)}, f32[256,128]{1,0:T(8,128)S(1)}, f32[256,128]{1,0:T(8,128)S(1)}) custom-call(s32[8,128]{1,0:T(8,128)S(1)} %bitcast.13, f32[1024,128]{1,0:T(8,128)S(1)} %copy-done.1, bf16[1,24,128,128]{3,2,1,0:T(8,128)(2,1)S(1)} %bitcast.11, s32[49,128]{1,0:T(8,128)S(1)} %squeeze.19.after_ref.info_ref), custom_call_target="tpu_custom_call" | custom-call | flops 131072 | bytes 524288 | tf_op jit(solution)/shard_map/pallas_call | solution.py:56
  11.1 3.5 %collective-permute-done.refs_0_ = s32[8,128]{1,0:T(8,128)S(1)} collective-permute-done((s32[8,128]{1,0:T(8,128)}, s32[8,128]{1,0:T(8,128)S(1)}, u32[]{:S(2)}, u32[]{:S(2)}) %collective-permute-start) | collective-permute-done | bytes 4128 | tf_op jit(solution)/shard_map/ppermute | solution.py:153
  14.6 0.0 collective-permute-done.1.refs_1_
  14.6 1.0 %shard_map.65 = (f32[256,128]{1,0:T(8,128)S(1)}, f32[256,128]{1,0:T(8,128)S(1)}, f32[256,128]{1,0:T(8,128)S(1)}, f32[256,128]{1,0:T(8,128)S(1)}) custom-call(s32[49,128]{1,0:T(8,128)S(1)} %squeeze.19.after_ref.info_ref, bf16[24,128,128]{2,1,0:T(8,128)(2,1)S(1)} %bitcast.9, s32[8,128]{1,0:T(8,128)S(1)} %collective-permute-done.refs_0_, ...), custom_call_target="tpu_custom_call" | custom-call | flops 201326592 | bytes 1048576 | tf_op jit(solution)/shard_map/pallas_call | solution.py:124
  15.6 0.8 %collective-permute-start.3 = (f32[256,128]{1,0:T(8,128)S(1)}, f32[256,128]{1,0:T(8,128)S(1)}, u32[]{:S(2)}, u32[]{:S(2)}) collective-permute-start(f32[256,128]{1,0:T(8,128)S(1)} %get-tuple-element.21), channel_id=1, source_target_pairs={{0,1},{1,0},{2,3},{3,2},{4,5},{5,4},{6,7},{7,6},{8,9},{9,8},{10,11... | collective-permute-start | bytes 393224 | tf_op jit(solution)/shard_map/ppermute | solution.py:163
  16.4 0.1 collective-permute-start.2
  16.5 0.9 %collective-permute-done.3 = f32[256,128]{1,0:T(8,128)S(1)} collective-permute-done((f32[256,128]{1,0:T(8,128)S(1)}, f32[256,128]{1,0:T(8,128)S(1)}, u32[]{:S(2)}, u32[]{:S(2)}) %collective-permute-start.3) | collective-permute-done | bytes 131104 | tf_op jit(solution)/shard_map/ppermute | solution.py:163
  17.4 4.0 %collective-permute-start.4 = (f32[256,128]{1,0:T(8,128)S(1)}, f32[256,128]{1,0:T(8,128)S(1)}, u32[]{:S(2)}, u32[]{:S(2)}) collective-permute-start(f32[256,128]{1,0:T(8,128)S(1)} %add.16), channel_id=1, source_target_pairs={{2,0},{3,1},{0,2},{1,3},{6,4},{7,5},{4,6},{5,7},{10,8},{11,9},{8,1... | collective-permute-start | bytes 393224 | tf_op jit(solution)/shard_map/ppermute | solution.py:169
  21.4 3.8 %collective-permute-done.4 = f32[256,128]{1,0:T(8,128)S(1)} collective-permute-done((f32[256,128]{1,0:T(8,128)S(1)}, f32[256,128]{1,0:T(8,128)S(1)}, u32[]{:S(2)}, u32[]{:S(2)}) %collective-permute-start.4) | collective-permute-done | bytes 131104 | tf_op jit(solution)/shard_map/ppermute | solution.py:169
  25.3 3.7 %collective-permute-start.8 = (f32[256,128]{1,0:T(8,128)S(1)}, f32[256,128]{1,0:T(8,128)S(1)}, u32[]{:S(2)}, u32[]{:S(2)}) collective-permute-start(f32[256,128]{1,0:T(8,128)S(1)} %get-tuple-element.27), channel_id=1, source_target_pairs={{2,0},{1,5},{3,10},{0,15},{6,4},{5,9},{7,14},{4,3},{10,8},{9,13},{... | collective-permute-start | bytes 393224 | tf_op jit(solution)/shard_map/ppermute | solution.py:153
  28.9 0.7 %collective-permute-start.6 = (f32[256,128]{1,0:T(8,128)S(1)}, f32[256,128]{1,0:T(8,128)S(1)}, u32[]{:S(2)}, u32[]{:S(2)}) collective-permute-start(f32[256,128]{1,0:T(8,128)S(1)} %get-tuple-element.27), channel_id=1, source_target_pairs={{0,0},{3,5},{1,10},{2,15},{4,4},{7,9},{5,14},{6,3},{8,8},{11,13},{... | collective-permute-start | bytes 393224 | tf_op jit(solution)/shard_map/ppermute | solution.py:153
  29.6 2.9 %collective-permute-start.5 = (f32[256,128]{1,0:T(8,128)S(1)}, f32[256,128]{1,0:T(8,128)S(1)}, u32[]{:S(2)}, u32[]{:S(2)}) collective-permute-start(f32[256,128]{1,0:T(8,128)S(1)} %get-tuple-element.27), channel_id=1, source_target_pairs={{3,0},{0,5},{2,10},{1,15},{7,4},{4,9},{6,14},{5,3},{11,8},{8,13},{... | collective-permute-start | bytes 393224 | tf_op jit(solution)/shard_map/ppermute | solution.py:153
  32.5 0.0 collective-permute-done.8.refs_3_
  32.6 1.1 %collective-permute-done.7.refs_2_ = f32[256,128]{1,0:T(8,128)S(1)} collective-permute-done((f32[256,128]{1,0:T(8,128)S(1)}, f32[256,128]{1,0:T(8,128)S(1)}, u32[]{:S(2)}, u32[]{:S(2)}) %collective-permute-start.7) | collective-permute-done | bytes 131104 | tf_op jit(solution)/shard_map/ppermute | solution.py:153
  33.6 2.0 %collective-permute-done.5.refs_0_ = f32[256,128]{1,0:T(8,128)S(1)} collective-permute-done((f32[256,128]{1,0:T(8,128)S(1)}, f32[256,128]{1,0:T(8,128)S(1)}, u32[]{:S(2)}, u32[]{:S(2)}) %collective-permute-start.5) | collective-permute-done | bytes 131104 | tf_op jit(solution)/shard_map/ppermute | solution.py:153
  35.7 0.8 %shard_map.66 = (f32[256,128]{1,0:T(8,128)S(1)}, f32[256,128]{1,0:T(8,128)S(1)}, f32[256,128]{1,0:T(8,128)S(1)}, f32[256,128]{1,0:T(8,128)S(1)}) custom-call(s32[49,128]{1,0:T(8,128)S(1)} %squeeze.19.after_ref.info_ref, bf16[24,128,128]{2,1,0:T(8,128)(2,1)S(1)} %bitcast.10, f32[256,128]{1,0:T(8,128)S(1)} %collective-permute-done.5.refs_0_, ...), custom_call_target="tpu_custom_call" | custom-call | flops 201326592 | bytes 1048576 | tf_op jit(solution)/shard_map/pallas_call | solution.py:124
  36.4 3.7 %collective-permute-start.10 = (f32[256,128]{1,0:T(8,128)S(1)}, f32[256,128]{1,0:T(8,128)S(1)}, u32[]{:S(2)}, u32[]{:S(2)}) collective-permute-start(f32[256,128]{1,0:T(8,128)S(1)} %get-tuple-element.26), channel_id=1, source_target_pairs={{0,1},{1,0},{2,3},{3,2},{4,5},{5,4},{6,7},{7,6},{8,9},{9,8},{10,11... | collective-permute-start | bytes 393224 | tf_op jit(solution)/shard_map/ppermute | solution.py:163
  40.2 0.1 collective-permute-start.9
  40.3 0.9 %collective-permute-done.10 = f32[256,128]{1,0:T(8,128)S(1)} collective-permute-done((f32[256,128]{1,0:T(8,128)S(1)}, f32[256,128]{1,0:T(8,128)S(1)}, u32[]{:S(2)}, u32[]{:S(2)}) %collective-permute-start.10) | collective-permute-done | bytes 131104 | tf_op jit(solution)/shard_map/ppermute | solution.py:163
  41.2 3.3 %collective-permute-start.11 = (f32[256,128]{1,0:T(8,128)S(1)}, f32[256,128]{1,0:T(8,128)S(1)}, u32[]{:S(2)}, u32[]{:S(2)}) collective-permute-start(f32[256,128]{1,0:T(8,128)S(1)} %add.19), channel_id=1, source_target_pairs={{2,0},{3,1},{0,2},{1,3},{6,4},{7,5},{4,6},{5,7},{10,8},{11,9},{8,1... | collective-permute-start | bytes 393224 | tf_op jit(solution)/shard_map/ppermute | solution.py:169
  44.5 0.0 collective-permute-done.9.refs_1_
  44.5 3.8 %collective-permute-done.11.refs_2_ = f32[256,128]{1,0:T(8,128)S(1)} collective-permute-done((f32[256,128]{1,0:T(8,128)S(1)}, f32[256,128]{1,0:T(8,128)S(1)}, u32[]{:S(2)}, u32[]{:S(2)}) %collective-permute-start.11) | collective-permute-done | bytes 131104 | tf_op jit(solution)/shard_map/ppermute | solution.py:169
  48.3 0.7 %shard_map.67 = f32[256,128]{1,0:T(8,128)} custom-call(f32[256,128]{1,0:T(8,128)S(1)} %get-tuple-element.28.base_ref, f32[256,128]{1,0:T(8,128)S(1)} %get-tuple-element.22.norm_ref, f32[256,128]{1,0:T(8,128)S(1)} %get-tuple-element.23.refs_0_, f32[256,128]{1,0:T(8,128)S(1)} %collective-permute-done.9.refs_1_, f32[256,128]{1,0:T(8,128)S(1)} %collective-permute-done.11.refs_2_), custom_call_target="tpu_custom_call" | custom-call | tf_op jit(solution)/shard_map/pallas_call | solution.py:199
  (11 shorter events, 0.1 us)
Async XLA Ops:
  0.0 14.6 %collective-permute-start.1 = (f32[1024,128]{1,0:T(8,128)}, f32[1024,128]{1,0:T(8,128)S(1)}, u32[]{:S(2)}, u32[]{:S(2)}) collective-permute-start(f32[1024,128]{1,0:T(8,128)} %embeddings_ref.1), channel_id=1, source_target_pairs={{3,0},{1,5},{2,10},{0,15},{7,4},{5,9},{6,14},{4,3},{11,8},{9,13},{... | collective-permute-start | bytes 1572872 | tf_op jit(solution)/shard_map/ppermute | solution.py:153
  5.4 9.2 %collective-permute-start = (s32[8,128]{1,0:T(8,128)}, s32[8,128]{1,0:T(8,128)S(1)}, u32[]{:S(2)}, u32[]{:S(2)}) collective-permute-start(s32[8,128]{1,0:T(8,128)} %bitcast.12), channel_id=1, source_target_pairs={{3,0},{1,5},{2,10},{0,15},{7,4},{5,9},{6,14},{4,3},{11,8},{9,13},{... | collective-permute-start | bytes 12296 | tf_op jit(solution)/shard_map/ppermute | solution.py:153
  6.9 0.7 %copy-start.3 = (s32[1,1,1,24]{3,2,1,0:T(1,128)S(1)}, s32[1,1,1,24]{3,2,1,0:T(1,128)}, u32[]{:S(2)}) copy-start(s32[1,1,1,24]{3,2,1,0:T(1,128)} %param.10) | copy-start | bytes 292
  6.9 0.7 %copy-start.4 = (s32[1,1,1,24]{3,2,1,0:T(1,128)S(1)}, s32[1,1,1,24]{3,2,1,0:T(1,128)}, u32[]{:S(2)}) copy-start(s32[1,1,1,24]{3,2,1,0:T(1,128)} %param.9) | copy-start | bytes 292
  7.6 0.7 %copy-start.2 = (s32[1024]{0:T(1024)S(1)}, s32[1024]{0:T(1024)}, u32[]{:S(2)}) copy-start(s32[1024]{0:T(1024)} %param.7) | copy-start | bytes 12292
  8.3 1.1 %copy-start = (bf16[1,1,1,24,128,128]{5,4,3,2,1,0:T(8,128)(2,1)S(1)}, bf16[1,1,1,24,128,128]{5,4,3,2,1,0:T(8,128)(2,1)}, u32[]{:S(2)}) copy-start(bf16[1,1,1,24,128,128]{5,4,3,2,1,0:T(8,128)(2,1)} %param.8) | copy-start | bytes 2359300
  9.5 1.0 %copy-start.1 = (f32[1024,128]{1,0:T(8,128)S(1)}, f32[1024,128]{1,0:T(8,128)}, u32[]{:S(2)}) copy-start(f32[1024,128]{1,0:T(8,128)} %embeddings_ref.1) | copy-start | bytes 1572868
  15.6 1.8 %collective-permute-start.3 = (f32[256,128]{1,0:T(8,128)S(1)}, f32[256,128]{1,0:T(8,128)S(1)}, u32[]{:S(2)}, u32[]{:S(2)}) collective-permute-start(f32[256,128]{1,0:T(8,128)S(1)} %get-tuple-element.21), channel_id=1, source_target_pairs={{0,1},{1,0},{2,3},{3,2},{4,5},{5,4},{6,7},{7,6},{8,9},{9,8},{10,11... | collective-permute-start | bytes 393224 | tf_op jit(solution)/shard_map/ppermute | solution.py:163
  16.4 5.0 %collective-permute-start.2 = (f32[256,128]{1,0:T(8,128)S(1)}, f32[256,128]{1,0:T(8,128)S(1)}, u32[]{:S(2)}, u32[]{:S(2)}) collective-permute-start(f32[256,128]{1,0:T(8,128)S(1)} %get-tuple-element.19), channel_id=1, source_target_pairs={{0,1},{1,0},{2,3},{3,2},{4,5},{5,4},{6,7},{7,6},{8,9},{9,8},{10,11... | collective-permute-start | bytes 393224 | tf_op jit(solution)/shard_map/ppermute | solution.py:163
  17.4 7.8 %collective-permute-start.4 = (f32[256,128]{1,0:T(8,128)S(1)}, f32[256,128]{1,0:T(8,128)S(1)}, u32[]{:S(2)}, u32[]{:S(2)}) collective-permute-start(f32[256,128]{1,0:T(8,128)S(1)} %add.16), channel_id=1, source_target_pairs={{2,0},{3,1},{0,2},{1,3},{6,4},{7,5},{4,6},{5,7},{10,8},{11,9},{8,1... | collective-permute-start | bytes 393224 | tf_op jit(solution)/shard_map/ppermute | solution.py:169
  25.3 7.3 %collective-permute-start.8 = (f32[256,128]{1,0:T(8,128)S(1)}, f32[256,128]{1,0:T(8,128)S(1)}, u32[]{:S(2)}, u32[]{:S(2)}) collective-permute-start(f32[256,128]{1,0:T(8,128)S(1)} %get-tuple-element.27), channel_id=1, source_target_pairs={{2,0},{1,5},{3,10},{0,15},{6,4},{5,9},{7,14},{4,3},{10,8},{9,13},{... | collective-permute-start | bytes 393224 | tf_op jit(solution)/shard_map/ppermute | solution.py:153
  28.9 4.7 %collective-permute-start.7 = (f32[256,128]{1,0:T(8,128)S(1)}, f32[256,128]{1,0:T(8,128)S(1)}, u32[]{:S(2)}, u32[]{:S(2)}) collective-permute-start(f32[256,128]{1,0:T(8,128)S(1)} %get-tuple-element.27), channel_id=1, source_target_pairs={{1,0},{2,5},{0,10},{3,15},{5,4},{6,9},{4,14},{7,3},{9,8},{10,13},{... | collective-permute-start | bytes 393224 | tf_op jit(solution)/shard_map/ppermute | solution.py:153
  28.9 4.7 %collective-permute-start.6 = (f32[256,128]{1,0:T(8,128)S(1)}, f32[256,128]{1,0:T(8,128)S(1)}, u32[]{:S(2)}, u32[]{:S(2)}) collective-permute-start(f32[256,128]{1,0:T(8,128)S(1)} %get-tuple-element.27), channel_id=1, source_target_pairs={{0,0},{3,5},{1,10},{2,15},{4,4},{7,9},{5,14},{6,3},{8,8},{11,13},{... | collective-permute-start | bytes 393224 | tf_op jit(solution)/shard_map/ppermute | solution.py:153
  29.6 6.1 %collective-permute-start.5 = (f32[256,128]{1,0:T(8,128)S(1)}, f32[256,128]{1,0:T(8,128)S(1)}, u32[]{:S(2)}, u32[]{:S(2)}) collective-permute-start(f32[256,128]{1,0:T(8,128)S(1)} %get-tuple-element.27), channel_id=1, source_target_pairs={{3,0},{0,5},{2,10},{1,15},{7,4},{4,9},{6,14},{5,3},{11,8},{8,13},{... | collective-permute-start | bytes 393224 | tf_op jit(solution)/shard_map/ppermute | solution.py:153
  36.4 4.7 %collective-permute-start.10 = (f32[256,128]{1,0:T(8,128)S(1)}, f32[256,128]{1,0:T(8,128)S(1)}, u32[]{:S(2)}, u32[]{:S(2)}) collective-permute-start(f32[256,128]{1,0:T(8,128)S(1)} %get-tuple-element.26), channel_id=1, source_target_pairs={{0,1},{1,0},{2,3},{3,2},{4,5},{5,4},{6,7},{7,6},{8,9},{9,8},{10,11... | collective-permute-start | bytes 393224 | tf_op jit(solution)/shard_map/ppermute | solution.py:163
  40.2 4.3 %collective-permute-start.9 = (f32[256,128]{1,0:T(8,128)S(1)}, f32[256,128]{1,0:T(8,128)S(1)}, u32[]{:S(2)}, u32[]{:S(2)}) collective-permute-start(f32[256,128]{1,0:T(8,128)S(1)} %get-tuple-element.24), channel_id=1, source_target_pairs={{0,1},{1,0},{2,3},{3,2},{4,5},{5,4},{6,7},{7,6},{8,9},{9,8},{10,11... | collective-permute-start | bytes 393224 | tf_op jit(solution)/shard_map/ppermute | solution.py:163
  41.2 7.1 %collective-permute-start.11 = (f32[256,128]{1,0:T(8,128)S(1)}, f32[256,128]{1,0:T(8,128)S(1)}, u32[]{:S(2)}, u32[]{:S(2)}) collective-permute-start(f32[256,128]{1,0:T(8,128)S(1)} %add.19), channel_id=1, source_target_pairs={{2,0},{3,1},{0,2},{1,3},{6,4},{7,5},{4,6},{5,7},{10,8},{11,9},{8,1... | collective-permute-start | bytes 393224 | tf_op jit(solution)/shard_map/ppermute | solution.py:169

commit v21 on v12

--- a/solution.py
+++ b/solution.py
@@ -210,7 +210,7 @@
     arc_length, _, tile_size, _ = tile_values.shape[2:]
     panel_rows = embeddings.shape[0]
     team_count = lax.axis_size("rep")
-    spread = (3, 1, 2, 0) if team_count == 4 else tuple(range(team_count))
+    spread = (3, 0, 2, 1) if team_count == 4 else tuple(range(team_count))
     degrees = degrees.reshape(panel_rows // tile_size, tile_size)
 
     panel = fetch(embeddings, lambda team: spread[team], arc_length)

time: 48.9 us -> 48.9 us (level)
  waiting for transfers between devices: 19.9 us -> 21.1 us
  starting transfers between devices: 21.3 us -> 20.2 us
    ppermute x4, starting transfers between devices: 3.54 us -> 7.8 us  [from_mate(): lax.ppermute(value, 'rep', [(team, team ^ 1) for team in range(team_count)])]
    ppermute x6, starting transfers between devices: 11 us -> 8.01 us  [fetch(): return lax.ppermute(value, ('blk', 'rep'), pairs)]
    ppermute x2, starting transfers between devices: 6.72 us -> 4.37 us  [from_column(): return lax.ppermute(value, 'rep', pairs)]
    ppermute x6, waiting for transfers between devices: 10.5 us -> 11.3 us  [fetch(): return lax.ppermute(value, ('blk', 'rep'), pairs)]
where the time goes in v21:
time: 48.9 us; the launch traced here: 48.6 us
  waiting for transfers between devices  21.1 us (43%)
  starting transfers between devices  20.2 us (41%)
  local copies, waits for them, and re-layouts  3.52 us (7%)
  Pallas kernels  3.01 us (6%)
  between operations  0.72 us (1%)
    ppermute x6, waiting for transfers between devices, fetch(): return lax.ppermute(value, ('blk', 'rep'), pairs)  11.3 us
    ppermute x6, starting transfers between devices, fetch(): return lax.ppermute(value, ('blk', 'rep'), pairs)  8.01 us
    ppermute x2, waiting for transfers between devices, from_column(): return lax.ppermute(value, 'rep', pairs)  7.97 us
    ppermute x4, starting transfers between devices, from_mate(): lax.ppermute(value, 'rep', [(team, team ^ 1) for team in range(team_count)])  7.8 us
    ppermute x2, starting transfers between devices, from_column(): return lax.ppermute(value, 'rep', pairs)  4.37 us
    unnamed x10, local copies, waits for them, and re-layouts  3.44 us
    ppermute x4, waiting for transfers between devices, from_mate(): lax.ppermute(value, 'rep', [(team, team ^ 1) for team in range(team_count)])  1.82 us
    pallas_call x2, Pallas kernels, arc_step(): pl.pallas_call(functools.partial(arc_kernel, team_count=team_count, piece...  1.74 us
  transfers between devices with their start and end apart: 12, of which 8 were waited for; matrix products, arithmetic and copies ran while one was open for 0% of the time, Pallas kernels for 1%

profile of v21, /device:TPU:0, one launch (start us, length us, event | category | flops | bytes accessed | tf_op | source)
XLA Modules:
  0.0 48.6 jit_solution(2568807230356269202)
XLA Ops:
  0.0 2.5 %collective-permute-start.1 = (f32[1024,128]{1,0:T(8,128)}, f32[1024,128]{1,0:T(8,128)S(1)}, u32[]{:S(2)}, u32[]{:S(2)}) collective-permute-start(f32[1024,128]{1,0:T(8,128)} %embeddings_ref.1), channel_id=1, source_target_pairs={{3,0},{0,5},{2,10},{1,15},{7,4},{4,9},{6,14},{5,3},{11,8},{8,13},{... | collective-permute-start | bytes 1572872 | tf_op jit(solution)/shard_map/ppermute | solution.py:153
  2.5 1.1 %collective-permute-start = (s32[8,128]{1,0:T(8,128)}, s32[8,128]{1,0:T(8,128)S(1)}, u32[]{:S(2)}, u32[]{:S(2)}) collective-permute-start(s32[8,128]{1,0:T(8,128)} %bitcast.12), channel_id=1, source_target_pairs={{3,0},{0,5},{2,10},{1,15},{7,4},{4,9},{6,14},{5,3},{11,8},{8,13},{... | collective-permute-start | bytes 12296 | tf_op jit(solution)/shard_map/ppermute | solution.py:153
  4.2 0.6 %copy-done.3 = s32[1,1,1,24]{3,2,1,0:T(1,128)S(1)} copy-done((s32[1,1,1,24]{3,2,1,0:T(1,128)S(1)}, s32[1,1,1,24]{3,2,1,0:T(1,128)}, u32[]{:S(2)}) %copy-start.3) | copy-done | bytes 120
  4.9 0.0 copy-done.4
  4.9 0.1 add_bitcast_fusion
  5.0 0.1 squeeze.19.after_ref.info_ref
  5.0 0.6 %copy-done.2 = s32[1024]{0:T(1024)S(1)} copy-done((s32[1024]{0:T(1024)S(1)}, s32[1024]{0:T(1024)}, u32[]{:S(2)}) %copy-start.2) | copy-done | bytes 4120
  5.7 1.1 %copy-done = bf16[1,1,1,24,128,128]{5,4,3,2,1,0:T(8,128)(2,1)S(1)} copy-done((bf16[1,1,1,24,128,128]{5,4,3,2,1,0:T(8,128)(2,1)S(1)}, bf16[1,1,1,24,128,128]{5,4,3,2,1,0:T(8,128)(2,1)}, u32[]{:S(2)}) %copy-start) | copy-done | bytes 786456
  6.8 1.0 %copy-done.1 = f32[1024,128]{1,0:T(8,128)S(1)} copy-done((f32[1024,128]{1,0:T(8,128)S(1)}, f32[1024,128]{1,0:T(8,128)}, u32[]{:S(2)}) %copy-start.1) | copy-done | bytes 524312
  7.8 0.6 %shard_map.64 = (bf16[1,24,128,128]{3,2,1,0:T(8,128)(2,1)S(1)}, f32[256,128]{1,0:T(8,128)S(1)}, f32[256,128]{1,0:T(8,128)S(1)}) custom-call(s32[8,128]{1,0:T(8,128)S(1)} %bitcast.13, f32[1024,128]{1,0:T(8,128)S(1)} %copy-done.1, bf16[1,24,128,128]{3,2,1,0:T(8,128)(2,1)S(1)} %bitcast.11, s32[49,128]{1,0:T(8,128)S(1)} %squeeze.19.after_ref.info_ref), custom_call_target="tpu_custom_call" | custom-call | flops 131072 | bytes 524288 | tf_op jit(solution)/shard_map/pallas_call | solution.py:56
  8.4 4.2 %collective-permute-done.refs_0_ = s32[8,128]{1,0:T(8,128)S(1)} collective-permute-done((s32[8,128]{1,0:T(8,128)}, s32[8,128]{1,0:T(8,128)S(1)}, u32[]{:S(2)}, u32[]{:S(2)}) %collective-permute-start) | collective-permute-done | bytes 4128 | tf_op jit(solution)/shard_map/ppermute | solution.py:153
  12.7 0.0 collective-permute-done.1.refs_1_
  12.7 1.0 %shard_map.65 = (f32[256,128]{1,0:T(8,128)S(1)}, f32[256,128]{1,0:T(8,128)S(1)}, f32[256,128]{1,0:T(8,128)S(1)}, f32[256,128]{1,0:T(8,128)S(1)}) custom-call(s32[49,128]{1,0:T(8,128)S(1)} %squeeze.19.after_ref.info_ref, bf16[24,128,128]{2,1,0:T(8,128)(2,1)S(1)} %bitcast.9, s32[8,128]{1,0:T(8,128)S(1)} %collective-permute-done.refs_0_, ...), custom_call_target="tpu_custom_call" | custom-call | flops 201326592 | bytes 1048576 | tf_op jit(solution)/shard_map/pallas_call | solution.py:124
  13.6 5.1 %collective-permute-start.3 = (f32[256,128]{1,0:T(8,128)S(1)}, f32[256,128]{1,0:T(8,128)S(1)}, u32[]{:S(2)}, u32[]{:S(2)}) collective-permute-start(f32[256,128]{1,0:T(8,128)S(1)} %get-tuple-element.21), channel_id=1, source_target_pairs={{0,1},{1,0},{2,3},{3,2},{4,5},{5,4},{6,7},{7,6},{8,9},{9,8},{10,11... | collective-permute-start | bytes 393224 | tf_op jit(solution)/shard_map/ppermute | solution.py:163
  18.8 0.1 collective-permute-start.2
  18.8 0.9 %collective-permute-done.3 = f32[256,128]{1,0:T(8,128)S(1)} collective-permute-done((f32[256,128]{1,0:T(8,128)S(1)}, f32[256,128]{1,0:T(8,128)S(1)}, u32[]{:S(2)}, u32[]{:S(2)}) %collective-permute-start.3) | collective-permute-done | bytes 131104 | tf_op jit(solution)/shard_map/ppermute | solution.py:163
  19.8 1.7 %collective-permute-start.4 = (f32[256,128]{1,0:T(8,128)S(1)}, f32[256,128]{1,0:T(8,128)S(1)}, u32[]{:S(2)}, u32[]{:S(2)}) collective-permute-start(f32[256,128]{1,0:T(8,128)S(1)} %add.16), channel_id=1, source_target_pairs={{2,0},{3,1},{0,2},{1,3},{6,4},{7,5},{4,6},{5,7},{10,8},{11,9},{8,1... | collective-permute-start | bytes 393224 | tf_op jit(solution)/shard_map/ppermute | solution.py:169
  21.4 4.2 %collective-permute-done.4 = f32[256,128]{1,0:T(8,128)S(1)} collective-permute-done((f32[256,128]{1,0:T(8,128)S(1)}, f32[256,128]{1,0:T(8,128)S(1)}, u32[]{:S(2)}, u32[]{:S(2)}) %collective-permute-start.4) | collective-permute-done | bytes 131104 | tf_op jit(solution)/shard_map/ppermute | solution.py:169
  25.6 3.3 %collective-permute-start.8 = (f32[256,128]{1,0:T(8,128)S(1)}, f32[256,128]{1,0:T(8,128)S(1)}, u32[]{:S(2)}, u32[]{:S(2)}) collective-permute-start(f32[256,128]{1,0:T(8,128)S(1)} %get-tuple-element.27), channel_id=1, source_target_pairs={{3,0},{1,5},{2,10},{0,15},{7,4},{5,9},{6,14},{4,3},{11,8},{9,13},{... | collective-permute-start | bytes 393224 | tf_op jit(solution)/shard_map/ppermute | solution.py:153
  28.9 0.5 %collective-permute-start.7 = (f32[256,128]{1,0:T(8,128)S(1)}, f32[256,128]{1,0:T(8,128)S(1)}, u32[]{:S(2)}, u32[]{:S(2)}) collective-permute-start(f32[256,128]{1,0:T(8,128)S(1)} %get-tuple-element.27), channel_id=1, source_target_pairs={{1,0},{3,5},{0,10},{2,15},{5,4},{7,9},{4,14},{6,3},{9,8},{11,13},{... | collective-permute-start | bytes 393224 | tf_op jit(solution)/shard_map/ppermute | solution.py:153
  29.4 0.7 %collective-permute-start.5 = (f32[256,128]{1,0:T(8,128)S(1)}, f32[256,128]{1,0:T(8,128)S(1)}, u32[]{:S(2)}, u32[]{:S(2)}) collective-permute-start(f32[256,128]{1,0:T(8,128)S(1)} %get-tuple-element.27), channel_id=1, source_target_pairs={{0,0},{2,5},{1,10},{3,15},{4,4},{6,9},{5,14},{7,3},{8,8},{10,13},{... | collective-permute-start | bytes 393224 | tf_op jit(solution)/shard_map/ppermute | solution.py:153
  30.1 2.4 %collective-permute-done.8.refs_3_ = f32[256,128]{1,0:T(8,128)S(1)} collective-permute-done((f32[256,128]{1,0:T(8,128)S(1)}, f32[256,128]{1,0:T(8,128)S(1)}, u32[]{:S(2)}, u32[]{:S(2)}) %collective-permute-start.8) | collective-permute-done | bytes 131104 | tf_op jit(solution)/shard_map/ppermute | solution.py:153
  32.5 1.8 %collective-permute-done.7.refs_2_ = f32[256,128]{1,0:T(8,128)S(1)} collective-permute-done((f32[256,128]{1,0:T(8,128)S(1)}, f32[256,128]{1,0:T(8,128)S(1)}, u32[]{:S(2)}, u32[]{:S(2)}) %collective-permute-start.7) | collective-permute-done | bytes 131104 | tf_op jit(solution)/shard_map/ppermute | solution.py:153
  34.3 2.8 %collective-permute-done.6.refs_1_ = f32[256,128]{1,0:T(8,128)S(1)} collective-permute-done((f32[256,128]{1,0:T(8,128)S(1)}, f32[256,128]{1,0:T(8,128)S(1)}, u32[]{:S(2)}, u32[]{:S(2)}) %collective-permute-start.6) | collective-permute-done | bytes 131104 | tf_op jit(solution)/shard_map/ppermute | solution.py:153
  37.1 0.0 collective-permute-done.5.refs_0_
  37.1 0.8 %shard_map.66 = (f32[256,128]{1,0:T(8,128)S(1)}, f32[256,128]{1,0:T(8,128)S(1)}, f32[256,128]{1,0:T(8,128)S(1)}, f32[256,128]{1,0:T(8,128)S(1)}) custom-call(s32[49,128]{1,0:T(8,128)S(1)} %squeeze.19.after_ref.info_ref, bf16[24,128,128]{2,1,0:T(8,128)(2,1)S(1)} %bitcast.10, f32[256,128]{1,0:T(8,128)S(1)} %collective-permute-done.5.refs_0_, ...), custom_call_target="tpu_custom_call" | custom-call | flops 201326592 | bytes 1048576 | tf_op jit(solution)/shard_map/pallas_call | solution.py:124
  37.9 2.5 %collective-permute-start.10 = (f32[256,128]{1,0:T(8,128)S(1)}, f32[256,128]{1,0:T(8,128)S(1)}, u32[]{:S(2)}, u32[]{:S(2)}) collective-permute-start(f32[256,128]{1,0:T(8,128)S(1)} %get-tuple-element.26), channel_id=1, source_target_pairs={{0,1},{1,0},{2,3},{3,2},{4,5},{5,4},{6,7},{7,6},{8,9},{9,8},{10,11... | collective-permute-start | bytes 393224 | tf_op jit(solution)/shard_map/ppermute | solution.py:163
  40.4 0.1 collective-permute-start.9
  40.5 0.9 %collective-permute-done.10 = f32[256,128]{1,0:T(8,128)S(1)} collective-permute-done((f32[256,128]{1,0:T(8,128)S(1)}, f32[256,128]{1,0:T(8,128)S(1)}, u32[]{:S(2)}, u32[]{:S(2)}) %collective-permute-start.10) | collective-permute-done | bytes 131104 | tf_op jit(solution)/shard_map/ppermute | solution.py:163
  41.4 2.7 %collective-permute-start.11 = (f32[256,128]{1,0:T(8,128)S(1)}, f32[256,128]{1,0:T(8,128)S(1)}, u32[]{:S(2)}, u32[]{:S(2)}) collective-permute-start(f32[256,128]{1,0:T(8,128)S(1)} %add.19), channel_id=1, source_target_pairs={{2,0},{3,1},{0,2},{1,3},{6,4},{7,5},{4,6},{5,7},{10,8},{11,9},{8,1... | collective-permute-start | bytes 393224 | tf_op jit(solution)/shard_map/ppermute | solution.py:169
  44.1 3.8 %collective-permute-done.11.refs_2_ = f32[256,128]{1,0:T(8,128)S(1)} collective-permute-done((f32[256,128]{1,0:T(8,128)S(1)}, f32[256,128]{1,0:T(8,128)S(1)}, u32[]{:S(2)}, u32[]{:S(2)}) %collective-permute-start.11) | collective-permute-done | bytes 131104 | tf_op jit(solution)/shard_map/ppermute | solution.py:169
  47.9 0.7 %shard_map.67 = f32[256,128]{1,0:T(8,128)} custom-call(f32[256,128]{1,0:T(8,128)S(1)} %get-tuple-element.28.base_ref, f32[256,128]{1,0:T(8,128)S(1)} %get-tuple-element.22.norm_ref, f32[256,128]{1,0:T(8,128)S(1)} %get-tuple-element.23.refs_0_, f32[256,128]{1,0:T(8,128)S(1)} %collective-permute-done.9.refs_1_, f32[256,128]{1,0:T(8,128)S(1)} %collective-permute-done.11.refs_2_), custom_call_target="tpu_custom_call" | custom-call | tf_op jit(solution)/shard_map/pallas_call | solution.py:199
  (11 shorter events, 0.1 us)
Async XLA Ops:
  0.0 12.7 %collective-permute-start.1 = (f32[1024,128]{1,0:T(8,128)}, f32[1024,128]{1,0:T(8,128)S(1)}, u32[]{:S(2)}, u32[]{:S(2)}) collective-permute-start(f32[1024,128]{1,0:T(8,128)} %embeddings_ref.1), channel_id=1, source_target_pairs={{3,0},{0,5},{2,10},{1,15},{7,4},{4,9},{6,14},{5,3},{11,8},{8,13},{... | collective-permute-start | bytes 1572872 | tf_op jit(solution)/shard_map/ppermute | solution.py:153
  2.5 10.2 %collective-permute-start = (s32[8,128]{1,0:T(8,128)}, s32[8,128]{1,0:T(8,128)S(1)}, u32[]{:S(2)}, u32[]{:S(2)}) collective-permute-start(s32[8,128]{1,0:T(8,128)} %bitcast.12), channel_id=1, source_target_pairs={{3,0},{0,5},{2,10},{1,15},{7,4},{4,9},{6,14},{5,3},{11,8},{8,13},{... | collective-permute-start | bytes 12296 | tf_op jit(solution)/shard_map/ppermute | solution.py:153
  4.2 0.7 %copy-start.3 = (s32[1,1,1,24]{3,2,1,0:T(1,128)S(1)}, s32[1,1,1,24]{3,2,1,0:T(1,128)}, u32[]{:S(2)}) copy-start(s32[1,1,1,24]{3,2,1,0:T(1,128)} %param.10) | copy-start | bytes 292
  4.2 0.7 %copy-start.4 = (s32[1,1,1,24]{3,2,1,0:T(1,128)S(1)}, s32[1,1,1,24]{3,2,1,0:T(1,128)}, u32[]{:S(2)}) copy-start(s32[1,1,1,24]{3,2,1,0:T(1,128)} %param.9) | copy-start | bytes 292
  5.0 0.7 %copy-start.2 = (s32[1024]{0:T(1024)S(1)}, s32[1024]{0:T(1024)}, u32[]{:S(2)}) copy-start(s32[1024]{0:T(1024)} %param.7) | copy-start | bytes 12292
  5.6 1.1 %copy-start = (bf16[1,1,1,24,128,128]{5,4,3,2,1,0:T(8,128)(2,1)S(1)}, bf16[1,1,1,24,128,128]{5,4,3,2,1,0:T(8,128)(2,1)}, u32[]{:S(2)}) copy-start(bf16[1,1,1,24,128,128]{5,4,3,2,1,0:T(8,128)(2,1)} %param.8) | copy-start | bytes 2359300
  6.8 1.0 %copy-start.1 = (f32[1024,128]{1,0:T(8,128)S(1)}, f32[1024,128]{1,0:T(8,128)}, u32[]{:S(2)}) copy-start(f32[1024,128]{1,0:T(8,128)} %embeddings_ref.1) | copy-start | bytes 1572868
  13.6 6.1 %collective-permute-start.3 = (f32[256,128]{1,0:T(8,128)S(1)}, f32[256,128]{1,0:T(8,128)S(1)}, u32[]{:S(2)}, u32[]{:S(2)}) collective-permute-start(f32[256,128]{1,0:T(8,128)S(1)} %get-tuple-element.21), channel_id=1, source_target_pairs={{0,1},{1,0},{2,3},{3,2},{4,5},{5,4},{6,7},{7,6},{8,9},{9,8},{10,11... | collective-permute-start | bytes 393224 | tf_op jit(solution)/shard_map/ppermute | solution.py:163
  18.8 2.7 %collective-permute-start.2 = (f32[256,128]{1,0:T(8,128)S(1)}, f32[256,128]{1,0:T(8,128)S(1)}, u32[]{:S(2)}, u32[]{:S(2)}) collective-permute-start(f32[256,128]{1,0:T(8,128)S(1)} %get-tuple-element.19), channel_id=1, source_target_pairs={{0,1},{1,0},{2,3},{3,2},{4,5},{5,4},{6,7},{7,6},{8,9},{9,8},{10,11... | collective-permute-start | bytes 393224 | tf_op jit(solution)/shard_map/ppermute | solution.py:163
  19.8 5.8 %collective-permute-start.4 = (f32[256,128]{1,0:T(8,128)S(1)}, f32[256,128]{1,0:T(8,128)S(1)}, u32[]{:S(2)}, u32[]{:S(2)}) collective-permute-start(f32[256,128]{1,0:T(8,128)S(1)} %add.16), channel_id=1, source_target_pairs={{2,0},{3,1},{0,2},{1,3},{6,4},{7,5},{4,6},{5,7},{10,8},{11,9},{8,1... | collective-permute-start | bytes 393224 | tf_op jit(solution)/shard_map/ppermute | solution.py:169
  25.6 6.8 %collective-permute-start.8 = (f32[256,128]{1,0:T(8,128)S(1)}, f32[256,128]{1,0:T(8,128)S(1)}, u32[]{:S(2)}, u32[]{:S(2)}) collective-permute-start(f32[256,128]{1,0:T(8,128)S(1)} %get-tuple-element.27), channel_id=1, source_target_pairs={{3,0},{1,5},{2,10},{0,15},{7,4},{5,9},{6,14},{4,3},{11,8},{9,13},{... | collective-permute-start | bytes 393224 | tf_op jit(solution)/shard_map/ppermute | solution.py:153
  28.9 5.4 %collective-permute-start.7 = (f32[256,128]{1,0:T(8,128)S(1)}, f32[256,128]{1,0:T(8,128)S(1)}, u32[]{:S(2)}, u32[]{:S(2)}) collective-permute-start(f32[256,128]{1,0:T(8,128)S(1)} %get-tuple-element.27), channel_id=1, source_target_pairs={{1,0},{3,5},{0,10},{2,15},{5,4},{7,9},{4,14},{6,3},{9,8},{11,13},{... | collective-permute-start | bytes 393224 | tf_op jit(solution)/shard_map/ppermute | solution.py:153
  29.4 7.7 %collective-permute-start.6 = (f32[256,128]{1,0:T(8,128)S(1)}, f32[256,128]{1,0:T(8,128)S(1)}, u32[]{:S(2)}, u32[]{:S(2)}) collective-permute-start(f32[256,128]{1,0:T(8,128)S(1)} %get-tuple-element.27), channel_id=1, source_target_pairs={{2,0},{0,5},{3,10},{1,15},{6,4},{4,9},{7,14},{5,3},{10,8},{8,13},{... | collective-permute-start | bytes 393224 | tf_op jit(solution)/shard_map/ppermute | solution.py:153
  29.4 7.7 %collective-permute-start.5 = (f32[256,128]{1,0:T(8,128)S(1)}, f32[256,128]{1,0:T(8,128)S(1)}, u32[]{:S(2)}, u32[]{:S(2)}) collective-permute-start(f32[256,128]{1,0:T(8,128)S(1)} %get-tuple-element.27), channel_id=1, source_target_pairs={{0,0},{2,5},{1,10},{3,15},{4,4},{6,9},{5,14},{7,3},{8,8},{10,13},{... | collective-permute-start | bytes 393224 | tf_op jit(solution)/shard_map/ppermute | solution.py:153
  37.9 3.5 %collective-permute-start.10 = (f32[256,128]{1,0:T(8,128)S(1)}, f32[256,128]{1,0:T(8,128)S(1)}, u32[]{:S(2)}, u32[]{:S(2)}) collective-permute-start(f32[256,128]{1,0:T(8,128)S(1)} %get-tuple-element.26), channel_id=1, source_target_pairs={{0,1},{1,0},{2,3},{3,2},{4,5},{5,4},{6,7},{7,6},{8,9},{9,8},{10,11... | collective-permute-start | bytes 393224 | tf_op jit(solution)/shard_map/ppermute | solution.py:163
  40.4 3.7 %collective-permute-start.9 = (f32[256,128]{1,0:T(8,128)S(1)}, f32[256,128]{1,0:T(8,128)S(1)}, u32[]{:S(2)}, u32[]{:S(2)}) collective-permute-start(f32[256,128]{1,0:T(8,128)S(1)} %get-tuple-element.24), channel_id=1, source_target_pairs={{0,1},{1,0},{2,3},{3,2},{4,5},{5,4},{6,7},{7,6},{8,9},{9,8},{10,11... | collective-permute-start | bytes 393224 | tf_op jit(solution)/shard_map/ppermute | solution.py:163
  41.4 6.5 %collective-permute-start.11 = (f32[256,128]{1,0:T(8,128)S(1)}, f32[256,128]{1,0:T(8,128)S(1)}, u32[]{:S(2)}, u32[]{:S(2)}) collective-permute-start(f32[256,128]{1,0:T(8,128)S(1)} %add.19), channel_id=1, source_target_pairs={{2,0},{3,1},{0,2},{1,3},{6,4},{7,5},{4,6},{5,7},{10,8},{11,9},{8,1... | collective-permute-start | bytes 393224 | tf_op jit(solution)/shard_map/ppermute | solution.py:169

commit v22 on v18

--- a/solution.py
+++ b/solution.py
@@ -211,8 +211,8 @@
     panel_rows = embeddings.shape[0]
     cycle, team_count = lax.axis_size("blk"), lax.axis_size("rep")
     spread = [tuple(range(team_count))] * cycle
-    if (cycle, team_count) == (4, 4):
-        spread = [(2, 1, 0, 3), (0, 1, 2, 3), (3, 0, 2, 1), (0, 1, 2, 3)]
+    if team_count == 4:
+        spread = [(3, 0, 2, 1)] * (cycle - 1) + [(3, 1, 2, 0)]
     degrees = degrees.reshape(panel_rows // tile_size, tile_size)
 
     panel = fetch(embeddings, lambda shard, team: spread[shard][team], arc_length)

time: 50.7 us -> 48.9 us (0.964)
  starting transfers between devices: 23.6 us -> 20.6 us
  waiting for transfers between devices: 19.4 us -> 20.6 us
    ppermute x6, starting transfers between devices: 14.3 us -> 8.37 us  [fetch(): return lax.ppermute(value, ('blk', 'rep'), pairs)]
    ppermute x4, starting transfers between devices: 3.18 us -> 5.52 us  [from_mate(): lax.ppermute(value, 'rep', [(team, team ^ 1) for team in range(team_count)])]
    ppermute x6, waiting for transfers between devices: 10.1 us -> 11.2 us  [fetch(): return lax.ppermute(value, ('blk', 'rep'), pairs)]
    ppermute x2, starting transfers between devices: 6.12 us -> 6.69 us  [from_column(): return lax.ppermute(value, 'rep', pairs)]
where the time goes in v22:
time: 48.9 us; the launch traced here: 48.6 us
  starting transfers between devices  20.6 us (42%)
  waiting for transfers between devices  20.6 us (42%)
  local copies, waits for them, and re-layouts  3.52 us (7%)
  Pallas kernels  3.01 us (6%)
  between operations  0.72 us (1%)
    ppermute x6, waiting for transfers between devices, fetch(): return lax.ppermute(value, ('blk', 'rep'), pairs)  11.2 us
    ppermute x6, starting transfers between devices, fetch(): return lax.ppermute(value, ('blk', 'rep'), pairs)  8.37 us
    ppermute x2, waiting for transfers between devices, from_column(): return lax.ppermute(value, 'rep', pairs)  7.61 us
    ppermute x2, starting transfers between devices, from_column(): return lax.ppermute(value, 'rep', pairs)  6.69 us
    ppermute x4, starting transfers between devices, from_mate(): lax.ppermute(value, 'rep', [(team, team ^ 1) for team in range(team_count)])  5.52 us
    unnamed x10, local copies, waits for them, and re-layouts  3.44 us
    ppermute x4, waiting for transfers between devices, from_mate(): lax.ppermute(value, 'rep', [(team, team ^ 1) for team in range(team_count)])  1.82 us
    pallas_call x2, Pallas kernels, arc_step(): pl.pallas_call(functools.partial(arc_kernel, team_count=team_count, piece...  1.74 us
  transfers between devices with their start and end apart: 12, of which 8 were waited for; matrix products, arithmetic and copies ran while one was open for 0% of the time, Pallas kernels for 1%

profile of v22, /device:TPU:0, one launch (start us, length us, event | category | flops | bytes accessed | tf_op | source)
XLA Modules:
  0.0 48.6 jit_solution(2652036520342869278)
XLA Ops:
  0.0 2.5 %collective-permute-start.1 = (f32[1024,128]{1,0:T(8,128)}, f32[1024,128]{1,0:T(8,128)S(1)}, u32[]{:S(2)}, u32[]{:S(2)}) collective-permute-start(f32[1024,128]{1,0:T(8,128)} %embeddings_ref.1), channel_id=1, source_target_pairs={{3,0},{0,5},{2,10},{1,15},{7,4},{4,9},{6,14},{5,3},{11,8},{8,13},{... | collective-permute-start | bytes 1572872 | tf_op jit(solution)/shard_map/ppermute | solution.py:153
  2.5 1.1 %collective-permute-start = (s32[8,128]{1,0:T(8,128)}, s32[8,128]{1,0:T(8,128)S(1)}, u32[]{:S(2)}, u32[]{:S(2)}) collective-permute-start(s32[8,128]{1,0:T(8,128)} %bitcast.12), channel_id=1, source_target_pairs={{3,0},{0,5},{2,10},{1,15},{7,4},{4,9},{6,14},{5,3},{11,8},{8,13},{... | collective-permute-start | bytes 12296 | tf_op jit(solution)/shard_map/ppermute | solution.py:153
  4.2 0.6 %copy-done.3 = s32[1,1,1,24]{3,2,1,0:T(1,128)S(1)} copy-done((s32[1,1,1,24]{3,2,1,0:T(1,128)S(1)}, s32[1,1,1,24]{3,2,1,0:T(1,128)}, u32[]{:S(2)}) %copy-start.3) | copy-done | bytes 120
  4.9 0.0 copy-done.4
  4.9 0.1 add_bitcast_fusion
  5.0 0.1 squeeze.19.after_ref.info_ref
  5.0 0.6 %copy-done.2 = s32[1024]{0:T(1024)S(1)} copy-done((s32[1024]{0:T(1024)S(1)}, s32[1024]{0:T(1024)}, u32[]{:S(2)}) %copy-start.2) | copy-done | bytes 4120
  5.7 1.1 %copy-done = bf16[1,1,1,24,128,128]{5,4,3,2,1,0:T(8,128)(2,1)S(1)} copy-done((bf16[1,1,1,24,128,128]{5,4,3,2,1,0:T(8,128)(2,1)S(1)}, bf16[1,1,1,24,128,128]{5,4,3,2,1,0:T(8,128)(2,1)}, u32[]{:S(2)}) %copy-start) | copy-done | bytes 786456
  6.8 1.0 %copy-done.1 = f32[1024,128]{1,0:T(8,128)S(1)} copy-done((f32[1024,128]{1,0:T(8,128)S(1)}, f32[1024,128]{1,0:T(8,128)}, u32[]{:S(2)}) %copy-start.1) | copy-done | bytes 524312
  7.8 0.6 %shard_map.64 = (bf16[1,24,128,128]{3,2,1,0:T(8,128)(2,1)S(1)}, f32[256,128]{1,0:T(8,128)S(1)}, f32[256,128]{1,0:T(8,128)S(1)}) custom-call(s32[8,128]{1,0:T(8,128)S(1)} %bitcast.13, f32[1024,128]{1,0:T(8,128)S(1)} %copy-done.1, bf16[1,24,128,128]{3,2,1,0:T(8,128)(2,1)S(1)} %bitcast.11, s32[49,128]{1,0:T(8,128)S(1)} %squeeze.19.after_ref.info_ref), custom_call_target="tpu_custom_call" | custom-call | flops 131072 | bytes 524288 | tf_op jit(solution)/shard_map/pallas_call | solution.py:56
  8.4 4.2 %collective-permute-done.refs_0_ = s32[8,128]{1,0:T(8,128)S(1)} collective-permute-done((s32[8,128]{1,0:T(8,128)}, s32[8,128]{1,0:T(8,128)S(1)}, u32[]{:S(2)}, u32[]{:S(2)}) %collective-permute-start) | collective-permute-done | bytes 4128 | tf_op jit(solution)/shard_map/ppermute | solution.py:153
  12.7 0.0 collective-permute-done.1.refs_1_
  12.7 1.0 %shard_map.65 = (f32[256,128]{1,0:T(8,128)S(1)}, f32[256,128]{1,0:T(8,128)S(1)}, f32[256,128]{1,0:T(8,128)S(1)}, f32[256,128]{1,0:T(8,128)S(1)}) custom-call(s32[49,128]{1,0:T(8,128)S(1)} %squeeze.19.after_ref.info_ref, bf16[24,128,128]{2,1,0:T(8,128)(2,1)S(1)} %bitcast.9, s32[8,128]{1,0:T(8,128)S(1)} %collective-permute-done.refs_0_, ...), custom_call_target="tpu_custom_call" | custom-call | flops 201326592 | bytes 1048576 | tf_op jit(solution)/shard_map/pallas_call | solution.py:124
  13.6 2.8 %collective-permute-start.3 = (f32[256,128]{1,0:T(8,128)S(1)}, f32[256,128]{1,0:T(8,128)S(1)}, u32[]{:S(2)}, u32[]{:S(2)}) collective-permute-start(f32[256,128]{1,0:T(8,128)S(1)} %get-tuple-element.21), channel_id=1, source_target_pairs={{0,1},{1,0},{2,3},{3,2},{4,5},{5,4},{6,7},{7,6},{8,9},{9,8},{10,11... | collective-permute-start | bytes 393224 | tf_op jit(solution)/shard_map/ppermute | solution.py:163
  16.4 0.1 collective-permute-start.2
  16.5 0.9 %collective-permute-done.3 = f32[256,128]{1,0:T(8,128)S(1)} collective-permute-done((f32[256,128]{1,0:T(8,128)S(1)}, f32[256,128]{1,0:T(8,128)S(1)}, u32[]{:S(2)}, u32[]{:S(2)}) %collective-permute-start.3) | collective-permute-done | bytes 131104 | tf_op jit(solution)/shard_map/ppermute | solution.py:163
  17.4 4.0 %collective-permute-start.4 = (f32[256,128]{1,0:T(8,128)S(1)}, f32[256,128]{1,0:T(8,128)S(1)}, u32[]{:S(2)}, u32[]{:S(2)}) collective-permute-start(f32[256,128]{1,0:T(8,128)S(1)} %add.16), channel_id=1, source_target_pairs={{2,0},{3,1},{0,2},{1,3},{6,4},{7,5},{4,6},{5,7},{10,8},{11,9},{8,1... | collective-permute-start | bytes 393224 | tf_op jit(solution)/shard_map/ppermute | solution.py:169
  21.4 0.0 collective-permute-done.2
  21.4 3.8 %collective-permute-done.4 = f32[256,128]{1,0:T(8,128)S(1)} collective-permute-done((f32[256,128]{1,0:T(8,128)S(1)}, f32[256,128]{1,0:T(8,128)S(1)}, u32[]{:S(2)}, u32[]{:S(2)}) %collective-permute-start.4) | collective-permute-done | bytes 131104 | tf_op jit(solution)/shard_map/ppermute | solution.py:169
  25.3 3.6 %collective-permute-start.8 = (f32[256,128]{1,0:T(8,128)S(1)}, f32[256,128]{1,0:T(8,128)S(1)}, u32[]{:S(2)}, u32[]{:S(2)}) collective-permute-start(f32[256,128]{1,0:T(8,128)S(1)} %get-tuple-element.27), channel_id=1, source_target_pairs={{3,0},{1,5},{2,10},{0,15},{7,4},{5,9},{6,14},{4,3},{11,8},{9,13},{... | collective-permute-start | bytes 393224 | tf_op jit(solution)/shard_map/ppermute | solution.py:153
  28.9 0.5 %collective-permute-start.7 = (f32[256,128]{1,0:T(8,128)S(1)}, f32[256,128]{1,0:T(8,128)S(1)}, u32[]{:S(2)}, u32[]{:S(2)}) collective-permute-start(f32[256,128]{1,0:T(8,128)S(1)} %get-tuple-element.27), channel_id=1, source_target_pairs={{1,0},{3,5},{0,10},{2,15},{5,4},{7,9},{4,14},{6,3},{9,8},{11,13},{... | collective-permute-start | bytes 393224 | tf_op jit(solution)/shard_map/ppermute | solution.py:153
  29.4 0.7 %collective-permute-start.5 = (f32[256,128]{1,0:T(8,128)S(1)}, f32[256,128]{1,0:T(8,128)S(1)}, u32[]{:S(2)}, u32[]{:S(2)}) collective-permute-start(f32[256,128]{1,0:T(8,128)S(1)} %get-tuple-element.27), channel_id=1, source_target_pairs={{0,0},{2,5},{1,10},{3,15},{4,4},{6,9},{5,14},{7,3},{8,8},{10,13},{... | collective-permute-start | bytes 393224 | tf_op jit(solution)/shard_map/ppermute | solution.py:153
  30.1 2.3 %collective-permute-done.8.refs_3_ = f32[256,128]{1,0:T(8,128)S(1)} collective-permute-done((f32[256,128]{1,0:T(8,128)S(1)}, f32[256,128]{1,0:T(8,128)S(1)}, u32[]{:S(2)}, u32[]{:S(2)}) %collective-permute-start.8) | collective-permute-done | bytes 131104 | tf_op jit(solution)/shard_map/ppermute | solution.py:153
  32.4 2.7 %collective-permute-done.7.refs_2_ = f32[256,128]{1,0:T(8,128)S(1)} collective-permute-done((f32[256,128]{1,0:T(8,128)S(1)}, f32[256,128]{1,0:T(8,128)S(1)}, u32[]{:S(2)}, u32[]{:S(2)}) %collective-permute-start.7) | collective-permute-done | bytes 131104 | tf_op jit(solution)/shard_map/ppermute | solution.py:153
  35.1 2.0 %collective-permute-done.6.refs_1_ = f32[256,128]{1,0:T(8,128)S(1)} collective-permute-done((f32[256,128]{1,0:T(8,128)S(1)}, f32[256,128]{1,0:T(8,128)S(1)}, u32[]{:S(2)}, u32[]{:S(2)}) %collective-permute-start.6) | collective-permute-done | bytes 131104 | tf_op jit(solution)/shard_map/ppermute | solution.py:153
  37.1 0.8 %shard_map.66 = (f32[256,128]{1,0:T(8,128)S(1)}, f32[256,128]{1,0:T(8,128)S(1)}, f32[256,128]{1,0:T(8,128)S(1)}, f32[256,128]{1,0:T(8,128)S(1)}) custom-call(s32[49,128]{1,0:T(8,128)S(1)} %squeeze.19.after_ref.info_ref, bf16[24,128,128]{2,1,0:T(8,128)(2,1)S(1)} %bitcast.10, f32[256,128]{1,0:T(8,128)S(1)} %collective-permute-done.5.refs_0_, ...), custom_call_target="tpu_custom_call" | custom-call | flops 201326592 | bytes 1048576 | tf_op jit(solution)/shard_map/pallas_call | solution.py:124
  37.8 2.6 %collective-permute-start.10 = (f32[256,128]{1,0:T(8,128)S(1)}, f32[256,128]{1,0:T(8,128)S(1)}, u32[]{:S(2)}, u32[]{:S(2)}) collective-permute-start(f32[256,128]{1,0:T(8,128)S(1)} %get-tuple-element.26), channel_id=1, source_target_pairs={{0,1},{1,0},{2,3},{3,2},{4,5},{5,4},{6,7},{7,6},{8,9},{9,8},{10,11... | collective-permute-start | bytes 393224 | tf_op jit(solution)/shard_map/ppermute | solution.py:163
  40.4 0.1 collective-permute-start.9
  40.5 0.9 %collective-permute-done.10 = f32[256,128]{1,0:T(8,128)S(1)} collective-permute-done((f32[256,128]{1,0:T(8,128)S(1)}, f32[256,128]{1,0:T(8,128)S(1)}, u32[]{:S(2)}, u32[]{:S(2)}) %collective-permute-start.10) | collective-permute-done | bytes 131104 | tf_op jit(solution)/shard_map/ppermute | solution.py:163
  41.4 2.7 %collective-permute-start.11 = (f32[256,128]{1,0:T(8,128)S(1)}, f32[256,128]{1,0:T(8,128)S(1)}, u32[]{:S(2)}, u32[]{:S(2)}) collective-permute-start(f32[256,128]{1,0:T(8,128)S(1)} %add.19), channel_id=1, source_target_pairs={{2,0},{3,1},{0,2},{1,3},{6,4},{7,5},{4,6},{5,7},{10,8},{11,9},{8,1... | collective-permute-start | bytes 393224 | tf_op jit(solution)/shard_map/ppermute | solution.py:169
  44.1 3.8 %collective-permute-done.11.refs_2_ = f32[256,128]{1,0:T(8,128)S(1)} collective-permute-done((f32[256,128]{1,0:T(8,128)S(1)}, f32[256,128]{1,0:T(8,128)S(1)}, u32[]{:S(2)}, u32[]{:S(2)}) %collective-permute-start.11) | collective-permute-done | bytes 131104 | tf_op jit(solution)/shard_map/ppermute | solution.py:169
  47.9 0.7 %shard_map.67 = f32[256,128]{1,0:T(8,128)} custom-call(f32[256,128]{1,0:T(8,128)S(1)} %get-tuple-element.28.base_ref, f32[256,128]{1,0:T(8,128)S(1)} %get-tuple-element.22.norm_ref, f32[256,128]{1,0:T(8,128)S(1)} %get-tuple-element.23.refs_0_, f32[256,128]{1,0:T(8,128)S(1)} %collective-permute-done.9.refs_1_, f32[256,128]{1,0:T(8,128)S(1)} %collective-permute-done.11.refs_2_), custom_call_target="tpu_custom_call" | custom-call | tf_op jit(solution)/shard_map/pallas_call | solution.py:199
  (11 shorter events, 0.1 us)
Async XLA Ops:
  0.0 12.7 %collective-permute-start.1 = (f32[1024,128]{1,0:T(8,128)}, f32[1024,128]{1,0:T(8,128)S(1)}, u32[]{:S(2)}, u32[]{:S(2)}) collective-permute-start(f32[1024,128]{1,0:T(8,128)} %embeddings_ref.1), channel_id=1, source_target_pairs={{3,0},{0,5},{2,10},{1,15},{7,4},{4,9},{6,14},{5,3},{11,8},{8,13},{... | collective-permute-start | bytes 1572872 | tf_op jit(solution)/shard_map/ppermute | solution.py:153
  2.5 10.2 %collective-permute-start = (s32[8,128]{1,0:T(8,128)}, s32[8,128]{1,0:T(8,128)S(1)}, u32[]{:S(2)}, u32[]{:S(2)}) collective-permute-start(s32[8,128]{1,0:T(8,128)} %bitcast.12), channel_id=1, source_target_pairs={{3,0},{0,5},{2,10},{1,15},{7,4},{4,9},{6,14},{5,3},{11,8},{8,13},{... | collective-permute-start | bytes 12296 | tf_op jit(solution)/shard_map/ppermute | solution.py:153
  4.2 0.7 %copy-start.3 = (s32[1,1,1,24]{3,2,1,0:T(1,128)S(1)}, s32[1,1,1,24]{3,2,1,0:T(1,128)}, u32[]{:S(2)}) copy-start(s32[1,1,1,24]{3,2,1,0:T(1,128)} %param.10) | copy-start | bytes 292
  4.2 0.7 %copy-start.4 = (s32[1,1,1,24]{3,2,1,0:T(1,128)S(1)}, s32[1,1,1,24]{3,2,1,0:T(1,128)}, u32[]{:S(2)}) copy-start(s32[1,1,1,24]{3,2,1,0:T(1,128)} %param.9) | copy-start | bytes 292
  5.0 0.7 %copy-start.2 = (s32[1024]{0:T(1024)S(1)}, s32[1024]{0:T(1024)}, u32[]{:S(2)}) copy-start(s32[1024]{0:T(1024)} %param.7) | copy-start | bytes 12292
  5.6 1.1 %copy-start = (bf16[1,1,1,24,128,128]{5,4,3,2,1,0:T(8,128)(2,1)S(1)}, bf16[1,1,1,24,128,128]{5,4,3,2,1,0:T(8,128)(2,1)}, u32[]{:S(2)}) copy-start(bf16[1,1,1,24,128,128]{5,4,3,2,1,0:T(8,128)(2,1)} %param.8) | copy-start | bytes 2359300
  6.8 1.0 %copy-start.1 = (f32[1024,128]{1,0:T(8,128)S(1)}, f32[1024,128]{1,0:T(8,128)}, u32[]{:S(2)}) copy-start(f32[1024,128]{1,0:T(8,128)} %embeddings_ref.1) | copy-start | bytes 1572868
  13.6 3.8 %collective-permute-start.3 = (f32[256,128]{1,0:T(8,128)S(1)}, f32[256,128]{1,0:T(8,128)S(1)}, u32[]{:S(2)}, u32[]{:S(2)}) collective-permute-start(f32[256,128]{1,0:T(8,128)S(1)} %get-tuple-element.21), channel_id=1, source_target_pairs={{0,1},{1,0},{2,3},{3,2},{4,5},{5,4},{6,7},{7,6},{8,9},{9,8},{10,11... | collective-permute-start | bytes 393224 | tf_op jit(solution)/shard_map/ppermute | solution.py:163
  16.4 5.0 %collective-permute-start.2 = (f32[256,128]{1,0:T(8,128)S(1)}, f32[256,128]{1,0:T(8,128)S(1)}, u32[]{:S(2)}, u32[]{:S(2)}) collective-permute-start(f32[256,128]{1,0:T(8,128)S(1)} %get-tuple-element.19), channel_id=1, source_target_pairs={{0,1},{1,0},{2,3},{3,2},{4,5},{5,4},{6,7},{7,6},{8,9},{9,8},{10,11... | collective-permute-start | bytes 393224 | tf_op jit(solution)/shard_map/ppermute | solution.py:163
  17.4 7.8 %collective-permute-start.4 = (f32[256,128]{1,0:T(8,128)S(1)}, f32[256,128]{1,0:T(8,128)S(1)}, u32[]{:S(2)}, u32[]{:S(2)}) collective-permute-start(f32[256,128]{1,0:T(8,128)S(1)} %add.16), channel_id=1, source_target_pairs={{2,0},{3,1},{0,2},{1,3},{6,4},{7,5},{4,6},{5,7},{10,8},{11,9},{8,1... | collective-permute-start | bytes 393224 | tf_op jit(solution)/shard_map/ppermute | solution.py:169
  25.3 7.1 %collective-permute-start.8 = (f32[256,128]{1,0:T(8,128)S(1)}, f32[256,128]{1,0:T(8,128)S(1)}, u32[]{:S(2)}, u32[]{:S(2)}) collective-permute-start(f32[256,128]{1,0:T(8,128)S(1)} %get-tuple-element.27), channel_id=1, source_target_pairs={{3,0},{1,5},{2,10},{0,15},{7,4},{5,9},{6,14},{4,3},{11,8},{9,13},{... | collective-permute-start | bytes 393224 | tf_op jit(solution)/shard_map/ppermute | solution.py:153
  28.9 6.2 %collective-permute-start.7 = (f32[256,128]{1,0:T(8,128)S(1)}, f32[256,128]{1,0:T(8,128)S(1)}, u32[]{:S(2)}, u32[]{:S(2)}) collective-permute-start(f32[256,128]{1,0:T(8,128)S(1)} %get-tuple-element.27), channel_id=1, source_target_pairs={{1,0},{3,5},{0,10},{2,15},{5,4},{7,9},{4,14},{6,3},{9,8},{11,13},{... | collective-permute-start | bytes 393224 | tf_op jit(solution)/shard_map/ppermute | solution.py:153
  29.4 7.6 %collective-permute-start.6 = (f32[256,128]{1,0:T(8,128)S(1)}, f32[256,128]{1,0:T(8,128)S(1)}, u32[]{:S(2)}, u32[]{:S(2)}) collective-permute-start(f32[256,128]{1,0:T(8,128)S(1)} %get-tuple-element.27), channel_id=1, source_target_pairs={{2,0},{0,5},{3,10},{1,15},{6,4},{4,9},{7,14},{5,3},{10,8},{8,13},{... | collective-permute-start | bytes 393224 | tf_op jit(solution)/shard_map/ppermute | solution.py:153
  29.4 7.6 %collective-permute-start.5 = (f32[256,128]{1,0:T(8,128)S(1)}, f32[256,128]{1,0:T(8,128)S(1)}, u32[]{:S(2)}, u32[]{:S(2)}) collective-permute-start(f32[256,128]{1,0:T(8,128)S(1)} %get-tuple-element.27), channel_id=1, source_target_pairs={{0,0},{2,5},{1,10},{3,15},{4,4},{6,9},{5,14},{7,3},{8,8},{10,13},{... | collective-permute-start | bytes 393224 | tf_op jit(solution)/shard_map/ppermute | solution.py:153
  37.8 3.6 %collective-permute-start.10 = (f32[256,128]{1,0:T(8,128)S(1)}, f32[256,128]{1,0:T(8,128)S(1)}, u32[]{:S(2)}, u32[]{:S(2)}) collective-permute-start(f32[256,128]{1,0:T(8,128)S(1)} %get-tuple-element.26), channel_id=1, source_target_pairs={{0,1},{1,0},{2,3},{3,2},{4,5},{5,4},{6,7},{7,6},{8,9},{9,8},{10,11... | collective-permute-start | bytes 393224 | tf_op jit(solution)/shard_map/ppermute | solution.py:163
  40.4 3.7 %collective-permute-start.9 = (f32[256,128]{1,0:T(8,128)S(1)}, f32[256,128]{1,0:T(8,128)S(1)}, u32[]{:S(2)}, u32[]{:S(2)}) collective-permute-start(f32[256,128]{1,0:T(8,128)S(1)} %get-tuple-element.24), channel_id=1, source_target_pairs={{0,1},{1,0},{2,3},{3,2},{4,5},{5,4},{6,7},{7,6},{8,9},{9,8},{10,11... | collective-permute-start | bytes 393224 | tf_op jit(solution)/shard_map/ppermute | solution.py:163
  41.4 6.5 %collective-permute-start.11 = (f32[256,128]{1,0:T(8,128)S(1)}, f32[256,128]{1,0:T(8,128)S(1)}, u32[]{:S(2)}, u32[]{:S(2)}) collective-permute-start(f32[256,128]{1,0:T(8,128)S(1)} %add.19), channel_id=1, source_target_pairs={{2,0},{3,1},{0,2},{1,3},{6,4},{7,5},{4,6},{5,7},{10,8},{11,9},{8,1... | collective-permute-start | bytes 393224 | tf_op jit(solution)/shard_map/ppermute | solution.py:169

commit v23 on v22

--- a/solution.py
+++ b/solution.py
@@ -212,7 +212,7 @@
     cycle, team_count = lax.axis_size("blk"), lax.axis_size("rep")
     spread = [tuple(range(team_count))] * cycle
     if team_count == 4:
-        spread = [(3, 0, 2, 1)] * (cycle - 1) + [(3, 1, 2, 0)]
+        spread = [(1, 2, 0, 3)] + [(3, 0, 2, 1)] * (cycle - 2) + [(1, 3, 0, 2)]
     degrees = degrees.reshape(panel_rows // tile_size, tile_size)
 
     panel = fetch(embeddings, lambda shard, team: spread[shard][team], arc_length)

time: 48.9 us -> 48.9 us (level)
  starting transfers between devices: 20.6 us -> 22.8 us
  waiting for transfers between devices: 20.6 us -> 18.5 us
    ppermute x4, starting transfers between devices: 5.52 us -> 7.96 us  [from_mate(): lax.ppermute(value, 'rep', [(team, team ^ 1) for team in range(team_count)])]
    ppermute x6, waiting for transfers between devices: 11.2 us -> 9.05 us  [fetch(): return lax.ppermute(value, ('blk', 'rep'), pairs)]
    ppermute x2, starting transfers between devices: 6.69 us -> 4.71 us  [from_column(): return lax.ppermute(value, 'rep', pairs)]
    ppermute x6, starting transfers between devices: 8.37 us -> 10.1 us  [fetch(): return lax.ppermute(value, ('blk', 'rep'), pairs)]
where the time goes in v23:
time: 48.9 us; the launch traced here: 48.7 us
  starting transfers between devices  22.8 us (47%)
  waiting for transfers between devices  18.5 us (38%)
  local copies, waits for them, and re-layouts  3.52 us (7%)
  Pallas kernels  3.01 us (6%)
  between operations  0.72 us (1%)
    ppermute x6, starting transfers between devices, fetch(): return lax.ppermute(value, ('blk', 'rep'), pairs)  10.1 us
    ppermute x6, waiting for transfers between devices, fetch(): return lax.ppermute(value, ('blk', 'rep'), pairs)  9.05 us
    ppermute x4, starting transfers between devices, from_mate(): lax.ppermute(value, 'rep', [(team, team ^ 1) for team in range(team_count)])  7.96 us
    ppermute x2, waiting for transfers between devices, from_column(): return lax.ppermute(value, 'rep', pairs)  7.63 us
    ppermute x2, starting transfers between devices, from_column(): return lax.ppermute(value, 'rep', pairs)  4.71 us
    unnamed x10, local copies, waits for them, and re-layouts  3.44 us
    ppermute x4, waiting for transfers between devices, from_mate(): lax.ppermute(value, 'rep', [(team, team ^ 1) for team in range(team_count)])  1.82 us
    pallas_call x2, Pallas kernels, arc_step(): pl.pallas_call(functools.partial(arc_kernel, team_count=team_count, piece...  1.74 us
  transfers between devices with their start and end apart: 12, of which 8 were waited for; matrix products, arithmetic and copies ran while one was open for 0% of the time, Pallas kernels for 1%

profile of v23, /device:TPU:0, one launch (start us, length us, event | category | flops | bytes accessed | tf_op | source)
XLA Modules:
  0.0 48.7 jit_solution(16069971860194065240)
XLA Ops:
  0.0 5.0 %collective-permute-start.1 = (f32[1024,128]{1,0:T(8,128)}, f32[1024,128]{1,0:T(8,128)S(1)}, u32[]{:S(2)}, u32[]{:S(2)}) collective-permute-start(f32[1024,128]{1,0:T(8,128)} %embeddings_ref.1), channel_id=1, source_target_pairs={{1,0},{2,5},{0,10},{3,15},{7,4},{4,9},{6,14},{5,3},{11,8},{8,13},{... | collective-permute-start | bytes 1572872 | tf_op jit(solution)/shard_map/ppermute | solution.py:153
  5.0 0.3 collective-permute-start
  6.0 0.6 %copy-done.3 = s32[1,1,1,24]{3,2,1,0:T(1,128)S(1)} copy-done((s32[1,1,1,24]{3,2,1,0:T(1,128)S(1)}, s32[1,1,1,24]{3,2,1,0:T(1,128)}, u32[]{:S(2)}) %copy-start.3) | copy-done | bytes 120
  6.6 0.0 copy-done.4
  6.6 0.1 add_bitcast_fusion
  6.7 0.1 squeeze.19.after_ref.info_ref
  6.8 0.6 %copy-done.2 = s32[1024]{0:T(1024)S(1)} copy-done((s32[1024]{0:T(1024)S(1)}, s32[1024]{0:T(1024)}, u32[]{:S(2)}) %copy-start.2) | copy-done | bytes 4120
  7.4 1.1 %copy-done = bf16[1,1,1,24,128,128]{5,4,3,2,1,0:T(8,128)(2,1)S(1)} copy-done((bf16[1,1,1,24,128,128]{5,4,3,2,1,0:T(8,128)(2,1)S(1)}, bf16[1,1,1,24,128,128]{5,4,3,2,1,0:T(8,128)(2,1)}, u32[]{:S(2)}) %copy-start) | copy-done | bytes 786456
  8.5 1.0 %copy-done.1 = f32[1024,128]{1,0:T(8,128)S(1)} copy-done((f32[1024,128]{1,0:T(8,128)S(1)}, f32[1024,128]{1,0:T(8,128)}, u32[]{:S(2)}) %copy-start.1) | copy-done | bytes 524312
  9.6 0.6 %shard_map.64 = (bf16[1,24,128,128]{3,2,1,0:T(8,128)(2,1)S(1)}, f32[256,128]{1,0:T(8,128)S(1)}, f32[256,128]{1,0:T(8,128)S(1)}) custom-call(s32[8,128]{1,0:T(8,128)S(1)} %bitcast.13, f32[1024,128]{1,0:T(8,128)S(1)} %copy-done.1, bf16[1,24,128,128]{3,2,1,0:T(8,128)(2,1)S(1)} %bitcast.11, s32[49,128]{1,0:T(8,128)S(1)} %squeeze.19.after_ref.info_ref), custom_call_target="tpu_custom_call" | custom-call | flops 131072 | bytes 524288 | tf_op jit(solution)/shard_map/pallas_call | solution.py:56
  10.2 1.9 %collective-permute-done.refs_0_ = s32[8,128]{1,0:T(8,128)S(1)} collective-permute-done((s32[8,128]{1,0:T(8,128)}, s32[8,128]{1,0:T(8,128)S(1)}, u32[]{:S(2)}, u32[]{:S(2)}) %collective-permute-start) | collective-permute-done | bytes 4128 | tf_op jit(solution)/shard_map/ppermute | solution.py:153
  12.0 1.0 %shard_map.65 = (f32[256,128]{1,0:T(8,128)S(1)}, f32[256,128]{1,0:T(8,128)S(1)}, f32[256,128]{1,0:T(8,128)S(1)}, f32[256,128]{1,0:T(8,128)S(1)}) custom-call(s32[49,128]{1,0:T(8,128)S(1)} %squeeze.19.after_ref.info_ref, bf16[24,128,128]{2,1,0:T(8,128)(2,1)S(1)} %bitcast.9, s32[8,128]{1,0:T(8,128)S(1)} %collective-permute-done.refs_0_, ...), custom_call_target="tpu_custom_call" | custom-call | flops 201326592 | bytes 1048576 | tf_op jit(solution)/shard_map/pallas_call | solution.py:124
  13.0 5.2 %collective-permute-start.3 = (f32[256,128]{1,0:T(8,128)S(1)}, f32[256,128]{1,0:T(8,128)S(1)}, u32[]{:S(2)}, u32[]{:S(2)}) collective-permute-start(f32[256,128]{1,0:T(8,128)S(1)} %get-tuple-element.21), channel_id=1, source_target_pairs={{0,1},{1,0},{2,3},{3,2},{4,5},{5,4},{6,7},{7,6},{8,9},{9,8},{10,11... | collective-permute-start | bytes 393224 | tf_op jit(solution)/shard_map/ppermute | solution.py:163
  18.2 0.1 collective-permute-start.2
  18.3 0.9 %collective-permute-done.3 = f32[256,128]{1,0:T(8,128)S(1)} collective-permute-done((f32[256,128]{1,0:T(8,128)S(1)}, f32[256,128]{1,0:T(8,128)S(1)}, u32[]{:S(2)}, u32[]{:S(2)}) %collective-permute-start.3) | collective-permute-done | bytes 131104 | tf_op jit(solution)/shard_map/ppermute | solution.py:163
  19.2 2.0 %collective-permute-start.4 = (f32[256,128]{1,0:T(8,128)S(1)}, f32[256,128]{1,0:T(8,128)S(1)}, u32[]{:S(2)}, u32[]{:S(2)}) collective-permute-start(f32[256,128]{1,0:T(8,128)S(1)} %add.16), channel_id=1, source_target_pairs={{2,0},{3,1},{0,2},{1,3},{6,4},{7,5},{4,6},{5,7},{10,8},{11,9},{8,1... | collective-permute-start | bytes 393224 | tf_op jit(solution)/shard_map/ppermute | solution.py:169
  21.2 0.0 collective-permute-done.2
  21.2 3.8 %collective-permute-done.4 = f32[256,128]{1,0:T(8,128)S(1)} collective-permute-done((f32[256,128]{1,0:T(8,128)S(1)}, f32[256,128]{1,0:T(8,128)S(1)}, u32[]{:S(2)}, u32[]{:S(2)}) %collective-permute-start.4) | collective-permute-done | bytes 131104 | tf_op jit(solution)/shard_map/ppermute | solution.py:169
  25.1 3.8 %collective-permute-start.8 = (f32[256,128]{1,0:T(8,128)S(1)}, f32[256,128]{1,0:T(8,128)S(1)}, u32[]{:S(2)}, u32[]{:S(2)}) collective-permute-start(f32[256,128]{1,0:T(8,128)S(1)} %get-tuple-element.27), channel_id=1, source_target_pairs={{3,0},{1,5},{2,10},{0,15},{7,4},{5,9},{6,14},{4,3},{11,8},{9,13},{... | collective-permute-start | bytes 393224 | tf_op jit(solution)/shard_map/ppermute | solution.py:153
  28.9 0.3 collective-permute-start.7
  29.3 0.0 collective-permute-start.6
  29.3 0.7 %collective-permute-start.5 = (f32[256,128]{1,0:T(8,128)S(1)}, f32[256,128]{1,0:T(8,128)S(1)}, u32[]{:S(2)}, u32[]{:S(2)}) collective-permute-start(f32[256,128]{1,0:T(8,128)S(1)} %get-tuple-element.27), channel_id=1, source_target_pairs={{0,0},{2,5},{1,10},{3,15},{4,4},{6,9},{5,14},{7,3},{8,8},{10,13},{... | collective-permute-start | bytes 393224 | tf_op jit(solution)/shard_map/ppermute | solution.py:153
  29.9 2.5 %collective-permute-done.8.refs_3_ = f32[256,128]{1,0:T(8,128)S(1)} collective-permute-done((f32[256,128]{1,0:T(8,128)S(1)}, f32[256,128]{1,0:T(8,128)S(1)}, u32[]{:S(2)}, u32[]{:S(2)}) %collective-permute-start.8) | collective-permute-done | bytes 131104 | tf_op jit(solution)/shard_map/ppermute | solution.py:153
  32.4 2.7 %collective-permute-done.7.refs_2_ = f32[256,128]{1,0:T(8,128)S(1)} collective-permute-done((f32[256,128]{1,0:T(8,128)S(1)}, f32[256,128]{1,0:T(8,128)S(1)}, u32[]{:S(2)}, u32[]{:S(2)}) %collective-permute-start.7) | collective-permute-done | bytes 131104 | tf_op jit(solution)/shard_map/ppermute | solution.py:153
  35.2 1.9 %collective-permute-done.6.refs_1_ = f32[256,128]{1,0:T(8,128)S(1)} collective-permute-done((f32[256,128]{1,0:T(8,128)S(1)}, f32[256,128]{1,0:T(8,128)S(1)}, u32[]{:S(2)}, u32[]{:S(2)}) %collective-permute-start.6) | collective-permute-done | bytes 131104 | tf_op jit(solution)/shard_map/ppermute | solution.py:153
  37.1 0.8 %shard_map.66 = (f32[256,128]{1,0:T(8,128)S(1)}, f32[256,128]{1,0:T(8,128)S(1)}, f32[256,128]{1,0:T(8,128)S(1)}, f32[256,128]{1,0:T(8,128)S(1)}) custom-call(s32[49,128]{1,0:T(8,128)S(1)} %squeeze.19.after_ref.info_ref, bf16[24,128,128]{2,1,0:T(8,128)(2,1)S(1)} %bitcast.10, f32[256,128]{1,0:T(8,128)S(1)} %collective-permute-done.5.refs_0_, ...), custom_call_target="tpu_custom_call" | custom-call | flops 201326592 | bytes 1048576 | tf_op jit(solution)/shard_map/pallas_call | solution.py:124
  37.9 2.6 %collective-permute-start.10 = (f32[256,128]{1,0:T(8,128)S(1)}, f32[256,128]{1,0:T(8,128)S(1)}, u32[]{:S(2)}, u32[]{:S(2)}) collective-permute-start(f32[256,128]{1,0:T(8,128)S(1)} %get-tuple-element.26), channel_id=1, source_target_pairs={{0,1},{1,0},{2,3},{3,2},{4,5},{5,4},{6,7},{7,6},{8,9},{9,8},{10,11... | collective-permute-start | bytes 393224 | tf_op jit(solution)/shard_map/ppermute | solution.py:163
  40.5 0.1 collective-permute-start.9
  40.5 0.9 %collective-permute-done.10 = f32[256,128]{1,0:T(8,128)S(1)} collective-permute-done((f32[256,128]{1,0:T(8,128)S(1)}, f32[256,128]{1,0:T(8,128)S(1)}, u32[]{:S(2)}, u32[]{:S(2)}) %collective-permute-start.10) | collective-permute-done | bytes 131104 | tf_op jit(solution)/shard_map/ppermute | solution.py:163
  41.5 2.7 %collective-permute-start.11 = (f32[256,128]{1,0:T(8,128)S(1)}, f32[256,128]{1,0:T(8,128)S(1)}, u32[]{:S(2)}, u32[]{:S(2)}) collective-permute-start(f32[256,128]{1,0:T(8,128)S(1)} %add.19), channel_id=1, source_target_pairs={{2,0},{3,1},{0,2},{1,3},{6,4},{7,5},{4,6},{5,7},{10,8},{11,9},{8,1... | collective-permute-start | bytes 393224 | tf_op jit(solution)/shard_map/ppermute | solution.py:169
  44.2 3.8 %collective-permute-done.11.refs_2_ = f32[256,128]{1,0:T(8,128)S(1)} collective-permute-done((f32[256,128]{1,0:T(8,128)S(1)}, f32[256,128]{1,0:T(8,128)S(1)}, u32[]{:S(2)}, u32[]{:S(2)}) %collective-permute-start.11) | collective-permute-done | bytes 131104 | tf_op jit(solution)/shard_map/ppermute | solution.py:169
  48.0 0.7 %shard_map.67 = f32[256,128]{1,0:T(8,128)} custom-call(f32[256,128]{1,0:T(8,128)S(1)} %get-tuple-element.28.base_ref, f32[256,128]{1,0:T(8,128)S(1)} %get-tuple-element.22.norm_ref, f32[256,128]{1,0:T(8,128)S(1)} %get-tuple-element.23.refs_0_, f32[256,128]{1,0:T(8,128)S(1)} %collective-permute-done.9.refs_1_, f32[256,128]{1,0:T(8,128)S(1)} %collective-permute-done.11.refs_2_), custom_call_target="tpu_custom_call" | custom-call | tf_op jit(solution)/shard_map/pallas_call | solution.py:199
  (11 shorter events, 0.1 us)
Async XLA Ops:
  0.0 12.0 %collective-permute-start.1 = (f32[1024,128]{1,0:T(8,128)}, f32[1024,128]{1,0:T(8,128)S(1)}, u32[]{:S(2)}, u32[]{:S(2)}) collective-permute-start(f32[1024,128]{1,0:T(8,128)} %embeddings_ref.1), channel_id=1, source_target_pairs={{1,0},{2,5},{0,10},{3,15},{7,4},{4,9},{6,14},{5,3},{11,8},{8,13},{... | collective-permute-start | bytes 1572872 | tf_op jit(solution)/shard_map/ppermute | solution.py:153
  5.0 7.1 %collective-permute-start = (s32[8,128]{1,0:T(8,128)}, s32[8,128]{1,0:T(8,128)S(1)}, u32[]{:S(2)}, u32[]{:S(2)}) collective-permute-start(s32[8,128]{1,0:T(8,128)} %bitcast.12), channel_id=1, source_target_pairs={{1,0},{2,5},{0,10},{3,15},{7,4},{4,9},{6,14},{5,3},{11,8},{8,13},{... | collective-permute-start | bytes 12296 | tf_op jit(solution)/shard_map/ppermute | solution.py:153
  6.0 0.7 %copy-start.3 = (s32[1,1,1,24]{3,2,1,0:T(1,128)S(1)}, s32[1,1,1,24]{3,2,1,0:T(1,128)}, u32[]{:S(2)}) copy-start(s32[1,1,1,24]{3,2,1,0:T(1,128)} %param.10) | copy-start | bytes 292
  6.0 0.7 %copy-start.4 = (s32[1,1,1,24]{3,2,1,0:T(1,128)S(1)}, s32[1,1,1,24]{3,2,1,0:T(1,128)}, u32[]{:S(2)}) copy-start(s32[1,1,1,24]{3,2,1,0:T(1,128)} %param.9) | copy-start | bytes 292
  6.7 0.7 %copy-start.2 = (s32[1024]{0:T(1024)S(1)}, s32[1024]{0:T(1024)}, u32[]{:S(2)}) copy-start(s32[1024]{0:T(1024)} %param.7) | copy-start | bytes 12292
  7.4 1.1 %copy-start = (bf16[1,1,1,24,128,128]{5,4,3,2,1,0:T(8,128)(2,1)S(1)}, bf16[1,1,1,24,128,128]{5,4,3,2,1,0:T(8,128)(2,1)}, u32[]{:S(2)}) copy-start(bf16[1,1,1,24,128,128]{5,4,3,2,1,0:T(8,128)(2,1)} %param.8) | copy-start | bytes 2359300
  8.5 1.0 %copy-start.1 = (f32[1024,128]{1,0:T(8,128)S(1)}, f32[1024,128]{1,0:T(8,128)}, u32[]{:S(2)}) copy-start(f32[1024,128]{1,0:T(8,128)} %embeddings_ref.1) | copy-start | bytes 1572868
  13.0 6.2 %collective-permute-start.3 = (f32[256,128]{1,0:T(8,128)S(1)}, f32[256,128]{1,0:T(8,128)S(1)}, u32[]{:S(2)}, u32[]{:S(2)}) collective-permute-start(f32[256,128]{1,0:T(8,128)S(1)} %get-tuple-element.21), channel_id=1, source_target_pairs={{0,1},{1,0},{2,3},{3,2},{4,5},{5,4},{6,7},{7,6},{8,9},{9,8},{10,11... | collective-permute-start | bytes 393224 | tf_op jit(solution)/shard_map/ppermute | solution.py:163
  18.2 3.0 %collective-permute-start.2 = (f32[256,128]{1,0:T(8,128)S(1)}, f32[256,128]{1,0:T(8,128)S(1)}, u32[]{:S(2)}, u32[]{:S(2)}) collective-permute-start(f32[256,128]{1,0:T(8,128)S(1)} %get-tuple-element.19), channel_id=1, source_target_pairs={{0,1},{1,0},{2,3},{3,2},{4,5},{5,4},{6,7},{7,6},{8,9},{9,8},{10,11... | collective-permute-start | bytes 393224 | tf_op jit(solution)/shard_map/ppermute | solution.py:163
  19.2 5.8 %collective-permute-start.4 = (f32[256,128]{1,0:T(8,128)S(1)}, f32[256,128]{1,0:T(8,128)S(1)}, u32[]{:S(2)}, u32[]{:S(2)}) collective-permute-start(f32[256,128]{1,0:T(8,128)S(1)} %add.16), channel_id=1, source_target_pairs={{2,0},{3,1},{0,2},{1,3},{6,4},{7,5},{4,6},{5,7},{10,8},{11,9},{8,1... | collective-permute-start | bytes 393224 | tf_op jit(solution)/shard_map/ppermute | solution.py:169
  25.1 7.3 %collective-permute-start.8 = (f32[256,128]{1,0:T(8,128)S(1)}, f32[256,128]{1,0:T(8,128)S(1)}, u32[]{:S(2)}, u32[]{:S(2)}) collective-permute-start(f32[256,128]{1,0:T(8,128)S(1)} %get-tuple-element.27), channel_id=1, source_target_pairs={{3,0},{1,5},{2,10},{0,15},{7,4},{5,9},{6,14},{4,3},{11,8},{9,13},{... | collective-permute-start | bytes 393224 | tf_op jit(solution)/shard_map/ppermute | solution.py:153
  28.9 6.2 %collective-permute-start.7 = (f32[256,128]{1,0:T(8,128)S(1)}, f32[256,128]{1,0:T(8,128)S(1)}, u32[]{:S(2)}, u32[]{:S(2)}) collective-permute-start(f32[256,128]{1,0:T(8,128)S(1)} %get-tuple-element.27), channel_id=1, source_target_pairs={{1,0},{3,5},{0,10},{2,15},{5,4},{7,9},{4,14},{6,3},{9,8},{11,13},{... | collective-permute-start | bytes 393224 | tf_op jit(solution)/shard_map/ppermute | solution.py:153
  29.3 7.8 %collective-permute-start.6 = (f32[256,128]{1,0:T(8,128)S(1)}, f32[256,128]{1,0:T(8,128)S(1)}, u32[]{:S(2)}, u32[]{:S(2)}) collective-permute-start(f32[256,128]{1,0:T(8,128)S(1)} %get-tuple-element.27), channel_id=1, source_target_pairs={{2,0},{0,5},{3,10},{1,15},{6,4},{4,9},{7,14},{5,3},{10,8},{8,13},{... | collective-permute-start | bytes 393224 | tf_op jit(solution)/shard_map/ppermute | solution.py:153
  29.3 7.8 %collective-permute-start.5 = (f32[256,128]{1,0:T(8,128)S(1)}, f32[256,128]{1,0:T(8,128)S(1)}, u32[]{:S(2)}, u32[]{:S(2)}) collective-permute-start(f32[256,128]{1,0:T(8,128)S(1)} %get-tuple-element.27), channel_id=1, source_target_pairs={{0,0},{2,5},{1,10},{3,15},{4,4},{6,9},{5,14},{7,3},{8,8},{10,13},{... | collective-permute-start | bytes 393224 | tf_op jit(solution)/shard_map/ppermute | solution.py:153
  37.9 3.6 %collective-permute-start.10 = (f32[256,128]{1,0:T(8,128)S(1)}, f32[256,128]{1,0:T(8,128)S(1)}, u32[]{:S(2)}, u32[]{:S(2)}) collective-permute-start(f32[256,128]{1,0:T(8,128)S(1)} %get-tuple-element.26), channel_id=1, source_target_pairs={{0,1},{1,0},{2,3},{3,2},{4,5},{5,4},{6,7},{7,6},{8,9},{9,8},{10,11... | collective-permute-start | bytes 393224 | tf_op jit(solution)/shard_map/ppermute | solution.py:163
  40.5 3.7 %collective-permute-start.9 = (f32[256,128]{1,0:T(8,128)S(1)}, f32[256,128]{1,0:T(8,128)S(1)}, u32[]{:S(2)}, u32[]{:S(2)}) collective-permute-start(f32[256,128]{1,0:T(8,128)S(1)} %get-tuple-element.24), channel_id=1, source_target_pairs={{0,1},{1,0},{2,3},{3,2},{4,5},{5,4},{6,7},{7,6},{8,9},{9,8},{10,11... | collective-permute-start | bytes 393224 | tf_op jit(solution)/shard_map/ppermute | solution.py:163
  41.5 6.5 %collective-permute-start.11 = (f32[256,128]{1,0:T(8,128)S(1)}, f32[256,128]{1,0:T(8,128)S(1)}, u32[]{:S(2)}, u32[]{:S(2)}) collective-permute-start(f32[256,128]{1,0:T(8,128)S(1)} %add.19), channel_id=1, source_target_pairs={{2,0},{3,1},{0,2},{1,3},{6,4},{7,5},{4,6},{5,7},{10,8},{11,9},{8,1... | collective-permute-start | bytes 393224 | tf_op jit(solution)/shard_map/ppermute | solution.py:169

commit v24 on v21

--- a/solution.py
+++ b/solution.py
@@ -20,7 +20,7 @@
 
 def source_team(team, turn, team_count):
     if team_count == 4:
-        return (2 * (team % 2) + team // 2) ^ (0, 2, 1, 3)[turn]
+        return (2 * (team % 2) + team // 2) ^ (1, 0, 2, 3)[turn]
     return (team + turn) % team_count
 
 

time: 48.9 us -> 49.9 us (1.020)
  starting transfers between devices: 20.2 us -> 23.3 us
  waiting for transfers between devices: 21.1 us -> 18.9 us
    ppermute x6, waiting for transfers between devices: 11.3 us -> 9.09 us  [fetch(): return lax.ppermute(value, ('blk', 'rep'), pairs)]
    ppermute x6, starting transfers between devices: 8.01 us -> 10.1 us  [fetch(): return lax.ppermute(value, ('blk', 'rep'), pairs)]
    ppermute x4, starting transfers between devices: 7.8 us -> 8.54 us  [from_mate(): lax.ppermute(value, 'rep', [(team, team ^ 1) for team in range(team_count)])]
where the time goes in v24:
time: 49.9 us; the launch traced here: 49.6 us
  starting transfers between devices  23.3 us (47%)
  waiting for transfers between devices  18.9 us (38%)
  local copies, waits for them, and re-layouts  3.52 us (7%)
  Pallas kernels  3.01 us (6%)
  between operations  0.72 us (1%)
    ppermute x6, starting transfers between devices, fetch(): return lax.ppermute(value, ('blk', 'rep'), pairs)  10.1 us
    ppermute x6, waiting for transfers between devices, fetch(): return lax.ppermute(value, ('blk', 'rep'), pairs)  9.09 us
    ppermute x4, starting transfers between devices, from_mate(): lax.ppermute(value, 'rep', [(team, team ^ 1) for team in range(team_count)])  8.54 us
    ppermute x2, waiting for transfers between devices, from_column(): return lax.ppermute(value, 'rep', pairs)  7.97 us
    ppermute x2, starting transfers between devices, from_column(): return lax.ppermute(value, 'rep', pairs)  4.71 us
    unnamed x10, local copies, waits for them, and re-layouts  3.44 us
    ppermute x4, waiting for transfers between devices, from_mate(): lax.ppermute(value, 'rep', [(team, team ^ 1) for team in range(team_count)])  1.82 us
    pallas_call x2, Pallas kernels, arc_step(): pl.pallas_call(functools.partial(arc_kernel, team_count=team_count, piece...  1.73 us
  transfers between devices with their start and end apart: 12, of which 8 were waited for; matrix products, arithmetic and copies ran while one was open for 0% of the time, Pallas kernels for 1%

profile of v24, /device:TPU:0, one launch (start us, length us, event | category | flops | bytes accessed | tf_op | source)
XLA Modules:
  0.0 49.6 jit_solution(2429681831990894377)
XLA Ops:
  0.0 2.5 %collective-permute-start.1 = (f32[1024,128]{1,0:T(8,128)}, f32[1024,128]{1,0:T(8,128)S(1)}, u32[]{:S(2)}, u32[]{:S(2)}) collective-permute-start(f32[1024,128]{1,0:T(8,128)} %embeddings_ref.1), channel_id=1, source_target_pairs={{3,0},{0,5},{2,10},{1,15},{7,4},{4,9},{6,14},{5,3},{11,8},{8,13},{... | collective-permute-start | bytes 1572872 | tf_op jit(solution)/shard_map/ppermute | solution.py:153
  2.5 1.1 %collective-permute-start = (s32[8,128]{1,0:T(8,128)}, s32[8,128]{1,0:T(8,128)S(1)}, u32[]{:S(2)}, u32[]{:S(2)}) collective-permute-start(s32[8,128]{1,0:T(8,128)} %bitcast.12), channel_id=1, source_target_pairs={{3,0},{0,5},{2,10},{1,15},{7,4},{4,9},{6,14},{5,3},{11,8},{8,13},{... | collective-permute-start | bytes 12296 | tf_op jit(solution)/shard_map/ppermute | solution.py:153
  4.2 0.6 %copy-done.3 = s32[1,1,1,24]{3,2,1,0:T(1,128)S(1)} copy-done((s32[1,1,1,24]{3,2,1,0:T(1,128)S(1)}, s32[1,1,1,24]{3,2,1,0:T(1,128)}, u32[]{:S(2)}) %copy-start.3) | copy-done | bytes 120
  4.9 0.0 copy-done.4
  4.9 0.1 add_bitcast_fusion
  5.0 0.1 squeeze.19.after_ref.info_ref
  5.0 0.6 %copy-done.2 = s32[1024]{0:T(1024)S(1)} copy-done((s32[1024]{0:T(1024)S(1)}, s32[1024]{0:T(1024)}, u32[]{:S(2)}) %copy-start.2) | copy-done | bytes 4120
  5.7 1.1 %copy-done = bf16[1,1,1,24,128,128]{5,4,3,2,1,0:T(8,128)(2,1)S(1)} copy-done((bf16[1,1,1,24,128,128]{5,4,3,2,1,0:T(8,128)(2,1)S(1)}, bf16[1,1,1,24,128,128]{5,4,3,2,1,0:T(8,128)(2,1)}, u32[]{:S(2)}) %copy-start) | copy-done | bytes 786456
  6.8 1.0 %copy-done.1 = f32[1024,128]{1,0:T(8,128)S(1)} copy-done((f32[1024,128]{1,0:T(8,128)S(1)}, f32[1024,128]{1,0:T(8,128)}, u32[]{:S(2)}) %copy-start.1) | copy-done | bytes 524312
  7.8 0.6 %shard_map.64 = (bf16[1,24,128,128]{3,2,1,0:T(8,128)(2,1)S(1)}, f32[256,128]{1,0:T(8,128)S(1)}, f32[256,128]{1,0:T(8,128)S(1)}) custom-call(s32[8,128]{1,0:T(8,128)S(1)} %bitcast.13, f32[1024,128]{1,0:T(8,128)S(1)} %copy-done.1, bf16[1,24,128,128]{3,2,1,0:T(8,128)(2,1)S(1)} %bitcast.11, s32[49,128]{1,0:T(8,128)S(1)} %squeeze.19.after_ref.info_ref), custom_call_target="tpu_custom_call" | custom-call | flops 131072 | bytes 524288 | tf_op jit(solution)/shard_map/pallas_call | solution.py:56
  8.4 4.2 %collective-permute-done.refs_0_ = s32[8,128]{1,0:T(8,128)S(1)} collective-permute-done((s32[8,128]{1,0:T(8,128)}, s32[8,128]{1,0:T(8,128)S(1)}, u32[]{:S(2)}, u32[]{:S(2)}) %collective-permute-start) | collective-permute-done | bytes 4128 | tf_op jit(solution)/shard_map/ppermute | solution.py:153
  12.7 1.0 %shard_map.65 = (f32[256,128]{1,0:T(8,128)S(1)}, f32[256,128]{1,0:T(8,128)S(1)}, f32[256,128]{1,0:T(8,128)S(1)}, f32[256,128]{1,0:T(8,128)S(1)}) custom-call(s32[49,128]{1,0:T(8,128)S(1)} %squeeze.19.after_ref.info_ref, bf16[24,128,128]{2,1,0:T(8,128)(2,1)S(1)} %bitcast.9, s32[8,128]{1,0:T(8,128)S(1)} %collective-permute-done.refs_0_, ...), custom_call_target="tpu_custom_call" | custom-call | flops 201326592 | bytes 1048576 | tf_op jit(solution)/shard_map/pallas_call | solution.py:124
  13.6 5.1 %collective-permute-start.3 = (f32[256,128]{1,0:T(8,128)S(1)}, f32[256,128]{1,0:T(8,128)S(1)}, u32[]{:S(2)}, u32[]{:S(2)}) collective-permute-start(f32[256,128]{1,0:T(8,128)S(1)} %get-tuple-element.21), channel_id=1, source_target_pairs={{0,1},{1,0},{2,3},{3,2},{4,5},{5,4},{6,7},{7,6},{8,9},{9,8},{10,11... | collective-permute-start | bytes 393224 | tf_op jit(solution)/shard_map/ppermute | solution.py:163
  18.8 0.1 collective-permute-start.2
  18.8 0.9 %collective-permute-done.3 = f32[256,128]{1,0:T(8,128)S(1)} collective-permute-done((f32[256,128]{1,0:T(8,128)S(1)}, f32[256,128]{1,0:T(8,128)S(1)}, u32[]{:S(2)}, u32[]{:S(2)}) %collective-permute-start.3) | collective-permute-done | bytes 131104 | tf_op jit(solution)/shard_map/ppermute | solution.py:163
  19.8 1.7 %collective-permute-start.4 = (f32[256,128]{1,0:T(8,128)S(1)}, f32[256,128]{1,0:T(8,128)S(1)}, u32[]{:S(2)}, u32[]{:S(2)}) collective-permute-start(f32[256,128]{1,0:T(8,128)S(1)} %add.16), channel_id=1, source_target_pairs={{2,0},{3,1},{0,2},{1,3},{6,4},{7,5},{4,6},{5,7},{10,8},{11,9},{8,1... | collective-permute-start | bytes 393224 | tf_op jit(solution)/shard_map/ppermute | solution.py:169
  21.4 0.0 collective-permute-done.2
  21.4 4.2 %collective-permute-done.4 = f32[256,128]{1,0:T(8,128)S(1)} collective-permute-done((f32[256,128]{1,0:T(8,128)S(1)}, f32[256,128]{1,0:T(8,128)S(1)}, u32[]{:S(2)}, u32[]{:S(2)}) %collective-permute-start.4) | collective-permute-done | bytes 131104 | tf_op jit(solution)/shard_map/ppermute | solution.py:169
  25.6 3.3 %collective-permute-start.8 = (f32[256,128]{1,0:T(8,128)S(1)}, f32[256,128]{1,0:T(8,128)S(1)}, u32[]{:S(2)}, u32[]{:S(2)}) collective-permute-start(f32[256,128]{1,0:T(8,128)S(1)} %get-tuple-element.27), channel_id=1, source_target_pairs={{3,0},{1,5},{2,10},{0,15},{7,4},{5,9},{6,14},{4,3},{11,8},{9,13},{... | collective-permute-start | bytes 393224 | tf_op jit(solution)/shard_map/ppermute | solution.py:153
  28.9 0.7 %collective-permute-start.6 = (f32[256,128]{1,0:T(8,128)S(1)}, f32[256,128]{1,0:T(8,128)S(1)}, u32[]{:S(2)}, u32[]{:S(2)}) collective-permute-start(f32[256,128]{1,0:T(8,128)S(1)} %get-tuple-element.27), channel_id=1, source_target_pairs={{0,0},{2,5},{1,10},{3,15},{4,4},{6,9},{5,14},{7,3},{8,8},{10,13},{... | collective-permute-start | bytes 393224 | tf_op jit(solution)/shard_map/ppermute | solution.py:153
  29.6 2.6 %collective-permute-start.5 = (f32[256,128]{1,0:T(8,128)S(1)}, f32[256,128]{1,0:T(8,128)S(1)}, u32[]{:S(2)}, u32[]{:S(2)}) collective-permute-start(f32[256,128]{1,0:T(8,128)S(1)} %get-tuple-element.27), channel_id=1, source_target_pairs={{1,0},{3,5},{0,10},{2,15},{5,4},{7,9},{4,14},{6,3},{9,8},{11,13},{... | collective-permute-start | bytes 393224 | tf_op jit(solution)/shard_map/ppermute | solution.py:153
  32.2 0.2 collective-permute-done.8.refs_3_
  32.4 2.8 %collective-permute-done.7.refs_2_ = f32[256,128]{1,0:T(8,128)S(1)} collective-permute-done((f32[256,128]{1,0:T(8,128)S(1)}, f32[256,128]{1,0:T(8,128)S(1)}, u32[]{:S(2)}, u32[]{:S(2)}) %collective-permute-start.7) | collective-permute-done | bytes 131104 | tf_op jit(solution)/shard_map/ppermute | solution.py:153
  35.2 1.8 %collective-permute-done.5.refs_0_ = f32[256,128]{1,0:T(8,128)S(1)} collective-permute-done((f32[256,128]{1,0:T(8,128)S(1)}, f32[256,128]{1,0:T(8,128)S(1)}, u32[]{:S(2)}, u32[]{:S(2)}) %collective-permute-start.5) | collective-permute-done | bytes 131104 | tf_op jit(solution)/shard_map/ppermute | solution.py:153
  37.0 0.8 %shard_map.66 = (f32[256,128]{1,0:T(8,128)S(1)}, f32[256,128]{1,0:T(8,128)S(1)}, f32[256,128]{1,0:T(8,128)S(1)}, f32[256,128]{1,0:T(8,128)S(1)}) custom-call(s32[49,128]{1,0:T(8,128)S(1)} %squeeze.19.after_ref.info_ref, bf16[24,128,128]{2,1,0:T(8,128)(2,1)S(1)} %bitcast.10, f32[256,128]{1,0:T(8,128)S(1)} %collective-permute-done.5.refs_0_, ...), custom_call_target="tpu_custom_call" | custom-call | flops 201326592 | bytes 1048576 | tf_op jit(solution)/shard_map/pallas_call | solution.py:124
  37.8 3.3 %collective-permute-start.10 = (f32[256,128]{1,0:T(8,128)S(1)}, f32[256,128]{1,0:T(8,128)S(1)}, u32[]{:S(2)}, u32[]{:S(2)}) collective-permute-start(f32[256,128]{1,0:T(8,128)S(1)} %get-tuple-element.26), channel_id=1, source_target_pairs={{0,1},{1,0},{2,3},{3,2},{4,5},{5,4},{6,7},{7,6},{8,9},{9,8},{10,11... | collective-permute-start | bytes 393224 | tf_op jit(solution)/shard_map/ppermute | solution.py:163
  41.1 0.1 collective-permute-start.9
  41.1 0.9 %collective-permute-done.10 = f32[256,128]{1,0:T(8,128)S(1)} collective-permute-done((f32[256,128]{1,0:T(8,128)S(1)}, f32[256,128]{1,0:T(8,128)S(1)}, u32[]{:S(2)}, u32[]{:S(2)}) %collective-permute-start.10) | collective-permute-done | bytes 131104 | tf_op jit(solution)/shard_map/ppermute | solution.py:163
  42.1 3.1 %collective-permute-start.11 = (f32[256,128]{1,0:T(8,128)S(1)}, f32[256,128]{1,0:T(8,128)S(1)}, u32[]{:S(2)}, u32[]{:S(2)}) collective-permute-start(f32[256,128]{1,0:T(8,128)S(1)} %add.19), channel_id=1, source_target_pairs={{2,0},{3,1},{0,2},{1,3},{6,4},{7,5},{4,6},{5,7},{10,8},{11,9},{8,1... | collective-permute-start | bytes 393224 | tf_op jit(solution)/shard_map/ppermute | solution.py:169
  45.1 0.0 collective-permute-done.9.refs_1_
  45.1 3.8 %collective-permute-done.11.refs_2_ = f32[256,128]{1,0:T(8,128)S(1)} collective-permute-done((f32[256,128]{1,0:T(8,128)S(1)}, f32[256,128]{1,0:T(8,128)S(1)}, u32[]{:S(2)}, u32[]{:S(2)}) %collective-permute-start.11) | collective-permute-done | bytes 131104 | tf_op jit(solution)/shard_map/ppermute | solution.py:169
  48.9 0.7 %shard_map.67 = f32[256,128]{1,0:T(8,128)} custom-call(f32[256,128]{1,0:T(8,128)S(1)} %get-tuple-element.28.base_ref, f32[256,128]{1,0:T(8,128)S(1)} %get-tuple-element.22.norm_ref, f32[256,128]{1,0:T(8,128)S(1)} %get-tuple-element.23.refs_0_, f32[256,128]{1,0:T(8,128)S(1)} %collective-permute-done.9.refs_1_, f32[256,128]{1,0:T(8,128)S(1)} %collective-permute-done.11.refs_2_), custom_call_target="tpu_custom_call" | custom-call | tf_op jit(solution)/shard_map/pallas_call | solution.py:199
  (11 shorter events, 0.1 us)
Async XLA Ops:
  0.0 12.7 %collective-permute-start.1 = (f32[1024,128]{1,0:T(8,128)}, f32[1024,128]{1,0:T(8,128)S(1)}, u32[]{:S(2)}, u32[]{:S(2)}) collective-permute-start(f32[1024,128]{1,0:T(8,128)} %embeddings_ref.1), channel_id=1, source_target_pairs={{3,0},{0,5},{2,10},{1,15},{7,4},{4,9},{6,14},{5,3},{11,8},{8,13},{... | collective-permute-start | bytes 1572872 | tf_op jit(solution)/shard_map/ppermute | solution.py:153
  2.5 10.2 %collective-permute-start = (s32[8,128]{1,0:T(8,128)}, s32[8,128]{1,0:T(8,128)S(1)}, u32[]{:S(2)}, u32[]{:S(2)}) collective-permute-start(s32[8,128]{1,0:T(8,128)} %bitcast.12), channel_id=1, source_target_pairs={{3,0},{0,5},{2,10},{1,15},{7,4},{4,9},{6,14},{5,3},{11,8},{8,13},{... | collective-permute-start | bytes 12296 | tf_op jit(solution)/shard_map/ppermute | solution.py:153
  4.2 0.7 %copy-start.3 = (s32[1,1,1,24]{3,2,1,0:T(1,128)S(1)}, s32[1,1,1,24]{3,2,1,0:T(1,128)}, u32[]{:S(2)}) copy-start(s32[1,1,1,24]{3,2,1,0:T(1,128)} %param.10) | copy-start | bytes 292
  4.2 0.7 %copy-start.4 = (s32[1,1,1,24]{3,2,1,0:T(1,128)S(1)}, s32[1,1,1,24]{3,2,1,0:T(1,128)}, u32[]{:S(2)}) copy-start(s32[1,1,1,24]{3,2,1,0:T(1,128)} %param.9) | copy-start | bytes 292
  5.0 0.7 %copy-start.2 = (s32[1024]{0:T(1024)S(1)}, s32[1024]{0:T(1024)}, u32[]{:S(2)}) copy-start(s32[1024]{0:T(1024)} %param.7) | copy-start | bytes 12292
  5.6 1.1 %copy-start = (bf16[1,1,1,24,128,128]{5,4,3,2,1,0:T(8,128)(2,1)S(1)}, bf16[1,1,1,24,128,128]{5,4,3,2,1,0:T(8,128)(2,1)}, u32[]{:S(2)}) copy-start(bf16[1,1,1,24,128,128]{5,4,3,2,1,0:T(8,128)(2,1)} %param.8) | copy-start | bytes 2359300
  6.8 1.0 %copy-start.1 = (f32[1024,128]{1,0:T(8,128)S(1)}, f32[1024,128]{1,0:T(8,128)}, u32[]{:S(2)}) copy-start(f32[1024,128]{1,0:T(8,128)} %embeddings_ref.1) | copy-start | bytes 1572868
  13.6 6.1 %collective-permute-start.3 = (f32[256,128]{1,0:T(8,128)S(1)}, f32[256,128]{1,0:T(8,128)S(1)}, u32[]{:S(2)}, u32[]{:S(2)}) collective-permute-start(f32[256,128]{1,0:T(8,128)S(1)} %get-tuple-element.21), channel_id=1, source_target_pairs={{0,1},{1,0},{2,3},{3,2},{4,5},{5,4},{6,7},{7,6},{8,9},{9,8},{10,11... | collective-permute-start | bytes 393224 | tf_op jit(solution)/shard_map/ppermute | solution.py:163
  18.8 2.7 %collective-permute-start.2 = (f32[256,128]{1,0:T(8,128)S(1)}, f32[256,128]{1,0:T(8,128)S(1)}, u32[]{:S(2)}, u32[]{:S(2)}) collective-permute-start(f32[256,128]{1,0:T(8,128)S(1)} %get-tuple-element.19), channel_id=1, source_target_pairs={{0,1},{1,0},{2,3},{3,2},{4,5},{5,4},{6,7},{7,6},{8,9},{9,8},{10,11... | collective-permute-start | bytes 393224 | tf_op jit(solution)/shard_map/ppermute | solution.py:163
  19.8 5.8 %collective-permute-start.4 = (f32[256,128]{1,0:T(8,128)S(1)}, f32[256,128]{1,0:T(8,128)S(1)}, u32[]{:S(2)}, u32[]{:S(2)}) collective-permute-start(f32[256,128]{1,0:T(8,128)S(1)} %add.16), channel_id=1, source_target_pairs={{2,0},{3,1},{0,2},{1,3},{6,4},{7,5},{4,6},{5,7},{10,8},{11,9},{8,1... | collective-permute-start | bytes 393224 | tf_op jit(solution)/shard_map/ppermute | solution.py:169
  25.6 6.7 %collective-permute-start.8 = (f32[256,128]{1,0:T(8,128)S(1)}, f32[256,128]{1,0:T(8,128)S(1)}, u32[]{:S(2)}, u32[]{:S(2)}) collective-permute-start(f32[256,128]{1,0:T(8,128)S(1)} %get-tuple-element.27), channel_id=1, source_target_pairs={{3,0},{1,5},{2,10},{0,15},{7,4},{5,9},{6,14},{4,3},{11,8},{9,13},{... | collective-permute-start | bytes 393224 | tf_op jit(solution)/shard_map/ppermute | solution.py:153
  28.9 6.3 %collective-permute-start.7 = (f32[256,128]{1,0:T(8,128)S(1)}, f32[256,128]{1,0:T(8,128)S(1)}, u32[]{:S(2)}, u32[]{:S(2)}) collective-permute-start(f32[256,128]{1,0:T(8,128)S(1)} %get-tuple-element.27), channel_id=1, source_target_pairs={{2,0},{0,5},{3,10},{1,15},{6,4},{4,9},{7,14},{5,3},{10,8},{8,13},{... | collective-permute-start | bytes 393224 | tf_op jit(solution)/shard_map/ppermute | solution.py:153
  28.9 6.3 %collective-permute-start.6 = (f32[256,128]{1,0:T(8,128)S(1)}, f32[256,128]{1,0:T(8,128)S(1)}, u32[]{:S(2)}, u32[]{:S(2)}) collective-permute-start(f32[256,128]{1,0:T(8,128)S(1)} %get-tuple-element.27), channel_id=1, source_target_pairs={{0,0},{2,5},{1,10},{3,15},{4,4},{6,9},{5,14},{7,3},{8,8},{10,13},{... | collective-permute-start | bytes 393224 | tf_op jit(solution)/shard_map/ppermute | solution.py:153
  29.6 7.4 %collective-permute-start.5 = (f32[256,128]{1,0:T(8,128)S(1)}, f32[256,128]{1,0:T(8,128)S(1)}, u32[]{:S(2)}, u32[]{:S(2)}) collective-permute-start(f32[256,128]{1,0:T(8,128)S(1)} %get-tuple-element.27), channel_id=1, source_target_pairs={{1,0},{3,5},{0,10},{2,15},{5,4},{7,9},{4,14},{6,3},{9,8},{11,13},{... | collective-permute-start | bytes 393224 | tf_op jit(solution)/shard_map/ppermute | solution.py:153
  37.8 4.3 %collective-permute-start.10 = (f32[256,128]{1,0:T(8,128)S(1)}, f32[256,128]{1,0:T(8,128)S(1)}, u32[]{:S(2)}, u32[]{:S(2)}) collective-permute-start(f32[256,128]{1,0:T(8,128)S(1)} %get-tuple-element.26), channel_id=1, source_target_pairs={{0,1},{1,0},{2,3},{3,2},{4,5},{5,4},{6,7},{7,6},{8,9},{9,8},{10,11... | collective-permute-start | bytes 393224 | tf_op jit(solution)/shard_map/ppermute | solution.py:163
  41.1 4.1 %collective-permute-start.9 = (f32[256,128]{1,0:T(8,128)S(1)}, f32[256,128]{1,0:T(8,128)S(1)}, u32[]{:S(2)}, u32[]{:S(2)}) collective-permute-start(f32[256,128]{1,0:T(8,128)S(1)} %get-tuple-element.24), channel_id=1, source_target_pairs={{0,1},{1,0},{2,3},{3,2},{4,5},{5,4},{6,7},{7,6},{8,9},{9,8},{10,11... | collective-permute-start | bytes 393224 | tf_op jit(solution)/shard_map/ppermute | solution.py:163
  42.1 6.9 %collective-permute-start.11 = (f32[256,128]{1,0:T(8,128)S(1)}, f32[256,128]{1,0:T(8,128)S(1)}, u32[]{:S(2)}, u32[]{:S(2)}) collective-permute-start(f32[256,128]{1,0:T(8,128)S(1)} %add.19), channel_id=1, source_target_pairs={{2,0},{3,1},{0,2},{1,3},{6,4},{7,5},{4,6},{5,7},{10,8},{11,9},{8,1... | collective-permute-start | bytes 393224 | tf_op jit(solution)/shard_map/ppermute | solution.py:169

commit v25 on v24

--- a/solution.py
+++ b/solution.py
@@ -20,7 +20,7 @@
 
 def source_team(team, turn, team_count):
     if team_count == 4:
-        return (2 * (team % 2) + team // 2) ^ (1, 0, 2, 3)[turn]
+        return (3 * (team % 2)) ^ (team // 2) ^ (0, 2, 1, 3)[turn]
     return (team + turn) % team_count
 
 

time: 49.9 us -> 49.1 us (0.984)
  starting transfers between devices: 23.3 us -> 22.1 us
    ppermute x6, starting transfers between devices: 10.1 us -> 8.58 us  [fetch(): return lax.ppermute(value, ('blk', 'rep'), pairs)]
    ppermute x2, starting transfers between devices: 4.71 us -> 5.48 us  [from_column(): return lax.ppermute(value, 'rep', pairs)]
    ppermute x4, starting transfers between devices: 8.54 us -> 8.01 us  [from_mate(): lax.ppermute(value, 'rep', [(team, team ^ 1) for team in range(team_count)])]
  transfers between devices with their start and end apart: 12 -> 12, of which waited for: 8 -> 7; matrix products, arithmetic and copies ran while one was open for 0% -> 0% of each run, Pallas kernels for 1% -> 1%
where the time goes in v25:
time: 49.1 us; the launch traced here: 48.8 us
  starting transfers between devices  22.1 us (45%)
  waiting for transfers between devices  19.3 us (39%)
  local copies, waits for them, and re-layouts  3.52 us (7%)
  Pallas kernels  3.01 us (6%)
  between operations  0.74 us (2%)
    ppermute x6, waiting for transfers between devices, fetch(): return lax.ppermute(value, ('blk', 'rep'), pairs)  9.51 us
    ppermute x6, starting transfers between devices, fetch(): return lax.ppermute(value, ('blk', 'rep'), pairs)  8.58 us
    ppermute x4, starting transfers between devices, from_mate(): lax.ppermute(value, 'rep', [(team, team ^ 1) for team in range(team_count)])  8.01 us
    ppermute x2, waiting for transfers between devices, from_column(): return lax.ppermute(value, 'rep', pairs)  7.97 us
    ppermute x2, starting transfers between devices, from_column(): return lax.ppermute(value, 'rep', pairs)  5.48 us
    unnamed x10, local copies, waits for them, and re-layouts  3.44 us
    ppermute x4, waiting for transfers between devices, from_mate(): lax.ppermute(value, 'rep', [(team, team ^ 1) for team in range(team_count)])  1.82 us
    pallas_call x2, Pallas kernels, arc_step(): pl.pallas_call(functools.partial(arc_kernel, team_count=team_count, piece...  1.74 us
  transfers between devices with their start and end apart: 12, of which 7 were waited for; matrix products, arithmetic and copies ran while one was open for 0% of the time, Pallas kernels for 1%

profile of v25, /device:TPU:0, one launch (start us, length us, event | category | flops | bytes accessed | tf_op | source)
XLA Modules:
  0.0 48.8 jit_solution(7205164722354467775)
XLA Ops:
  0.0 2.5 %collective-permute-start.1 = (f32[1024,128]{1,0:T(8,128)}, f32[1024,128]{1,0:T(8,128)S(1)}, u32[]{:S(2)}, u32[]{:S(2)}) collective-permute-start(f32[1024,128]{1,0:T(8,128)} %embeddings_ref.1), channel_id=1, source_target_pairs={{3,0},{0,5},{2,10},{1,15},{7,4},{4,9},{6,14},{5,3},{11,8},{8,13},{... | collective-permute-start | bytes 1572872 | tf_op jit(solution)/shard_map/ppermute | solution.py:153
  2.5 1.1 %collective-permute-start = (s32[8,128]{1,0:T(8,128)}, s32[8,128]{1,0:T(8,128)S(1)}, u32[]{:S(2)}, u32[]{:S(2)}) collective-permute-start(s32[8,128]{1,0:T(8,128)} %bitcast.12), channel_id=1, source_target_pairs={{3,0},{0,5},{2,10},{1,15},{7,4},{4,9},{6,14},{5,3},{11,8},{8,13},{... | collective-permute-start | bytes 12296 | tf_op jit(solution)/shard_map/ppermute | solution.py:153
  4.2 0.6 %copy-done.3 = s32[1,1,1,24]{3,2,1,0:T(1,128)S(1)} copy-done((s32[1,1,1,24]{3,2,1,0:T(1,128)S(1)}, s32[1,1,1,24]{3,2,1,0:T(1,128)}, u32[]{:S(2)}) %copy-start.3) | copy-done | bytes 120
  4.9 0.0 copy-done.4
  4.9 0.1 add_bitcast_fusion
  5.0 0.1 squeeze.19.after_ref.info_ref
  5.0 0.6 %copy-done.2 = s32[1024]{0:T(1024)S(1)} copy-done((s32[1024]{0:T(1024)S(1)}, s32[1024]{0:T(1024)}, u32[]{:S(2)}) %copy-start.2) | copy-done | bytes 4120
  5.7 1.1 %copy-done = bf16[1,1,1,24,128,128]{5,4,3,2,1,0:T(8,128)(2,1)S(1)} copy-done((bf16[1,1,1,24,128,128]{5,4,3,2,1,0:T(8,128)(2,1)S(1)}, bf16[1,1,1,24,128,128]{5,4,3,2,1,0:T(8,128)(2,1)}, u32[]{:S(2)}) %copy-start) | copy-done | bytes 786456
  6.8 1.0 %copy-done.1 = f32[1024,128]{1,0:T(8,128)S(1)} copy-done((f32[1024,128]{1,0:T(8,128)S(1)}, f32[1024,128]{1,0:T(8,128)}, u32[]{:S(2)}) %copy-start.1) | copy-done | bytes 524312
  7.8 0.6 %shard_map.64 = (bf16[1,24,128,128]{3,2,1,0:T(8,128)(2,1)S(1)}, f32[256,128]{1,0:T(8,128)S(1)}, f32[256,128]{1,0:T(8,128)S(1)}) custom-call(s32[8,128]{1,0:T(8,128)S(1)} %bitcast.13, f32[1024,128]{1,0:T(8,128)S(1)} %copy-done.1, bf16[1,24,128,128]{3,2,1,0:T(8,128)(2,1)S(1)} %bitcast.11, s32[49,128]{1,0:T(8,128)S(1)} %squeeze.19.after_ref.info_ref), custom_call_target="tpu_custom_call" | custom-call | flops 131072 | bytes 524288 | tf_op jit(solution)/shard_map/pallas_call | solution.py:56
  8.4 4.2 %collective-permute-done.refs_0_ = s32[8,128]{1,0:T(8,128)S(1)} collective-permute-done((s32[8,128]{1,0:T(8,128)}, s32[8,128]{1,0:T(8,128)S(1)}, u32[]{:S(2)}, u32[]{:S(2)}) %collective-permute-start) | collective-permute-done | bytes 4128 | tf_op jit(solution)/shard_map/ppermute | solution.py:153
  12.7 0.0 collective-permute-done.1.refs_1_
  12.7 1.0 %shard_map.65 = (f32[256,128]{1,0:T(8,128)S(1)}, f32[256,128]{1,0:T(8,128)S(1)}, f32[256,128]{1,0:T(8,128)S(1)}, f32[256,128]{1,0:T(8,128)S(1)}) custom-call(s32[49,128]{1,0:T(8,128)S(1)} %squeeze.19.after_ref.info_ref, bf16[24,128,128]{2,1,0:T(8,128)(2,1)S(1)} %bitcast.9, s32[8,128]{1,0:T(8,128)S(1)} %collective-permute-done.refs_0_, ...), custom_call_target="tpu_custom_call" | custom-call | flops 201326592 | bytes 1048576 | tf_op jit(solution)/shard_map/pallas_call | solution.py:124
  13.6 5.1 %collective-permute-start.3 = (f32[256,128]{1,0:T(8,128)S(1)}, f32[256,128]{1,0:T(8,128)S(1)}, u32[]{:S(2)}, u32[]{:S(2)}) collective-permute-start(f32[256,128]{1,0:T(8,128)S(1)} %get-tuple-element.21), channel_id=1, source_target_pairs={{0,1},{1,0},{2,3},{3,2},{4,5},{5,4},{6,7},{7,6},{8,9},{9,8},{10,11... | collective-permute-start | bytes 393224 | tf_op jit(solution)/shard_map/ppermute | solution.py:163
  18.8 0.1 collective-permute-start.2
  18.8 0.9 %collective-permute-done.3 = f32[256,128]{1,0:T(8,128)S(1)} collective-permute-done((f32[256,128]{1,0:T(8,128)S(1)}, f32[256,128]{1,0:T(8,128)S(1)}, u32[]{:S(2)}, u32[]{:S(2)}) %collective-permute-start.3) | collective-permute-done | bytes 131104 | tf_op jit(solution)/shard_map/ppermute | solution.py:163
  19.8 1.7 %collective-permute-start.4 = (f32[256,128]{1,0:T(8,128)S(1)}, f32[256,128]{1,0:T(8,128)S(1)}, u32[]{:S(2)}, u32[]{:S(2)}) collective-permute-start(f32[256,128]{1,0:T(8,128)S(1)} %add.16), channel_id=1, source_target_pairs={{2,0},{3,1},{0,2},{1,3},{6,4},{7,5},{4,6},{5,7},{10,8},{11,9},{8,1... | collective-permute-start | bytes 393224 | tf_op jit(solution)/shard_map/ppermute | solution.py:169
  21.4 4.2 %collective-permute-done.4 = f32[256,128]{1,0:T(8,128)S(1)} collective-permute-done((f32[256,128]{1,0:T(8,128)S(1)}, f32[256,128]{1,0:T(8,128)S(1)}, u32[]{:S(2)}, u32[]{:S(2)}) %collective-permute-start.4) | collective-permute-done | bytes 131104 | tf_op jit(solution)/shard_map/ppermute | solution.py:169
  25.6 0.1 collective-permute-start.8
  25.7 3.7 %collective-permute-start.7 = (f32[256,128]{1,0:T(8,128)S(1)}, f32[256,128]{1,0:T(8,128)S(1)}, u32[]{:S(2)}, u32[]{:S(2)}) collective-permute-start(f32[256,128]{1,0:T(8,128)S(1)} %get-tuple-element.27), channel_id=1, source_target_pairs={{1,0},{2,5},{0,10},{3,15},{5,4},{6,9},{4,14},{7,3},{9,8},{10,13},{... | collective-permute-start | bytes 393224 | tf_op jit(solution)/shard_map/ppermute | solution.py:153
  29.4 0.6 %collective-permute-start.6 = (f32[256,128]{1,0:T(8,128)S(1)}, f32[256,128]{1,0:T(8,128)S(1)}, u32[]{:S(2)}, u32[]{:S(2)}) collective-permute-start(f32[256,128]{1,0:T(8,128)S(1)} %get-tuple-element.27), channel_id=1, source_target_pairs={{2,0},{1,5},{3,10},{0,15},{6,4},{5,9},{7,14},{4,3},{10,8},{9,13},{... | collective-permute-start | bytes 393224 | tf_op jit(solution)/shard_map/ppermute | solution.py:153
  30.0 0.7 %collective-permute-start.5 = (f32[256,128]{1,0:T(8,128)S(1)}, f32[256,128]{1,0:T(8,128)S(1)}, u32[]{:S(2)}, u32[]{:S(2)}) collective-permute-start(f32[256,128]{1,0:T(8,128)S(1)} %get-tuple-element.27), channel_id=1, source_target_pairs={{0,0},{3,5},{1,10},{2,15},{4,4},{7,9},{5,14},{6,3},{8,8},{11,13},{... | collective-permute-start | bytes 393224 | tf_op jit(solution)/shard_map/ppermute | solution.py:153
  30.7 2.7 %collective-permute-done.7.refs_2_ = f32[256,128]{1,0:T(8,128)S(1)} collective-permute-done((f32[256,128]{1,0:T(8,128)S(1)}, f32[256,128]{1,0:T(8,128)S(1)}, u32[]{:S(2)}, u32[]{:S(2)}) %collective-permute-start.7) | collective-permute-done | bytes 131104 | tf_op jit(solution)/shard_map/ppermute | solution.py:153
  33.3 2.6 %collective-permute-done.6.refs_1_ = f32[256,128]{1,0:T(8,128)S(1)} collective-permute-done((f32[256,128]{1,0:T(8,128)S(1)}, f32[256,128]{1,0:T(8,128)S(1)}, u32[]{:S(2)}, u32[]{:S(2)}) %collective-permute-start.6) | collective-permute-done | bytes 131104 | tf_op jit(solution)/shard_map/ppermute | solution.py:153
  36.0 0.8 %shard_map.66 = (f32[256,128]{1,0:T(8,128)S(1)}, f32[256,128]{1,0:T(8,128)S(1)}, f32[256,128]{1,0:T(8,128)S(1)}, f32[256,128]{1,0:T(8,128)S(1)}) custom-call(s32[49,128]{1,0:T(8,128)S(1)} %squeeze.19.after_ref.info_ref, bf16[24,128,128]{2,1,0:T(8,128)(2,1)S(1)} %bitcast.10, f32[256,128]{1,0:T(8,128)S(1)} %collective-permute-done.5.refs_0_, ...), custom_call_target="tpu_custom_call" | custom-call | flops 201326592 | bytes 1048576 | tf_op jit(solution)/shard_map/pallas_call | solution.py:124
  36.7 2.7 %collective-permute-start.10 = (f32[256,128]{1,0:T(8,128)S(1)}, f32[256,128]{1,0:T(8,128)S(1)}, u32[]{:S(2)}, u32[]{:S(2)}) collective-permute-start(f32[256,128]{1,0:T(8,128)S(1)} %get-tuple-element.26), channel_id=1, source_target_pairs={{0,1},{1,0},{2,3},{3,2},{4,5},{5,4},{6,7},{7,6},{8,9},{9,8},{10,11... | collective-permute-start | bytes 393224 | tf_op jit(solution)/shard_map/ppermute | solution.py:163
  39.5 0.1 collective-permute-start.9
  39.5 0.9 %collective-permute-done.10 = f32[256,128]{1,0:T(8,128)S(1)} collective-permute-done((f32[256,128]{1,0:T(8,128)S(1)}, f32[256,128]{1,0:T(8,128)S(1)}, u32[]{:S(2)}, u32[]{:S(2)}) %collective-permute-start.10) | collective-permute-done | bytes 131104 | tf_op jit(solution)/shard_map/ppermute | solution.py:163
  40.5 3.8 %collective-permute-start.11 = (f32[256,128]{1,0:T(8,128)S(1)}, f32[256,128]{1,0:T(8,128)S(1)}, u32[]{:S(2)}, u32[]{:S(2)}) collective-permute-start(f32[256,128]{1,0:T(8,128)S(1)} %add.19), channel_id=1, source_target_pairs={{2,0},{3,1},{0,2},{1,3},{6,4},{7,5},{4,6},{5,7},{10,8},{11,9},{8,1... | collective-permute-start | bytes 393224 | tf_op jit(solution)/shard_map/ppermute | solution.py:169
  44.3 0.0 collective-permute-done.9.refs_1_
  44.3 3.8 %collective-permute-done.11.refs_2_ = f32[256,128]{1,0:T(8,128)S(1)} collective-permute-done((f32[256,128]{1,0:T(8,128)S(1)}, f32[256,128]{1,0:T(8,128)S(1)}, u32[]{:S(2)}, u32[]{:S(2)}) %collective-permute-start.11) | collective-permute-done | bytes 131104 | tf_op jit(solution)/shard_map/ppermute | solution.py:169
  48.1 0.7 %shard_map.67 = f32[256,128]{1,0:T(8,128)} custom-call(f32[256,128]{1,0:T(8,128)S(1)} %get-tuple-element.28.base_ref, f32[256,128]{1,0:T(8,128)S(1)} %get-tuple-element.22.norm_ref, f32[256,128]{1,0:T(8,128)S(1)} %get-tuple-element.23.refs_0_, f32[256,128]{1,0:T(8,128)S(1)} %collective-permute-done.9.refs_1_, f32[256,128]{1,0:T(8,128)S(1)} %collective-permute-done.11.refs_2_), custom_call_target="tpu_custom_call" | custom-call | tf_op jit(solution)/shard_map/pallas_call | solution.py:199
  (11 shorter events, 0.1 us)
Async XLA Ops:
  0.0 12.7 %collective-permute-start.1 = (f32[1024,128]{1,0:T(8,128)}, f32[1024,128]{1,0:T(8,128)S(1)}, u32[]{:S(2)}, u32[]{:S(2)}) collective-permute-start(f32[1024,128]{1,0:T(8,128)} %embeddings_ref.1), channel_id=1, source_target_pairs={{3,0},{0,5},{2,10},{1,15},{7,4},{4,9},{6,14},{5,3},{11,8},{8,13},{... | collective-permute-start | bytes 1572872 | tf_op jit(solution)/shard_map/ppermute | solution.py:153
  2.5 10.2 %collective-permute-start = (s32[8,128]{1,0:T(8,128)}, s32[8,128]{1,0:T(8,128)S(1)}, u32[]{:S(2)}, u32[]{:S(2)}) collective-permute-start(s32[8,128]{1,0:T(8,128)} %bitcast.12), channel_id=1, source_target_pairs={{3,0},{0,5},{2,10},{1,15},{7,4},{4,9},{6,14},{5,3},{11,8},{8,13},{... | collective-permute-start | bytes 12296 | tf_op jit(solution)/shard_map/ppermute | solution.py:153
  4.2 0.7 %copy-start.3 = (s32[1,1,1,24]{3,2,1,0:T(1,128)S(1)}, s32[1,1,1,24]{3,2,1,0:T(1,128)}, u32[]{:S(2)}) copy-start(s32[1,1,1,24]{3,2,1,0:T(1,128)} %param.10) | copy-start | bytes 292
  4.2 0.7 %copy-start.4 = (s32[1,1,1,24]{3,2,1,0:T(1,128)S(1)}, s32[1,1,1,24]{3,2,1,0:T(1,128)}, u32[]{:S(2)}) copy-start(s32[1,1,1,24]{3,2,1,0:T(1,128)} %param.9) | copy-start | bytes 292
  5.0 0.7 %copy-start.2 = (s32[1024]{0:T(1024)S(1)}, s32[1024]{0:T(1024)}, u32[]{:S(2)}) copy-start(s32[1024]{0:T(1024)} %param.7) | copy-start | bytes 12292
  5.6 1.1 %copy-start = (bf16[1,1,1,24,128,128]{5,4,3,2,1,0:T(8,128)(2,1)S(1)}, bf16[1,1,1,24,128,128]{5,4,3,2,1,0:T(8,128)(2,1)}, u32[]{:S(2)}) copy-start(bf16[1,1,1,24,128,128]{5,4,3,2,1,0:T(8,128)(2,1)} %param.8) | copy-start | bytes 2359300
  6.8 1.0 %copy-start.1 = (f32[1024,128]{1,0:T(8,128)S(1)}, f32[1024,128]{1,0:T(8,128)}, u32[]{:S(2)}) copy-start(f32[1024,128]{1,0:T(8,128)} %embeddings_ref.1) | copy-start | bytes 1572868
  13.6 6.1 %collective-permute-start.3 = (f32[256,128]{1,0:T(8,128)S(1)}, f32[256,128]{1,0:T(8,128)S(1)}, u32[]{:S(2)}, u32[]{:S(2)}) collective-permute-start(f32[256,128]{1,0:T(8,128)S(1)} %get-tuple-element.21), channel_id=1, source_target_pairs={{0,1},{1,0},{2,3},{3,2},{4,5},{5,4},{6,7},{7,6},{8,9},{9,8},{10,11... | collective-permute-start | bytes 393224 | tf_op jit(solution)/shard_map/ppermute | solution.py:163
  18.8 2.7 %collective-permute-start.2 = (f32[256,128]{1,0:T(8,128)S(1)}, f32[256,128]{1,0:T(8,128)S(1)}, u32[]{:S(2)}, u32[]{:S(2)}) collective-permute-start(f32[256,128]{1,0:T(8,128)S(1)} %get-tuple-element.19), channel_id=1, source_target_pairs={{0,1},{1,0},{2,3},{3,2},{4,5},{5,4},{6,7},{7,6},{8,9},{9,8},{10,11... | collective-permute-start | bytes 393224 | tf_op jit(solution)/shard_map/ppermute | solution.py:163
  19.8 5.8 %collective-permute-start.4 = (f32[256,128]{1,0:T(8,128)S(1)}, f32[256,128]{1,0:T(8,128)S(1)}, u32[]{:S(2)}, u32[]{:S(2)}) collective-permute-start(f32[256,128]{1,0:T(8,128)S(1)} %add.16), channel_id=1, source_target_pairs={{2,0},{3,1},{0,2},{1,3},{6,4},{7,5},{4,6},{5,7},{10,8},{11,9},{8,1... | collective-permute-start | bytes 393224 | tf_op jit(solution)/shard_map/ppermute | solution.py:169
  25.6 5.0 %collective-permute-start.8 = (f32[256,128]{1,0:T(8,128)S(1)}, f32[256,128]{1,0:T(8,128)S(1)}, u32[]{:S(2)}, u32[]{:S(2)}) collective-permute-start(f32[256,128]{1,0:T(8,128)S(1)} %get-tuple-element.27), channel_id=1, source_target_pairs={{3,0},{0,5},{2,10},{1,15},{7,4},{4,9},{6,14},{5,3},{11,8},{8,13},{... | collective-permute-start | bytes 393224 | tf_op jit(solution)/shard_map/ppermute | solution.py:153
  25.7 7.6 %collective-permute-start.7 = (f32[256,128]{1,0:T(8,128)S(1)}, f32[256,128]{1,0:T(8,128)S(1)}, u32[]{:S(2)}, u32[]{:S(2)}) collective-permute-start(f32[256,128]{1,0:T(8,128)S(1)} %get-tuple-element.27), channel_id=1, source_target_pairs={{1,0},{2,5},{0,10},{3,15},{5,4},{6,9},{4,14},{7,3},{9,8},{10,13},{... | collective-permute-start | bytes 393224 | tf_op jit(solution)/shard_map/ppermute | solution.py:153
  29.4 6.5 %collective-permute-start.6 = (f32[256,128]{1,0:T(8,128)S(1)}, f32[256,128]{1,0:T(8,128)S(1)}, u32[]{:S(2)}, u32[]{:S(2)}) collective-permute-start(f32[256,128]{1,0:T(8,128)S(1)} %get-tuple-element.27), channel_id=1, source_target_pairs={{2,0},{1,5},{3,10},{0,15},{6,4},{5,9},{7,14},{4,3},{10,8},{9,13},{... | collective-permute-start | bytes 393224 | tf_op jit(solution)/shard_map/ppermute | solution.py:153
  30.0 5.9 %collective-permute-start.5 = (f32[256,128]{1,0:T(8,128)S(1)}, f32[256,128]{1,0:T(8,128)S(1)}, u32[]{:S(2)}, u32[]{:S(2)}) collective-permute-start(f32[256,128]{1,0:T(8,128)S(1)} %get-tuple-element.27), channel_id=1, source_target_pairs={{0,0},{3,5},{1,10},{2,15},{4,4},{7,9},{5,14},{6,3},{8,8},{11,13},{... | collective-permute-start | bytes 393224 | tf_op jit(solution)/shard_map/ppermute | solution.py:153
  36.7 3.7 %collective-permute-start.10 = (f32[256,128]{1,0:T(8,128)S(1)}, f32[256,128]{1,0:T(8,128)S(1)}, u32[]{:S(2)}, u32[]{:S(2)}) collective-permute-start(f32[256,128]{1,0:T(8,128)S(1)} %get-tuple-element.26), channel_id=1, source_target_pairs={{0,1},{1,0},{2,3},{3,2},{4,5},{5,4},{6,7},{7,6},{8,9},{9,8},{10,11... | collective-permute-start | bytes 393224 | tf_op jit(solution)/shard_map/ppermute | solution.py:163
  39.5 4.8 %collective-permute-start.9 = (f32[256,128]{1,0:T(8,128)S(1)}, f32[256,128]{1,0:T(8,128)S(1)}, u32[]{:S(2)}, u32[]{:S(2)}) collective-permute-start(f32[256,128]{1,0:T(8,128)S(1)} %get-tuple-element.24), channel_id=1, source_target_pairs={{0,1},{1,0},{2,3},{3,2},{4,5},{5,4},{6,7},{7,6},{8,9},{9,8},{10,11... | collective-permute-start | bytes 393224 | tf_op jit(solution)/shard_map/ppermute | solution.py:163
  40.5 7.6 %collective-permute-start.11 = (f32[256,128]{1,0:T(8,128)S(1)}, f32[256,128]{1,0:T(8,128)S(1)}, u32[]{:S(2)}, u32[]{:S(2)}) collective-permute-start(f32[256,128]{1,0:T(8,128)S(1)} %add.19), channel_id=1, source_target_pairs={{2,0},{3,1},{0,2},{1,3},{6,4},{7,5},{4,6},{5,7},{10,8},{11,9},{8,1... | collective-permute-start | bytes 393224 | tf_op jit(solution)/shard_map/ppermute | solution.py:169

commit v26 on v21

--- a/solution.py
+++ b/solution.py
@@ -210,7 +210,7 @@
     arc_length, _, tile_size, _ = tile_values.shape[2:]
     panel_rows = embeddings.shape[0]
     team_count = lax.axis_size("rep")
-    spread = (3, 0, 2, 1) if team_count == 4 else tuple(range(team_count))
+    spread = (2, 0, 3, 1) if team_count == 4 else tuple(range(team_count))
     degrees = degrees.reshape(panel_rows // tile_size, tile_size)
 
     panel = fetch(embeddings, lambda team: spread[team], arc_length)

time: 48.9 us -> 48.8 us (level)
    ppermute x2, waiting for transfers between devices: 7.97 us -> 8.55 us  [from_column(): return lax.ppermute(value, 'rep', pairs)]
    ppermute x6, starting transfers between devices: 8.01 us -> 7.44 us  [fetch(): return lax.ppermute(value, ('blk', 'rep'), pairs)]
    ppermute x4, starting transfers between devices: 7.8 us -> 8.33 us  [from_mate(): lax.ppermute(value, 'rep', [(team, team ^ 1) for team in range(team_count)])]
    ppermute x6, waiting for transfers between devices: 11.3 us -> 10.7 us  [fetch(): return lax.ppermute(value, ('blk', 'rep'), pairs)]
where the time goes in v26:
time: 48.8 us; the launch traced here: 48.5 us
  waiting for transfers between devices  21.1 us (43%)
  starting transfers between devices  20 us (41%)
  local copies, waits for them, and re-layouts  3.52 us (7%)
  Pallas kernels  3.01 us (6%)
  between operations  0.72 us (1%)
    ppermute x6, waiting for transfers between devices, fetch(): return lax.ppermute(value, ('blk', 'rep'), pairs)  10.7 us
    ppermute x2, waiting for transfers between devices, from_column(): return lax.ppermute(value, 'rep', pairs)  8.55 us
    ppermute x4, starting transfers between devices, from_mate(): lax.ppermute(value, 'rep', [(team, team ^ 1) for team in range(team_count)])  8.33 us
    ppermute x6, starting transfers between devices, fetch(): return lax.ppermute(value, ('blk', 'rep'), pairs)  7.44 us
    ppermute x2, starting transfers between devices, from_column(): return lax.ppermute(value, 'rep', pairs)  4.22 us
    unnamed x10, local copies, waits for them, and re-layouts  3.44 us
    ppermute x4, waiting for transfers between devices, from_mate(): lax.ppermute(value, 'rep', [(team, team ^ 1) for team in range(team_count)])  1.82 us
    pallas_call x2, Pallas kernels, arc_step(): pl.pallas_call(functools.partial(arc_kernel, team_count=team_count, piece...  1.73 us
  transfers between devices with their start and end apart: 12, of which 8 were waited for; matrix products, arithmetic and copies ran while one was open for 0% of the time, Pallas kernels for 1%

profile of v26, /device:TPU:0, one launch (start us, length us, event | category | flops | bytes accessed | tf_op | source)
XLA Modules:
  0.0 48.5 jit_solution(12392377997853642809)
XLA Ops:
  0.0 2.5 %collective-permute-start.1 = (f32[1024,128]{1,0:T(8,128)}, f32[1024,128]{1,0:T(8,128)S(1)}, u32[]{:S(2)}, u32[]{:S(2)}) collective-permute-start(f32[1024,128]{1,0:T(8,128)} %embeddings_ref.1), channel_id=1, source_target_pairs={{2,0},{0,5},{3,10},{1,15},{6,4},{4,9},{7,14},{5,3},{10,8},{8,13},{... | collective-permute-start | bytes 1572872 | tf_op jit(solution)/shard_map/ppermute | solution.py:153
  2.5 1.1 %collective-permute-start = (s32[8,128]{1,0:T(8,128)}, s32[8,128]{1,0:T(8,128)S(1)}, u32[]{:S(2)}, u32[]{:S(2)}) collective-permute-start(s32[8,128]{1,0:T(8,128)} %bitcast.12), channel_id=1, source_target_pairs={{2,0},{0,5},{3,10},{1,15},{6,4},{4,9},{7,14},{5,3},{10,8},{8,13},{... | collective-permute-start | bytes 12296 | tf_op jit(solution)/shard_map/ppermute | solution.py:153
  4.2 0.6 %copy-done.3 = s32[1,1,1,24]{3,2,1,0:T(1,128)S(1)} copy-done((s32[1,1,1,24]{3,2,1,0:T(1,128)S(1)}, s32[1,1,1,24]{3,2,1,0:T(1,128)}, u32[]{:S(2)}) %copy-start.3) | copy-done | bytes 120
  4.9 0.0 copy-done.4
  4.9 0.1 add_bitcast_fusion
  5.0 0.1 squeeze.19.after_ref.info_ref
  5.0 0.6 %copy-done.2 = s32[1024]{0:T(1024)S(1)} copy-done((s32[1024]{0:T(1024)S(1)}, s32[1024]{0:T(1024)}, u32[]{:S(2)}) %copy-start.2) | copy-done | bytes 4120
  5.7 1.1 %copy-done = bf16[1,1,1,24,128,128]{5,4,3,2,1,0:T(8,128)(2,1)S(1)} copy-done((bf16[1,1,1,24,128,128]{5,4,3,2,1,0:T(8,128)(2,1)S(1)}, bf16[1,1,1,24,128,128]{5,4,3,2,1,0:T(8,128)(2,1)}, u32[]{:S(2)}) %copy-start) | copy-done | bytes 786456
  6.8 1.0 %copy-done.1 = f32[1024,128]{1,0:T(8,128)S(1)} copy-done((f32[1024,128]{1,0:T(8,128)S(1)}, f32[1024,128]{1,0:T(8,128)}, u32[]{:S(2)}) %copy-start.1) | copy-done | bytes 524312
  7.8 0.6 %shard_map.64 = (bf16[1,24,128,128]{3,2,1,0:T(8,128)(2,1)S(1)}, f32[256,128]{1,0:T(8,128)S(1)}, f32[256,128]{1,0:T(8,128)S(1)}) custom-call(s32[8,128]{1,0:T(8,128)S(1)} %bitcast.13, f32[1024,128]{1,0:T(8,128)S(1)} %copy-done.1, bf16[1,24,128,128]{3,2,1,0:T(8,128)(2,1)S(1)} %bitcast.11, s32[49,128]{1,0:T(8,128)S(1)} %squeeze.19.after_ref.info_ref), custom_call_target="tpu_custom_call" | custom-call | flops 131072 | bytes 524288 | tf_op jit(solution)/shard_map/pallas_call | solution.py:56
  8.4 4.2 %collective-permute-done.refs_0_ = s32[8,128]{1,0:T(8,128)S(1)} collective-permute-done((s32[8,128]{1,0:T(8,128)}, s32[8,128]{1,0:T(8,128)S(1)}, u32[]{:S(2)}, u32[]{:S(2)}) %collective-permute-start) | collective-permute-done | bytes 4128 | tf_op jit(solution)/shard_map/ppermute | solution.py:153
  12.7 0.0 collective-permute-done.1.refs_1_
  12.7 1.0 %shard_map.65 = (f32[256,128]{1,0:T(8,128)S(1)}, f32[256,128]{1,0:T(8,128)S(1)}, f32[256,128]{1,0:T(8,128)S(1)}, f32[256,128]{1,0:T(8,128)S(1)}) custom-call(s32[49,128]{1,0:T(8,128)S(1)} %squeeze.19.after_ref.info_ref, bf16[24,128,128]{2,1,0:T(8,128)(2,1)S(1)} %bitcast.9, s32[8,128]{1,0:T(8,128)S(1)} %collective-permute-done.refs_0_, ...), custom_call_target="tpu_custom_call" | custom-call | flops 201326592 | bytes 1048576 | tf_op jit(solution)/shard_map/pallas_call | solution.py:124
  13.6 5.1 %collective-permute-start.3 = (f32[256,128]{1,0:T(8,128)S(1)}, f32[256,128]{1,0:T(8,128)S(1)}, u32[]{:S(2)}, u32[]{:S(2)}) collective-permute-start(f32[256,128]{1,0:T(8,128)S(1)} %get-tuple-element.21), channel_id=1, source_target_pairs={{0,1},{1,0},{2,3},{3,2},{4,5},{5,4},{6,7},{7,6},{8,9},{9,8},{10,11... | collective-permute-start | bytes 393224 | tf_op jit(solution)/shard_map/ppermute | solution.py:163
  18.8 0.1 collective-permute-start.2
  18.8 0.9 %collective-permute-done.3 = f32[256,128]{1,0:T(8,128)S(1)} collective-permute-done((f32[256,128]{1,0:T(8,128)S(1)}, f32[256,128]{1,0:T(8,128)S(1)}, u32[]{:S(2)}, u32[]{:S(2)}) %collective-permute-start.3) | collective-permute-done | bytes 131104 | tf_op jit(solution)/shard_map/ppermute | solution.py:163
  19.8 1.1 %collective-permute-start.4 = (f32[256,128]{1,0:T(8,128)S(1)}, f32[256,128]{1,0:T(8,128)S(1)}, u32[]{:S(2)}, u32[]{:S(2)}) collective-permute-start(f32[256,128]{1,0:T(8,128)S(1)} %add.16), channel_id=1, source_target_pairs={{2,0},{3,1},{0,2},{1,3},{6,4},{7,5},{4,6},{5,7},{10,8},{11,9},{8,1... | collective-permute-start | bytes 393224 | tf_op jit(solution)/shard_map/ppermute | solution.py:169
  20.8 0.0 collective-permute-done.2
  20.8 4.7 %collective-permute-done.4 = f32[256,128]{1,0:T(8,128)S(1)} collective-permute-done((f32[256,128]{1,0:T(8,128)S(1)}, f32[256,128]{1,0:T(8,128)S(1)}, u32[]{:S(2)}, u32[]{:S(2)}) %collective-permute-start.4) | collective-permute-done | bytes 131104 | tf_op jit(solution)/shard_map/ppermute | solution.py:169
  25.6 2.7 %collective-permute-start.8 = (f32[256,128]{1,0:T(8,128)S(1)}, f32[256,128]{1,0:T(8,128)S(1)}, u32[]{:S(2)}, u32[]{:S(2)}) collective-permute-start(f32[256,128]{1,0:T(8,128)S(1)} %get-tuple-element.27), channel_id=1, source_target_pairs={{3,0},{1,5},{2,10},{0,15},{7,4},{5,9},{6,14},{4,3},{11,8},{9,13},{... | collective-permute-start | bytes 393224 | tf_op jit(solution)/shard_map/ppermute | solution.py:153
  28.3 0.5 %collective-permute-start.7 = (f32[256,128]{1,0:T(8,128)S(1)}, f32[256,128]{1,0:T(8,128)S(1)}, u32[]{:S(2)}, u32[]{:S(2)}) collective-permute-start(f32[256,128]{1,0:T(8,128)S(1)} %get-tuple-element.27), channel_id=1, source_target_pairs={{1,0},{3,5},{0,10},{2,15},{5,4},{7,9},{4,14},{6,3},{9,8},{11,13},{... | collective-permute-start | bytes 393224 | tf_op jit(solution)/shard_map/ppermute | solution.py:153
  28.9 0.7 %collective-permute-start.5 = (f32[256,128]{1,0:T(8,128)S(1)}, f32[256,128]{1,0:T(8,128)S(1)}, u32[]{:S(2)}, u32[]{:S(2)}) collective-permute-start(f32[256,128]{1,0:T(8,128)S(1)} %get-tuple-element.27), channel_id=1, source_target_pairs={{0,0},{2,5},{1,10},{3,15},{4,4},{6,9},{5,14},{7,3},{8,8},{10,13},{... | collective-permute-start | bytes 393224 | tf_op jit(solution)/shard_map/ppermute | solution.py:153
  29.5 2.4 %collective-permute-done.8.refs_3_ = f32[256,128]{1,0:T(8,128)S(1)} collective-permute-done((f32[256,128]{1,0:T(8,128)S(1)}, f32[256,128]{1,0:T(8,128)S(1)}, u32[]{:S(2)}, u32[]{:S(2)}) %collective-permute-start.8) | collective-permute-done | bytes 131104 | tf_op jit(solution)/shard_map/ppermute | solution.py:153
  31.9 1.8 %collective-permute-done.7.refs_2_ = f32[256,128]{1,0:T(8,128)S(1)} collective-permute-done((f32[256,128]{1,0:T(8,128)S(1)}, f32[256,128]{1,0:T(8,128)S(1)}, u32[]{:S(2)}, u32[]{:S(2)}) %collective-permute-start.7) | collective-permute-done | bytes 131104 | tf_op jit(solution)/shard_map/ppermute | solution.py:153
  33.7 2.3 %collective-permute-done.6.refs_1_ = f32[256,128]{1,0:T(8,128)S(1)} collective-permute-done((f32[256,128]{1,0:T(8,128)S(1)}, f32[256,128]{1,0:T(8,128)S(1)}, u32[]{:S(2)}, u32[]{:S(2)}) %collective-permute-start.6) | collective-permute-done | bytes 131104 | tf_op jit(solution)/shard_map/ppermute | solution.py:153
  36.0 0.8 %shard_map.66 = (f32[256,128]{1,0:T(8,128)S(1)}, f32[256,128]{1,0:T(8,128)S(1)}, f32[256,128]{1,0:T(8,128)S(1)}, f32[256,128]{1,0:T(8,128)S(1)}) custom-call(s32[49,128]{1,0:T(8,128)S(1)} %squeeze.19.after_ref.info_ref, bf16[24,128,128]{2,1,0:T(8,128)(2,1)S(1)} %bitcast.10, f32[256,128]{1,0:T(8,128)S(1)} %collective-permute-done.5.refs_0_, ...), custom_call_target="tpu_custom_call" | custom-call | flops 201326592 | bytes 1048576 | tf_op jit(solution)/shard_map/pallas_call | solution.py:124
  36.8 3.1 %collective-permute-start.10 = (f32[256,128]{1,0:T(8,128)S(1)}, f32[256,128]{1,0:T(8,128)S(1)}, u32[]{:S(2)}, u32[]{:S(2)}) collective-permute-start(f32[256,128]{1,0:T(8,128)S(1)} %get-tuple-element.26), channel_id=1, source_target_pairs={{0,1},{1,0},{2,3},{3,2},{4,5},{5,4},{6,7},{7,6},{8,9},{9,8},{10,11... | collective-permute-start | bytes 393224 | tf_op jit(solution)/shard_map/ppermute | solution.py:163
  39.8 0.1 collective-permute-start.9
  39.9 0.9 %collective-permute-done.10 = f32[256,128]{1,0:T(8,128)S(1)} collective-permute-done((f32[256,128]{1,0:T(8,128)S(1)}, f32[256,128]{1,0:T(8,128)S(1)}, u32[]{:S(2)}, u32[]{:S(2)}) %collective-permute-start.10) | collective-permute-done | bytes 131104 | tf_op jit(solution)/shard_map/ppermute | solution.py:163
  40.9 3.1 %collective-permute-start.11 = (f32[256,128]{1,0:T(8,128)S(1)}, f32[256,128]{1,0:T(8,128)S(1)}, u32[]{:S(2)}, u32[]{:S(2)}) collective-permute-start(f32[256,128]{1,0:T(8,128)S(1)} %add.19), channel_id=1, source_target_pairs={{2,0},{3,1},{0,2},{1,3},{6,4},{7,5},{4,6},{5,7},{10,8},{11,9},{8,1... | collective-permute-start | bytes 393224 | tf_op jit(solution)/shard_map/ppermute | solution.py:169
  44.0 3.8 %collective-permute-done.11.refs_2_ = f32[256,128]{1,0:T(8,128)S(1)} collective-permute-done((f32[256,128]{1,0:T(8,128)S(1)}, f32[256,128]{1,0:T(8,128)S(1)}, u32[]{:S(2)}, u32[]{:S(2)}) %collective-permute-start.11) | collective-permute-done | bytes 131104 | tf_op jit(solution)/shard_map/ppermute | solution.py:169
  47.8 0.7 %shard_map.67 = f32[256,128]{1,0:T(8,128)} custom-call(f32[256,128]{1,0:T(8,128)S(1)} %get-tuple-element.28.base_ref, f32[256,128]{1,0:T(8,128)S(1)} %get-tuple-element.22.norm_ref, f32[256,128]{1,0:T(8,128)S(1)} %get-tuple-element.23.refs_0_, f32[256,128]{1,0:T(8,128)S(1)} %collective-permute-done.9.refs_1_, f32[256,128]{1,0:T(8,128)S(1)} %collective-permute-done.11.refs_2_), custom_call_target="tpu_custom_call" | custom-call | tf_op jit(solution)/shard_map/pallas_call | solution.py:199
  (11 shorter events, 0.1 us)
Async XLA Ops:
  0.0 12.7 %collective-permute-start.1 = (f32[1024,128]{1,0:T(8,128)}, f32[1024,128]{1,0:T(8,128)S(1)}, u32[]{:S(2)}, u32[]{:S(2)}) collective-permute-start(f32[1024,128]{1,0:T(8,128)} %embeddings_ref.1), channel_id=1, source_target_pairs={{2,0},{0,5},{3,10},{1,15},{6,4},{4,9},{7,14},{5,3},{10,8},{8,13},{... | collective-permute-start | bytes 1572872 | tf_op jit(solution)/shard_map/ppermute | solution.py:153
  2.5 10.2 %collective-permute-start = (s32[8,128]{1,0:T(8,128)}, s32[8,128]{1,0:T(8,128)S(1)}, u32[]{:S(2)}, u32[]{:S(2)}) collective-permute-start(s32[8,128]{1,0:T(8,128)} %bitcast.12), channel_id=1, source_target_pairs={{2,0},{0,5},{3,10},{1,15},{6,4},{4,9},{7,14},{5,3},{10,8},{8,13},{... | collective-permute-start | bytes 12296 | tf_op jit(solution)/shard_map/ppermute | solution.py:153
  4.2 0.7 %copy-start.3 = (s32[1,1,1,24]{3,2,1,0:T(1,128)S(1)}, s32[1,1,1,24]{3,2,1,0:T(1,128)}, u32[]{:S(2)}) copy-start(s32[1,1,1,24]{3,2,1,0:T(1,128)} %param.10) | copy-start | bytes 292
  4.2 0.7 %copy-start.4 = (s32[1,1,1,24]{3,2,1,0:T(1,128)S(1)}, s32[1,1,1,24]{3,2,1,0:T(1,128)}, u32[]{:S(2)}) copy-start(s32[1,1,1,24]{3,2,1,0:T(1,128)} %param.9) | copy-start | bytes 292
  5.0 0.7 %copy-start.2 = (s32[1024]{0:T(1024)S(1)}, s32[1024]{0:T(1024)}, u32[]{:S(2)}) copy-start(s32[1024]{0:T(1024)} %param.7) | copy-start | bytes 12292
  5.6 1.1 %copy-start = (bf16[1,1,1,24,128,128]{5,4,3,2,1,0:T(8,128)(2,1)S(1)}, bf16[1,1,1,24,128,128]{5,4,3,2,1,0:T(8,128)(2,1)}, u32[]{:S(2)}) copy-start(bf16[1,1,1,24,128,128]{5,4,3,2,1,0:T(8,128)(2,1)} %param.8) | copy-start | bytes 2359300
  6.8 1.0 %copy-start.1 = (f32[1024,128]{1,0:T(8,128)S(1)}, f32[1024,128]{1,0:T(8,128)}, u32[]{:S(2)}) copy-start(f32[1024,128]{1,0:T(8,128)} %embeddings_ref.1) | copy-start | bytes 1572868
  13.6 6.1 %collective-permute-start.3 = (f32[256,128]{1,0:T(8,128)S(1)}, f32[256,128]{1,0:T(8,128)S(1)}, u32[]{:S(2)}, u32[]{:S(2)}) collective-permute-start(f32[256,128]{1,0:T(8,128)S(1)} %get-tuple-element.21), channel_id=1, source_target_pairs={{0,1},{1,0},{2,3},{3,2},{4,5},{5,4},{6,7},{7,6},{8,9},{9,8},{10,11... | collective-permute-start | bytes 393224 | tf_op jit(solution)/shard_map/ppermute | solution.py:163
  18.8 2.1 %collective-permute-start.2 = (f32[256,128]{1,0:T(8,128)S(1)}, f32[256,128]{1,0:T(8,128)S(1)}, u32[]{:S(2)}, u32[]{:S(2)}) collective-permute-start(f32[256,128]{1,0:T(8,128)S(1)} %get-tuple-element.19), channel_id=1, source_target_pairs={{0,1},{1,0},{2,3},{3,2},{4,5},{5,4},{6,7},{7,6},{8,9},{9,8},{10,11... | collective-permute-start | bytes 393224 | tf_op jit(solution)/shard_map/ppermute | solution.py:163
  19.8 5.8 %collective-permute-start.4 = (f32[256,128]{1,0:T(8,128)S(1)}, f32[256,128]{1,0:T(8,128)S(1)}, u32[]{:S(2)}, u32[]{:S(2)}) collective-permute-start(f32[256,128]{1,0:T(8,128)S(1)} %add.16), channel_id=1, source_target_pairs={{2,0},{3,1},{0,2},{1,3},{6,4},{7,5},{4,6},{5,7},{10,8},{11,9},{8,1... | collective-permute-start | bytes 393224 | tf_op jit(solution)/shard_map/ppermute | solution.py:169
  25.6 6.2 %collective-permute-start.8 = (f32[256,128]{1,0:T(8,128)S(1)}, f32[256,128]{1,0:T(8,128)S(1)}, u32[]{:S(2)}, u32[]{:S(2)}) collective-permute-start(f32[256,128]{1,0:T(8,128)S(1)} %get-tuple-element.27), channel_id=1, source_target_pairs={{3,0},{1,5},{2,10},{0,15},{7,4},{5,9},{6,14},{4,3},{11,8},{9,13},{... | collective-permute-start | bytes 393224 | tf_op jit(solution)/shard_map/ppermute | solution.py:153
  28.3 5.4 %collective-permute-start.7 = (f32[256,128]{1,0:T(8,128)S(1)}, f32[256,128]{1,0:T(8,128)S(1)}, u32[]{:S(2)}, u32[]{:S(2)}) collective-permute-start(f32[256,128]{1,0:T(8,128)S(1)} %get-tuple-element.27), channel_id=1, source_target_pairs={{1,0},{3,5},{0,10},{2,15},{5,4},{7,9},{4,14},{6,3},{9,8},{11,13},{... | collective-permute-start | bytes 393224 | tf_op jit(solution)/shard_map/ppermute | solution.py:153
  28.9 7.2 %collective-permute-start.6 = (f32[256,128]{1,0:T(8,128)S(1)}, f32[256,128]{1,0:T(8,128)S(1)}, u32[]{:S(2)}, u32[]{:S(2)}) collective-permute-start(f32[256,128]{1,0:T(8,128)S(1)} %get-tuple-element.27), channel_id=1, source_target_pairs={{2,0},{0,5},{3,10},{1,15},{6,4},{4,9},{7,14},{5,3},{10,8},{8,13},{... | collective-permute-start | bytes 393224 | tf_op jit(solution)/shard_map/ppermute | solution.py:153
  28.9 7.2 %collective-permute-start.5 = (f32[256,128]{1,0:T(8,128)S(1)}, f32[256,128]{1,0:T(8,128)S(1)}, u32[]{:S(2)}, u32[]{:S(2)}) collective-permute-start(f32[256,128]{1,0:T(8,128)S(1)} %get-tuple-element.27), channel_id=1, source_target_pairs={{0,0},{2,5},{1,10},{3,15},{4,4},{6,9},{5,14},{7,3},{8,8},{10,13},{... | collective-permute-start | bytes 393224 | tf_op jit(solution)/shard_map/ppermute | solution.py:153
  36.8 4.0 %collective-permute-start.10 = (f32[256,128]{1,0:T(8,128)S(1)}, f32[256,128]{1,0:T(8,128)S(1)}, u32[]{:S(2)}, u32[]{:S(2)}) collective-permute-start(f32[256,128]{1,0:T(8,128)S(1)} %get-tuple-element.26), channel_id=1, source_target_pairs={{0,1},{1,0},{2,3},{3,2},{4,5},{5,4},{6,7},{7,6},{8,9},{9,8},{10,11... | collective-permute-start | bytes 393224 | tf_op jit(solution)/shard_map/ppermute | solution.py:163
  39.8 4.1 %collective-permute-start.9 = (f32[256,128]{1,0:T(8,128)S(1)}, f32[256,128]{1,0:T(8,128)S(1)}, u32[]{:S(2)}, u32[]{:S(2)}) collective-permute-start(f32[256,128]{1,0:T(8,128)S(1)} %get-tuple-element.24), channel_id=1, source_target_pairs={{0,1},{1,0},{2,3},{3,2},{4,5},{5,4},{6,7},{7,6},{8,9},{9,8},{10,11... | collective-permute-start | bytes 393224 | tf_op jit(solution)/shard_map/ppermute | solution.py:163
  40.9 6.9 %collective-permute-start.11 = (f32[256,128]{1,0:T(8,128)S(1)}, f32[256,128]{1,0:T(8,128)S(1)}, u32[]{:S(2)}, u32[]{:S(2)}) collective-permute-start(f32[256,128]{1,0:T(8,128)S(1)} %add.19), channel_id=1, source_target_pairs={{2,0},{3,1},{0,2},{1,3},{6,4},{7,5},{4,6},{5,7},{10,8},{11,9},{8,1... | collective-permute-start | bytes 393224 | tf_op jit(solution)/shard_map/ppermute | solution.py:169

commit v27 on v26

--- a/solution.py
+++ b/solution.py
@@ -214,7 +214,8 @@
     degrees = degrees.reshape(panel_rows // tile_size, tile_size)
 
     panel = fetch(embeddings, lambda team: spread[team], arc_length)
-    pieces = [fetch(degrees, lambda team: spread[team], arc_length), panel]
+    beside = (3, 1, 2, 0) if team_count == 4 else spread
+    pieces = [fetch(degrees, lambda team: beside[team], arc_length), panel]
     info = jnp.concatenate([slot_counts[0, 0][:, None], tile_rows[0, 0], tile_columns[0, 0]], axis=1)
     info = jnp.broadcast_to(info[:, :, None], (*info.shape, embeddings.shape[1]))
     info = [info[at] for at in range(arc_length)]

time: 48.8 us -> 49 us (level)
  starting transfers between devices: 20 us -> 22.4 us
  waiting for transfers between devices: 21.1 us -> 18.9 us
    ppermute x6, waiting for transfers between devices: 10.7 us -> 8.31 us  [fetch(): return lax.ppermute(value, ('blk', 'rep'), pairs)]
    ppermute x6, starting transfers between devices: 7.44 us -> 9.66 us  [fetch(): return lax.ppermute(value, ('blk', 'rep'), pairs)]
where the time goes in v27:
time: 49 us; the launch traced here: 48.7 us
  starting transfers between devices  22.4 us (46%)
  waiting for transfers between devices  18.9 us (39%)
  local copies, waits for them, and re-layouts  3.52 us (7%)
  Pallas kernels  3.01 us (6%)
  between operations  0.72 us (1%)
    ppermute x6, starting transfers between devices, fetch(): return lax.ppermute(value, ('blk', 'rep'), pairs)  9.66 us
    ppermute x2, waiting for transfers between devices, from_column(): return lax.ppermute(value, 'rep', pairs)  8.79 us
    ppermute x4, starting transfers between devices, from_mate(): lax.ppermute(value, 'rep', [(team, team ^ 1) for team in range(team_count)])  8.75 us
    ppermute x6, waiting for transfers between devices, fetch(): return lax.ppermute(value, ('blk', 'rep'), pairs)  8.31 us
    ppermute x2, starting transfers between devices, from_column(): return lax.ppermute(value, 'rep', pairs)  3.95 us
    unnamed x10, local copies, waits for them, and re-layouts  3.44 us
    ppermute x4, waiting for transfers between devices, from_mate(): lax.ppermute(value, 'rep', [(team, team ^ 1) for team in range(team_count)])  1.82 us
    pallas_call x2, Pallas kernels, arc_step(): pl.pallas_call(functools.partial(arc_kernel, team_count=team_count, piece...  1.73 us
  transfers between devices with their start and end apart: 12, of which 8 were waited for; matrix products, arithmetic and copies ran while one was open for 0% of the time, Pallas kernels for 1%

profile of v27, /device:TPU:0, one launch (start us, length us, event | category | flops | bytes accessed | tf_op | source)
XLA Modules:
  0.0 48.7 jit_solution(7781395664922851409)
XLA Ops:
  0.0 2.5 %collective-permute-start.1 = (f32[1024,128]{1,0:T(8,128)}, f32[1024,128]{1,0:T(8,128)S(1)}, u32[]{:S(2)}, u32[]{:S(2)}) collective-permute-start(f32[1024,128]{1,0:T(8,128)} %embeddings_ref.1), channel_id=1, source_target_pairs={{2,0},{0,5},{3,10},{1,15},{6,4},{4,9},{7,14},{5,3},{10,8},{8,13},{... | collective-permute-start | bytes 1572872 | tf_op jit(solution)/shard_map/ppermute | solution.py:153
  2.5 3.6 %collective-permute-start = (s32[8,128]{1,0:T(8,128)}, s32[8,128]{1,0:T(8,128)S(1)}, u32[]{:S(2)}, u32[]{:S(2)}) collective-permute-start(s32[8,128]{1,0:T(8,128)} %bitcast.12), channel_id=1, source_target_pairs={{3,0},{1,5},{2,10},{0,15},{7,4},{5,9},{6,14},{4,3},{11,8},{9,13},{... | collective-permute-start | bytes 12296 | tf_op jit(solution)/shard_map/ppermute | solution.py:153
  6.7 0.6 %copy-done.3 = s32[1,1,1,24]{3,2,1,0:T(1,128)S(1)} copy-done((s32[1,1,1,24]{3,2,1,0:T(1,128)S(1)}, s32[1,1,1,24]{3,2,1,0:T(1,128)}, u32[]{:S(2)}) %copy-start.3) | copy-done | bytes 120
  7.3 0.0 copy-done.4
  7.4 0.1 add_bitcast_fusion
  7.4 0.1 squeeze.19.after_ref.info_ref
  7.5 0.6 %copy-done.2 = s32[1024]{0:T(1024)S(1)} copy-done((s32[1024]{0:T(1024)S(1)}, s32[1024]{0:T(1024)}, u32[]{:S(2)}) %copy-start.2) | copy-done | bytes 4120
  8.1 1.1 %copy-done = bf16[1,1,1,24,128,128]{5,4,3,2,1,0:T(8,128)(2,1)S(1)} copy-done((bf16[1,1,1,24,128,128]{5,4,3,2,1,0:T(8,128)(2,1)S(1)}, bf16[1,1,1,24,128,128]{5,4,3,2,1,0:T(8,128)(2,1)}, u32[]{:S(2)}) %copy-start) | copy-done | bytes 786456
  9.3 1.0 %copy-done.1 = f32[1024,128]{1,0:T(8,128)S(1)} copy-done((f32[1024,128]{1,0:T(8,128)S(1)}, f32[1024,128]{1,0:T(8,128)}, u32[]{:S(2)}) %copy-start.1) | copy-done | bytes 524312
  10.3 0.6 %shard_map.64 = (bf16[1,24,128,128]{3,2,1,0:T(8,128)(2,1)S(1)}, f32[256,128]{1,0:T(8,128)S(1)}, f32[256,128]{1,0:T(8,128)S(1)}) custom-call(s32[8,128]{1,0:T(8,128)S(1)} %bitcast.13, f32[1024,128]{1,0:T(8,128)S(1)} %copy-done.1, bf16[1,24,128,128]{3,2,1,0:T(8,128)(2,1)S(1)} %bitcast.11, s32[49,128]{1,0:T(8,128)S(1)} %squeeze.19.after_ref.info_ref), custom_call_target="tpu_custom_call" | custom-call | flops 131072 | bytes 524288 | tf_op jit(solution)/shard_map/pallas_call | solution.py:56
  10.9 1.8 %collective-permute-done.refs_0_ = s32[8,128]{1,0:T(8,128)S(1)} collective-permute-done((s32[8,128]{1,0:T(8,128)}, s32[8,128]{1,0:T(8,128)S(1)}, u32[]{:S(2)}, u32[]{:S(2)}) %collective-permute-start) | collective-permute-done | bytes 4128 | tf_op jit(solution)/shard_map/ppermute | solution.py:153
  12.7 0.0 collective-permute-done.1.refs_1_
  12.7 1.0 %shard_map.65 = (f32[256,128]{1,0:T(8,128)S(1)}, f32[256,128]{1,0:T(8,128)S(1)}, f32[256,128]{1,0:T(8,128)S(1)}, f32[256,128]{1,0:T(8,128)S(1)}) custom-call(s32[49,128]{1,0:T(8,128)S(1)} %squeeze.19.after_ref.info_ref, bf16[24,128,128]{2,1,0:T(8,128)(2,1)S(1)} %bitcast.9, s32[8,128]{1,0:T(8,128)S(1)} %collective-permute-done.refs_0_, ...), custom_call_target="tpu_custom_call" | custom-call | flops 201326592 | bytes 1048576 | tf_op jit(solution)/shard_map/pallas_call | solution.py:124
  13.6 5.4 %collective-permute-start.3 = (f32[256,128]{1,0:T(8,128)S(1)}, f32[256,128]{1,0:T(8,128)S(1)}, u32[]{:S(2)}, u32[]{:S(2)}) collective-permute-start(f32[256,128]{1,0:T(8,128)S(1)} %get-tuple-element.21), channel_id=1, source_target_pairs={{0,1},{1,0},{2,3},{3,2},{4,5},{5,4},{6,7},{7,6},{8,9},{9,8},{10,11... | collective-permute-start | bytes 393224 | tf_op jit(solution)/shard_map/ppermute | solution.py:163
  19.0 0.1 collective-permute-start.2
  19.1 0.9 %collective-permute-done.3 = f32[256,128]{1,0:T(8,128)S(1)} collective-permute-done((f32[256,128]{1,0:T(8,128)S(1)}, f32[256,128]{1,0:T(8,128)S(1)}, u32[]{:S(2)}, u32[]{:S(2)}) %collective-permute-start.3) | collective-permute-done | bytes 131104 | tf_op jit(solution)/shard_map/ppermute | solution.py:163
  20.0 0.8 %collective-permute-start.4 = (f32[256,128]{1,0:T(8,128)S(1)}, f32[256,128]{1,0:T(8,128)S(1)}, u32[]{:S(2)}, u32[]{:S(2)}) collective-permute-start(f32[256,128]{1,0:T(8,128)S(1)} %add.16), channel_id=1, source_target_pairs={{2,0},{3,1},{0,2},{1,3},{6,4},{7,5},{4,6},{5,7},{10,8},{11,9},{8,1... | collective-permute-start | bytes 393224 | tf_op jit(solution)/shard_map/ppermute | solution.py:169
  20.8 0.0 collective-permute-done.2
  20.8 5.0 %collective-permute-done.4 = f32[256,128]{1,0:T(8,128)S(1)} collective-permute-done((f32[256,128]{1,0:T(8,128)S(1)}, f32[256,128]{1,0:T(8,128)S(1)}, u32[]{:S(2)}, u32[]{:S(2)}) %collective-permute-start.4) | collective-permute-done | bytes 131104 | tf_op jit(solution)/shard_map/ppermute | solution.py:169
  25.9 2.5 %collective-permute-start.8 = (f32[256,128]{1,0:T(8,128)S(1)}, f32[256,128]{1,0:T(8,128)S(1)}, u32[]{:S(2)}, u32[]{:S(2)}) collective-permute-start(f32[256,128]{1,0:T(8,128)S(1)} %get-tuple-element.27), channel_id=1, source_target_pairs={{3,0},{1,5},{2,10},{0,15},{7,4},{5,9},{6,14},{4,3},{11,8},{9,13},{... | collective-permute-start | bytes 393224 | tf_op jit(solution)/shard_map/ppermute | solution.py:153
  28.3 0.5 %collective-permute-start.7 = (f32[256,128]{1,0:T(8,128)S(1)}, f32[256,128]{1,0:T(8,128)S(1)}, u32[]{:S(2)}, u32[]{:S(2)}) collective-permute-start(f32[256,128]{1,0:T(8,128)S(1)} %get-tuple-element.27), channel_id=1, source_target_pairs={{1,0},{3,5},{0,10},{2,15},{5,4},{7,9},{4,14},{6,3},{9,8},{11,13},{... | collective-permute-start | bytes 393224 | tf_op jit(solution)/shard_map/ppermute | solution.py:153
  28.9 0.7 %collective-permute-start.5 = (f32[256,128]{1,0:T(8,128)S(1)}, f32[256,128]{1,0:T(8,128)S(1)}, u32[]{:S(2)}, u32[]{:S(2)}) collective-permute-start(f32[256,128]{1,0:T(8,128)S(1)} %get-tuple-element.27), channel_id=1, source_target_pairs={{0,0},{2,5},{1,10},{3,15},{4,4},{6,9},{5,14},{7,3},{8,8},{10,13},{... | collective-permute-start | bytes 393224 | tf_op jit(solution)/shard_map/ppermute | solution.py:153
  29.5 2.2 %collective-permute-done.8.refs_3_ = f32[256,128]{1,0:T(8,128)S(1)} collective-permute-done((f32[256,128]{1,0:T(8,128)S(1)}, f32[256,128]{1,0:T(8,128)S(1)}, u32[]{:S(2)}, u32[]{:S(2)}) %collective-permute-start.8) | collective-permute-done | bytes 131104 | tf_op jit(solution)/shard_map/ppermute | solution.py:153
  31.7 2.0 %collective-permute-done.7.refs_2_ = f32[256,128]{1,0:T(8,128)S(1)} collective-permute-done((f32[256,128]{1,0:T(8,128)S(1)}, f32[256,128]{1,0:T(8,128)S(1)}, u32[]{:S(2)}, u32[]{:S(2)}) %collective-permute-start.7) | collective-permute-done | bytes 131104 | tf_op jit(solution)/shard_map/ppermute | solution.py:153
  33.7 2.3 %collective-permute-done.6.refs_1_ = f32[256,128]{1,0:T(8,128)S(1)} collective-permute-done((f32[256,128]{1,0:T(8,128)S(1)}, f32[256,128]{1,0:T(8,128)S(1)}, u32[]{:S(2)}, u32[]{:S(2)}) %collective-permute-start.6) | collective-permute-done | bytes 131104 | tf_op jit(solution)/shard_map/ppermute | solution.py:153
  36.1 0.8 %shard_map.66 = (f32[256,128]{1,0:T(8,128)S(1)}, f32[256,128]{1,0:T(8,128)S(1)}, f32[256,128]{1,0:T(8,128)S(1)}, f32[256,128]{1,0:T(8,128)S(1)}) custom-call(s32[49,128]{1,0:T(8,128)S(1)} %squeeze.19.after_ref.info_ref, bf16[24,128,128]{2,1,0:T(8,128)(2,1)S(1)} %bitcast.10, f32[256,128]{1,0:T(8,128)S(1)} %collective-permute-done.5.refs_0_, ...), custom_call_target="tpu_custom_call" | custom-call | flops 201326592 | bytes 1048576 | tf_op jit(solution)/shard_map/pallas_call | solution.py:124
  36.8 3.2 %collective-permute-start.10 = (f32[256,128]{1,0:T(8,128)S(1)}, f32[256,128]{1,0:T(8,128)S(1)}, u32[]{:S(2)}, u32[]{:S(2)}) collective-permute-start(f32[256,128]{1,0:T(8,128)S(1)} %get-tuple-element.26), channel_id=1, source_target_pairs={{0,1},{1,0},{2,3},{3,2},{4,5},{5,4},{6,7},{7,6},{8,9},{9,8},{10,11... | collective-permute-start | bytes 393224 | tf_op jit(solution)/shard_map/ppermute | solution.py:163
  40.1 0.1 collective-permute-start.9
  40.1 0.9 %collective-permute-done.10 = f32[256,128]{1,0:T(8,128)S(1)} collective-permute-done((f32[256,128]{1,0:T(8,128)S(1)}, f32[256,128]{1,0:T(8,128)S(1)}, u32[]{:S(2)}, u32[]{:S(2)}) %collective-permute-start.10) | collective-permute-done | bytes 131104 | tf_op jit(solution)/shard_map/ppermute | solution.py:163
  41.1 3.1 %collective-permute-start.11 = (f32[256,128]{1,0:T(8,128)S(1)}, f32[256,128]{1,0:T(8,128)S(1)}, u32[]{:S(2)}, u32[]{:S(2)}) collective-permute-start(f32[256,128]{1,0:T(8,128)S(1)} %add.19), channel_id=1, source_target_pairs={{2,0},{3,1},{0,2},{1,3},{6,4},{7,5},{4,6},{5,7},{10,8},{11,9},{8,1... | collective-permute-start | bytes 393224 | tf_op jit(solution)/shard_map/ppermute | solution.py:169
  44.2 3.8 %collective-permute-done.11.refs_2_ = f32[256,128]{1,0:T(8,128)S(1)} collective-permute-done((f32[256,128]{1,0:T(8,128)S(1)}, f32[256,128]{1,0:T(8,128)S(1)}, u32[]{:S(2)}, u32[]{:S(2)}) %collective-permute-start.11) | collective-permute-done | bytes 131104 | tf_op jit(solution)/shard_map/ppermute | solution.py:169
  48.0 0.7 %shard_map.67 = f32[256,128]{1,0:T(8,128)} custom-call(f32[256,128]{1,0:T(8,128)S(1)} %get-tuple-element.28.base_ref, f32[256,128]{1,0:T(8,128)S(1)} %get-tuple-element.22.norm_ref, f32[256,128]{1,0:T(8,128)S(1)} %get-tuple-element.23.refs_0_, f32[256,128]{1,0:T(8,128)S(1)} %collective-permute-done.9.refs_1_, f32[256,128]{1,0:T(8,128)S(1)} %collective-permute-done.11.refs_2_), custom_call_target="tpu_custom_call" | custom-call | tf_op jit(solution)/shard_map/pallas_call | solution.py:199
  (11 shorter events, 0.1 us)
Async XLA Ops:
  0.0 12.7 %collective-permute-start.1 = (f32[1024,128]{1,0:T(8,128)}, f32[1024,128]{1,0:T(8,128)S(1)}, u32[]{:S(2)}, u32[]{:S(2)}) collective-permute-start(f32[1024,128]{1,0:T(8,128)} %embeddings_ref.1), channel_id=1, source_target_pairs={{2,0},{0,5},{3,10},{1,15},{6,4},{4,9},{7,14},{5,3},{10,8},{8,13},{... | collective-permute-start | bytes 1572872 | tf_op jit(solution)/shard_map/ppermute | solution.py:153
  2.5 10.2 %collective-permute-start = (s32[8,128]{1,0:T(8,128)}, s32[8,128]{1,0:T(8,128)S(1)}, u32[]{:S(2)}, u32[]{:S(2)}) collective-permute-start(s32[8,128]{1,0:T(8,128)} %bitcast.12), channel_id=1, source_target_pairs={{3,0},{1,5},{2,10},{0,15},{7,4},{5,9},{6,14},{4,3},{11,8},{9,13},{... | collective-permute-start | bytes 12296 | tf_op jit(solution)/shard_map/ppermute | solution.py:153
  6.7 0.7 %copy-start.3 = (s32[1,1,1,24]{3,2,1,0:T(1,128)S(1)}, s32[1,1,1,24]{3,2,1,0:T(1,128)}, u32[]{:S(2)}) copy-start(s32[1,1,1,24]{3,2,1,0:T(1,128)} %param.10) | copy-start | bytes 292
  6.7 0.7 %copy-start.4 = (s32[1,1,1,24]{3,2,1,0:T(1,128)S(1)}, s32[1,1,1,24]{3,2,1,0:T(1,128)}, u32[]{:S(2)}) copy-start(s32[1,1,1,24]{3,2,1,0:T(1,128)} %param.9) | copy-start | bytes 292
  7.4 0.7 %copy-start.2 = (s32[1024]{0:T(1024)S(1)}, s32[1024]{0:T(1024)}, u32[]{:S(2)}) copy-start(s32[1024]{0:T(1024)} %param.7) | copy-start | bytes 12292
  8.1 1.1 %copy-start = (bf16[1,1,1,24,128,128]{5,4,3,2,1,0:T(8,128)(2,1)S(1)}, bf16[1,1,1,24,128,128]{5,4,3,2,1,0:T(8,128)(2,1)}, u32[]{:S(2)}) copy-start(bf16[1,1,1,24,128,128]{5,4,3,2,1,0:T(8,128)(2,1)} %param.8) | copy-start | bytes 2359300
  9.3 1.0 %copy-start.1 = (f32[1024,128]{1,0:T(8,128)S(1)}, f32[1024,128]{1,0:T(8,128)}, u32[]{:S(2)}) copy-start(f32[1024,128]{1,0:T(8,128)} %embeddings_ref.1) | copy-start | bytes 1572868
  13.6 6.3 %collective-permute-start.3 = (f32[256,128]{1,0:T(8,128)S(1)}, f32[256,128]{1,0:T(8,128)S(1)}, u32[]{:S(2)}, u32[]{:S(2)}) collective-permute-start(f32[256,128]{1,0:T(8,128)S(1)} %get-tuple-element.21), channel_id=1, source_target_pairs={{0,1},{1,0},{2,3},{3,2},{4,5},{5,4},{6,7},{7,6},{8,9},{9,8},{10,11... | collective-permute-start | bytes 393224 | tf_op jit(solution)/shard_map/ppermute | solution.py:163
  19.0 1.8 %collective-permute-start.2 = (f32[256,128]{1,0:T(8,128)S(1)}, f32[256,128]{1,0:T(8,128)S(1)}, u32[]{:S(2)}, u32[]{:S(2)}) collective-permute-start(f32[256,128]{1,0:T(8,128)S(1)} %get-tuple-element.19), channel_id=1, source_target_pairs={{0,1},{1,0},{2,3},{3,2},{4,5},{5,4},{6,7},{7,6},{8,9},{9,8},{10,11... | collective-permute-start | bytes 393224 | tf_op jit(solution)/shard_map/ppermute | solution.py:163
  20.0 5.8 %collective-permute-start.4 = (f32[256,128]{1,0:T(8,128)S(1)}, f32[256,128]{1,0:T(8,128)S(1)}, u32[]{:S(2)}, u32[]{:S(2)}) collective-permute-start(f32[256,128]{1,0:T(8,128)S(1)} %add.16), channel_id=1, source_target_pairs={{2,0},{3,1},{0,2},{1,3},{6,4},{7,5},{4,6},{5,7},{10,8},{11,9},{8,1... | collective-permute-start | bytes 393224 | tf_op jit(solution)/shard_map/ppermute | solution.py:169
  25.9 5.8 %collective-permute-start.8 = (f32[256,128]{1,0:T(8,128)S(1)}, f32[256,128]{1,0:T(8,128)S(1)}, u32[]{:S(2)}, u32[]{:S(2)}) collective-permute-start(f32[256,128]{1,0:T(8,128)S(1)} %get-tuple-element.27), channel_id=1, source_target_pairs={{3,0},{1,5},{2,10},{0,15},{7,4},{5,9},{6,14},{4,3},{11,8},{9,13},{... | collective-permute-start | bytes 393224 | tf_op jit(solution)/shard_map/ppermute | solution.py:153
  28.3 5.4 %collective-permute-start.7 = (f32[256,128]{1,0:T(8,128)S(1)}, f32[256,128]{1,0:T(8,128)S(1)}, u32[]{:S(2)}, u32[]{:S(2)}) collective-permute-start(f32[256,128]{1,0:T(8,128)S(1)} %get-tuple-element.27), channel_id=1, source_target_pairs={{1,0},{3,5},{0,10},{2,15},{5,4},{7,9},{4,14},{6,3},{9,8},{11,13},{... | collective-permute-start | bytes 393224 | tf_op jit(solution)/shard_map/ppermute | solution.py:153
  28.9 7.2 %collective-permute-start.6 = (f32[256,128]{1,0:T(8,128)S(1)}, f32[256,128]{1,0:T(8,128)S(1)}, u32[]{:S(2)}, u32[]{:S(2)}) collective-permute-start(f32[256,128]{1,0:T(8,128)S(1)} %get-tuple-element.27), channel_id=1, source_target_pairs={{2,0},{0,5},{3,10},{1,15},{6,4},{4,9},{7,14},{5,3},{10,8},{8,13},{... | collective-permute-start | bytes 393224 | tf_op jit(solution)/shard_map/ppermute | solution.py:153
  28.9 7.2 %collective-permute-start.5 = (f32[256,128]{1,0:T(8,128)S(1)}, f32[256,128]{1,0:T(8,128)S(1)}, u32[]{:S(2)}, u32[]{:S(2)}) collective-permute-start(f32[256,128]{1,0:T(8,128)S(1)} %get-tuple-element.27), channel_id=1, source_target_pairs={{0,0},{2,5},{1,10},{3,15},{4,4},{6,9},{5,14},{7,3},{8,8},{10,13},{... | collective-permute-start | bytes 393224 | tf_op jit(solution)/shard_map/ppermute | solution.py:153
  36.8 4.2 %collective-permute-start.10 = (f32[256,128]{1,0:T(8,128)S(1)}, f32[256,128]{1,0:T(8,128)S(1)}, u32[]{:S(2)}, u32[]{:S(2)}) collective-permute-start(f32[256,128]{1,0:T(8,128)S(1)} %get-tuple-element.26), channel_id=1, source_target_pairs={{0,1},{1,0},{2,3},{3,2},{4,5},{5,4},{6,7},{7,6},{8,9},{9,8},{10,11... | collective-permute-start | bytes 393224 | tf_op jit(solution)/shard_map/ppermute | solution.py:163
  40.1 4.1 %collective-permute-start.9 = (f32[256,128]{1,0:T(8,128)S(1)}, f32[256,128]{1,0:T(8,128)S(1)}, u32[]{:S(2)}, u32[]{:S(2)}) collective-permute-start(f32[256,128]{1,0:T(8,128)S(1)} %get-tuple-element.24), channel_id=1, source_target_pairs={{0,1},{1,0},{2,3},{3,2},{4,5},{5,4},{6,7},{7,6},{8,9},{9,8},{10,11... | collective-permute-start | bytes 393224 | tf_op jit(solution)/shard_map/ppermute | solution.py:163
  41.1 6.9 %collective-permute-start.11 = (f32[256,128]{1,0:T(8,128)S(1)}, f32[256,128]{1,0:T(8,128)S(1)}, u32[]{:S(2)}, u32[]{:S(2)}) collective-permute-start(f32[256,128]{1,0:T(8,128)S(1)} %add.19), channel_id=1, source_target_pairs={{2,0},{3,1},{0,2},{1,3},{6,4},{7,5},{4,6},{5,7},{10,8},{11,9},{8,1... | collective-permute-start | bytes 393224 | tf_op jit(solution)/shard_map/ppermute | solution.py:169
